TPU v7x, 256 devices: a whole 4x4x8 slice. The times are simulated.
256 devices in a mesh: dp: 64 (over y_hi, z, x), tensor: 4 (over y_lo, core).
Axes of the slice: x: 4, y: 4 (y_hi: 2, y_lo: 2; y = y_hi * 2 + y_lo), z: 8, core: 2. Of those that a mesh axis runs over, the one named last changes fastest.
Arguments:
- image_vectors_raw: bfloat16 [16384, 1152], P('dp'), may hold values from -0.5 to 0.5
- text_vectors_raw: bfloat16 [16384, 1152], P('dp'), may hold values from -0.5 to 0.5
- logit_scale_logarithm: float32 [1], replicated, may hold values from 2 to 3
- logit_offset_bias: float32 [1], replicated, may hold values from -10 to -7
Outputs:
- grad_image: float32 [16384, 1152], P(('dp', 'tensor'))
- grad_text: float32 [16384, 1152], P(('dp', 'tensor'))
- image_loss: float32 [16384], P(('dp', 'tensor'))
- text_loss: float32 [16384], P(('dp', 'tensor'))
- param_grads: float32 [2], replicated
All inputs are finite; a program needn't handle non-finite values.
Results may differ from a plain program's by a relative error of at most 0.0023.
Values may be sent and summed in bfloat16 or wider, within the bound.
No kernel may reach another device: no remote copies, remote signals or barrier semaphores. Data moves between devices by JAX's collectives and lax.ppermute only.
A program may use at most 64 MiB of HBM per device.

v0:
```python
import jax
import jax.numpy as jnp
from jax import lax
from jax.experimental import pallas as pl
from jax.experimental.pallas import tpu as pltpu
from jax.sharding import Mesh, PartitionSpec as P

AXES = ("yh", "z", "x", "yl", "core")
YH, NZ, NX, YL, NC = 2, 8, 4, 2, 2
Q = 64


def table(move):
    pairs = []
    for yh in range(YH):
        for z in range(NZ):
            for x in range(NX):
                for yl in range(YL):
                    for c in range(NC):
                        y2, z2, x2, c2 = move(yh * 2 + yl, z, x, c)
                        y2, z2, x2 = y2 % 4, z2 % NZ, x2 % NX
                        source = (((yh * NZ + z) * NX + x) * YL + yl) * NC + c
                        target = (((y2 // 2 * NZ + z2) * NX + x2) * YL + y2 % 2) * NC + c2
                        pairs.append((source, target))
    return pairs


def send(value, dx=0, dz=0, fy=0, fz=0, fx=0, fc=0, split_z=0):
    pairs = table(
        lambda y, z, x, c: (y ^ fy, (z + dz + (1 - 2 * c) * split_z) ^ fz, (x + dx) ^ fx, c ^ fc)
    )
    return lax.ppermute(value, AXES, pairs)


def rounded(value):
    return lax.reduce_precision(value, 8, 7)


def normalize(embedding):
    floats = embedding.astype(jnp.float32)
    inverse = lax.rsqrt(jnp.sum(floats * floats, axis=-1, keepdims=True) + 1e-06)
    return (floats * inverse, inverse)


ROWS = 256


def pair_kernel(par_ref, *refs):
    a0, r1, r2, r3, r4, e12, e34 = refs[:7]
    txt_in = refs[7:15]
    gi_ref, gt_ref, li_ref, lt_ref, sums_ref, img, txt = refs[15:]
    z, x = lax.axis_index("z"), lax.axis_index("x")
    yh, core = lax.axis_index("yh"), lax.axis_index("core")
    sign = 1 - 2 * core
    img[0:64, :] = a0[pl.ds(pl.multiple_of(core * Q, Q), Q), :]
    img[64:320, :] = e12[...]
    img[320:448, :] = e34[0:128, :]
    img[448:512, :] = r4[...]
    img[512:576, :] = a0[pl.ds(pl.multiple_of((1 - core) * Q, Q), Q), :]
    img[576:704, :] = r1[...]
    img[704:832, :] = r2[...]
    img[832:960, :] = r3[...]
    img[960:1024, :] = e34[128:192, :]
    image_places = [(z, core)]
    image_places += [(z + sign * k, q) for k in range(1, 4) for q in range(2)]
    image_places += [(z + 4, core), (z, 1 - core)]
    image_places += [(z - sign * k, q) for k in range(1, 4) for q in range(2)]
    image_places += [(z + 4, 1 - core)]
    text_places = [
        (h * NX + lax.rem(x + dx, NX)) * 2 for h in (yh, 1 - yh) for dx in (0, NX - 1, 1, 2)
    ]
    own_column = (text_places[0] + lax.axis_index("yl")) * Q
    for k, ref in enumerate(txt_in):
        rows = ref.shape[0]
        txt[pl.ds(pl.multiple_of(text_places[k] * Q, Q), rows), :] = ref[...]
    temperature = par_ref[0]
    offset = par_ref[1]
    texts = txt[...]
    loss_cols = slope_sum = scale_sum = None
    for r in range(1024 // ROWS):
        images = img[r * ROWS : (r + 1) * ROWS, :]
        scores = lax.dot_general(
            images, texts, (((1,), (1,)), ((), ())), preferred_element_type=jnp.float32
        )
        p = jnp.exp(scores * temperature + offset)
        if r == 0:
            row = lax.broadcasted_iota(jnp.int32, (ROWS, 1024), 0)
            column = lax.broadcasted_iota(jnp.int32, (ROWS, 1024), 1)
            match = (column - row == own_column) & (row < Q)
            p = jnp.where(match, 0.0, p)
        q = 1.0 + p
        slopes = p / q
        losses = jnp.where(p < 0.0009765625, p - 0.5 * p * p, jnp.log(q))
        weights = (temperature * slopes).astype(jnp.bfloat16)
        gi_ref[r * ROWS : (r + 1) * ROWS, :] = jnp.dot(
            weights, texts, preferred_element_type=jnp.float32
        )
        back = lax.dot_general(
            weights, images, (((0,), (0,)), ((), ())), preferred_element_type=jnp.float32
        )
        row_losses = jnp.sum(losses, axis=1, keepdims=True)
        for k in range(ROWS // Q):
            zz, q = image_places[r * ROWS // Q + k]
            start = (q * NZ + lax.rem(zz + NZ, NZ)) * Q
            li_ref[pl.ds(pl.multiple_of(start, Q), Q), :] = row_losses[k * Q : (k + 1) * Q]
        cols = jnp.sum(losses, axis=0, keepdims=True)
        s1 = jnp.sum(slopes, axis=0, keepdims=True)
        s2 = jnp.sum(slopes * scores, axis=0, keepdims=True)
        if r == 0:
            gt_ref[...] = back
            loss_cols, slope_sum, scale_sum = cols, s1, s2
        else:
            gt_ref[...] += back
            loss_cols, slope_sum, scale_sum = loss_cols + cols, slope_sum + s1, scale_sum + s2
    lt_ref[...] = loss_cols
    sums_ref[0:1, :] = temperature * scale_sum
    sums_ref[1:2, :] = slope_sum


def pairs_on_device(params, chunks):
    width = chunks[0].shape[1]
    vmem = pl.BlockSpec(memory_space=pltpu.VMEM)
    smem = pl.BlockSpec(memory_space=pltpu.SMEM)
    f32 = jnp.float32
    return pl.pallas_call(
        pair_kernel,
        out_shape=(
            jax.ShapeDtypeStruct((1024, width), f32),
            jax.ShapeDtypeStruct((1024, width), f32),
            jax.ShapeDtypeStruct((1024, 1), f32),
            jax.ShapeDtypeStruct((1, 1024), f32),
            jax.ShapeDtypeStruct((2, 1024), f32),
        ),
        in_specs=[smem] + [vmem] * len(chunks),
        out_specs=(vmem,) * 5,
        scratch_shapes=[
            pltpu.VMEM((1024, width), jnp.bfloat16),
            pltpu.VMEM((1024, width), jnp.bfloat16),
        ],
        compiler_params=pltpu.CompilerParams(vmem_limit_bytes=48 * 1024 * 1024),
        cost_estimate=pl.CostEstimate(
            flops=6 * 1024 * 1024 * width, bytes_accessed=14 * 1024 * 1024, transcendentals=3 * 1024 * 1024
        ),
        name="pairs",
    )(params, *chunks)


def tied(*values):
    return lax.optimization_barrier(values)


def gather(a0, t0, core, own):
    r1 = send(a0, split_z=1)
    xm, xp, c0 = send(t0, dx=1), send(t0, dx=-1), send(t0, fy=3)
    a0, t0, r1, xm, xp, c0 = tied(a0, t0, r1, xm, xp, c0)
    r2 = send(r1, split_z=1)
    cm, cp = send(c0, dx=1), send(c0, dx=-1)
    f1, f2 = send(xm[:Q], dx=1), send(xp[Q:], dx=-1)
    r2, cm, cp, f1, f2, *own = tied(r2, cm, cp, f1, f2, *own)
    r3 = send(r2, split_z=1)
    g1, g2 = send(cm[:Q], dx=1), send(cp[Q:], dx=-1)
    e12 = send(jnp.concatenate([r1, r2], axis=0), fc=1)
    r3, g1, g2, e12 = tied(r3, g1, g2, e12)
    r4 = send(lax.dynamic_slice_in_dim(r3, core * Q, Q, 0), split_z=1)
    e34 = send(jnp.concatenate([r3, r4], axis=0), fc=1)
    far, far_h = jnp.concatenate([f1, f2], axis=0), jnp.concatenate([g1, g2], axis=0)
    return [a0, r1, r2, r3, r4, e12, e34, t0, xm, xp, far, c0, cm, cp, far_h], own


def per_device(image_raw, text_raw, logit_scale_logarithm, logit_offset_bias):
    z, x = lax.axis_index("z"), lax.axis_index("x")
    yh, yl, core = lax.axis_index("yh"), lax.axis_index("yl"), lax.axis_index("core")
    f32, f16, bf16 = jnp.float32, jnp.float16, jnp.bfloat16

    def quarter(block, l, c):
        return lax.dynamic_slice_in_dim(block, (l * 2 + c) * Q, Q, 0)

    a0 = normalize(lax.dynamic_slice_in_dim(image_raw, yl * 2 * Q, 2 * Q, 0))[0].astype(bf16)
    t0 = jnp.concatenate([quarter(text_raw, 0, core), quarter(text_raw, 1, core)], axis=0)
    t0 = normalize(t0)[0].astype(bf16)
    image_unit, image_inv = normalize(quarter(image_raw, yl, core))
    text_unit, text_inv = normalize(quarter(text_raw, yl, core))
    temperature, offset = jnp.exp(logit_scale_logarithm[0]), logit_offset_bias[0]
    params = jnp.stack([temperature, offset])

    image_low, text_low = rounded(image_unit), rounded(text_unit)
    match = jnp.sum(image_low * text_low, axis=-1)
    match_logit = temperature * match + offset
    match_loss = jnp.log1p(jnp.exp(-match_logit))
    match_slope = -1.0 / (1.0 + jnp.exp(match_logit))
    match_weight = rounded(temperature * match_slope)
    match_sums = jnp.stack([temperature * jnp.sum(match_slope * match), jnp.sum(match_slope)])
    own = (image_unit, text_unit, image_inv, text_inv, image_low, text_low, match_loss, match_weight, match_sums)
    chunks, own = gather(a0, t0, core, own)
    image_unit, text_unit, image_inv, text_inv, image_low, text_low, match_loss, match_weight, match_sums = own
    gi, gt, li, lt, sums = pairs_on_device(params, chunks)

    half = gi[:512] + send(gi[512:].astype(f16), fc=1).astype(f32)
    flight = half[Q:].astype(f16)
    far = send(flight[384:], dz=4)
    three, two, one = (send(flight[(k - 1) * 128 : k * 128], split_z=k) for k in (3, 2, 1))
    back_xy = lax.all_to_all(gt.astype(f16), ("yh", "x", "yl"), 0, 0, tiled=True)
    both = jnp.sum(sums, axis=1) + match_sums
    pack_c = jnp.concatenate([li.reshape(-1), both])
    for move in (dict(fc=1), dict(fz=1), dict(fz=2), dict(fz=4)):
        pack_c = pack_c + send(pack_c, **move)
    pack_r = lt.reshape(-1)
    for move in (dict(fy=1), dict(fx=1), dict(fy=3), dict(fx=2)):
        pack_r = pack_r + send(pack_r, **move)
    both = pack_c[1024:]
    for move in (dict(fy=1), dict(fx=1), dict(fy=3), dict(fx=2)):
        both = both + send(both, **move)
    far, three, two, one, pack_c, pack_r, both = tied(far, three, two, one, pack_c, pack_r, both)
    arrived = one.astype(f32) + two.astype(f32) + three.astype(f32)
    theirs = lax.dynamic_slice_in_dim(arrived, (1 - core) * Q, Q, 0)
    gi_own = half[:Q] + far.astype(f32) + lax.dynamic_slice_in_dim(arrived, core * Q, Q, 0)
    gi_own = gi_own + send(theirs, fc=1)
    gt_own = jnp.sum(back_xy.reshape(16, Q, -1).astype(f32), axis=0)

    gi_own = gi_own + match_weight[:, None] * text_low
    gt_own = gt_own + match_weight[:, None] * image_low
    grad_image = image_inv * (
        gi_own - image_unit * jnp.sum(image_unit * gi_own, axis=-1, keepdims=True)
    )
    grad_text = text_inv * (gt_own - text_unit * jnp.sum(text_unit * gt_own, axis=-1, keepdims=True))

    image_loss = lax.dynamic_slice_in_dim(pack_c, (core * 8 + z) * Q, Q, 0) + match_loss
    text_loss = lax.dynamic_slice_in_dim(pack_r, ((yh * 4 + x) * 2 + yl) * Q, Q, 0) + match_loss
    return (grad_image, grad_text, image_loss, text_loss, both)


def solution(mesh):
    fine = Mesh(mesh.devices.reshape(YH, NZ, NX, YL, NC), AXES)
    dp = ("yh", "z", "x")
    in_specs = (P(dp, None), P(dp, None), P(), P())
    out_specs = (P(AXES, None), P(AXES, None), P(AXES), P(AXES), P())
    return jax.shard_map(
        per_device, mesh=fine, in_specs=in_specs, out_specs=out_specs, check_vma=False
    )
```

profile of v0, /device:TPU:1, one launch (start us, length us, event | category | flops | bytes accessed | tf_op | source)
XLA Modules:
  0.0 160.0 jit_solution(3618792224137222469)
XLA Ops:
  0.7 1.1 constant_dynamic-slice_fusion.3
  2.0 3.7 %collective-permute-start.3 = (bf16[128,1152]{1,0:T(8,128)(2,1)S(1)}, bf16[128,1152]{1,0:T(8,128)(2,1)S(1)}, u32[]{:S(2)}, u32[]{:S(2)}) collective-permute-start(bf16[128,1152]{1,0:T(8,128)(2,1)S(1)} %fusion.3.refs_7_), channel_id=1, source_target_pairs={{0,130},{1,131},{2,128},{3,129},{4,134},{5,135},{6,132},{7,133},{8... | collective-permute-start | bytes 884744 | tf_op jit(solution)/shard_map/ppermute | solution.py:32
  5.7 2.5 %collective-permute-start.2 = (bf16[128,1152]{1,0:T(8,128)(2,1)S(1)}, bf16[128,1152]{1,0:T(8,128)(2,1)S(1)}, u32[]{:S(2)}, u32[]{:S(2)}) collective-permute-start(bf16[128,1152]{1,0:T(8,128)(2,1)S(1)} %fusion.3.refs_7_), channel_id=1, source_target_pairs={{0,12},{1,13},{2,14},{3,15},{4,0},{5,1},{6,2},{7,3},{8,4},{9,5},{1... | collective-permute-start | bytes 884744 | tf_op jit(solution)/shard_map/ppermute | solution.py:32
  8.2 1.1 fusion
  9.3 1.1 fusion.1.refs_0_
  10.4 5.7 %collective-permute-start = (bf16[128,1152]{1,0:T(8,128)(2,1)S(1)}, bf16[128,1152]{1,0:T(8,128)(2,1)S(1)}, u32[]{:S(2)}, u32[]{:S(2)}) collective-permute-start(bf16[128,1152]{1,0:T(8,128)(2,1)S(1)} %fusion.1.refs_0_), channel_id=1, source_target_pairs={{0,16},{1,113},{2,18},{3,115},{4,20},{5,117},{6,22},{7,119},{8,24}... | collective-permute-start | bytes 884744 | tf_op jit(solution)/shard_map/ppermute | solution.py:32
  16.3 0.6 fusion.10
  16.9 0.6 fusion.11
  17.4 1.2 multiply_reduce_fusion.2
  20.0 1.2 multiply_reduce_fusion.3
  21.3 2.8 %collective-permute-start.6 = (bf16[128,1152]{1,0:T(8,128)(2,1)S(1)}, bf16[128,1152]{1,0:T(8,128)(2,1)S(1)}, u32[]{:S(2)}, u32[]{:S(2)}) collective-permute-start(bf16[128,1152]{1,0:T(8,128)(2,1)S(1)} %collective-permute-done.3.refs_11_), channel_id=1, source_target_pairs={{0,12},{1,13},{2,14},{3,15},{4,0},{5,1},{6,2},{7,3},{8,4},{9,5},{1... | collective-permute-start | bytes 884744 | tf_op jit(solution)/shard_map/ppermute | solution.py:32
  24.1 2.8 %collective-permute-start.8 = (bf16[64,1152]{1,0:T(8,128)(2,1)S(1)}, bf16[64,1152]{1,0:T(8,128)(2,1)S(1)}, u32[]{:S(2)}, u32[]{:S(2)}) collective-permute-start(bf16[64,1152]{1,0:T(8,128)(2,1)S(1)} %slice.44), channel_id=1, source_target_pairs={{0,12},{1,13},{2,14},{3,15},{4,0},{5,1},{6,2},{7,3},{8,4},{9,5},{1... | collective-permute-start | bytes 442376 | tf_op jit(solution)/shard_map/ppermute | solution.py:32
  26.9 1.4 collective-permute-start.4
  28.3 0.6 multiply_reduce-precision_fusion
  29.5 0.8 pad_maximum_fusion.6
  30.3 2.1 %collective-permute-done.8 = bf16[64,1152]{1,0:T(8,128)(2,1)S(1)} collective-permute-done((bf16[64,1152]{1,0:T(8,128)(2,1)S(1)}, bf16[64,1152]{1,0:T(8,128)(2,1)S(1)}, u32[]{:S(2)}, u32[]{:S(2)}) %collective-permute-start.8) | collective-permute-done | bytes 147488 | tf_op jit(solution)/shard_map/ppermute | solution.py:32
  32.4 3.1 %collective-permute-done.7 = bf16[64,1152]{1,0:T(8,128)(2,1)S(1)} collective-permute-done((bf16[64,1152]{1,0:T(8,128)(2,1)S(1)}, bf16[64,1152]{1,0:T(8,128)(2,1)S(1)}, u32[]{:S(2)}, u32[]{:S(2)}) %collective-permute-start.7) | collective-permute-done | bytes 147488 | tf_op jit(solution)/shard_map/ppermute | solution.py:32
  35.5 0.6 copy-done.11
  36.2 2.4 %collective-permute-start.12 = (bf16[256,1152]{1,0:T(8,128)(2,1)S(1)}, bf16[256,1152]{1,0:T(8,128)(2,1)}, u32[]{:S(2)}, u32[]{:S(2)}) collective-permute-start(bf16[256,1152]{1,0:T(8,128)(2,1)S(1)} %pad_maximum_fusion), channel_id=1, source_target_pairs={{0,1},{1,0},{2,3},{3,2},{4,5},{5,4},{6,7},{7,6},{8,9},{9,8},{10,11... | collective-permute-start | bytes 1769480 | tf_op jit(solution)/shard_map/ppermute | solution.py:32
  38.6 1.4 collective-permute-start.9
  40.1 0.7 slice.45
  40.8 0.7 slice.46
  41.8 1.1 collective-permute-start.10
  42.9 3.9 %collective-permute-done.11 = bf16[64,1152]{1,0:T(8,128)(2,1)} collective-permute-done((bf16[64,1152]{1,0:T(8,128)(2,1)}, bf16[64,1152]{1,0:T(8,128)(2,1)}, u32[]{:S(2)}, u32[]{:S(2)}) %collective-permute-start.11) | collective-permute-done | bytes 147488 | tf_op jit(solution)/shard_map/ppermute | solution.py:32
  46.7 2.1 %collective-permute-done.10 = bf16[64,1152]{1,0:T(8,128)(2,1)} collective-permute-done((bf16[64,1152]{1,0:T(8,128)(2,1)}, bf16[64,1152]{1,0:T(8,128)(2,1)}, u32[]{:S(2)}, u32[]{:S(2)}) %collective-permute-start.10) | collective-permute-done | bytes 147488 | tf_op jit(solution)/shard_map/ppermute | solution.py:32
  49.0 3.9 %collective-permute-done.13.refs_4_ = bf16[64,1152]{1,0:T(8,128)(2,1)S(1)} collective-permute-done((bf16[64,1152]{1,0:T(8,128)(2,1)S(1)}, bf16[64,1152]{1,0:T(8,128)(2,1)S(1)}, u32[]{:S(2)}, u32[]{:S(2)}) %collective-permute-start.13) | collective-permute-done | bytes 147488 | tf_op jit(solution)/shard_map/ppermute | solution.py:32
  53.0 3.3 %collective-permute-start.14 = (bf16[192,1152]{1,0:T(8,128)(2,1)S(1)}, bf16[192,1152]{1,0:T(8,128)(2,1)S(1)}, u32[]{:S(2)}, u32[]{:S(2)}) collective-permute-start(bf16[192,1152]{1,0:T(8,128)(2,1)S(1)} %pad_maximum_fusion.1), channel_id=1, source_target_pairs={{0,1},{1,0},{2,3},{3,2},{4,5},{5,4},{6,7},{7,6},{8,9},{9,8},{10,11... | collective-permute-start | bytes 1327112 | tf_op jit(solution)/shard_map/ppermute | solution.py:32
  56.3 1.0 pad_maximum_fusion.3.refs_10_
  57.3 1.0 pad_maximum_fusion.4.refs_14_
  58.3 13.8 %pairs.1 = (f32[1024,1152]{1,0:T(8,128)}, f32[1024,1152]{1,0:T(8,128)}, f32[1024,1]{1,0:T(8,128)S(1)}, f32[1,1024]{1,0:T(1,128)S(1)}, f32[2,1024]{1,0:T(2,128)S(1)}) custom-call(f32[2]{0:T(128)S(1)} %pad_maximum_fusion.7.par_ref, bf16[128,1152]{1,0:T(8,128)(2,1)S(1)} %fusion.1.refs_0_, bf16[128,1152]{1,0:T(8,128)(2,1)S(1)} %collective-permute-done.refs_1_, ...), custom_call_target="tpu_custom_call" | custom-call | flops 7247757312 | bytes 14680064 | tf_op jit(solution)/shard_map/pairs/pallas_call | solution.py:125
  72.2 2.8 %slice_convert_fusion = f16[512,1152]{1,0:T(8,128)(2,1)} fusion(f32[1024,1152]{1,0:T(8,128)} %get-tuple-element.57), kind=kLoop, calls=%fused_computation.1 | loop fusion | flops 589824 | bytes 3538944 | tf_op jit(solution)/shard_map/convert.1
  75.4 0.7 collective-permute-start.20
  76.1 4.0 %convert_element_type.52 = f16[1024,1152]{1,0:T(8,128)(2,1)} convert(f32[1024,1152]{1,0:T(8,128)} %get-tuple-element.70) | non-fusion elementwise | flops 1179648 | bytes 7077888 | tf_op jit(solution)/shard_map/convert_element_type | solution.py:202
  80.1 3.7 %all-to-all-start = ((f16[16,64,1152]{2,1,0:T(8,128)(2,1)}), f16[16,64,1152]{2,1,0:T(8,128)(2,1)S(1)}, u32[]{:S(2)}, u32[]{:S(2)}) async-start(f16[16,64,1152]{2,1,0:T(8,128)(2,1)} %bitcast.9), calls=%async_computation | async-start | bytes 4718592 | tf_op jit(solution)/shard_map/all_to_all | solution.py:202
  83.8 1.6 collective-permute-start.25
  85.4 3.7 %fusion.15 = (f16[512,1152]{1,0:T(8,128)(2,1)S(1)}, f32[512,1152]{1,0:T(8,128)}) fusion(f16[512,1152]{1,0:T(8,128)(2,1)} %collective-permute-done.15, f32[1024,1152]{1,0:T(8,128)} %get-tuple-element.57), kind=kLoop, calls=%fused_computation.57 | loop fusion | flops 1769472 | bytes 7077888 | tf_op jit(solution)/shard_map/convert
  89.1 1.0 fusion.16
  90.1 0.5 collective-permute-start.19
  90.6 0.9 collective-permute-start.18
  91.5 3.4 %collective-permute-start.17 = (f16[128,1152]{1,0:T(8,128)(2,1)}, f16[128,1152]{1,0:T(8,128)(2,1)}, u32[]{:S(2)}, u32[]{:S(2)}) collective-permute-start(f16[128,1152]{1,0:T(8,128)(2,1)} %get-tuple-element.86), channel_id=1, source_target_pairs={{0,48},{1,81},{2,50},{3,83},{4,52},{5,85},{6,54},{7,87},{8,56},{9,... | collective-permute-start | bytes 884744 | tf_op jit(solution)/shard_map/ppermute | solution.py:32
  94.9 0.7 fusion.9
  95.6 1.5 collective-permute-start.21
  97.0 21.0 %collective-permute-done.25 = f32[1024]{0:T(1024)S(1)} collective-permute-done((f32[1024]{0:T(1024)S(1)}, f32[1024]{0:T(1024)S(1)}, u32[]{:S(2)}, u32[]{:S(2)}) %collective-permute-start.25) | collective-permute-done | bytes 4128 | tf_op jit(solution)/shard_map/ppermute | solution.py:32
  118.0 2.2 %collective-permute-start.26 = (f32[1024]{0:T(1024)S(1)}, f32[1024]{0:T(1024)S(1)}, u32[]{:S(2)}, u32[]{:S(2)}) collective-permute-start(f32[1024]{0:T(1024)S(1)} %add.187), channel_id=1, source_target_pairs={{0,130},{1,131},{2,128},{3,129},{4,134},{5,135},{6,132},{7,133},{8... | collective-permute-start | bytes 12296 | tf_op jit(solution)/shard_map/ppermute | solution.py:32
  120.3 0.5 collective-permute-start.22
  120.7 1.0 collective-permute-done.26
  121.7 2.1 %collective-permute-done.22 = f32[1026]{0:T(1024)S(1)} collective-permute-done((f32[1026]{0:T(1024)S(1)}, f32[1026]{0:T(1024)S(1)}, u32[]{:S(2)}, u32[]{:S(2)}) %collective-permute-start.22) | collective-permute-done | bytes 4136 | tf_op jit(solution)/shard_map/ppermute | solution.py:32
  123.8 3.7 %collective-permute-start.23 = (f32[1026]{0:T(1024)S(1)}, f32[1026]{0:T(1024)}, u32[]{:S(2)}, u32[]{:S(2)}) collective-permute-start(f32[1026]{0:T(1024)S(1)} %add.184), channel_id=1, source_target_pairs={{0,64},{1,65},{2,66},{3,67},{4,68},{5,69},{6,70},{7,71},{8,72},{9,... | collective-permute-start | bytes 12320 | tf_op jit(solution)/shard_map/ppermute | solution.py:32
  127.5 2.8 %collective-permute-done.23 = f32[1026]{0:T(1024)} collective-permute-done((f32[1026]{0:T(1024)S(1)}, f32[1026]{0:T(1024)}, u32[]{:S(2)}, u32[]{:S(2)}) %collective-permute-start.23) | collective-permute-done | bytes 4136 | tf_op jit(solution)/shard_map/ppermute | solution.py:32
  130.3 0.7 add.185
  131.1 3.8 %collective-permute-start.16 = (f16[64,1152]{1,0:T(8,128)(2,1)S(1)}, f16[64,1152]{1,0:T(8,128)(2,1)S(1)}, u32[]{:S(2)}, u32[]{:S(2)}) collective-permute-start(f16[64,1152]{1,0:T(8,128)(2,1)S(1)} %slice.57), channel_id=1, source_target_pairs={{0,64},{1,65},{2,66},{3,67},{4,68},{5,69},{6,70},{7,71},{8,72},{9,... | collective-permute-start | bytes 442376 | tf_op jit(solution)/shard_map/ppermute | solution.py:32
  134.9 2.4 %collective-permute-done.29 = f32[2]{0:T(128)S(1)} collective-permute-done((f32[2]{0:T(128)S(1)}, f32[2]{0:T(128)S(1)}, u32[]{:S(2)}, u32[]{:S(2)}) %collective-permute-start.29) | collective-permute-done | bytes 40 | tf_op jit(solution)/shard_map/ppermute | solution.py:32
  137.3 0.7 collective-permute-start.30
  138.0 2.9 %collective-permute-done.30 = f32[2]{0:T(128)S(1)} collective-permute-done((f32[2]{0:T(128)S(1)}, f32[2]{0:T(128)S(1)}, u32[]{:S(2)}, u32[]{:S(2)}) %collective-permute-start.30) | collective-permute-done | bytes 40 | tf_op jit(solution)/shard_map/ppermute | solution.py:32
  140.9 0.9 collective-permute-start.31
  141.8 3.0 %collective-permute-done.31 = f32[2]{0:T(128)S(1)} collective-permute-done((f32[2]{0:T(128)S(1)}, f32[2]{0:T(128)S(1)}, u32[]{:S(2)}, u32[]{:S(2)}) %collective-permute-start.31) | collective-permute-done | bytes 40 | tf_op jit(solution)/shard_map/ppermute | solution.py:32
  144.8 0.5 add.193
  145.4 0.6 copy-done.8
  146.0 1.2 convert_add_fusion.1
  147.3 0.8 constant_dynamic-slice_fusion
  148.1 7.4 %collective-permute-start.32 = (f32[64,1152]{1,0:T(8,128)}, f32[64,1152]{1,0:T(8,128)}, u32[]{:S(2)}, u32[]{:S(2)}) collective-permute-start(f32[64,1152]{1,0:T(8,128)} %constant_dynamic-slice_fusion), channel_id=1, source_target_pairs={{0,1},{1,0},{2,3},{3,2},{4,5},{5,4},{6,7},{7,6},{8,9},{9,8},{10,11... | collective-permute-start | bytes 884744 | tf_op jit(solution)/shard_map/ppermute | solution.py:32
  155.4 0.6 dynamic-slice_add_fusion
  157.1 2.1 %multiply_reduce_fusion.1 = (f32[64]{0:T(128)S(1)}, f32[64,1152]{1,0:T(8,128)S(1)}, f32[64,1152]{1,0:T(8,128)}) fusion(f32[64,1152]{1,0:T(8,128)S(1)} %copy-done, f32[64,1152]{1,0:T(8,128)S(1)} %copy-done.6, f32[64]{0:T(128)S(1)} %copy-done.12, f32[64,1152]{1,0:T(8,128)} %collective-permute-done.32, f32[128,1152]{1,0:T(8,128)S(1)} %copy-done.4, ...), kind=kLoop, calls=%fused_computation.31 | loop fusion | flops 958400 | bytes 3097604 | tf_op jit(solution)/shard_map/reduce_sum | solution.py:223
  159.2 0.8 subtract_multiply_fusion.1
  (91 shorter events, 2.8 us)
Async XLA Ops:
  0.6 15.4 %copy-start.7 = (bf16[256,1152]{1,0:T(8,128)(2,1)S(1)}, bf16[256,1152]{1,0:T(8,128)(2,1)}, u32[]{:S(2)}) copy-start(bf16[256,1152]{1,0:T(8,128)(2,1)} %param.5) | copy-start | bytes 1769476
  0.6 15.5 %copy-start.5 = (bf16[256,1152]{1,0:T(8,128)(2,1)S(1)}, bf16[256,1152]{1,0:T(8,128)(2,1)}, u32[]{:S(2)}) copy-start(bf16[256,1152]{1,0:T(8,128)(2,1)} %param.4) | copy-start | bytes 1769476
  2.0 19.2 %collective-permute-start.3 = (bf16[128,1152]{1,0:T(8,128)(2,1)S(1)}, bf16[128,1152]{1,0:T(8,128)(2,1)S(1)}, u32[]{:S(2)}, u32[]{:S(2)}) collective-permute-start(bf16[128,1152]{1,0:T(8,128)(2,1)S(1)} %fusion.3.refs_7_), channel_id=1, source_target_pairs={{0,130},{1,131},{2,128},{3,129},{4,134},{5,135},{6,132},{7,133},{8... | collective-permute-start | bytes 884744 | tf_op jit(solution)/shard_map/ppermute | solution.py:32
  5.7 15.6 %collective-permute-start.2 = (bf16[128,1152]{1,0:T(8,128)(2,1)S(1)}, bf16[128,1152]{1,0:T(8,128)(2,1)S(1)}, u32[]{:S(2)}, u32[]{:S(2)}) collective-permute-start(bf16[128,1152]{1,0:T(8,128)(2,1)S(1)} %fusion.3.refs_7_), channel_id=1, source_target_pairs={{0,12},{1,13},{2,14},{3,15},{4,0},{5,1},{6,2},{7,3},{8,4},{9,5},{1... | collective-permute-start | bytes 884744 | tf_op jit(solution)/shard_map/ppermute | solution.py:32
  8.2 13.1 %collective-permute-start.1 = (bf16[128,1152]{1,0:T(8,128)(2,1)S(1)}, bf16[128,1152]{1,0:T(8,128)(2,1)S(1)}, u32[]{:S(2)}, u32[]{:S(2)}) collective-permute-start(bf16[128,1152]{1,0:T(8,128)(2,1)S(1)} %fusion.3.refs_7_), channel_id=1, source_target_pairs={{0,4},{1,5},{2,6},{3,7},{4,8},{5,9},{6,10},{7,11},{8,12},{9,13},{1... | collective-permute-start | bytes 884744 | tf_op jit(solution)/shard_map/ppermute | solution.py:32
  10.4 10.9 %collective-permute-start = (bf16[128,1152]{1,0:T(8,128)(2,1)S(1)}, bf16[128,1152]{1,0:T(8,128)(2,1)S(1)}, u32[]{:S(2)}, u32[]{:S(2)}) collective-permute-start(bf16[128,1152]{1,0:T(8,128)(2,1)S(1)} %fusion.1.refs_0_), channel_id=1, source_target_pairs={{0,16},{1,113},{2,18},{3,115},{4,20},{5,117},{6,22},{7,119},{8,24}... | collective-permute-start | bytes 884744 | tf_op jit(solution)/shard_map/ppermute | solution.py:32
  21.3 14.2 %collective-permute-start.6 = (bf16[128,1152]{1,0:T(8,128)(2,1)S(1)}, bf16[128,1152]{1,0:T(8,128)(2,1)S(1)}, u32[]{:S(2)}, u32[]{:S(2)}) collective-permute-start(bf16[128,1152]{1,0:T(8,128)(2,1)S(1)} %collective-permute-done.3.refs_11_), channel_id=1, source_target_pairs={{0,12},{1,13},{2,14},{3,15},{4,0},{5,1},{6,2},{7,3},{8,4},{9,5},{1... | collective-permute-start | bytes 884744 | tf_op jit(solution)/shard_map/ppermute | solution.py:32
  24.1 11.5 %collective-permute-start.5 = (bf16[128,1152]{1,0:T(8,128)(2,1)S(1)}, bf16[128,1152]{1,0:T(8,128)(2,1)S(1)}, u32[]{:S(2)}, u32[]{:S(2)}) collective-permute-start(bf16[128,1152]{1,0:T(8,128)(2,1)S(1)} %collective-permute-done.3.refs_11_), channel_id=1, source_target_pairs={{0,4},{1,5},{2,6},{3,7},{4,8},{5,9},{6,10},{7,11},{8,12},{9,13},{1... | collective-permute-start | bytes 884744 | tf_op jit(solution)/shard_map/ppermute | solution.py:32
  24.1 8.3 %collective-permute-start.8 = (bf16[64,1152]{1,0:T(8,128)(2,1)S(1)}, bf16[64,1152]{1,0:T(8,128)(2,1)S(1)}, u32[]{:S(2)}, u32[]{:S(2)}) collective-permute-start(bf16[64,1152]{1,0:T(8,128)(2,1)S(1)} %slice.44), channel_id=1, source_target_pairs={{0,12},{1,13},{2,14},{3,15},{4,0},{5,1},{6,2},{7,3},{8,4},{9,5},{1... | collective-permute-start | bytes 442376 | tf_op jit(solution)/shard_map/ppermute | solution.py:32
  26.9 8.7 %collective-permute-start.7 = (bf16[64,1152]{1,0:T(8,128)(2,1)S(1)}, bf16[64,1152]{1,0:T(8,128)(2,1)S(1)}, u32[]{:S(2)}, u32[]{:S(2)}) collective-permute-start(bf16[64,1152]{1,0:T(8,128)(2,1)S(1)} %slice.43), channel_id=1, source_target_pairs={{0,4},{1,5},{2,6},{3,7},{4,8},{5,9},{6,10},{7,11},{8,12},{9,13},{1... | collective-permute-start | bytes 442376 | tf_op jit(solution)/shard_map/ppermute | solution.py:32
  26.9 8.7 %collective-permute-start.4 = (bf16[128,1152]{1,0:T(8,128)(2,1)S(1)}, bf16[128,1152]{1,0:T(8,128)(2,1)S(1)}, u32[]{:S(2)}, u32[]{:S(2)}) collective-permute-start(bf16[128,1152]{1,0:T(8,128)(2,1)S(1)} %collective-permute-done.refs_1_), channel_id=1, source_target_pairs={{0,16},{1,113},{2,18},{3,115},{4,20},{5,117},{6,22},{7,119},{8,24}... | collective-permute-start | bytes 884744 | tf_op jit(solution)/shard_map/ppermute | solution.py:32
  32.4 3.2 %copy-start.10 = (bf16[64,1152]{1,0:T(8,128)(2,1)}, bf16[64,1152]{1,0:T(8,128)(2,1)S(1)}, u32[]{:S(2)}) copy-start(bf16[64,1152]{1,0:T(8,128)(2,1)S(1)} %collective-permute-done.8) | copy-start | bytes 442372
  35.5 0.7 copy-start.11
  36.2 12.6 %collective-permute-start.12 = (bf16[256,1152]{1,0:T(8,128)(2,1)S(1)}, bf16[256,1152]{1,0:T(8,128)(2,1)}, u32[]{:S(2)}, u32[]{:S(2)}) collective-permute-start(bf16[256,1152]{1,0:T(8,128)(2,1)S(1)} %pad_maximum_fusion), channel_id=1, source_target_pairs={{0,1},{1,0},{2,3},{3,2},{4,5},{5,4},{6,7},{7,6},{8,9},{9,8},{10,11... | collective-permute-start | bytes 1769480 | tf_op jit(solution)/shard_map/ppermute | solution.py:32
  38.6 10.2 %collective-permute-start.9 = (bf16[128,1152]{1,0:T(8,128)(2,1)S(1)}, bf16[128,1152]{1,0:T(8,128)(2,1)S(1)}, u32[]{:S(2)}, u32[]{:S(2)}) collective-permute-start(bf16[128,1152]{1,0:T(8,128)(2,1)S(1)} %collective-permute-done.4.refs_2_), channel_id=1, source_target_pairs={{0,16},{1,113},{2,18},{3,115},{4,20},{5,117},{6,22},{7,119},{8,24}... | collective-permute-start | bytes 884744 | tf_op jit(solution)/shard_map/ppermute | solution.py:32
  41.4 5.3 %collective-permute-start.11 = (bf16[64,1152]{1,0:T(8,128)(2,1)}, bf16[64,1152]{1,0:T(8,128)(2,1)}, u32[]{:S(2)}, u32[]{:S(2)}) collective-permute-start(bf16[64,1152]{1,0:T(8,128)(2,1)} %slice.46), channel_id=1, source_target_pairs={{0,12},{1,13},{2,14},{3,15},{4,0},{5,1},{6,2},{7,3},{8,4},{9,5},{1... | collective-permute-start | bytes 442376 | tf_op jit(solution)/shard_map/ppermute | solution.py:32
  41.8 7.1 %collective-permute-start.10 = (bf16[64,1152]{1,0:T(8,128)(2,1)}, bf16[64,1152]{1,0:T(8,128)(2,1)}, u32[]{:S(2)}, u32[]{:S(2)}) collective-permute-start(bf16[64,1152]{1,0:T(8,128)(2,1)} %slice.45), channel_id=1, source_target_pairs={{0,4},{1,5},{2,6},{3,7},{4,8},{5,9},{6,10},{7,11},{8,12},{9,13},{1... | collective-permute-start | bytes 442376 | tf_op jit(solution)/shard_map/ppermute | solution.py:32
  48.9 4.1 %collective-permute-start.13 = (bf16[64,1152]{1,0:T(8,128)(2,1)S(1)}, bf16[64,1152]{1,0:T(8,128)(2,1)S(1)}, u32[]{:S(2)}, u32[]{:S(2)}) collective-permute-start(bf16[64,1152]{1,0:T(8,128)(2,1)S(1)} %constant_dynamic-slice_fusion.1), channel_id=1, source_target_pairs={{0,16},{1,113},{2,18},{3,115},{4,20},{5,117},{6,22},{7,119},{8,24}... | collective-permute-start | bytes 442376 | tf_op jit(solution)/shard_map/ppermute | solution.py:32
  53.0 5.4 %collective-permute-start.14 = (bf16[192,1152]{1,0:T(8,128)(2,1)S(1)}, bf16[192,1152]{1,0:T(8,128)(2,1)S(1)}, u32[]{:S(2)}, u32[]{:S(2)}) collective-permute-start(bf16[192,1152]{1,0:T(8,128)(2,1)S(1)} %pad_maximum_fusion.1), channel_id=1, source_target_pairs={{0,1},{1,0},{2,3},{3,2},{4,5},{5,4},{6,7},{7,6},{8,9},{9,8},{10,11... | collective-permute-start | bytes 1327112 | tf_op jit(solution)/shard_map/ppermute | solution.py:32
  75.0 10.4 %collective-permute-start.15 = (f16[512,1152]{1,0:T(8,128)(2,1)}, f16[512,1152]{1,0:T(8,128)(2,1)}, u32[]{:S(2)}, u32[]{:S(2)}) collective-permute-start(f16[512,1152]{1,0:T(8,128)(2,1)} %slice_convert_fusion), channel_id=1, source_target_pairs={{0,1},{1,0},{2,3},{3,2},{4,5},{5,4},{6,7},{7,6},{8,9},{9,8},{10,11... | collective-permute-start | bytes 3538952 | tf_op jit(solution)/shard_map/ppermute | solution.py:32
  75.0 8.8 %collective-permute-start.24 = (f32[1024]{0:T(1024)S(1)}, f32[1024]{0:T(1024)S(1)}, u32[]{:S(2)}, u32[]{:S(2)}) collective-permute-start(f32[1024]{0:T(1024)S(1)} %bitcast.13), channel_id=1, source_target_pairs={{0,2},{1,3},{2,0},{3,1},{4,6},{5,7},{6,4},{7,5},{8,10},{9,11},{10,... | collective-permute-start | bytes 12296 | tf_op jit(solution)/shard_map/ppermute | solution.py:32
  75.4 19.5 %collective-permute-start.20 = (f32[1026]{0:T(1024)S(1)}, f32[1026]{0:T(1024)}, u32[]{:S(2)}, u32[]{:S(2)}) collective-permute-start(f32[1026]{0:T(1024)S(1)} %pad_maximum_fusion.5), channel_id=1, source_target_pairs={{0,1},{1,0},{2,3},{3,2},{4,5},{5,4},{6,7},{7,6},{8,9},{9,8},{10,11... | collective-permute-start | bytes 12320 | tf_op jit(solution)/shard_map/ppermute | solution.py:32
  80.1 76.0 %all-to-all-start = ((f16[16,64,1152]{2,1,0:T(8,128)(2,1)}), f16[16,64,1152]{2,1,0:T(8,128)(2,1)S(1)}, u32[]{:S(2)}, u32[]{:S(2)}) async-start(f16[16,64,1152]{2,1,0:T(8,128)(2,1)} %bitcast.9), calls=%async_computation | async-start | bytes 4718592 | tf_op jit(solution)/shard_map/all_to_all | solution.py:202
  83.8 34.2 %collective-permute-start.25 = (f32[1024]{0:T(1024)S(1)}, f32[1024]{0:T(1024)S(1)}, u32[]{:S(2)}, u32[]{:S(2)}) collective-permute-start(f32[1024]{0:T(1024)S(1)} %add.186), channel_id=1, source_target_pairs={{0,4},{1,5},{2,6},{3,7},{4,0},{5,1},{6,2},{7,3},{8,12},{9,13},{10,... | collective-permute-start | bytes 12296 | tf_op jit(solution)/shard_map/ppermute | solution.py:32
  90.1 55.2 %collective-permute-start.19 = (f16[128,1152]{1,0:T(8,128)(2,1)}, f16[128,1152]{1,0:T(8,128)(2,1)}, u32[]{:S(2)}, u32[]{:S(2)}) collective-permute-start(f16[128,1152]{1,0:T(8,128)(2,1)} %get-tuple-element.84), channel_id=1, source_target_pairs={{0,16},{1,113},{2,18},{3,115},{4,20},{5,117},{6,22},{7,119},{8,24}... | collective-permute-start | bytes 884744 | tf_op jit(solution)/shard_map/ppermute | solution.py:32
  90.6 54.8 %collective-permute-start.18 = (f16[128,1152]{1,0:T(8,128)(2,1)}, f16[128,1152]{1,0:T(8,128)(2,1)}, u32[]{:S(2)}, u32[]{:S(2)}) collective-permute-start(f16[128,1152]{1,0:T(8,128)(2,1)} %get-tuple-element.85), channel_id=1, source_target_pairs={{0,32},{1,97},{2,34},{3,99},{4,36},{5,101},{6,38},{7,103},{8,40},{... | collective-permute-start | bytes 884744 | tf_op jit(solution)/shard_map/ppermute | solution.py:32
  91.5 53.9 %collective-permute-start.17 = (f16[128,1152]{1,0:T(8,128)(2,1)}, f16[128,1152]{1,0:T(8,128)(2,1)}, u32[]{:S(2)}, u32[]{:S(2)}) collective-permute-start(f16[128,1152]{1,0:T(8,128)(2,1)} %get-tuple-element.86), channel_id=1, source_target_pairs={{0,48},{1,81},{2,50},{3,83},{4,52},{5,85},{6,54},{7,87},{8,56},{9,... | collective-permute-start | bytes 884744 | tf_op jit(solution)/shard_map/ppermute | solution.py:32
  95.6 24.7 %collective-permute-start.21 = (f32[1026]{0:T(1024)S(1)}, f32[1026]{0:T(1024)S(1)}, u32[]{:S(2)}, u32[]{:S(2)}) collective-permute-start(f32[1026]{0:T(1024)S(1)} %fusion.9), channel_id=1, source_target_pairs={{0,16},{1,17},{2,18},{3,19},{4,20},{5,21},{6,22},{7,23},{8,24},{9,... | collective-permute-start | bytes 12320 | tf_op jit(solution)/shard_map/ppermute | solution.py:32
  118.0 3.7 %collective-permute-start.26 = (f32[1024]{0:T(1024)S(1)}, f32[1024]{0:T(1024)S(1)}, u32[]{:S(2)}, u32[]{:S(2)}) collective-permute-start(f32[1024]{0:T(1024)S(1)} %add.187), channel_id=1, source_target_pairs={{0,130},{1,131},{2,128},{3,129},{4,134},{5,135},{6,132},{7,133},{8... | collective-permute-start | bytes 12296 | tf_op jit(solution)/shard_map/ppermute | solution.py:32
  120.3 3.5 %collective-permute-start.22 = (f32[1026]{0:T(1024)S(1)}, f32[1026]{0:T(1024)S(1)}, u32[]{:S(2)}, u32[]{:S(2)}) collective-permute-start(f32[1026]{0:T(1024)S(1)} %add.183), channel_id=1, source_target_pairs={{0,32},{1,33},{2,34},{3,35},{4,36},{5,37},{6,38},{7,39},{8,40},{9,... | collective-permute-start | bytes 12320 | tf_op jit(solution)/shard_map/ppermute | solution.py:32
  121.7 5.8 %collective-permute-start.27 = (f32[1024]{0:T(1024)S(1)}, f32[1024]{0:T(1024)S(1)}, u32[]{:S(2)}, u32[]{:S(2)}) collective-permute-start(f32[1024]{0:T(1024)S(1)} %add.188), channel_id=1, source_target_pairs={{0,8},{1,9},{2,10},{3,11},{4,12},{5,13},{6,14},{7,15},{8,0},{9,1},... | collective-permute-start | bytes 12296 | tf_op jit(solution)/shard_map/ppermute | solution.py:32
  123.8 6.5 %collective-permute-start.23 = (f32[1026]{0:T(1024)S(1)}, f32[1026]{0:T(1024)}, u32[]{:S(2)}, u32[]{:S(2)}) collective-permute-start(f32[1026]{0:T(1024)S(1)} %add.184), channel_id=1, source_target_pairs={{0,64},{1,65},{2,66},{3,67},{4,68},{5,69},{6,70},{7,71},{8,72},{9,... | collective-permute-start | bytes 12320 | tf_op jit(solution)/shard_map/ppermute | solution.py:32
  127.5 28.0 %copy-start.13 = (f32[64]{0:T(128)S(1)}, f32[64]{0:T(128)}, u32[]{:S(2)}) copy-start(f32[64]{0:T(128)} %get-tuple-element.74) | copy-start | bytes 772
  131.0 3.9 %collective-permute-start.28 = (f32[2]{0:T(128)S(1)}, f32[2]{0:T(128)S(1)}, u32[]{:S(2)}, u32[]{:S(2)}) collective-permute-start(f32[2]{0:T(128)S(1)} %slice.61), channel_id=1, source_target_pairs={{0,2},{1,3},{2,0},{3,1},{4,6},{5,7},{6,4},{7,5},{8,10},{9,11},{10,... | collective-permute-start | bytes 32 | tf_op jit(solution)/shard_map/ppermute | solution.py:32
  131.1 14.2 %collective-permute-start.16 = (f16[64,1152]{1,0:T(8,128)(2,1)S(1)}, f16[64,1152]{1,0:T(8,128)(2,1)S(1)}, u32[]{:S(2)}, u32[]{:S(2)}) collective-permute-start(f16[64,1152]{1,0:T(8,128)(2,1)S(1)} %slice.57), channel_id=1, source_target_pairs={{0,64},{1,65},{2,66},{3,67},{4,68},{5,69},{6,70},{7,71},{8,72},{9,... | collective-permute-start | bytes 442376 | tf_op jit(solution)/shard_map/ppermute | solution.py:32
  134.9 2.4 %collective-permute-start.29 = (f32[2]{0:T(128)S(1)}, f32[2]{0:T(128)S(1)}, u32[]{:S(2)}, u32[]{:S(2)}) collective-permute-start(f32[2]{0:T(128)S(1)} %slice_add_fusion.1), channel_id=1, source_target_pairs={{0,4},{1,5},{2,6},{3,7},{4,0},{5,1},{6,2},{7,3},{8,12},{9,13},{10,... | collective-permute-start | bytes 32 | tf_op jit(solution)/shard_map/ppermute | solution.py:32
  137.3 3.6 %collective-permute-start.30 = (f32[2]{0:T(128)S(1)}, f32[2]{0:T(128)S(1)}, u32[]{:S(2)}, u32[]{:S(2)}) collective-permute-start(f32[2]{0:T(128)S(1)} %add.191), channel_id=1, source_target_pairs={{0,130},{1,131},{2,128},{3,129},{4,134},{5,135},{6,132},{7,133},{8... | collective-permute-start | bytes 32 | tf_op jit(solution)/shard_map/ppermute | solution.py:32
  140.9 3.9 %collective-permute-start.31 = (f32[2]{0:T(128)S(1)}, f32[2]{0:T(128)S(1)}, u32[]{:S(2)}, u32[]{:S(2)}) collective-permute-start(f32[2]{0:T(128)S(1)} %add.192), channel_id=1, source_target_pairs={{0,8},{1,9},{2,10},{3,11},{4,12},{5,13},{6,14},{7,15},{8,0},{9,1},... | collective-permute-start | bytes 32 | tf_op jit(solution)/shard_map/ppermute | solution.py:32
  145.3 11.0 %copy-start.1 = (f32[64,1152]{1,0:T(8,128)S(1)}, f32[64,1152]{1,0:T(8,128)}, u32[]{:S(2)}) copy-start(f32[64,1152]{1,0:T(8,128)} %get-tuple-element.72) | copy-start | bytes 884740
  145.3 11.0 %copy-start.2 = (f32[64,1152]{1,0:T(8,128)S(1)}, f32[64,1152]{1,0:T(8,128)}, u32[]{:S(2)}) copy-start(f32[64,1152]{1,0:T(8,128)} %get-tuple-element.71) | copy-start | bytes 884740
  145.3 11.1 %copy-start.12 = (f32[64]{0:T(128)S(1)}, f32[64]{0:T(128)}, u32[]{:S(2)}) copy-start(f32[64]{0:T(128)} %multiply_reduce-precision_fusion) | copy-start | bytes 772
  145.3 0.7 copy-start.8
  147.2 8.2 %copy-start.3 = (f32[128,1152]{1,0:T(8,128)}, f32[128,1152]{1,0:T(8,128)S(1)}, u32[]{:S(2)}) copy-start(f32[128,1152]{1,0:T(8,128)S(1)} %convert_add_fusion.1) | copy-start | bytes 1769476
  147.3 9.7 %copy-start = (f32[64,1152]{1,0:T(8,128)S(1)}, f32[64,1152]{1,0:T(8,128)}, u32[]{:S(2)}) copy-start(f32[64,1152]{1,0:T(8,128)} %get-tuple-element.68) | copy-start | bytes 884740
  147.3 9.7 %copy-start.6 = (f32[64,1152]{1,0:T(8,128)S(1)}, f32[64,1152]{1,0:T(8,128)}, u32[]{:S(2)}) copy-start(f32[64,1152]{1,0:T(8,128)} %get-tuple-element.67) | copy-start | bytes 884740
  147.3 9.7 %copy-start.15 = (f32[64,1]{0,1:T(1,128)S(1)}, f32[64,1]{0,1:T(1,128)}, u32[]{:S(2)}) copy-start(f32[64,1]{0,1:T(1,128)} %get-tuple-element.69) | copy-start | bytes 772
  148.1 8.9 %collective-permute-start.32 = (f32[64,1152]{1,0:T(8,128)}, f32[64,1152]{1,0:T(8,128)}, u32[]{:S(2)}, u32[]{:S(2)}) collective-permute-start(f32[64,1152]{1,0:T(8,128)} %constant_dynamic-slice_fusion), channel_id=1, source_target_pairs={{0,1},{1,0},{2,3},{3,2},{4,5},{5,4},{6,7},{7,6},{8,9},{9,8},{10,11... | collective-permute-start | bytes 884744 | tf_op jit(solution)/shard_map/ppermute | solution.py:32
  156.0 1.1 copy-start.4
  156.0 1.1 copy-start.9
  156.4 2.8 %copy-start.14 = (f32[64,1]{0,1:T(1,128)S(1)}, f32[64,1]{0,1:T(1,128)}, u32[]{:S(2)}) copy-start(f32[64,1]{0,1:T(1,128)} %get-tuple-element.45) | copy-start | bytes 772
where the time goes:
time: 161 us; the launch traced here: 160 us
  starting transfers between devices  59 us (37%)
  waiting for transfers between devices  50.6 us (31%)
  other arithmetic  27.9 us (17%)
  Pallas kernels  13.8 us (9%)
  local copies, waits for them, and re-layouts  5.69 us (4%)
  between operations  2.97 us (2%)
    ppermute x33, starting transfers between devices, send(): return lax.ppermute(value, AXES, pairs)  55.3 us
    ppermute x33, waiting for transfers between devices, send(): return lax.ppermute(value, AXES, pairs)  50.6 us
    pallas_call x1, Pallas kernels, pairs_on_device(): pl.pallas_call(pair_kernel, out_shape=(jax.ShapeDtypeStruct((1024, width)...  13.8 us
    another operation x2, other arithmetic  6.55 us
    convert_element_type x1, other arithmetic, per_device(): gt.astype(f16)  4 us
    all_to_all x1, starting transfers between devices, per_device(): lax.all_to_all(gt.astype(f16), ('yh', 'x', 'yl'), 0, 0, tiled=True)  3.72 us
  transfers between devices with their start and end apart: 34, of which 13 were waited for; matrix products, arithmetic and copies ran while one was open for 16% of the time, Pallas kernels for 0%

commit v1 on v0

--- a/solution.py
+++ b/solution.py
@@ -46,26 +46,20 @@
 
 
 def pair_kernel(par_ref, *refs):
-    a0, r1, r2, r3, r4, e12, e34 = refs[:7]
-    txt_in = refs[7:15]
-    gi_ref, gt_ref, li_ref, lt_ref, sums_ref, img, txt = refs[15:]
+    all_images = refs[0]
+    txt_in = refs[1:9]
+    gi_ref, gt_ref, li_ref, lt_ref, sums_ref, img, txt = refs[9:]
     z, x = lax.axis_index("z"), lax.axis_index("x")
     yh, core = lax.axis_index("yh"), lax.axis_index("core")
     sign = 1 - 2 * core
-    img[0:64, :] = a0[pl.ds(pl.multiple_of(core * Q, Q), Q), :]
-    img[64:320, :] = e12[...]
-    img[320:448, :] = e34[0:128, :]
-    img[448:512, :] = r4[...]
-    img[512:576, :] = a0[pl.ds(pl.multiple_of((1 - core) * Q, Q), Q), :]
-    img[576:704, :] = r1[...]
-    img[704:832, :] = r2[...]
-    img[832:960, :] = r3[...]
-    img[960:1024, :] = e34[128:192, :]
     image_places = [(z, core)]
     image_places += [(z + sign * k, q) for k in range(1, 4) for q in range(2)]
     image_places += [(z + 4, core), (z, 1 - core)]
     image_places += [(z - sign * k, q) for k in range(1, 4) for q in range(2)]
     image_places += [(z + 4, 1 - core)]
+    for k, (zz, q) in enumerate(image_places):
+        start = (lax.rem(zz + NZ, NZ) * NC + q) * Q
+        img[k * Q : (k + 1) * Q, :] = all_images[pl.ds(pl.multiple_of(start, Q), Q), :]
     text_places = [
         (h * NX + lax.rem(x + dx, NX)) * 2 for h in (yh, 1 - yh) for dx in (0, NX - 1, 1, 2)
     ]
@@ -98,11 +92,7 @@
         back = lax.dot_general(
             weights, images, (((0,), (0,)), ((), ())), preferred_element_type=jnp.float32
         )
-        row_losses = jnp.sum(losses, axis=1, keepdims=True)
-        for k in range(ROWS // Q):
-            zz, q = image_places[r * ROWS // Q + k]
-            start = (q * NZ + lax.rem(zz + NZ, NZ)) * Q
-            li_ref[pl.ds(pl.multiple_of(start, Q), Q), :] = row_losses[k * Q : (k + 1) * Q]
+        li_ref[r * ROWS : (r + 1) * ROWS, :] = jnp.sum(losses, axis=1, keepdims=True)
         cols = jnp.sum(losses, axis=0, keepdims=True)
         s1 = jnp.sum(slopes, axis=0, keepdims=True)
         s2 = jnp.sum(slopes * scores, axis=0, keepdims=True)
@@ -149,22 +139,16 @@
     return lax.optimization_barrier(values)
 
 
-def gather(a0, t0, core, own):
-    r1 = send(a0, split_z=1)
+def gather_texts(t0, own):
     xm, xp, c0 = send(t0, dx=1), send(t0, dx=-1), send(t0, fy=3)
-    a0, t0, r1, xm, xp, c0 = tied(a0, t0, r1, xm, xp, c0)
-    r2 = send(r1, split_z=1)
+    t0, xm, xp, c0 = tied(t0, xm, xp, c0)
     cm, cp = send(c0, dx=1), send(c0, dx=-1)
     f1, f2 = send(xm[:Q], dx=1), send(xp[Q:], dx=-1)
-    r2, cm, cp, f1, f2, *own = tied(r2, cm, cp, f1, f2, *own)
-    r3 = send(r2, split_z=1)
+    cm, cp, f1, f2, *own = tied(cm, cp, f1, f2, *own)
     g1, g2 = send(cm[:Q], dx=1), send(cp[Q:], dx=-1)
-    e12 = send(jnp.concatenate([r1, r2], axis=0), fc=1)
-    r3, g1, g2, e12 = tied(r3, g1, g2, e12)
-    r4 = send(lax.dynamic_slice_in_dim(r3, core * Q, Q, 0), split_z=1)
-    e34 = send(jnp.concatenate([r3, r4], axis=0), fc=1)
-    far, far_h = jnp.concatenate([f1, f2], axis=0), jnp.concatenate([g1, g2], axis=0)
-    return [a0, r1, r2, r3, r4, e12, e34, t0, xm, xp, far, c0, cm, cp, far_h], own
+    far = jnp.concatenate([f1, f2], axis=0)
+    g1, g2, far = tied(g1, g2, far)
+    return [t0, xm, xp, far, c0, cm, cp, jnp.concatenate([g1, g2], axis=0)], own
 
 
 def per_device(image_raw, text_raw, logit_scale_logarithm, logit_offset_bias):
@@ -175,10 +159,10 @@
     def quarter(block, l, c):
         return lax.dynamic_slice_in_dim(block, (l * 2 + c) * Q, Q, 0)
 
-    a0 = normalize(lax.dynamic_slice_in_dim(image_raw, yl * 2 * Q, 2 * Q, 0))[0].astype(bf16)
     t0 = jnp.concatenate([quarter(text_raw, 0, core), quarter(text_raw, 1, core)], axis=0)
     t0 = normalize(t0)[0].astype(bf16)
     image_unit, image_inv = normalize(quarter(image_raw, yl, core))
+    all_images = lax.all_gather(image_unit.astype(bf16), ("z", "core"), tiled=True)
     text_unit, text_inv = normalize(quarter(text_raw, yl, core))
     temperature, offset = jnp.exp(logit_scale_logarithm[0]), logit_offset_bias[0]
     params = jnp.stack([temperature, offset])
@@ -191,26 +175,41 @@
     match_weight = rounded(temperature * match_slope)
     match_sums = jnp.stack([temperature * jnp.sum(match_slope * match), jnp.sum(match_slope)])
     own = (image_unit, text_unit, image_inv, text_inv, image_low, text_low, match_loss, match_weight, match_sums)
-    chunks, own = gather(a0, t0, core, own)
+    texts, own = gather_texts(t0, own)
     image_unit, text_unit, image_inv, text_inv, image_low, text_low, match_loss, match_weight, match_sums = own
-    gi, gt, li, lt, sums = pairs_on_device(params, chunks)
-
-    half = gi[:512] + send(gi[512:].astype(f16), fc=1).astype(f32)
+    gi, gt, li, lt, sums = pairs_on_device(params, [all_images, *texts])
+
+    li = li.reshape(-1)
+    both = jnp.sum(sums, axis=1) + match_sums
+    met = send(jnp.concatenate([li[512:], both]), fc=1)
+    rows_met = send(gi[512:].astype(f16), fc=1)
+    li_half, both = li[:512] + met[:512], both + met[512:]
+    plane = jnp.concatenate([lt.reshape(-1), both])
+    for move in (dict(fy=1), dict(fx=1), dict(fy=3), dict(fx=2)):
+        plane = plane + send(plane, **move)
+    place = (lax.broadcasted_iota(jnp.int32, (NZ, 2), 0) == z).astype(f32)
+    here = (place * plane[None, 1024:]).reshape(-1)
+    far_small = send(jnp.concatenate([li_half[448:], here]), dz=4)
+    smalls = [
+        send(jnp.concatenate([li_half[k * 128 - Q : k * 128 + Q], here]), split_z=k) for k in (1, 2, 3)
+    ]
+    half = gi[:512] + rows_met.astype(f32)
     flight = half[Q:].astype(f16)
+    gt16 = gt.astype(f16)
+    plane, gt16 = tied(plane, gt16)
+    back_xy = lax.all_to_all(gt16, ("yh", "x", "yl"), 0, 0, tiled=True)
+    far_small, one, two, three, flight = tied(far_small, *smalls, flight)
+    small = one + two + three
+    small_met = send(
+        jnp.concatenate([lax.dynamic_slice_in_dim(small, (1 - core) * Q, Q, 0), small[128:]]), fc=1
+    )
+    image_loss = li_half[:Q] + far_small[:Q] + lax.dynamic_slice_in_dim(small, core * Q, Q, 0) + small_met[:Q]
+    every_z = here + far_small[Q:] + small[128:] + small_met[Q:]
+    both = jnp.sum(every_z.reshape(NZ, 2), axis=0)
+    text_loss = lax.dynamic_slice_in_dim(plane, ((yh * 4 + x) * 2 + yl) * Q, Q, 0)
     far = send(flight[384:], dz=4)
     three, two, one = (send(flight[(k - 1) * 128 : k * 128], split_z=k) for k in (3, 2, 1))
-    back_xy = lax.all_to_all(gt.astype(f16), ("yh", "x", "yl"), 0, 0, tiled=True)
-    both = jnp.sum(sums, axis=1) + match_sums
-    pack_c = jnp.concatenate([li.reshape(-1), both])
-    for move in (dict(fc=1), dict(fz=1), dict(fz=2), dict(fz=4)):
-        pack_c = pack_c + send(pack_c, **move)
-    pack_r = lt.reshape(-1)
-    for move in (dict(fy=1), dict(fx=1), dict(fy=3), dict(fx=2)):
-        pack_r = pack_r + send(pack_r, **move)
-    both = pack_c[1024:]
-    for move in (dict(fy=1), dict(fx=1), dict(fy=3), dict(fx=2)):
-        both = both + send(both, **move)
-    far, three, two, one, pack_c, pack_r, both = tied(far, three, two, one, pack_c, pack_r, both)
+    far, three, two, one, image_loss, both = tied(far, three, two, one, image_loss, both)
     arrived = one.astype(f32) + two.astype(f32) + three.astype(f32)
     theirs = lax.dynamic_slice_in_dim(arrived, (1 - core) * Q, Q, 0)
     gi_own = half[:Q] + far.astype(f32) + lax.dynamic_slice_in_dim(arrived, core * Q, Q, 0)
@@ -224,8 +223,7 @@
     )
     grad_text = text_inv * (gt_own - text_unit * jnp.sum(text_unit * gt_own, axis=-1, keepdims=True))
 
-    image_loss = lax.dynamic_slice_in_dim(pack_c, (core * 8 + z) * Q, Q, 0) + match_loss
-    text_loss = lax.dynamic_slice_in_dim(pack_r, ((yh * 4 + x) * 2 + yl) * Q, Q, 0) + match_loss
+    image_loss, text_loss = image_loss + match_loss, text_loss + match_loss
     return (grad_image, grad_text, image_loss, text_loss, both)
 
 

time: 161 us -> 165 us (1.025)
  between operations: 2.97 us -> 16.3 us
  waiting for transfers between devices: 50.6 us -> 43 us
  starting transfers between devices: 59 us -> 54 us
  local copies, waits for them, and re-layouts: 5.69 us -> 8.66 us
    ppermute x33 -> x25, waiting for transfers between devices: 50.6 us -> 27.2 us  [send(): return lax.ppermute(value, AXES, pairs)]
    all_gather x0 -> x1, waiting for transfers between devices: none -> 15.8 us  [per_device(): lax.all_gather(image_unit.astype(bf16), ('z', 'core'), tiled=True)]
    ppermute x33 -> x25, starting transfers between devices: 55.3 us -> 48.6 us  [send(): return lax.ppermute(value, AXES, pairs)]
    another operation x2, other arithmetic: 6.55 us -> 1.9 us
    add x13 -> x10, other arithmetic: 2.53 us -> 5.12 us  [the longest x1 1.9 us: per_device(): half = gi[:512] + rows_met.astype(f32)]
    reduce_sum x1, other arithmetic: 0.31 us -> 2.07 us  [per_device(): gt_own = jnp.sum(back_xy.reshape(16, Q, -1).astype(f32), axis=0)]
    all_to_all x1, starting transfers between devices: 3.72 us -> 5.41 us  [per_device(): back_xy = lax.all_to_all(gt16, ('yh', 'x', 'yl'), 0, 0, tiled=True)]
  transfers between devices with their start and end apart: 34 -> 27, of which waited for: 13 -> 12; matrix products, arithmetic and copies ran while one was open for 16% -> 16% of each run, Pallas kernels for 0% -> 0%
where the time goes in v1:
time: 165 us; the launch traced here: 164 us
  starting transfers between devices  54 us (33%)
  waiting for transfers between devices  43 us (26%)
  other arithmetic  28.7 us (17%)
  between operations  16.3 us (10%)
  Pallas kernels  13.3 us (8%)
  local copies, waits for them, and re-layouts  8.66 us (5%)
    ppermute x25, starting transfers between devices, send(): return lax.ppermute(value, AXES, pairs)  48.6 us
    ppermute x25, waiting for transfers between devices, send(): return lax.ppermute(value, AXES, pairs)  27.2 us
    all_gather x1, waiting for transfers between devices, per_device(): lax.all_gather(image_unit.astype(bf16), ('z', 'core'), tiled=True)  15.8 us
    pallas_call x1, Pallas kernels, pairs_on_device(): pl.pallas_call(pair_kernel, out_shape=(jax.ShapeDtypeStruct((1024, width)...  13.3 us
    all_to_all x1, starting transfers between devices, per_device(): back_xy = lax.all_to_all(gt16, ('yh', 'x', 'yl'), 0, 0, tiled=True)  5.41 us
    convert_element_type x1, other arithmetic, per_device(): gt16 = gt.astype(f16)  4 us
  transfers between devices with their start and end apart: 27, of which 12 were waited for; matrix products, arithmetic and copies ran while one was open for 16% of the time, Pallas kernels for 0%

profile of v1, /device:TPU:1, one launch (start us, length us, event | category | flops | bytes accessed | tf_op | source)
XLA Modules:
  0.0 164.0 jit_solution(3566597395517346076)
XLA Ops:
  7.2 1.0 fusion.3
  8.3 0.6 fusion.9
  8.8 1.0 fusion.2
  9.9 0.6 fusion.8
  10.5 2.3 %fusion.11 = (bf16[64,1152]{1,0:T(8,128)(2,1)}, f32[64,1152]{1,0:T(8,128)}, f32[64]{0:T(128)S(1)}, f32[64,1152]{1,0:T(8,128)}, f32[64,1152]{1,0:T(8,128)}, /*index=5*/f32[64,1152]{1,0:T(8,128)}) fusion(f32[64]{0:T(128)S(1)} %get-tuple-element.112, bf16[256,1152]{1,0:T(8,128)(2,1)} %param.4, s32[]{:T(128)S(6)} %select_n.27, f32[64]{0:T(128)S(1)} %get-tuple-element.110, ...), kind=kLoop, calls=%fused_computation.62 | loop fusion | flops 663488 | bytes 1622788 | tf_op jit(solution)/shard_map/convert_element_type | solution.py:165
  12.8 1.0 constant_dynamic-slice_fusion.2
  14.1 2.1 %collective-permute-start = (bf16[128,1152]{1,0:T(8,128)(2,1)S(1)}, bf16[128,1152]{1,0:T(8,128)(2,1)S(1)}, u32[]{:S(2)}, u32[]{:S(2)}) collective-permute-start(bf16[128,1152]{1,0:T(8,128)(2,1)S(1)} %fusion.1.refs_1_), channel_id=1, source_target_pairs={{0,4},{1,5},{2,6},{3,7},{4,8},{5,9},{6,10},{7,11},{8,12},{9,13},{1... | collective-permute-start | bytes 884744 | tf_op jit(solution)/shard_map/ppermute | solution.py:32
  16.2 1.4 collective-permute-start.1
  17.6 2.8 %collective-permute-start.2 = (bf16[128,1152]{1,0:T(8,128)(2,1)S(1)}, bf16[128,1152]{1,0:T(8,128)(2,1)S(1)}, u32[]{:S(2)}, u32[]{:S(2)}) collective-permute-start(bf16[128,1152]{1,0:T(8,128)(2,1)S(1)} %fusion.1.refs_1_), channel_id=1, source_target_pairs={{0,130},{1,131},{2,128},{3,129},{4,134},{5,135},{6,132},{7,133},{8... | collective-permute-start | bytes 884744 | tf_op jit(solution)/shard_map/ppermute | solution.py:32
  21.8 1.2 multiply_reduce_fusion.3
  22.9 0.5 collective-permute-done.1.refs_3_
  23.4 2.1 %collective-permute-done.2.refs_5_ = bf16[128,1152]{1,0:T(8,128)(2,1)S(1)} collective-permute-done((bf16[128,1152]{1,0:T(8,128)(2,1)S(1)}, bf16[128,1152]{1,0:T(8,128)(2,1)S(1)}, u32[]{:S(2)}, u32[]{:S(2)}) %collective-permute-start.2) | collective-permute-done | bytes 294944 | tf_op jit(solution)/shard_map/ppermute | solution.py:32
  25.9 2.2 %collective-permute-start.4 = (bf16[128,1152]{1,0:T(8,128)(2,1)S(1)}, bf16[128,1152]{1,0:T(8,128)(2,1)S(1)}, u32[]{:S(2)}, u32[]{:S(2)}) collective-permute-start(bf16[128,1152]{1,0:T(8,128)(2,1)S(1)} %collective-permute-done.2.refs_5_), channel_id=1, source_target_pairs={{0,12},{1,13},{2,14},{3,15},{4,0},{5,1},{6,2},{7,3},{8,4},{9,5},{1... | collective-permute-start | bytes 884744 | tf_op jit(solution)/shard_map/ppermute | solution.py:32
  28.2 0.5 multiply_reduce-precision_fusion
  28.8 2.7 %collective-permute-start.6 = (bf16[64,1152]{1,0:T(8,128)(2,1)S(1)}, bf16[64,1152]{1,0:T(8,128)(2,1)S(1)}, u32[]{:S(2)}, u32[]{:S(2)}) collective-permute-start(bf16[64,1152]{1,0:T(8,128)(2,1)S(1)} %slice.121), channel_id=1, source_target_pairs={{0,12},{1,13},{2,14},{3,15},{4,0},{5,1},{6,2},{7,3},{8,4},{9,5},{1... | collective-permute-start | bytes 442376 | tf_op jit(solution)/shard_map/ppermute | solution.py:32
  32.2 0.7 pad_maximum_fusion.8
  32.9 2.6 %collective-permute-done.5 = bf16[64,1152]{1,0:T(8,128)(2,1)S(1)} collective-permute-done((bf16[64,1152]{1,0:T(8,128)(2,1)S(1)}, bf16[64,1152]{1,0:T(8,128)(2,1)S(1)}, u32[]{:S(2)}, u32[]{:S(2)}) %collective-permute-start.5) | collective-permute-done | bytes 147488 | tf_op jit(solution)/shard_map/ppermute | solution.py:32
  35.5 1.5 collective-permute-start.7
  37.0 1.5 collective-permute-start.8
  38.6 2.4 %collective-permute-done.7 = bf16[64,1152]{1,0:T(8,128)(2,1)S(1)} collective-permute-done((bf16[64,1152]{1,0:T(8,128)(2,1)S(1)}, bf16[64,1152]{1,0:T(8,128)(2,1)S(1)}, u32[]{:S(2)}, u32[]{:S(2)}) %collective-permute-start.7) | collective-permute-done | bytes 147488 | tf_op jit(solution)/shard_map/ppermute | solution.py:32
  41.3 15.8 %all-gather.2.cloned.1.call-done.refs_0_ = bf16[1024,1152]{1,0:T(8,128)(2,1)} async-done(((bf16[64,1152]{1,0:T(8,128)(2,1)}), bf16[1024,1152]{1,0:T(8,128)(2,1)}) %all-gather.2.cloned.1.call-update) | async-done | bytes 2359312 | tf_op jit(solution)/shard_map/all_gather | solution.py:165
  57.1 1.7 %copy-done = bf16[1024,1152]{1,0:T(8,128)(2,1)S(1)} copy-done((bf16[1024,1152]{1,0:T(8,128)(2,1)S(1)}, bf16[1024,1152]{1,0:T(8,128)(2,1)}, u32[]{:S(2)}) %copy-start) | copy-done | bytes 2359320
  58.7 13.3 %pairs.1 = (f32[1024,1152]{1,0:T(8,128)}, f32[1024,1152]{1,0:T(8,128)}, f32[1024,1]{1,0:T(8,128)S(1)}, f32[1,1024]{1,0:T(1,128)S(1)}, f32[2,1024]{1,0:T(2,128)S(1)}) custom-call(f32[2]{0:T(128)S(1)} %pad_maximum_fusion.9.par_ref, bf16[1024,1152]{1,0:T(8,128)(2,1)S(1)} %copy-done, bf16[128,1152]{1,0:T(8,128)(2,1)S(1)} %fusion.1.refs_1_, ...), custom_call_target="tpu_custom_call" | custom-call | flops 7247757312 | bytes 14680064 | tf_op jit(solution)/shard_map/pairs/pallas_call | solution.py:115
  72.7 0.9 collective-permute-done.10
  73.6 1.1 collective-permute-start.11
  74.7 1.8 %slice_convert_fusion = f16[512,1152]{1,0:T(8,128)(2,1)S(1)} fusion(f32[1024,1152]{1,0:T(8,128)} %get-tuple-element.55), kind=kLoop, calls=%fused_computation.1 | loop fusion | flops 589824 | bytes 3538944 | tf_op jit(solution)/shard_map/convert.1
  76.5 0.6 collective-permute-start.9
  77.2 1.4 collective-permute-start.12
  78.5 4.0 %convert_element_type.49 = f16[1024,1152]{1,0:T(8,128)(2,1)} convert(f32[1024,1152]{1,0:T(8,128)} %get-tuple-element.73) | non-fusion elementwise | flops 1179648 | bytes 7077888 | tf_op jit(solution)/shard_map/convert_element_type | solution.py:198
  82.5 2.0 %collective-permute-start.13 = (f32[1026]{0:T(1024)S(1)}, f32[1026]{0:T(1024)S(1)}, u32[]{:S(2)}, u32[]{:S(2)}) collective-permute-start(f32[1026]{0:T(1024)S(1)} %add.183), channel_id=1, source_target_pairs={{0,130},{1,131},{2,128},{3,129},{4,134},{5,135},{6,132},{7,133},{8... | collective-permute-start | bytes 12320 | tf_op jit(solution)/shard_map/ppermute | solution.py:32
  84.5 1.7 %collective-permute-done.13 = f32[1026]{0:T(1024)S(1)} collective-permute-done((f32[1026]{0:T(1024)S(1)}, f32[1026]{0:T(1024)S(1)}, u32[]{:S(2)}, u32[]{:S(2)}) %collective-permute-start.13) | collective-permute-done | bytes 4136 | tf_op jit(solution)/shard_map/ppermute | solution.py:32
  86.2 2.3 %collective-permute-start.14 = (f32[1026]{0:T(1024)S(1)}, f32[1026]{0:T(1024)S(1)}, u32[]{:S(2)}, u32[]{:S(2)}) collective-permute-start(f32[1026]{0:T(1024)S(1)} %add.184), channel_id=1, source_target_pairs={{0,8},{1,9},{2,10},{3,11},{4,12},{5,13},{6,14},{7,15},{8,0},{9,1},... | collective-permute-start | bytes 12320 | tf_op jit(solution)/shard_map/ppermute | solution.py:32
  88.7 1.5 collective-permute-done.14
  90.4 0.6 pad_maximum_fusion.5
  91.0 1.6 collective-permute-start.16
  92.6 1.5 collective-permute-start.17
  94.1 2.1 %collective-permute-start.18 = (f32[144]{0:T(256)}, f32[144]{0:T(256)}, u32[]{:S(2)}, u32[]{:S(2)}) collective-permute-start(f32[144]{0:T(256)} %get-tuple-element.105), channel_id=1, source_target_pairs={{0,48},{1,81},{2,50},{3,83},{4,52},{5,85},{6,54},{7,87},{8,56},{9,... | collective-permute-start | bytes 1736 | tf_op jit(solution)/shard_map/ppermute | solution.py:32
  96.2 0.6 pad_maximum_fusion.10
  96.8 1.9 %collective-permute-start.15 = (f32[80]{0:T(128)}, f32[80]{0:T(128)S(1)}, u32[]{:S(2)}, u32[]{:S(2)}) collective-permute-start(f32[80]{0:T(128)} %pad_maximum_fusion.10), channel_id=1, source_target_pairs={{0,64},{1,65},{2,66},{3,67},{4,68},{5,69},{6,70},{7,71},{8,72},{9,... | collective-permute-start | bytes 968 | tf_op jit(solution)/shard_map/ppermute | solution.py:32
  98.7 5.4 %all-to-all-start = ((f16[16,64,1152]{2,1,0:T(8,128)(2,1)}), f16[16,64,1152]{2,1,0:T(8,128)(2,1)}, u32[]{:S(2)}, u32[]{:S(2)}) async-start(f16[16,64,1152]{2,1,0:T(8,128)(2,1)} %bitcast.9), calls=%async_computation | async-start | bytes 4718592 | tf_op jit(solution)/shard_map/all_to_all | solution.py:200
  104.2 1.9 %convert_add_fusion = f32[512,1152]{1,0:T(8,128)S(1)} fusion(f16[512,1152]{1,0:T(8,128)(2,1)S(1)} %collective-permute-done.9, f32[1024,1152]{1,0:T(8,128)} %get-tuple-element.55), kind=kLoop, calls=%fused_computation.2 | loop fusion | flops 1179648 | bytes 5898240 | tf_op jit(solution)/shard_map/add | solution.py:196
  106.7 0.7 add_add_fusion
  107.6 0.6 pad_maximum_fusion.11
  108.1 4.2 %collective-permute-start.23 = (f32[80]{0:T(128)}, f32[80]{0:T(128)}, u32[]{:S(2)}, u32[]{:S(2)}) collective-permute-start(f32[80]{0:T(128)} %pad_maximum_fusion.11), channel_id=1, source_target_pairs={{0,1},{1,0},{2,3},{3,2},{4,5},{5,4},{6,7},{7,6},{8,9},{9,8},{10,11... | collective-permute-start | bytes 968 | tf_op jit(solution)/shard_map/ppermute | solution.py:32
  112.3 0.7 slice.147
  113.1 0.7 slice.139
  113.8 1.0 fusion.14
  114.8 2.8 %collective-permute-start.20 = (f16[128,1152]{1,0:T(8,128)(2,1)}, f16[128,1152]{1,0:T(8,128)(2,1)S(1)}, u32[]{:S(2)}, u32[]{:S(2)}) collective-permute-start(f16[128,1152]{1,0:T(8,128)(2,1)} %get-tuple-element.90), channel_id=1, source_target_pairs={{0,48},{1,81},{2,50},{3,83},{4,52},{5,85},{6,54},{7,87},{8,56},{9,... | collective-permute-start | bytes 884744 | tf_op jit(solution)/shard_map/ppermute | solution.py:32
  117.6 2.7 %collective-permute-start.21 = (f16[128,1152]{1,0:T(8,128)(2,1)}, f16[128,1152]{1,0:T(8,128)(2,1)S(1)}, u32[]{:S(2)}, u32[]{:S(2)}) collective-permute-start(f16[128,1152]{1,0:T(8,128)(2,1)} %get-tuple-element.89), channel_id=1, source_target_pairs={{0,32},{1,97},{2,34},{3,99},{4,36},{5,101},{6,38},{7,103},{8,40},{... | collective-permute-start | bytes 884744 | tf_op jit(solution)/shard_map/ppermute | solution.py:32
  120.5 2.8 %collective-permute-start.19 = (f16[64,1152]{1,0:T(8,128)(2,1)}, f16[64,1152]{1,0:T(8,128)(2,1)}, u32[]{:S(2)}, u32[]{:S(2)}) collective-permute-start(f16[64,1152]{1,0:T(8,128)(2,1)} %slice.139), channel_id=1, source_target_pairs={{0,64},{1,65},{2,66},{3,67},{4,68},{5,69},{6,70},{7,71},{8,72},{9,... | collective-permute-start | bytes 442376 | tf_op jit(solution)/shard_map/ppermute | solution.py:32
  123.3 1.3 slice_add_fusion.2
  124.6 0.6 slice.150
  125.3 1.2 add_reduce_fusion
  126.6 9.8 %collective-permute-done.19 = f16[64,1152]{1,0:T(8,128)(2,1)} collective-permute-done((f16[64,1152]{1,0:T(8,128)(2,1)}, f16[64,1152]{1,0:T(8,128)(2,1)}, u32[]{:S(2)}, u32[]{:S(2)}) %collective-permute-start.19) | collective-permute-done | bytes 147488 | tf_op jit(solution)/shard_map/ppermute | solution.py:32
  136.3 1.9 %collective-permute-done.21 = f16[128,1152]{1,0:T(8,128)(2,1)S(1)} collective-permute-done((f16[128,1152]{1,0:T(8,128)(2,1)}, f16[128,1152]{1,0:T(8,128)(2,1)S(1)}, u32[]{:S(2)}, u32[]{:S(2)}) %collective-permute-start.21) | collective-permute-done | bytes 294944 | tf_op jit(solution)/shard_map/ppermute | solution.py:32
  138.3 3.5 %collective-permute-done.22 = f16[128,1152]{1,0:T(8,128)(2,1)} collective-permute-done((f16[128,1152]{1,0:T(8,128)(2,1)}, f16[128,1152]{1,0:T(8,128)(2,1)}, u32[]{:S(2)}, u32[]{:S(2)}) %collective-permute-start.22) | collective-permute-done | bytes 294944 | tf_op jit(solution)/shard_map/ppermute | solution.py:32
  141.8 1.1 convert_add_fusion.1
  142.9 0.8 copy-done.4
  143.7 0.8 constant_dynamic-slice_fusion
  144.5 6.2 %collective-permute-start.24 = (f32[64,1152]{1,0:T(8,128)}, f32[64,1152]{1,0:T(8,128)}, u32[]{:S(2)}, u32[]{:S(2)}) collective-permute-start(f32[64,1152]{1,0:T(8,128)} %constant_dynamic-slice_fusion), channel_id=1, source_target_pairs={{0,1},{1,0},{2,3},{3,2},{4,5},{5,4},{6,7},{7,6},{8,9},{9,8},{10,11... | collective-permute-start | bytes 884744 | tf_op jit(solution)/shard_map/ppermute | solution.py:32
  150.7 1.2 dynamic-slice_add_fusion
  151.9 2.1 %convert_reduce_fusion = f32[64,1152]{1,0:T(8,128)S(1)} fusion(f16[16,64,1152]{2,1,0:T(8,128)(2,1)} %all-to-all-done), kind=kLoop, calls=%fused_computation | loop fusion | flops 2285568 | bytes 2654208 | tf_op jit(solution)/shard_map/reduce_sum | solution.py:217
  154.3 2.0 %multiply_reduce_fusion.1 = (f32[64]{0:T(128)S(1)}, f32[64,1152]{1,0:T(8,128)S(1)}, f32[64,1152]{1,0:T(8,128)}) fusion(f32[64,1152]{1,0:T(8,128)S(1)} %copy-done.1, f32[64,1152]{1,0:T(8,128)S(1)} %copy-done.6, f32[64]{0:T(128)S(1)} %copy-done.9, f32[64,1152]{1,0:T(8,128)} %collective-permute-done.24, f32[128,1152]{1,0:T(8,128)S(1)} %copy-done.5, ...), kind=kLoop, calls=%fused_computation.26 | loop fusion | flops 958400 | bytes 3097604 | tf_op jit(solution)/shard_map/reduce_sum | solution.py:222
  156.3 0.8 subtract_multiply_fusion.1
  (84 shorter events, 3.7 us)
Async XLA Ops:
  7.2 49.9 %all-gather.2.cloned.1.call-start = ((), (), s32[]{:S(2)}) async-start(), calls=%async_computation.1 | async-start | bytes 2506752 | tf_op jit(solution)/shard_map/all_gather | solution.py:165
  14.1 8.9 %collective-permute-start = (bf16[128,1152]{1,0:T(8,128)(2,1)S(1)}, bf16[128,1152]{1,0:T(8,128)(2,1)S(1)}, u32[]{:S(2)}, u32[]{:S(2)}) collective-permute-start(bf16[128,1152]{1,0:T(8,128)(2,1)S(1)} %fusion.1.refs_1_), channel_id=1, source_target_pairs={{0,4},{1,5},{2,6},{3,7},{4,8},{5,9},{6,10},{7,11},{8,12},{9,13},{1... | collective-permute-start | bytes 884744 | tf_op jit(solution)/shard_map/ppermute | solution.py:32
  16.2 7.2 %collective-permute-start.1 = (bf16[128,1152]{1,0:T(8,128)(2,1)S(1)}, bf16[128,1152]{1,0:T(8,128)(2,1)S(1)}, u32[]{:S(2)}, u32[]{:S(2)}) collective-permute-start(bf16[128,1152]{1,0:T(8,128)(2,1)S(1)} %fusion.1.refs_1_), channel_id=1, source_target_pairs={{0,12},{1,13},{2,14},{3,15},{4,0},{5,1},{6,2},{7,3},{8,4},{9,5},{1... | collective-permute-start | bytes 884744 | tf_op jit(solution)/shard_map/ppermute | solution.py:32
  17.6 7.9 %collective-permute-start.2 = (bf16[128,1152]{1,0:T(8,128)(2,1)S(1)}, bf16[128,1152]{1,0:T(8,128)(2,1)S(1)}, u32[]{:S(2)}, u32[]{:S(2)}) collective-permute-start(bf16[128,1152]{1,0:T(8,128)(2,1)S(1)} %fusion.1.refs_1_), channel_id=1, source_target_pairs={{0,130},{1,131},{2,128},{3,129},{4,134},{5,135},{6,132},{7,133},{8... | collective-permute-start | bytes 884744 | tf_op jit(solution)/shard_map/ppermute | solution.py:32
  25.5 10.0 %collective-permute-start.3 = (bf16[128,1152]{1,0:T(8,128)(2,1)S(1)}, bf16[128,1152]{1,0:T(8,128)(2,1)S(1)}, u32[]{:S(2)}, u32[]{:S(2)}) collective-permute-start(bf16[128,1152]{1,0:T(8,128)(2,1)S(1)} %collective-permute-done.2.refs_5_), channel_id=1, source_target_pairs={{0,4},{1,5},{2,6},{3,7},{4,8},{5,9},{6,10},{7,11},{8,12},{9,13},{1... | collective-permute-start | bytes 884744 | tf_op jit(solution)/shard_map/ppermute | solution.py:32
  25.9 9.6 %collective-permute-start.4 = (bf16[128,1152]{1,0:T(8,128)(2,1)S(1)}, bf16[128,1152]{1,0:T(8,128)(2,1)S(1)}, u32[]{:S(2)}, u32[]{:S(2)}) collective-permute-start(bf16[128,1152]{1,0:T(8,128)(2,1)S(1)} %collective-permute-done.2.refs_5_), channel_id=1, source_target_pairs={{0,12},{1,13},{2,14},{3,15},{4,0},{5,1},{6,2},{7,3},{8,4},{9,5},{1... | collective-permute-start | bytes 884744 | tf_op jit(solution)/shard_map/ppermute | solution.py:32
  28.6 6.8 %collective-permute-start.5 = (bf16[64,1152]{1,0:T(8,128)(2,1)S(1)}, bf16[64,1152]{1,0:T(8,128)(2,1)S(1)}, u32[]{:S(2)}, u32[]{:S(2)}) collective-permute-start(bf16[64,1152]{1,0:T(8,128)(2,1)S(1)} %slice.120), channel_id=1, source_target_pairs={{0,4},{1,5},{2,6},{3,7},{4,8},{5,9},{6,10},{7,11},{8,12},{9,13},{1... | collective-permute-start | bytes 442376 | tf_op jit(solution)/shard_map/ppermute | solution.py:32
  28.8 6.7 %collective-permute-start.6 = (bf16[64,1152]{1,0:T(8,128)(2,1)S(1)}, bf16[64,1152]{1,0:T(8,128)(2,1)S(1)}, u32[]{:S(2)}, u32[]{:S(2)}) collective-permute-start(bf16[64,1152]{1,0:T(8,128)(2,1)S(1)} %slice.121), channel_id=1, source_target_pairs={{0,12},{1,13},{2,14},{3,15},{4,0},{5,1},{6,2},{7,3},{8,4},{9,5},{1... | collective-permute-start | bytes 442376 | tf_op jit(solution)/shard_map/ppermute | solution.py:32
  35.5 5.5 %collective-permute-start.7 = (bf16[64,1152]{1,0:T(8,128)(2,1)S(1)}, bf16[64,1152]{1,0:T(8,128)(2,1)S(1)}, u32[]{:S(2)}, u32[]{:S(2)}) collective-permute-start(bf16[64,1152]{1,0:T(8,128)(2,1)S(1)} %slice.122), channel_id=1, source_target_pairs={{0,4},{1,5},{2,6},{3,7},{4,8},{5,9},{6,10},{7,11},{8,12},{9,13},{1... | collective-permute-start | bytes 442376 | tf_op jit(solution)/shard_map/ppermute | solution.py:32
  37.0 4.3 %collective-permute-start.8 = (bf16[64,1152]{1,0:T(8,128)(2,1)S(1)}, bf16[64,1152]{1,0:T(8,128)(2,1)S(1)}, u32[]{:S(2)}, u32[]{:S(2)}) collective-permute-start(bf16[64,1152]{1,0:T(8,128)(2,1)S(1)} %slice.123), channel_id=1, source_target_pairs={{0,12},{1,13},{2,14},{3,15},{4,0},{5,1},{6,2},{7,3},{8,4},{9,5},{1... | collective-permute-start | bytes 442376 | tf_op jit(solution)/shard_map/ppermute | solution.py:32
  57.1 1.7 %copy-start = (bf16[1024,1152]{1,0:T(8,128)(2,1)S(1)}, bf16[1024,1152]{1,0:T(8,128)(2,1)}, u32[]{:S(2)}) copy-start(bf16[1024,1152]{1,0:T(8,128)(2,1)} %all-gather.2.cloned.1.call-done.refs_0_) | copy-start | bytes 7077892
  72.4 1.3 collective-permute-start.10
  73.6 3.5 %collective-permute-start.11 = (f32[1026]{0:T(1024)S(1)}, f32[1026]{0:T(1024)S(1)}, u32[]{:S(2)}, u32[]{:S(2)}) collective-permute-start(f32[1026]{0:T(1024)S(1)} %pad_maximum_fusion.3), channel_id=1, source_target_pairs={{0,2},{1,3},{2,0},{3,1},{4,6},{5,7},{6,4},{7,5},{8,10},{9,11},{10,... | collective-permute-start | bytes 12320 | tf_op jit(solution)/shard_map/ppermute | solution.py:32
  76.5 27.6 %collective-permute-start.9 = (f16[512,1152]{1,0:T(8,128)(2,1)S(1)}, f16[512,1152]{1,0:T(8,128)(2,1)S(1)}, u32[]{:S(2)}, u32[]{:S(2)}) collective-permute-start(f16[512,1152]{1,0:T(8,128)(2,1)S(1)} %slice_convert_fusion), channel_id=1, source_target_pairs={{0,1},{1,0},{2,3},{3,2},{4,5},{5,4},{6,7},{7,6},{8,9},{9,8},{10,11... | collective-permute-start | bytes 3538952 | tf_op jit(solution)/shard_map/ppermute | solution.py:32
  77.2 5.4 %collective-permute-start.12 = (f32[1026]{0:T(1024)S(1)}, f32[1026]{0:T(1024)S(1)}, u32[]{:S(2)}, u32[]{:S(2)}) collective-permute-start(f32[1026]{0:T(1024)S(1)} %fusion.7), channel_id=1, source_target_pairs={{0,4},{1,5},{2,6},{3,7},{4,0},{5,1},{6,2},{7,3},{8,12},{9,13},{10,... | collective-permute-start | bytes 12320 | tf_op jit(solution)/shard_map/ppermute | solution.py:32
  78.5 25.6 %copy-start.10 = (pred[8]{0:T(512)(128)(4,1)}, pred[8]{0:T(512)(128)(4,1)S(1)}, u32[]{:S(2)}) copy-start(pred[8]{0:T(512)(128)(4,1)S(1)} %iota_compare_fusion) | copy-start | bytes 28
  82.5 3.7 %collective-permute-start.13 = (f32[1026]{0:T(1024)S(1)}, f32[1026]{0:T(1024)S(1)}, u32[]{:S(2)}, u32[]{:S(2)}) collective-permute-start(f32[1026]{0:T(1024)S(1)} %add.183), channel_id=1, source_target_pairs={{0,130},{1,131},{2,128},{3,129},{4,134},{5,135},{6,132},{7,133},{8... | collective-permute-start | bytes 12320 | tf_op jit(solution)/shard_map/ppermute | solution.py:32
  84.5 19.6 %copy-start.7 = (f32[512]{0:T(512)}, f32[512]{0:T(512)S(1)}, u32[]{:S(2)}) copy-start(f32[512]{0:T(512)S(1)} %slice_add_fusion.1) | copy-start | bytes 6148
  86.2 4.0 %collective-permute-start.14 = (f32[1026]{0:T(1024)S(1)}, f32[1026]{0:T(1024)S(1)}, u32[]{:S(2)}, u32[]{:S(2)}) collective-permute-start(f32[1026]{0:T(1024)S(1)} %add.184), channel_id=1, source_target_pairs={{0,8},{1,9},{2,10},{3,11},{4,12},{5,13},{6,14},{7,15},{8,0},{9,1},... | collective-permute-start | bytes 12320 | tf_op jit(solution)/shard_map/ppermute | solution.py:32
  90.3 8.5 %copy-start.11 = (f32[2]{0:T(128)}, f32[2]{0:T(128)S(1)}, u32[]{:S(2)}) copy-start(f32[2]{0:T(128)S(1)} %slice.154) | copy-start | bytes 28
  91.0 15.2 %collective-permute-start.16 = (f32[144]{0:T(256)}, f32[144]{0:T(256)}, u32[]{:S(2)}, u32[]{:S(2)}) collective-permute-start(f32[144]{0:T(256)} %get-tuple-element.107), channel_id=1, source_target_pairs={{0,16},{1,113},{2,18},{3,115},{4,20},{5,117},{6,22},{7,119},{8,24}... | collective-permute-start | bytes 1736 | tf_op jit(solution)/shard_map/ppermute | solution.py:32
  92.6 13.6 %collective-permute-start.17 = (f32[144]{0:T(256)}, f32[144]{0:T(256)}, u32[]{:S(2)}, u32[]{:S(2)}) collective-permute-start(f32[144]{0:T(256)} %get-tuple-element.106), channel_id=1, source_target_pairs={{0,32},{1,97},{2,34},{3,99},{4,36},{5,101},{6,38},{7,103},{8,40},{... | collective-permute-start | bytes 1736 | tf_op jit(solution)/shard_map/ppermute | solution.py:32
  94.1 12.2 %collective-permute-start.18 = (f32[144]{0:T(256)}, f32[144]{0:T(256)}, u32[]{:S(2)}, u32[]{:S(2)}) collective-permute-start(f32[144]{0:T(256)} %get-tuple-element.105), channel_id=1, source_target_pairs={{0,48},{1,81},{2,50},{3,83},{4,52},{5,85},{6,54},{7,87},{8,56},{9,... | collective-permute-start | bytes 1736 | tf_op jit(solution)/shard_map/ppermute | solution.py:32
  96.8 9.4 %collective-permute-start.15 = (f32[80]{0:T(128)}, f32[80]{0:T(128)S(1)}, u32[]{:S(2)}, u32[]{:S(2)}) collective-permute-start(f32[80]{0:T(128)} %pad_maximum_fusion.10), channel_id=1, source_target_pairs={{0,64},{1,65},{2,66},{3,67},{4,68},{5,69},{6,70},{7,71},{8,72},{9,... | collective-permute-start | bytes 968 | tf_op jit(solution)/shard_map/ppermute | solution.py:32
  98.7 53.2 %all-to-all-start = ((f16[16,64,1152]{2,1,0:T(8,128)(2,1)}), f16[16,64,1152]{2,1,0:T(8,128)(2,1)}, u32[]{:S(2)}, u32[]{:S(2)}) async-start(f16[16,64,1152]{2,1,0:T(8,128)(2,1)} %bitcast.9), calls=%async_computation | async-start | bytes 4718592 | tf_op jit(solution)/shard_map/all_to_all | solution.py:200
  106.2 0.5 copy-start.14
  107.4 10.2 %copy-start.8 = (f32[144]{0:T(256)}, f32[144]{0:T(256)S(1)}, u32[]{:S(2)}) copy-start(f32[144]{0:T(256)S(1)} %add_add_fusion) | copy-start | bytes 1732
  108.1 15.2 %collective-permute-start.23 = (f32[80]{0:T(128)}, f32[80]{0:T(128)}, u32[]{:S(2)}, u32[]{:S(2)}) collective-permute-start(f32[80]{0:T(128)} %pad_maximum_fusion.11), channel_id=1, source_target_pairs={{0,1},{1,0},{2,3},{3,2},{4,5},{5,4},{6,7},{7,6},{8,9},{9,8},{10,11... | collective-permute-start | bytes 968 | tf_op jit(solution)/shard_map/ppermute | solution.py:32
  114.8 21.5 %collective-permute-start.20 = (f16[128,1152]{1,0:T(8,128)(2,1)}, f16[128,1152]{1,0:T(8,128)(2,1)S(1)}, u32[]{:S(2)}, u32[]{:S(2)}) collective-permute-start(f16[128,1152]{1,0:T(8,128)(2,1)} %get-tuple-element.90), channel_id=1, source_target_pairs={{0,48},{1,81},{2,50},{3,83},{4,52},{5,85},{6,54},{7,87},{8,56},{9,... | collective-permute-start | bytes 884744 | tf_op jit(solution)/shard_map/ppermute | solution.py:32
  117.6 20.7 %collective-permute-start.21 = (f16[128,1152]{1,0:T(8,128)(2,1)}, f16[128,1152]{1,0:T(8,128)(2,1)S(1)}, u32[]{:S(2)}, u32[]{:S(2)}) collective-permute-start(f16[128,1152]{1,0:T(8,128)(2,1)} %get-tuple-element.89), channel_id=1, source_target_pairs={{0,32},{1,97},{2,34},{3,99},{4,36},{5,101},{6,38},{7,103},{8,40},{... | collective-permute-start | bytes 884744 | tf_op jit(solution)/shard_map/ppermute | solution.py:32
  120.3 21.5 %collective-permute-start.22 = (f16[128,1152]{1,0:T(8,128)(2,1)}, f16[128,1152]{1,0:T(8,128)(2,1)}, u32[]{:S(2)}, u32[]{:S(2)}) collective-permute-start(f16[128,1152]{1,0:T(8,128)(2,1)} %get-tuple-element.88), channel_id=1, source_target_pairs={{0,16},{1,113},{2,18},{3,115},{4,20},{5,117},{6,22},{7,119},{8,24}... | collective-permute-start | bytes 884744 | tf_op jit(solution)/shard_map/ppermute | solution.py:32
  120.5 15.8 %collective-permute-start.19 = (f16[64,1152]{1,0:T(8,128)(2,1)}, f16[64,1152]{1,0:T(8,128)(2,1)}, u32[]{:S(2)}, u32[]{:S(2)}) collective-permute-start(f16[64,1152]{1,0:T(8,128)(2,1)} %slice.139), channel_id=1, source_target_pairs={{0,64},{1,65},{2,66},{3,67},{4,68},{5,69},{6,70},{7,71},{8,72},{9,... | collective-permute-start | bytes 442376 | tf_op jit(solution)/shard_map/ppermute | solution.py:32
  126.6 27.5 %copy-start.2 = (f32[64,1152]{1,0:T(8,128)S(1)}, f32[64,1152]{1,0:T(8,128)}, u32[]{:S(2)}) copy-start(f32[64,1152]{1,0:T(8,128)} %get-tuple-element.75) | copy-start | bytes 884740
  126.6 27.5 %copy-start.3 = (f32[64,1152]{1,0:T(8,128)S(1)}, f32[64,1152]{1,0:T(8,128)}, u32[]{:S(2)}) copy-start(f32[64,1152]{1,0:T(8,128)} %get-tuple-element.76) | copy-start | bytes 884740
  126.6 27.5 %copy-start.9 = (f32[64]{0:T(128)S(1)}, f32[64]{0:T(128)}, u32[]{:S(2)}) copy-start(f32[64]{0:T(128)} %multiply_reduce-precision_fusion) | copy-start | bytes 772
  142.9 0.8 copy-start.4
  143.7 10.6 %copy-start.1 = (f32[64,1152]{1,0:T(8,128)S(1)}, f32[64,1152]{1,0:T(8,128)}, u32[]{:S(2)}) copy-start(f32[64,1152]{1,0:T(8,128)} %get-tuple-element.71) | copy-start | bytes 884740
  143.7 10.6 %copy-start.6 = (f32[64,1152]{1,0:T(8,128)S(1)}, f32[64,1152]{1,0:T(8,128)}, u32[]{:S(2)}) copy-start(f32[64,1152]{1,0:T(8,128)} %get-tuple-element.70) | copy-start | bytes 884740
  143.7 10.6 %copy-start.13 = (f32[64,1]{0,1:T(1,128)S(1)}, f32[64,1]{0,1:T(1,128)}, u32[]{:S(2)}) copy-start(f32[64,1]{0,1:T(1,128)} %get-tuple-element.72) | copy-start | bytes 772
  144.5 9.8 %collective-permute-start.24 = (f32[64,1152]{1,0:T(8,128)}, f32[64,1152]{1,0:T(8,128)}, u32[]{:S(2)}, u32[]{:S(2)}) collective-permute-start(f32[64,1152]{1,0:T(8,128)} %constant_dynamic-slice_fusion), channel_id=1, source_target_pairs={{0,1},{1,0},{2,3},{3,2},{4,5},{5,4},{6,7},{7,6},{8,9},{9,8},{10,11... | collective-permute-start | bytes 884744 | tf_op jit(solution)/shard_map/ppermute | solution.py:32
  151.9 2.4 %copy-start.5 = (f32[128,1152]{1,0:T(8,128)S(1)}, f32[128,1152]{1,0:T(8,128)}, u32[]{:S(2)}) copy-start(f32[128,1152]{1,0:T(8,128)} %copy-done.4) | copy-start | bytes 1769476
  154.0 2.3 %copy-start.12 = (f32[64,1]{0,1:T(1,128)S(1)}, f32[64,1]{0,1:T(1,128)}, u32[]{:S(2)}) copy-start(f32[64,1]{0,1:T(1,128)} %get-tuple-element.46) | copy-start | bytes 772
Sparse Core Ops, SparseCore 0:
  12.9 44.0 all-gather.1

commit v2 on v1

v2 whole, which is shorter than its diff:
```python
import jax
import jax.numpy as jnp
from jax import lax
from jax.experimental import pallas as pl
from jax.experimental.pallas import tpu as pltpu
from jax.sharding import Mesh, PartitionSpec as P

AXES = ("yh", "z", "x", "yl", "core")
YH, NZ, NX, YL, NC = 2, 8, 4, 2, 2
Q = 64


def table(move):
    pairs = []
    for yh in range(YH):
        for z in range(NZ):
            for x in range(NX):
                for yl in range(YL):
                    for c in range(NC):
                        y2, z2, x2, c2 = move(yh * 2 + yl, z, x, c)
                        y2, z2, x2 = y2 % 4, z2 % NZ, x2 % NX
                        source = (((yh * NZ + z) * NX + x) * YL + yl) * NC + c
                        target = (((y2 // 2 * NZ + z2) * NX + x2) * YL + y2 % 2) * NC + c2
                        pairs.append((source, target))
    return pairs


def send(value, dx=0, dz=0, fy=0, fz=0, fx=0, fc=0, split_z=0):
    pairs = table(
        lambda y, z, x, c: (y ^ fy, (z + dz + (1 - 2 * c) * split_z) ^ fz, (x + dx) ^ fx, c ^ fc)
    )
    return lax.ppermute(value, AXES, pairs)


def rounded(value):
    return lax.reduce_precision(value, 8, 7)


SUM_SCALE = 2.0**-14


def parts_of(values):
    high = lax.reduce_precision(values, 5, 10)
    return high, lax.reduce_precision(values - high, 5, 10)


def extra_rows(losses, sums, width):
    rows = [jnp.pad(v, (0, width - v.shape[0])) for v in (*losses, *sums)]
    return jnp.pad(jnp.stack(rows), ((0, 4), (0, 0))).astype(jnp.float16)


def normalize(embedding):
    floats = embedding.astype(jnp.float32)
    inverse = lax.rsqrt(jnp.sum(floats * floats, axis=-1, keepdims=True) + 1e-06)
    return (floats * inverse, inverse)


ROWS = 256


def pair_kernel(par_ref, *refs):
    a0, r1, r2, r3, r4, met = refs[:6]
    txt_in = refs[6:14]
    w_ref, img, txt, li_ref, lt_ref, sums_ref = refs[14:]
    x, yh, core = lax.axis_index("x"), lax.axis_index("yh"), lax.axis_index("core")
    img[0:64, :] = a0[pl.ds(pl.multiple_of(core * Q, Q), Q), :]
    img[64:448, :] = met[0:384, :]
    img[448:512, :] = r4[...]
    img[512:576, :] = a0[pl.ds(pl.multiple_of((1 - core) * Q, Q), Q), :]
    img[576:704, :] = r1[...]
    img[704:832, :] = r2[...]
    img[832:960, :] = r3[...]
    img[960:1024, :] = met[384:448, :]
    text_places = [
        (h * NX + lax.rem(x + dx, NX)) * 2 for h in (yh, 1 - yh) for dx in (0, NX - 1, 1, 2)
    ]
    own_column = (text_places[0] + lax.axis_index("yl")) * Q
    for k, ref in enumerate(txt_in):
        rows = ref.shape[0]
        txt[pl.ds(pl.multiple_of(text_places[k] * Q, Q), rows), :] = ref[...]
    temperature = par_ref[0]
    offset = par_ref[1]
    texts = txt[...]
    loss_cols = slope_sum = scale_sum = None
    for r in range(1024 // ROWS):
        images = img[r * ROWS : (r + 1) * ROWS, :]
        scores = lax.dot_general(
            images, texts, (((1,), (1,)), ((), ())), preferred_element_type=jnp.float32
        )
        p = jnp.exp(scores * temperature + offset)
        if r == 0:
            row = lax.broadcasted_iota(jnp.int32, (ROWS, 1024), 0)
            column = lax.broadcasted_iota(jnp.int32, (ROWS, 1024), 1)
            match = (column - row == own_column) & (row < Q)
            p = jnp.where(match, 0.0, p)
        q = 1.0 + p
        slopes = p / q
        losses = jnp.where(p < 0.0009765625, p - 0.5 * p * p, jnp.log(q))
        weights = (temperature * slopes).astype(jnp.bfloat16)
        w_ref[r * ROWS : (r + 1) * ROWS, :] = weights
        li_ref[r * ROWS : (r + 1) * ROWS, :] = jnp.sum(losses, axis=1, keepdims=True)
        cols = jnp.sum(losses, axis=0, keepdims=True)
        s1 = jnp.sum(slopes, axis=0, keepdims=True)
        s2 = jnp.sum(slopes * scores, axis=0, keepdims=True)
        if r == 0:
            loss_cols, slope_sum, scale_sum = cols, s1, s2
        else:
            loss_cols, slope_sum, scale_sum = loss_cols + cols, slope_sum + s1, scale_sum + s2
    lt_ref[...] = loss_cols
    sums_ref[0:1, :] = temperature * scale_sum
    sums_ref[1:2, :] = slope_sum


def pairs_on_device(params, chunks):
    width = chunks[0].shape[1]
    vmem = pl.BlockSpec(memory_space=pltpu.VMEM)
    smem = pl.BlockSpec(memory_space=pltpu.SMEM)
    f32 = jnp.float32
    return pl.pallas_call(
        pair_kernel,
        out_shape=(
            jax.ShapeDtypeStruct((1024, 1024), jnp.bfloat16),
            jax.ShapeDtypeStruct((1024, width), jnp.bfloat16),
            jax.ShapeDtypeStruct((1024, width), jnp.bfloat16),
            jax.ShapeDtypeStruct((1024, 1), f32),
            jax.ShapeDtypeStruct((1, 1024), f32),
            jax.ShapeDtypeStruct((2, 1024), f32),
        ),
        in_specs=[smem] + [vmem] * len(chunks),
        out_specs=(vmem,) * 6,
        compiler_params=pltpu.CompilerParams(vmem_limit_bytes=28 * 1024 * 1024),
        cost_estimate=pl.CostEstimate(
            flops=2 * 1024 * 1024 * width, bytes_accessed=12 * 1024 * 1024, transcendentals=3 * 1024 * 1024
        ),
        name="pairs",
    )(params, *chunks)


def tied(*values):
    return lax.optimization_barrier(values)


def gather(a0, t0, core, own):
    r3, r2 = send(a0, split_z=3), send(a0, split_z=2)
    xm, xp, c0 = send(t0, dx=1), send(t0, dx=-1), send(t0, fy=3)
    a0, t0, xm, xp, c0 = tied(a0, t0, xm, xp, c0)
    cm, cp = send(c0, dx=1), send(c0, dx=-1)
    f1, f2 = send(xm[:Q], dx=1), send(xp[Q:], dx=-1)
    a0, r3, r2, cm, cp, f1, f2, *own = tied(a0, r3, r2, cm, cp, f1, f2, *own)
    g1, g2 = send(cm[:Q], dx=1), send(cp[Q:], dx=-1)
    r1 = send(a0, split_z=1)
    r4 = send(lax.dynamic_slice_in_dim(a0, core * Q, Q, 0), dz=4)
    far = jnp.concatenate([f1, f2], axis=0)
    r1, r4, g1, g2, far = tied(r1, r4, g1, g2, far)
    met = send(jnp.concatenate([r1, r2, r3, r4], axis=0), fc=1)
    far_h = jnp.concatenate([g1, g2], axis=0)
    return [a0, r1, r2, r3, r4, met, t0, xm, xp, far, c0, cm, cp, far_h], own


def per_device(image_raw, text_raw, logit_scale_logarithm, logit_offset_bias):
    z, x = lax.axis_index("z"), lax.axis_index("x")
    width = image_raw.shape[1]
    yh, yl, core = lax.axis_index("yh"), lax.axis_index("yl"), lax.axis_index("core")
    f32, f16, bf16 = jnp.float32, jnp.float16, jnp.bfloat16

    def quarter(block, l, c):
        return lax.dynamic_slice_in_dim(block, (l * 2 + c) * Q, Q, 0)

    a0 = normalize(lax.dynamic_slice_in_dim(image_raw, yl * 2 * Q, 2 * Q, 0))[0].astype(bf16)
    t0 = jnp.concatenate([quarter(text_raw, 0, core), quarter(text_raw, 1, core)], axis=0)
    t0 = normalize(t0)[0].astype(bf16)
    image_unit, image_inv = normalize(quarter(image_raw, yl, core))
    text_unit, text_inv = normalize(quarter(text_raw, yl, core))
    temperature, offset = jnp.exp(logit_scale_logarithm[0]), logit_offset_bias[0]
    params = jnp.stack([temperature, offset])

    image_low, text_low = rounded(image_unit), rounded(text_unit)
    match = jnp.sum(image_low * text_low, axis=-1)
    match_logit = temperature * match + offset
    match_loss = jnp.log1p(jnp.exp(-match_logit))
    match_slope = -1.0 / (1.0 + jnp.exp(match_logit))
    match_weight = rounded(temperature * match_slope)
    match_sums = jnp.stack([temperature * jnp.sum(match_slope * match), jnp.sum(match_slope)])
    own = (image_unit, text_unit, image_inv, text_inv, image_low, text_low, match_loss, match_weight, match_sums)
    chunks, own = gather(a0, t0, core, own)
    image_unit, text_unit, image_inv, text_inv, image_low, text_low, match_loss, match_weight, match_sums = own
    weights, images, texts, li, lt, sums = pairs_on_device(params, chunks)

    li = li.reshape(-1)
    both = jnp.sum(sums, axis=1) + match_sums
    met = send(jnp.concatenate([li[512:], both]), fc=1)
    others = jnp.dot(weights[512:], texts, preferred_element_type=f32).astype(f16)
    met, others = tied(met, others)
    rows_met = send(others, fc=1)
    li_half, both = li[:512] + met[:512], both + met[512:]
    plane = jnp.concatenate([lt.reshape(-1), both])
    plane = plane + send(plane, fy=1)
    half = jnp.dot(weights[:512], texts, preferred_element_type=f32) + rows_met.astype(f32)
    flight = half[Q:].astype(f16)
    plane, half, flight = tied(plane, half, flight)
    plane = plane + send(plane, fx=1)
    gt16 = lax.dot_general(
        weights, images, (((0,), (0,)), ((), ())), preferred_element_type=f32
    ).astype(f16)
    plane, gt16 = tied(plane, gt16)
    for move in (dict(fy=3), dict(fx=2)):
        plane = plane + send(plane, **move)
    back_xy = lax.all_to_all(gt16, ("yh", "x", "yl"), 0, 0, tiled=True)
    text_loss = lax.dynamic_slice_in_dim(plane, ((yh * 4 + x) * 2 + yl) * Q, Q, 0)
    place = (lax.broadcasted_iota(jnp.int32, (NZ, 2), 0) == z).astype(f32)
    here = parts_of((place * plane[None, 1024:]).reshape(-1) * SUM_SCALE)
    far = send(jnp.concatenate([flight[384:], extra_rows(parts_of(li_half[448:]), here, width)]), dz=4)
    three, two, one = (
        send(
            jnp.concatenate(
                [
                    flight[(k - 1) * 128 : k * 128],
                    extra_rows(parts_of(li_half[k * 128 - Q : k * 128 + Q]), here, width),
                ]
            ),
            split_z=k,
        )
        for k in (3, 2, 1)
    )
    far, three, two, one = tied(far, three, two, one)
    arrived = one.astype(f32) + two.astype(f32) + three.astype(f32)
    theirs = jnp.concatenate([lax.dynamic_slice_in_dim(arrived, (1 - core) * Q, Q, 0), arrived[128:]])
    met = send(theirs, fc=1)
    gi_own = half[:Q] + far[:Q].astype(f32) + lax.dynamic_slice_in_dim(arrived, core * Q, Q, 0) + met[:Q]

    def own_losses(rows):
        return lax.dynamic_slice_in_dim(rows[0, :128] + rows[1, :128], core * Q, Q, 0)

    far_rows = far[Q:].astype(f32)
    image_loss = li_half[:Q] + far_rows[0, :Q] + far_rows[1, :Q] + own_losses(arrived[128:]) + own_losses(met[Q:])
    every_z = far_rows[2:4, : 2 * NZ] + arrived[130:132, : 2 * NZ] + met[Q + 2 : Q + 4, : 2 * NZ] + jnp.stack(here)
    both = jnp.sum((every_z[0] + every_z[1]).reshape(NZ, 2), axis=0) / SUM_SCALE
    gt_own = jnp.sum(back_xy.reshape(16, Q, -1).astype(f32), axis=0)

    gi_own = gi_own + match_weight[:, None] * text_low
    gt_own = gt_own + match_weight[:, None] * image_low
    grad_image = image_inv * (
        gi_own - image_unit * jnp.sum(image_unit * gi_own, axis=-1, keepdims=True)
    )
    grad_text = text_inv * (gt_own - text_unit * jnp.sum(text_unit * gt_own, axis=-1, keepdims=True))

    image_loss, text_loss = image_loss + match_loss, text_loss + match_loss
    return (grad_image, grad_text, image_loss, text_loss, both)


def solution(mesh):
    fine = Mesh(mesh.devices.reshape(YH, NZ, NX, YL, NC), AXES)
    dp = ("yh", "z", "x")
    in_specs = (P(dp, None), P(dp, None), P(), P())
    out_specs = (P(AXES, None), P(AXES, None), P(AXES), P(AXES), P())
    return jax.shard_map(
        per_device, mesh=fine, in_specs=in_specs, out_specs=out_specs, check_vma=False
    )
```

time: 165 us -> 143 us (0.87)
  between operations: 16.3 us -> 3.23 us
  matrix products: 0 us -> 9.45 us
  Pallas kernels: 13.3 us -> 6.25 us
  other arithmetic: 28.7 us -> 23.5 us
  waiting for transfers between devices: 43 us -> 38.9 us
  starting transfers between devices: 54 us -> 52.3 us
    all_gather x1 -> x0, waiting for transfers between devices: 15.8 us -> none  [per_device(): lax.all_gather(image_unit.astype(bf16), ('z', 'core'), tiled=True)]
    ppermute x25, waiting for transfers between devices: 27.2 us -> 38.9 us  [send(): return lax.ppermute(value, AXES, pairs)]
    dot_general x0 -> x3, matrix products: none -> 9.45 us  [the longest x1 4.25 us: per_device(): lax.dot_general(weights, images, (((0,), (0,)), ((), ())), preferred_elem...]
    pallas_call x1, Pallas kernels: 13.3 us -> 6.25 us  [pairs_on_device(): pl.pallas_call(pair_kernel, out_shape=(jax.ShapeDtypeStruct((1024, 1024),...]
    convert_element_type x2, other arithmetic: 6.29 us -> 1.09 us  [the longest x1 1.09 us: per_device(): normalize(lax.dynamic_slice_in_dim(image_raw, yl * 2 * Q, 2 * Q, 0))[0]]
    concatenate x5 -> x8, other arithmetic: 1.83 us -> 5.42 us  [the longest x3 2.37 us: per_device(): jnp.concatenate([flight[(k - 1) * 128:k * 128], extra_rows(parts_of(li_ha...]
    unnamed x30 -> x46, local copies, waits for them, and re-layouts: 2.98 us -> 5.65 us
    slice x14 -> x7, local copies, waits for them, and re-layouts: 2.5 us -> 0.09 us  [the longest x1 0.03 us: per_device(): flight[384:]]
  transfers between devices with their start and end apart: 27 -> 26, of which waited for: 12 -> 10; matrix products, arithmetic and copies ran while one was open for 16% -> 19% of each run, Pallas kernels for 0% -> 0%
where the time goes in v2:
time: 143 us; the launch traced here: 142 us
  starting transfers between devices  52.3 us (37%)
  waiting for transfers between devices  38.9 us (27%)
  other arithmetic  23.5 us (16%)
  matrix products  9.45 us (7%)
  local copies, waits for them, and re-layouts  8.3 us (6%)
  Pallas kernels  6.25 us (4%)
  between operations  3.23 us (2%)
    ppermute x25, starting transfers between devices, send(): return lax.ppermute(value, AXES, pairs)  48.6 us
    ppermute x25, waiting for transfers between devices, send(): return lax.ppermute(value, AXES, pairs)  38.9 us
    pallas_call x1, Pallas kernels, pairs_on_device(): pl.pallas_call(pair_kernel, out_shape=(jax.ShapeDtypeStruct((1024, 1024),...  6.25 us
    unnamed x46, local copies, waits for them, and re-layouts  5.65 us
    dot_general x1, matrix products, per_device(): lax.dot_general(weights, images, (((0,), (0,)), ((), ())), preferred_elem...  4.25 us
    all_to_all x1, starting transfers between devices, per_device(): back_xy = lax.all_to_all(gt16, ('yh', 'x', 'yl'), 0, 0, tiled=True)  3.74 us
    dot_general x1, matrix products, per_device(): jnp.dot(weights[512:], texts, preferred_element_type=f32).astype(f16)  3.65 us
  transfers between devices with their start and end apart: 26, of which 10 were waited for; matrix products, arithmetic and copies ran while one was open for 19% of the time, Pallas kernels for 0%

profile of v2, /device:TPU:1, one launch (start us, length us, event | category | flops | bytes accessed | tf_op | source)
XLA Modules:
  0.0 142.0 jit_solution(13105274906897452741)
XLA Ops:
  0.7 1.1 constant_dynamic-slice_fusion.5
  2.0 3.7 %collective-permute-start.2 = (bf16[128,1152]{1,0:T(8,128)(2,1)S(1)}, bf16[128,1152]{1,0:T(8,128)(2,1)S(1)}, u32[]{:S(2)}, u32[]{:S(2)}) collective-permute-start(bf16[128,1152]{1,0:T(8,128)(2,1)S(1)} %fusion.8.refs_6_), channel_id=1, source_target_pairs={{0,130},{1,131},{2,128},{3,129},{4,134},{5,135},{6,132},{7,133},{8... | collective-permute-start | bytes 884744 | tf_op jit(solution)/shard_map/ppermute | solution.py:32
  5.7 2.5 %collective-permute-start.1 = (bf16[128,1152]{1,0:T(8,128)(2,1)S(1)}, bf16[128,1152]{1,0:T(8,128)(2,1)S(1)}, u32[]{:S(2)}, u32[]{:S(2)}) collective-permute-start(bf16[128,1152]{1,0:T(8,128)(2,1)S(1)} %fusion.8.refs_6_), channel_id=1, source_target_pairs={{0,12},{1,13},{2,14},{3,15},{4,0},{5,1},{6,2},{7,3},{8,4},{9,5},{1... | collective-permute-start | bytes 884744 | tf_op jit(solution)/shard_map/ppermute | solution.py:32
  8.2 1.1 fusion.5
  9.3 1.1 fusion.6.refs_0_
  10.4 6.1 %collective-permute-start.4 = (bf16[128,1152]{1,0:T(8,128)(2,1)S(1)}, bf16[128,1152]{1,0:T(8,128)(2,1)S(1)}, u32[]{:S(2)}, u32[]{:S(2)}) collective-permute-start(bf16[128,1152]{1,0:T(8,128)(2,1)S(1)} %fusion.6.refs_0_), channel_id=1, source_target_pairs={{0,32},{1,97},{2,34},{3,99},{4,36},{5,101},{6,38},{7,103},{8,40},{... | collective-permute-start | bytes 884744 | tf_op jit(solution)/shard_map/ppermute | solution.py:32
  16.5 0.7 collective-permute-start.3
  17.5 0.6 fusion.34
  18.1 1.2 multiply_reduce_fusion.2
  20.7 1.3 multiply_reduce_fusion.3
  22.0 2.8 %collective-permute-start.6 = (bf16[128,1152]{1,0:T(8,128)(2,1)S(1)}, bf16[128,1152]{1,0:T(8,128)(2,1)S(1)}, u32[]{:S(2)}, u32[]{:S(2)}) collective-permute-start(bf16[128,1152]{1,0:T(8,128)(2,1)S(1)} %collective-permute-done.2.refs_10_), channel_id=1, source_target_pairs={{0,12},{1,13},{2,14},{3,15},{4,0},{5,1},{6,2},{7,3},{8,4},{9,5},{1... | collective-permute-start | bytes 884744 | tf_op jit(solution)/shard_map/ppermute | solution.py:32
  24.8 2.8 %collective-permute-start.8 = (bf16[64,1152]{1,0:T(8,128)(2,1)S(1)}, bf16[64,1152]{1,0:T(8,128)(2,1)S(1)}, u32[]{:S(2)}, u32[]{:S(2)}) collective-permute-start(bf16[64,1152]{1,0:T(8,128)(2,1)S(1)} %slice.125), channel_id=1, source_target_pairs={{0,12},{1,13},{2,14},{3,15},{4,0},{5,1},{6,2},{7,3},{8,4},{9,5},{1... | collective-permute-start | bytes 442376 | tf_op jit(solution)/shard_map/ppermute | solution.py:32
  27.5 0.5 multiply_reduce-precision_fusion
  28.7 0.8 pad_maximum_fusion.15
  29.5 3.3 %collective-permute-done.3.refs_3_ = bf16[128,1152]{1,0:T(8,128)(2,1)S(1)} collective-permute-done((bf16[128,1152]{1,0:T(8,128)(2,1)S(1)}, bf16[128,1152]{1,0:T(8,128)(2,1)S(1)}, u32[]{:S(2)}, u32[]{:S(2)}) %collective-permute-start.3) | collective-permute-done | bytes 294944 | tf_op jit(solution)/shard_map/ppermute | solution.py:32
  32.8 1.5 %collective-permute-done.7 = bf16[64,1152]{1,0:T(8,128)(2,1)S(1)} collective-permute-done((bf16[64,1152]{1,0:T(8,128)(2,1)S(1)}, bf16[64,1152]{1,0:T(8,128)(2,1)S(1)}, u32[]{:S(2)}, u32[]{:S(2)}) %collective-permute-start.7) | collective-permute-done | bytes 147488 | tf_op jit(solution)/shard_map/ppermute | solution.py:32
  34.3 3.8 %collective-permute-start.9 = (bf16[128,1152]{1,0:T(8,128)(2,1)S(1)}, bf16[128,1152]{1,0:T(8,128)(2,1)S(1)}, u32[]{:S(2)}, u32[]{:S(2)}) collective-permute-start(bf16[128,1152]{1,0:T(8,128)(2,1)S(1)} %fusion.6.refs_0_), channel_id=1, source_target_pairs={{0,16},{1,113},{2,18},{3,115},{4,20},{5,117},{6,22},{7,119},{8,24}... | collective-permute-start | bytes 884744 | tf_op jit(solution)/shard_map/ppermute | solution.py:32
  38.2 3.6 %collective-permute-start.10 = (bf16[64,1152]{1,0:T(8,128)(2,1)S(1)}, bf16[64,1152]{1,0:T(8,128)(2,1)S(1)}, u32[]{:S(2)}, u32[]{:S(2)}) collective-permute-start(bf16[64,1152]{1,0:T(8,128)(2,1)S(1)} %constant_dynamic-slice_fusion.3), channel_id=1, source_target_pairs={{0,64},{1,65},{2,66},{3,67},{4,68},{5,69},{6,70},{7,71},{8,72},{9,... | collective-permute-start | bytes 442376 | tf_op jit(solution)/shard_map/ppermute | solution.py:32
  41.9 1.1 collective-permute-start.12
  43.0 0.3 collective-permute-start.11
  43.3 1.0 pad_maximum_fusion.3.refs_9_
  44.3 5.0 %collective-permute-done.10.refs_4_ = bf16[64,1152]{1,0:T(8,128)(2,1)S(1)} collective-permute-done((bf16[64,1152]{1,0:T(8,128)(2,1)S(1)}, bf16[64,1152]{1,0:T(8,128)(2,1)S(1)}, u32[]{:S(2)}, u32[]{:S(2)}) %collective-permute-start.10) | collective-permute-done | bytes 147488 | tf_op jit(solution)/shard_map/ppermute | solution.py:32
  49.3 0.7 copy-done.18
  50.0 1.1 pad_maximum_fusion
  51.0 4.8 %collective-permute-start.13 = (bf16[448,1152]{1,0:T(8,128)(2,1)}, bf16[448,1152]{1,0:T(8,128)(2,1)}, u32[]{:S(2)}, u32[]{:S(2)}) collective-permute-start(bf16[448,1152]{1,0:T(8,128)(2,1)} %pad_maximum_fusion), channel_id=1, source_target_pairs={{0,1},{1,0},{2,3},{3,2},{4,5},{5,4},{6,7},{7,6},{8,9},{9,8},{10,11... | collective-permute-start | bytes 3096584 | tf_op jit(solution)/shard_map/ppermute | solution.py:32
  55.9 0.9 pad_maximum_fusion.4.refs_13_
  56.9 1.6 %collective-permute-done.13.refs_5_ = bf16[448,1152]{1,0:T(8,128)(2,1)} collective-permute-done((bf16[448,1152]{1,0:T(8,128)(2,1)}, bf16[448,1152]{1,0:T(8,128)(2,1)}, u32[]{:S(2)}, u32[]{:S(2)}) %collective-permute-start.13) | collective-permute-done | bytes 1032224 | tf_op jit(solution)/shard_map/ppermute | solution.py:32
  58.4 6.2 %pairs.1 = (bf16[1024,1024]{1,0:T(8,128)(2,1)S(1)}, bf16[1024,1152]{1,0:T(8,128)(2,1)S(1)}, bf16[1024,1152]{1,0:T(8,128)(2,1)S(1)}, f32[1024,1]{1,0:T(8,128)S(1)...) custom-call(f32[2]{0:T(128)S(1)} %pad_maximum_fusion.16.par_ref, bf16[128,1152]{1,0:T(8,128)(2,1)S(1)} %fusion.6.refs_0_, ...), custom_call_target="tpu_custom_call" | custom-call | flops 2415919104 | bytes 12582912 | tf_op jit(solution)/shard_map/pairs/pallas_call | solution.py:119
  64.7 1.4 %copy-done = bf16[1024,1152]{1,0:T(8,128)(2,1)} copy-done((bf16[1024,1152]{1,0:T(8,128)(2,1)}, bf16[1024,1152]{1,0:T(8,128)(2,1)S(1)}, u32[]{:S(2)}) %copy-start) | copy-done | bytes 2359320
  66.1 1.4 copy-done.2
  67.5 1.4 copy-done.4
  69.3 0.5 collective-permute-start.14
  69.7 3.6 %convolution_convert_fusion.1 = f16[512,1152]{1,0:T(8,128)(2,1)S(1)} fusion(bf16[1024,1152]{1,0:T(8,128)(2,1)} %copy-done, bf16[1024,1024]{1,0:T(8,128)(2,1)} %copy-done.2), kind=kOutput, calls=%fused_computation.3 | convolution fusion | flops 1208549376 | bytes 4587520 | tf_op jit(solution)/shard_map/dot_general | solution.py:192
  73.4 0.2 collective-permute-start.16
  73.6 4.3 %convolution_convert_fusion = f16[1024,1152]{1,0:T(8,128)(2,1)} fusion(bf16[1024,1024]{1,0:T(8,128)(2,1)S(1)} %copy-done.3, bf16[1024,1152]{1,0:T(8,128)(2,1)S(1)} %copy-done.5), kind=kOutput, calls=%fused_computation.1 | convolution fusion | flops 2417098752 | bytes 6815744 | tf_op jit(solution)/shard_map/dot_general | solution.py:202
  78.0 2.5 %collective-permute-done.15 = f32[1026]{0:T(1024)S(1)} collective-permute-done((f32[1026]{0:T(1024)S(1)}, f32[1026]{0:T(1024)S(1)}, u32[]{:S(2)}, u32[]{:S(2)}) %collective-permute-start.15) | collective-permute-done | bytes 4136 | tf_op jit(solution)/shard_map/ppermute | solution.py:32
  80.5 1.5 %convolution_add_fusion = f32[512,1152]{1,0:T(8,128)S(1)} fusion(bf16[1024,1152]{1,0:T(8,128)(2,1)S(1)} %copy-done.1, f16[512,1152]{1,0:T(8,128)(2,1)S(1)} %collective-permute-done.16, bf16[1024,1024]{1,0:T(8,128)(2,1)S(1)} %copy-done.3), kind=kOutput, calls=%fused_computation.2 | convolution fusion | flops 1209139200 | bytes 6946816 | tf_op jit(solution)/shard_map/dot_general | solution.py:198
  82.4 2.4 %collective-permute-done.17 = f32[1026]{0:T(1024)S(1)} collective-permute-done((f32[1026]{0:T(1024)S(1)}, f32[1026]{0:T(1024)S(1)}, u32[]{:S(2)}, u32[]{:S(2)}) %collective-permute-start.17) | collective-permute-done | bytes 4136 | tf_op jit(solution)/shard_map/ppermute | solution.py:32
  85.2 3.3 %collective-permute-done.18 = f32[1026]{0:T(1024)S(1)} collective-permute-done((f32[1026]{0:T(1024)S(1)}, f32[1026]{0:T(1024)S(1)}, u32[]{:S(2)}, u32[]{:S(2)}) %collective-permute-start.18) | collective-permute-done | bytes 4136 | tf_op jit(solution)/shard_map/ppermute | solution.py:32
  88.5 1.5 %collective-permute-start.19 = (f32[1026]{0:T(1024)S(1)}, f32[1026]{0:T(1024)S(1)}, u32[]{:S(2)}, u32[]{:S(2)}) collective-permute-start(f32[1026]{0:T(1024)S(1)} %add.234), channel_id=1, source_target_pairs={{0,8},{1,9},{2,10},{3,11},{4,12},{5,13},{6,14},{7,15},{8,0},{9,1},... | collective-permute-start | bytes 12320 | tf_op jit(solution)/shard_map/ppermute | solution.py:32
  90.2 3.7 %all-to-all-start = ((f16[16,64,1152]{2,1,0:T(8,128)(2,1)}), f16[16,64,1152]{2,1,0:T(8,128)(2,1)S(1)}, u32[]{:S(2)}, u32[]{:S(2)}) async-start(f16[16,64,1152]{2,1,0:T(8,128)(2,1)} %bitcast.43), calls=%async_computation | async-start | bytes 4718592 | tf_op jit(solution)/shard_map/all_to_all | solution.py:208
  94.3 0.8 fusion.10
  95.1 0.8 fusion.11
  95.9 1.2 collective-permute-start.22
  97.0 0.8 fusion.12
  97.8 1.3 collective-permute-start.23
  99.3 3.2 %collective-permute-start.20 = (f16[72,1152]{1,0:T(8,128)(2,1)S(1)}, f16[72,1152]{1,0:T(8,128)(2,1)S(1)}, u32[]{:S(2)}, u32[]{:S(2)}) collective-permute-start(f16[72,1152]{1,0:T(8,128)(2,1)S(1)} %fusion.16), channel_id=1, source_target_pairs={{0,64},{1,65},{2,66},{3,67},{4,68},{5,69},{6,70},{7,71},{8,72},{9,... | collective-permute-start | bytes 497672 | tf_op jit(solution)/shard_map/ppermute | solution.py:32
  102.5 13.8 %collective-permute-done.20 = f16[72,1152]{1,0:T(8,128)(2,1)S(1)} collective-permute-done((f16[72,1152]{1,0:T(8,128)(2,1)S(1)}, f16[72,1152]{1,0:T(8,128)(2,1)S(1)}, u32[]{:S(2)}, u32[]{:S(2)}) %collective-permute-start.20) | collective-permute-done | bytes 165920 | tf_op jit(solution)/shard_map/ppermute | solution.py:32
  116.3 4.9 %collective-permute-done.23 = f16[136,1152]{1,0:T(8,128)(2,1)} collective-permute-done((f16[136,1152]{1,0:T(8,128)(2,1)}, f16[136,1152]{1,0:T(8,128)(2,1)}, u32[]{:S(2)}, u32[]{:S(2)}) %collective-permute-start.23) | collective-permute-done | bytes 313376 | tf_op jit(solution)/shard_map/ppermute | solution.py:32
  121.2 1.2 convert_add_fusion
  122.5 8.3 %collective-permute-start.24 = (f32[72,1152]{1,0:T(8,128)S(1)}, f32[72,1152]{1,0:T(8,128)S(1)}, u32[]{:S(2)}, u32[]{:S(2)}) collective-permute-start(f32[72,1152]{1,0:T(8,128)S(1)} %pad_maximum_fusion.1), channel_id=1, source_target_pairs={{0,1},{1,0},{2,3},{3,2},{4,5},{5,4},{6,7},{7,6},{8,9},{9,8},{10,11... | collective-permute-start | bytes 995336 | tf_op jit(solution)/shard_map/ppermute | solution.py:32
  130.8 0.6 slice_add_fusion.5
  131.4 0.7 collective-permute-done.24
  132.1 0.7 copy-done.14
  132.8 0.5 add_reduce_fusion
  133.3 0.7 add.260
  134.0 0.5 reduce_sum.119
  134.6 1.2 broadcast_multiply_fusion
  135.7 0.7 slice_add_fusion.4
  136.5 1.3 dynamic-slice_add_fusion
  137.9 0.3 convert_reduce_fusion
  138.2 0.9 multiply_reduce_fusion
  139.1 2.1 %multiply_reduce_fusion.1 = (f32[64]{0:T(128)S(1)}, f32[64,1152]{1,0:T(8,128)S(1)}, f32[64,1152]{1,0:T(8,128)}) fusion(f32[64,1152]{1,0:T(8,128)S(1)} %copy-done.6, f32[64,1152]{1,0:T(8,128)S(1)} %copy-done.12, f32[64]{0:T(128)} %multiply_reduce-precision_fusion, f32[72,1152]{1,0:T(8,128)S(1)} %copy-done.15, f32[136,1152]{1,0:T(8,128)} %copy-done.9, ...), kind=kLoop, calls=%fused_computation.42 | loop fusion | flops 958400 | bytes 3097604 | tf_op jit(solution)/shard_map/reduce_sum | solution.py:243
  141.2 0.8 subtract_multiply_fusion.1
  (126 shorter events, 2.6 us)
Async XLA Ops:
  0.6 16.6 %copy-start.13 = (bf16[256,1152]{1,0:T(8,128)(2,1)S(1)}, bf16[256,1152]{1,0:T(8,128)(2,1)}, u32[]{:S(2)}) copy-start(bf16[256,1152]{1,0:T(8,128)(2,1)} %param.5) | copy-start | bytes 1769476
  0.6 16.7 %copy-start.11 = (bf16[256,1152]{1,0:T(8,128)(2,1)S(1)}, bf16[256,1152]{1,0:T(8,128)(2,1)}, u32[]{:S(2)}) copy-start(bf16[256,1152]{1,0:T(8,128)(2,1)} %param.4) | copy-start | bytes 1769476
  2.0 19.9 %collective-permute-start.2 = (bf16[128,1152]{1,0:T(8,128)(2,1)S(1)}, bf16[128,1152]{1,0:T(8,128)(2,1)S(1)}, u32[]{:S(2)}, u32[]{:S(2)}) collective-permute-start(bf16[128,1152]{1,0:T(8,128)(2,1)S(1)} %fusion.8.refs_6_), channel_id=1, source_target_pairs={{0,130},{1,131},{2,128},{3,129},{4,134},{5,135},{6,132},{7,133},{8... | collective-permute-start | bytes 884744 | tf_op jit(solution)/shard_map/ppermute | solution.py:32
  5.7 16.3 %collective-permute-start.1 = (bf16[128,1152]{1,0:T(8,128)(2,1)S(1)}, bf16[128,1152]{1,0:T(8,128)(2,1)S(1)}, u32[]{:S(2)}, u32[]{:S(2)}) collective-permute-start(bf16[128,1152]{1,0:T(8,128)(2,1)S(1)} %fusion.8.refs_6_), channel_id=1, source_target_pairs={{0,12},{1,13},{2,14},{3,15},{4,0},{5,1},{6,2},{7,3},{8,4},{9,5},{1... | collective-permute-start | bytes 884744 | tf_op jit(solution)/shard_map/ppermute | solution.py:32
  8.2 13.8 %collective-permute-start = (bf16[128,1152]{1,0:T(8,128)(2,1)S(1)}, bf16[128,1152]{1,0:T(8,128)(2,1)S(1)}, u32[]{:S(2)}, u32[]{:S(2)}) collective-permute-start(bf16[128,1152]{1,0:T(8,128)(2,1)S(1)} %fusion.8.refs_6_), channel_id=1, source_target_pairs={{0,4},{1,5},{2,6},{3,7},{4,8},{5,9},{6,10},{7,11},{8,12},{9,13},{1... | collective-permute-start | bytes 884744 | tf_op jit(solution)/shard_map/ppermute | solution.py:32
  10.4 17.1 %collective-permute-start.4 = (bf16[128,1152]{1,0:T(8,128)(2,1)S(1)}, bf16[128,1152]{1,0:T(8,128)(2,1)S(1)}, u32[]{:S(2)}, u32[]{:S(2)}) collective-permute-start(bf16[128,1152]{1,0:T(8,128)(2,1)S(1)} %fusion.6.refs_0_), channel_id=1, source_target_pairs={{0,32},{1,97},{2,34},{3,99},{4,36},{5,101},{6,38},{7,103},{8,40},{... | collective-permute-start | bytes 884744 | tf_op jit(solution)/shard_map/ppermute | solution.py:32
  16.5 16.3 %collective-permute-start.3 = (bf16[128,1152]{1,0:T(8,128)(2,1)S(1)}, bf16[128,1152]{1,0:T(8,128)(2,1)S(1)}, u32[]{:S(2)}, u32[]{:S(2)}) collective-permute-start(bf16[128,1152]{1,0:T(8,128)(2,1)S(1)} %fusion.6.refs_0_), channel_id=1, source_target_pairs={{0,48},{1,81},{2,50},{3,83},{4,52},{5,85},{6,54},{7,87},{8,56},{9,... | collective-permute-start | bytes 884744 | tf_op jit(solution)/shard_map/ppermute | solution.py:32
  22.0 12.4 %collective-permute-start.6 = (bf16[128,1152]{1,0:T(8,128)(2,1)S(1)}, bf16[128,1152]{1,0:T(8,128)(2,1)S(1)}, u32[]{:S(2)}, u32[]{:S(2)}) collective-permute-start(bf16[128,1152]{1,0:T(8,128)(2,1)S(1)} %collective-permute-done.2.refs_10_), channel_id=1, source_target_pairs={{0,12},{1,13},{2,14},{3,15},{4,0},{5,1},{6,2},{7,3},{8,4},{9,5},{1... | collective-permute-start | bytes 884744 | tf_op jit(solution)/shard_map/ppermute | solution.py:32
  24.7 9.6 %collective-permute-start.5 = (bf16[128,1152]{1,0:T(8,128)(2,1)S(1)}, bf16[128,1152]{1,0:T(8,128)(2,1)S(1)}, u32[]{:S(2)}, u32[]{:S(2)}) collective-permute-start(bf16[128,1152]{1,0:T(8,128)(2,1)S(1)} %collective-permute-done.2.refs_10_), channel_id=1, source_target_pairs={{0,4},{1,5},{2,6},{3,7},{4,8},{5,9},{6,10},{7,11},{8,12},{9,13},{1... | collective-permute-start | bytes 884744 | tf_op jit(solution)/shard_map/ppermute | solution.py:32
  24.8 8.0 %collective-permute-start.8 = (bf16[64,1152]{1,0:T(8,128)(2,1)S(1)}, bf16[64,1152]{1,0:T(8,128)(2,1)S(1)}, u32[]{:S(2)}, u32[]{:S(2)}) collective-permute-start(bf16[64,1152]{1,0:T(8,128)(2,1)S(1)} %slice.125), channel_id=1, source_target_pairs={{0,12},{1,13},{2,14},{3,15},{4,0},{5,1},{6,2},{7,3},{8,4},{9,5},{1... | collective-permute-start | bytes 442376 | tf_op jit(solution)/shard_map/ppermute | solution.py:32
  27.5 6.8 %collective-permute-start.7 = (bf16[64,1152]{1,0:T(8,128)(2,1)S(1)}, bf16[64,1152]{1,0:T(8,128)(2,1)S(1)}, u32[]{:S(2)}, u32[]{:S(2)}) collective-permute-start(bf16[64,1152]{1,0:T(8,128)(2,1)S(1)} %slice.124), channel_id=1, source_target_pairs={{0,4},{1,5},{2,6},{3,7},{4,8},{5,9},{6,10},{7,11},{8,12},{9,13},{1... | collective-permute-start | bytes 442376 | tf_op jit(solution)/shard_map/ppermute | solution.py:32
  32.8 5.4 %copy-start.19 = (bf16[64,1152]{1,0:T(8,128)(2,1)}, bf16[64,1152]{1,0:T(8,128)(2,1)S(1)}, u32[]{:S(2)}) copy-start(bf16[64,1152]{1,0:T(8,128)(2,1)S(1)} %collective-permute-done.8) | copy-start | bytes 442372
  34.3 8.7 %copy-start.20 = (bf16[64,1152]{1,0:T(8,128)(2,1)}, bf16[64,1152]{1,0:T(8,128)(2,1)S(1)}, u32[]{:S(2)}) copy-start(bf16[64,1152]{1,0:T(8,128)(2,1)S(1)} %collective-permute-done.7) | copy-start | bytes 442372
  34.3 15.7 %collective-permute-start.9 = (bf16[128,1152]{1,0:T(8,128)(2,1)S(1)}, bf16[128,1152]{1,0:T(8,128)(2,1)S(1)}, u32[]{:S(2)}, u32[]{:S(2)}) collective-permute-start(bf16[128,1152]{1,0:T(8,128)(2,1)S(1)} %fusion.6.refs_0_), channel_id=1, source_target_pairs={{0,16},{1,113},{2,18},{3,115},{4,20},{5,117},{6,22},{7,119},{8,24}... | collective-permute-start | bytes 884744 | tf_op jit(solution)/shard_map/ppermute | solution.py:32
  38.2 11.1 %collective-permute-start.10 = (bf16[64,1152]{1,0:T(8,128)(2,1)S(1)}, bf16[64,1152]{1,0:T(8,128)(2,1)S(1)}, u32[]{:S(2)}, u32[]{:S(2)}) collective-permute-start(bf16[64,1152]{1,0:T(8,128)(2,1)S(1)} %constant_dynamic-slice_fusion.3), channel_id=1, source_target_pairs={{0,64},{1,65},{2,66},{3,67},{4,68},{5,69},{6,70},{7,71},{8,72},{9,... | collective-permute-start | bytes 442376 | tf_op jit(solution)/shard_map/ppermute | solution.py:32
  41.9 7.5 %collective-permute-start.12 = (bf16[64,1152]{1,0:T(8,128)(2,1)S(1)}, bf16[64,1152]{1,0:T(8,128)(2,1)S(1)}, u32[]{:S(2)}, u32[]{:S(2)}) collective-permute-start(bf16[64,1152]{1,0:T(8,128)(2,1)S(1)} %slice.127), channel_id=1, source_target_pairs={{0,12},{1,13},{2,14},{3,15},{4,0},{5,1},{6,2},{7,3},{8,4},{9,5},{1... | collective-permute-start | bytes 442376 | tf_op jit(solution)/shard_map/ppermute | solution.py:32
  43.0 6.3 %collective-permute-start.11 = (bf16[64,1152]{1,0:T(8,128)(2,1)S(1)}, bf16[64,1152]{1,0:T(8,128)(2,1)S(1)}, u32[]{:S(2)}, u32[]{:S(2)}) collective-permute-start(bf16[64,1152]{1,0:T(8,128)(2,1)S(1)} %slice.126), channel_id=1, source_target_pairs={{0,4},{1,5},{2,6},{3,7},{4,8},{5,9},{6,10},{7,11},{8,12},{9,13},{1... | collective-permute-start | bytes 442376 | tf_op jit(solution)/shard_map/ppermute | solution.py:32
  49.3 0.7 copy-start.18
  51.0 7.4 %collective-permute-start.13 = (bf16[448,1152]{1,0:T(8,128)(2,1)}, bf16[448,1152]{1,0:T(8,128)(2,1)}, u32[]{:S(2)}, u32[]{:S(2)}) collective-permute-start(bf16[448,1152]{1,0:T(8,128)(2,1)} %pad_maximum_fusion), channel_id=1, source_target_pairs={{0,1},{1,0},{2,3},{3,2},{4,5},{5,4},{6,7},{7,6},{8,9},{9,8},{10,11... | collective-permute-start | bytes 3096584 | tf_op jit(solution)/shard_map/ppermute | solution.py:32
  64.7 1.4 %copy-start = (bf16[1024,1152]{1,0:T(8,128)(2,1)}, bf16[1024,1152]{1,0:T(8,128)(2,1)S(1)}, u32[]{:S(2)}) copy-start(bf16[1024,1152]{1,0:T(8,128)(2,1)S(1)} %get-tuple-element.71) | copy-start | bytes 7077892
  66.1 1.4 copy-start.2
  67.5 1.4 copy-start.4
  69.3 4.1 %collective-permute-start.14 = (f32[514]{0:T(1024)S(1)}, f32[514]{0:T(1024)S(1)}, u32[]{:S(2)}, u32[]{:S(2)}) collective-permute-start(f32[514]{0:T(1024)S(1)} %pad_maximum_fusion.14), channel_id=1, source_target_pairs={{0,1},{1,0},{2,3},{3,2},{4,5},{5,4},{6,7},{7,6},{8,9},{9,8},{10,11... | collective-permute-start | bytes 6176 | tf_op jit(solution)/shard_map/ppermute | solution.py:32
  69.7 3.9 %copy-start.3 = (bf16[1024,1024]{1,0:T(8,128)(2,1)S(1)}, bf16[1024,1024]{1,0:T(8,128)(2,1)}, u32[]{:S(2)}) copy-start(bf16[1024,1024]{1,0:T(8,128)(2,1)} %copy-done.2) | copy-start | bytes 6291460
  69.7 3.9 %copy-start.5 = (bf16[1024,1152]{1,0:T(8,128)(2,1)S(1)}, bf16[1024,1152]{1,0:T(8,128)(2,1)}, u32[]{:S(2)}) copy-start(bf16[1024,1152]{1,0:T(8,128)(2,1)} %copy-done.4) | copy-start | bytes 7077892
  73.4 7.1 %collective-permute-start.16 = (f16[512,1152]{1,0:T(8,128)(2,1)S(1)}, f16[512,1152]{1,0:T(8,128)(2,1)S(1)}, u32[]{:S(2)}, u32[]{:S(2)}) collective-permute-start(f16[512,1152]{1,0:T(8,128)(2,1)S(1)} %convolution_convert_fusion.1), channel_id=1, source_target_pairs={{0,1},{1,0},{2,3},{3,2},{4,5},{5,4},{6,7},{7,6},{8,9},{9,8},{10,11... | collective-permute-start | bytes 3538952 | tf_op jit(solution)/shard_map/ppermute | solution.py:32
  73.6 6.9 %copy-start.1 = (bf16[1024,1152]{1,0:T(8,128)(2,1)S(1)}, bf16[1024,1152]{1,0:T(8,128)(2,1)}, u32[]{:S(2)}) copy-start(bf16[1024,1152]{1,0:T(8,128)(2,1)} %copy-done) | copy-start | bytes 7077892
  77.9 2.6 %collective-permute-start.15 = (f32[1026]{0:T(1024)S(1)}, f32[1026]{0:T(1024)S(1)}, u32[]{:S(2)}, u32[]{:S(2)}) collective-permute-start(f32[1026]{0:T(1024)S(1)} %pad_maximum_fusion.13), channel_id=1, source_target_pairs={{0,2},{1,3},{2,0},{3,1},{4,6},{5,7},{6,4},{7,5},{8,10},{9,11},{10,... | collective-permute-start | bytes 12320 | tf_op jit(solution)/shard_map/ppermute | solution.py:32
  82.1 8.1 %copy-start.10 = (f32[512,1152]{1,0:T(8,128)}, f32[512,1152]{1,0:T(8,128)S(1)}, u32[]{:S(2)}) copy-start(f32[512,1152]{1,0:T(8,128)S(1)} %convolution_add_fusion) | copy-start | bytes 7077892
  82.2 2.6 %collective-permute-start.17 = (f32[1026]{0:T(1024)S(1)}, f32[1026]{0:T(1024)S(1)}, u32[]{:S(2)}, u32[]{:S(2)}) collective-permute-start(f32[1026]{0:T(1024)S(1)} %fusion.33), channel_id=1, source_target_pairs={{0,4},{1,5},{2,6},{3,7},{4,0},{5,1},{6,2},{7,3},{8,12},{9,13},{10,... | collective-permute-start | bytes 12320 | tf_op jit(solution)/shard_map/ppermute | solution.py:32
  84.8 3.7 %collective-permute-start.18 = (f32[1026]{0:T(1024)S(1)}, f32[1026]{0:T(1024)S(1)}, u32[]{:S(2)}, u32[]{:S(2)}) collective-permute-start(f32[1026]{0:T(1024)S(1)} %add.233), channel_id=1, source_target_pairs={{0,130},{1,131},{2,128},{3,129},{4,134},{5,135},{6,132},{7,133},{8... | collective-permute-start | bytes 12320 | tf_op jit(solution)/shard_map/ppermute | solution.py:32
  88.5 5.4 %collective-permute-start.19 = (f32[1026]{0:T(1024)S(1)}, f32[1026]{0:T(1024)S(1)}, u32[]{:S(2)}, u32[]{:S(2)}) collective-permute-start(f32[1026]{0:T(1024)S(1)} %add.234), channel_id=1, source_target_pairs={{0,8},{1,9},{2,10},{3,11},{4,12},{5,13},{6,14},{7,15},{8,0},{9,1},... | collective-permute-start | bytes 12320 | tf_op jit(solution)/shard_map/ppermute | solution.py:32
  90.2 47.7 %all-to-all-start = ((f16[16,64,1152]{2,1,0:T(8,128)(2,1)}), f16[16,64,1152]{2,1,0:T(8,128)(2,1)S(1)}, u32[]{:S(2)}, u32[]{:S(2)}) async-start(f16[16,64,1152]{2,1,0:T(8,128)(2,1)} %bitcast.43), calls=%async_computation | async-start | bytes 4718592 | tf_op jit(solution)/shard_map/all_to_all | solution.py:208
  95.1 21.2 %collective-permute-start.21 = (f16[136,1152]{1,0:T(8,128)(2,1)}, f16[136,1152]{1,0:T(8,128)(2,1)}, u32[]{:S(2)}, u32[]{:S(2)}) collective-permute-start(f16[136,1152]{1,0:T(8,128)(2,1)} %fusion.10), channel_id=1, source_target_pairs={{0,48},{1,81},{2,50},{3,83},{4,52},{5,85},{6,54},{7,87},{8,56},{9,... | collective-permute-start | bytes 940040 | tf_op jit(solution)/shard_map/ppermute | solution.py:32
  95.9 20.4 %collective-permute-start.22 = (f16[136,1152]{1,0:T(8,128)(2,1)}, f16[136,1152]{1,0:T(8,128)(2,1)S(1)}, u32[]{:S(2)}, u32[]{:S(2)}) collective-permute-start(f16[136,1152]{1,0:T(8,128)(2,1)} %fusion.11), channel_id=1, source_target_pairs={{0,32},{1,97},{2,34},{3,99},{4,36},{5,101},{6,38},{7,103},{8,40},{... | collective-permute-start | bytes 940040 | tf_op jit(solution)/shard_map/ppermute | solution.py:32
  97.8 23.3 %collective-permute-start.23 = (f16[136,1152]{1,0:T(8,128)(2,1)}, f16[136,1152]{1,0:T(8,128)(2,1)}, u32[]{:S(2)}, u32[]{:S(2)}) collective-permute-start(f16[136,1152]{1,0:T(8,128)(2,1)} %fusion.12), channel_id=1, source_target_pairs={{0,16},{1,113},{2,18},{3,115},{4,20},{5,117},{6,22},{7,119},{8,24}... | collective-permute-start | bytes 940040 | tf_op jit(solution)/shard_map/ppermute | solution.py:32
  99.3 17.0 %collective-permute-start.20 = (f16[72,1152]{1,0:T(8,128)(2,1)S(1)}, f16[72,1152]{1,0:T(8,128)(2,1)S(1)}, u32[]{:S(2)}, u32[]{:S(2)}) collective-permute-start(f16[72,1152]{1,0:T(8,128)(2,1)S(1)} %fusion.16), channel_id=1, source_target_pairs={{0,64},{1,65},{2,66},{3,67},{4,68},{5,69},{6,70},{7,71},{8,72},{9,... | collective-permute-start | bytes 497672 | tf_op jit(solution)/shard_map/ppermute | solution.py:32
  116.3 15.8 %copy-start.16 = (f16[72,1152]{1,0:T(8,128)(2,1)}, f16[72,1152]{1,0:T(8,128)(2,1)S(1)}, u32[]{:S(2)}) copy-start(f16[72,1152]{1,0:T(8,128)(2,1)S(1)} %collective-permute-done.20) | copy-start | bytes 497668
  122.3 9.7 %copy-start.9 = (f32[136,1152]{1,0:T(8,128)}, f32[136,1152]{1,0:T(8,128)S(1)}, u32[]{:S(2)}) copy-start(f32[136,1152]{1,0:T(8,128)S(1)} %convert_add_fusion) | copy-start | bytes 1880068
  122.3 15.8 %copy-start.7 = (f32[64,1152]{1,0:T(8,128)S(1)}, f32[64,1152]{1,0:T(8,128)}, u32[]{:S(2)}) copy-start(f32[64,1152]{1,0:T(8,128)} %get-tuple-element.89) | copy-start | bytes 884740
  122.3 15.8 %copy-start.8 = (f32[64,1152]{1,0:T(8,128)S(1)}, f32[64,1152]{1,0:T(8,128)}, u32[]{:S(2)}) copy-start(f32[64,1152]{1,0:T(8,128)} %get-tuple-element.88) | copy-start | bytes 884740
  122.4 16.7 %copy-start.6 = (f32[64,1152]{1,0:T(8,128)S(1)}, f32[64,1152]{1,0:T(8,128)}, u32[]{:S(2)}) copy-start(f32[64,1152]{1,0:T(8,128)} %get-tuple-element.85) | copy-start | bytes 884740
  122.4 16.7 %copy-start.12 = (f32[64,1152]{1,0:T(8,128)S(1)}, f32[64,1152]{1,0:T(8,128)}, u32[]{:S(2)}) copy-start(f32[64,1152]{1,0:T(8,128)} %get-tuple-element.84) | copy-start | bytes 884740
  122.5 9.6 %collective-permute-start.24 = (f32[72,1152]{1,0:T(8,128)S(1)}, f32[72,1152]{1,0:T(8,128)S(1)}, u32[]{:S(2)}, u32[]{:S(2)}) collective-permute-start(f32[72,1152]{1,0:T(8,128)S(1)} %pad_maximum_fusion.1), channel_id=1, source_target_pairs={{0,1},{1,0},{2,3},{3,2},{4,5},{5,4},{6,7},{7,6},{8,9},{9,8},{10,11... | collective-permute-start | bytes 995336 | tf_op jit(solution)/shard_map/ppermute | solution.py:32
  130.8 1.3 copy-start.21
  132.0 0.7 copy-start.14
  137.8 1.2 copy-start.15
  137.8 1.2 copy-start.17
  138.2 3.0 %copy-start.22 = (f32[64,1]{0,1:T(1,128)S(1)}, f32[64,1]{0,1:T(1,128)}, u32[]{:S(2)}) copy-start(f32[64,1]{0,1:T(1,128)} %get-tuple-element.52) | copy-start | bytes 772

commit v3 on v2

--- a/solution.py
+++ b/solution.py
@@ -61,7 +61,7 @@
 def pair_kernel(par_ref, *refs):
     a0, r1, r2, r3, r4, met = refs[:6]
     txt_in = refs[6:14]
-    w_ref, img, txt, li_ref, lt_ref, sums_ref = refs[14:]
+    w_out, img_out, txt_out, li_ref, lt_ref, sums_ref, w_ref, img, txt, sems = refs[14:]
     x, yh, core = lax.axis_index("x"), lax.axis_index("yh"), lax.axis_index("core")
     img[0:64, :] = a0[pl.ds(pl.multiple_of(core * Q, Q), Q), :]
     img[64:448, :] = met[0:384, :]
@@ -78,6 +78,9 @@
     for k, ref in enumerate(txt_in):
         rows = ref.shape[0]
         txt[pl.ds(pl.multiple_of(text_places[k] * Q, Q), rows), :] = ref[...]
+    copies = [pltpu.make_async_copy(txt, txt_out, sems.at[0]), pltpu.make_async_copy(img, img_out, sems.at[1])]
+    for copy in copies:
+        copy.start()
     temperature = par_ref[0]
     offset = par_ref[1]
     texts = txt[...]
@@ -97,7 +100,11 @@
         slopes = p / q
         losses = jnp.where(p < 0.0009765625, p - 0.5 * p * p, jnp.log(q))
         weights = (temperature * slopes).astype(jnp.bfloat16)
-        w_ref[r * ROWS : (r + 1) * ROWS, :] = weights
+        band = pl.ds(r * ROWS, ROWS)
+        w_ref[band, :] = weights
+        copy = pltpu.make_async_copy(w_ref.at[band], w_out.at[band], sems.at[2 + r])
+        copy.start()
+        copies.append(copy)
         li_ref[r * ROWS : (r + 1) * ROWS, :] = jnp.sum(losses, axis=1, keepdims=True)
         cols = jnp.sum(losses, axis=0, keepdims=True)
         s1 = jnp.sum(slopes, axis=0, keepdims=True)
@@ -109,6 +116,8 @@
     lt_ref[...] = loss_cols
     sums_ref[0:1, :] = temperature * scale_sum
     sums_ref[1:2, :] = slope_sum
+    for copy in copies:
+        copy.wait()
 
 
 def pairs_on_device(params, chunks):
@@ -127,7 +136,13 @@
             jax.ShapeDtypeStruct((2, 1024), f32),
         ),
         in_specs=[smem] + [vmem] * len(chunks),
-        out_specs=(vmem,) * 6,
+        out_specs=(pl.BlockSpec(memory_space=pltpu.HBM),) * 3 + (vmem,) * 3,
+        scratch_shapes=[
+            pltpu.VMEM((1024, 1024), jnp.bfloat16),
+            pltpu.VMEM((1024, width), jnp.bfloat16),
+            pltpu.VMEM((1024, width), jnp.bfloat16),
+            pltpu.SemaphoreType.DMA((6,)),
+        ],
         compiler_params=pltpu.CompilerParams(vmem_limit_bytes=28 * 1024 * 1024),
         cost_estimate=pl.CostEstimate(
             flops=2 * 1024 * 1024 * width, bytes_accessed=12 * 1024 * 1024, transcendentals=3 * 1024 * 1024
@@ -136,22 +151,61 @@
     )(params, *chunks)
 
 
+def finish_kernel(
+    half, far, arrived, met, gt, image_unit, text_unit, image_inv, text_inv, weight, loss, here, gi_out, gt_out, loss_out, both_out
+):
+    core = lax.axis_index("core")
+    own = arrived[pl.ds(pl.multiple_of(core * Q, Q), Q), :]
+    gi = half[...] + far[0:Q, :] + own + met[0:Q, :]
+    images, texts, w = image_unit[...], text_unit[...], weight[...]
+    gi = gi + w * texts.astype(jnp.bfloat16).astype(jnp.float32)
+    gi_out[...] = image_inv[...] * (gi - images * jnp.sum(images * gi, axis=-1, keepdims=True))
+    gt = gt[...] + w * images.astype(jnp.bfloat16).astype(jnp.float32)
+    gt_out[...] = text_inv[...] * (gt - texts * jnp.sum(texts * gt, axis=-1, keepdims=True))
+    near = arrived[128:130, 0:128] + met[Q : Q + 2, 0:128]
+    near = jnp.where(core == 0, near[:, :Q], near[:, Q:]) + far[Q : Q + 2, 0:Q]
+    loss_out[...] = loss[...] + near[0:1] + near[1:2]
+    sums = arrived[130:132, 0:128] + met[Q + 2 : Q + 4, 0:128] + far[Q + 2 : Q + 4, 0:128] + here[...]
+    sums = sums[0:1] + sums[1:2]
+    total = sums[:, 0:2]
+    for k in range(1, NZ):
+        total = total + sums[:, 2 * k : 2 * k + 2]
+    both_out[...] = total * (1.0 / SUM_SCALE)
+
+
+def finish(*args):
+    width = args[0].shape[1]
+    shape = jax.ShapeDtypeStruct((Q, width), jnp.float32)
+    return pl.pallas_call(
+        finish_kernel,
+        out_shape=(
+            shape,
+            shape,
+            jax.ShapeDtypeStruct((1, Q), jnp.float32),
+            jax.ShapeDtypeStruct((1, 2), jnp.float32),
+        ),
+        compiler_params=pltpu.CompilerParams(vmem_limit_bytes=12 * 1024 * 1024),
+        name="finish",
+    )(*args)
+
+
 def tied(*values):
     return lax.optimization_barrier(values)
 
 
 def gather(a0, t0, core, own):
-    r3, r2 = send(a0, split_z=3), send(a0, split_z=2)
+    r4 = send(lax.dynamic_slice_in_dim(a0, core * Q, Q, 0), dz=4)
+    r3 = send(a0, split_z=3)
     xm, xp, c0 = send(t0, dx=1), send(t0, dx=-1), send(t0, fy=3)
     a0, t0, xm, xp, c0 = tied(a0, t0, xm, xp, c0)
     cm, cp = send(c0, dx=1), send(c0, dx=-1)
     f1, f2 = send(xm[:Q], dx=1), send(xp[Q:], dx=-1)
-    a0, r3, r2, cm, cp, f1, f2, *own = tied(a0, r3, r2, cm, cp, f1, f2, *own)
+    r2 = send(a0, split_z=2)
+    a0, r3, r4, cm, cp, f1, f2, *own = tied(a0, r3, r4, cm, cp, f1, f2, *own)
     g1, g2 = send(cm[:Q], dx=1), send(cp[Q:], dx=-1)
     r1 = send(a0, split_z=1)
-    r4 = send(lax.dynamic_slice_in_dim(a0, core * Q, Q, 0), dz=4)
     far = jnp.concatenate([f1, f2], axis=0)
-    r1, r4, g1, g2, far = tied(r1, r4, g1, g2, far)
+    r1, r2, g1, g2, far = tied(r1, r2, g1, g2, far)
     met = send(jnp.concatenate([r1, r2, r3, r4], axis=0), fc=1)
     far_h = jnp.concatenate([g1, g2], axis=0)
     return [a0, r1, r2, r3, r4, met, t0, xm, xp, far, c0, cm, cp, far_h], own
@@ -181,30 +235,31 @@
     match_slope = -1.0 / (1.0 + jnp.exp(match_logit))
     match_weight = rounded(temperature * match_slope)
     match_sums = jnp.stack([temperature * jnp.sum(match_slope * match), jnp.sum(match_slope)])
-    own = (image_unit, text_unit, image_inv, text_inv, image_low, text_low, match_loss, match_weight, match_sums)
+    own = (image_unit, text_unit, image_inv, text_inv, match_loss, match_weight, match_sums)
     chunks, own = gather(a0, t0, core, own)
-    image_unit, text_unit, image_inv, text_inv, image_low, text_low, match_loss, match_weight, match_sums = own
+    image_unit, text_unit, image_inv, text_inv, match_loss, match_weight, match_sums = own
     weights, images, texts, li, lt, sums = pairs_on_device(params, chunks)
 
     li = li.reshape(-1)
     both = jnp.sum(sums, axis=1) + match_sums
     met = send(jnp.concatenate([li[512:], both]), fc=1)
-    others = jnp.dot(weights[512:], texts, preferred_element_type=f32).astype(f16)
-    met, others = tied(met, others)
-    rows_met = send(others, fc=1)
+    met, weights = tied(met, weights)
     li_half, both = li[:512] + met[:512], both + met[512:]
     plane = jnp.concatenate([lt.reshape(-1), both])
     plane = plane + send(plane, fy=1)
-    half = jnp.dot(weights[:512], texts, preferred_element_type=f32) + rows_met.astype(f32)
-    flight = half[Q:].astype(f16)
-    plane, half, flight = tied(plane, half, flight)
+    others = jnp.dot(weights[512:], texts, preferred_element_type=f32).astype(f16)
+    plane, others = tied(plane, others)
     plane = plane + send(plane, fx=1)
+    rows_met = send(others, fc=1)
     gt16 = lax.dot_general(
         weights, images, (((0,), (0,)), ((), ())), preferred_element_type=f32
     ).astype(f16)
-    plane, gt16 = tied(plane, gt16)
-    for move in (dict(fy=3), dict(fx=2)):
-        plane = plane + send(plane, **move)
+    plane, gt16, rows_met = tied(plane, gt16, rows_met)
+    plane = plane + send(plane, fy=3)
+    half = jnp.dot(weights[:512], texts, preferred_element_type=f32) + rows_met.astype(f32)
+    flight = half[Q:].astype(f16)
+    plane, gt16, half, flight = tied(plane, gt16, half, flight)
+    plane = plane + send(plane, fx=2)
     back_xy = lax.all_to_all(gt16, ("yh", "x", "yl"), 0, 0, tiled=True)
     text_loss = lax.dynamic_slice_in_dim(plane, ((yh * 4 + x) * 2 + yl) * Q, Q, 0)
     place = (lax.broadcasted_iota(jnp.int32, (NZ, 2), 0) == z).astype(f32)
@@ -226,25 +281,13 @@
     arrived = one.astype(f32) + two.astype(f32) + three.astype(f32)
     theirs = jnp.concatenate([lax.dynamic_slice_in_dim(arrived, (1 - core) * Q, Q, 0), arrived[128:]])
     met = send(theirs, fc=1)
-    gi_own = half[:Q] + far[:Q].astype(f32) + lax.dynamic_slice_in_dim(arrived, core * Q, Q, 0) + met[:Q]
-
-    def own_losses(rows):
-        return lax.dynamic_slice_in_dim(rows[0, :128] + rows[1, :128], core * Q, Q, 0)
-
-    far_rows = far[Q:].astype(f32)
-    image_loss = li_half[:Q] + far_rows[0, :Q] + far_rows[1, :Q] + own_losses(arrived[128:]) + own_losses(met[Q:])
-    every_z = far_rows[2:4, : 2 * NZ] + arrived[130:132, : 2 * NZ] + met[Q + 2 : Q + 4, : 2 * NZ] + jnp.stack(here)
-    both = jnp.sum((every_z[0] + every_z[1]).reshape(NZ, 2), axis=0) / SUM_SCALE
     gt_own = jnp.sum(back_xy.reshape(16, Q, -1).astype(f32), axis=0)
-
-    gi_own = gi_own + match_weight[:, None] * text_low
-    gt_own = gt_own + match_weight[:, None] * image_low
-    grad_image = image_inv * (
-        gi_own - image_unit * jnp.sum(image_unit * gi_own, axis=-1, keepdims=True)
+    here_row = jnp.pad(jnp.stack(here), ((0, 0), (0, 128 - 2 * NZ)))
+    grad_image, grad_text, image_loss, both = finish(
+        half[:Q], far.astype(f32), arrived, met, gt_own, image_unit, text_unit, image_inv, text_inv,
+        match_weight[:, None], (li_half[:Q] + match_loss)[None], here_row,
     )
-    grad_text = text_inv * (gt_own - text_unit * jnp.sum(text_unit * gt_own, axis=-1, keepdims=True))
-
-    image_loss, text_loss = image_loss + match_loss, text_loss + match_loss
+    image_loss, both, text_loss = image_loss.reshape(Q), both.reshape(2), text_loss + match_loss
     return (grad_image, grad_text, image_loss, text_loss, both)
 
 

time: 143 us -> 134 us (0.937)
  other arithmetic: 23.5 us -> 12 us
  starting transfers between devices: 52.3 us -> 47 us
  matrix products: 9.45 us -> 13.6 us
  waiting for transfers between devices: 38.9 us -> 41.4 us
  Pallas kernels: 6.25 us -> 7.72 us
    ppermute x25, starting transfers between devices: 48.6 us -> 42.6 us  [send(): return lax.ppermute(value, AXES, pairs)]
    reduce_sum x3 -> x0, other arithmetic: 3.47 us -> none  [the longest x1 2.08 us: per_device(): jnp.sum(image_unit * gi_own, axis=-1, keepdims=True)]
    add x7 -> x2, other arithmetic: 3.23 us -> 0.01 us  [the longest x1 0.01 us: per_device(): plane = plane + send(plane, fx=2)]
    ppermute x25, waiting for transfers between devices: 38.9 us -> 41.4 us  [send(): return lax.ppermute(value, AXES, pairs)]
    concatenate x3, other arithmetic: 2.37 us -> 0.18 us  [per_device(): jnp.concatenate([flight[(k - 1) * 128:k * 128], extra_rows(parts_of(li_ha...]
    dot_general x1, matrix products: 4.25 us -> 6.03 us  [per_device(): lax.dot_general(weights, images, (((0,), (0,)), ((), ())), preferred_elem...]
    reduce_sum x1, other arithmetic: 0.31 us -> 2.01 us  [per_device(): gt_own = jnp.sum(back_xy.reshape(16, Q, -1).astype(f32), axis=0)]
    unnamed x46 -> x20, local copies, waits for them, and re-layouts: 5.65 us -> 4.22 us
  transfers between devices with their start and end apart: 26 -> 26, of which waited for: 10 -> 10; matrix products, arithmetic and copies ran while one was open for 19% -> 18% of each run, Pallas kernels for 0% -> 0%
where the time goes in v3:
time: 134 us; the launch traced here: 132 us
  starting transfers between devices  47 us (35%)
  waiting for transfers between devices  41.4 us (31%)
  matrix products  13.6 us (10%)
  other arithmetic  12 us (9%)
  Pallas kernels  7.72 us (6%)
  local copies, waits for them, and re-layouts  7.39 us (6%)
  between operations  3.12 us (2%)
    ppermute x25, starting transfers between devices, send(): return lax.ppermute(value, AXES, pairs)  42.6 us
    ppermute x25, waiting for transfers between devices, send(): return lax.ppermute(value, AXES, pairs)  41.4 us
    pallas_call x1, Pallas kernels, pairs_on_device(): pl.pallas_call(pair_kernel, out_shape=(jax.ShapeDtypeStruct((1024, 1024),...  6.65 us
    dot_general x1, matrix products, per_device(): lax.dot_general(weights, images, (((0,), (0,)), ((), ())), preferred_elem...  6.03 us
    dot_general x1, matrix products, per_device(): jnp.dot(weights[512:], texts, preferred_element_type=f32).astype(f16)  4.75 us
    all_to_all x1, starting transfers between devices, per_device(): back_xy = lax.all_to_all(gt16, ('yh', 'x', 'yl'), 0, 0, tiled=True)  4.45 us
    unnamed x20, local copies, waits for them, and re-layouts  4.22 us
    dot_general x1, matrix products, per_device(): jnp.dot(weights[:512], texts, preferred_element_type=f32)  2.82 us
  transfers between devices with their start and end apart: 26, of which 10 were waited for; matrix products, arithmetic and copies ran while one was open for 18% of the time, Pallas kernels for 0%

profile of v3, /device:TPU:1, one launch (start us, length us, event | category | flops | bytes accessed | tf_op | source)
XLA Modules:
  0.0 132.2 jit_solution(2301315687290533968)
XLA Ops:
  0.6 1.1 constant_dynamic-slice_fusion.3
  1.7 0.1 fusion.7
  1.9 0.1 fusion.8.refs_6_
  2.0 2.1 %collective-permute-start = (bf16[128,1152]{1,0:T(8,128)(2,1)S(1)}, bf16[128,1152]{1,0:T(8,128)(2,1)S(1)}, u32[]{:S(2)}, u32[]{:S(2)}) collective-permute-start(bf16[128,1152]{1,0:T(8,128)(2,1)S(1)} %fusion.8.refs_6_), channel_id=1, source_target_pairs={{0,4},{1,5},{2,6},{3,7},{4,8},{5,9},{6,10},{7,11},{8,12},{9,13},{1... | collective-permute-start | bytes 884744 | tf_op jit(solution)/shard_map/ppermute | solution.py:32
  4.1 1.4 %collective-permute-start.1 = (bf16[128,1152]{1,0:T(8,128)(2,1)S(1)}, bf16[128,1152]{1,0:T(8,128)(2,1)S(1)}, u32[]{:S(2)}, u32[]{:S(2)}) collective-permute-start(bf16[128,1152]{1,0:T(8,128)(2,1)S(1)} %fusion.8.refs_6_), channel_id=1, source_target_pairs={{0,12},{1,13},{2,14},{3,15},{4,0},{5,1},{6,2},{7,3},{8,4},{9,5},{1... | collective-permute-start | bytes 884744 | tf_op jit(solution)/shard_map/ppermute | solution.py:32
  5.5 2.8 %collective-permute-start.2 = (bf16[128,1152]{1,0:T(8,128)(2,1)S(1)}, bf16[128,1152]{1,0:T(8,128)(2,1)S(1)}, u32[]{:S(2)}, u32[]{:S(2)}) collective-permute-start(bf16[128,1152]{1,0:T(8,128)(2,1)S(1)} %fusion.8.refs_6_), channel_id=1, source_target_pairs={{0,130},{1,131},{2,128},{3,129},{4,134},{5,135},{6,132},{7,133},{8... | collective-permute-start | bytes 884744 | tf_op jit(solution)/shard_map/ppermute | solution.py:32
  8.3 1.1 fusion.5
  9.4 1.1 fusion.6.refs_0_
  10.5 6.5 %collective-permute-start.3 = (bf16[128,1152]{1,0:T(8,128)(2,1)S(1)}, bf16[128,1152]{1,0:T(8,128)(2,1)S(1)}, u32[]{:S(2)}, u32[]{:S(2)}) collective-permute-start(bf16[128,1152]{1,0:T(8,128)(2,1)S(1)} %fusion.6.refs_0_), channel_id=1, source_target_pairs={{0,48},{1,81},{2,50},{3,83},{4,52},{5,85},{6,54},{7,87},{8,56},{9,... | collective-permute-start | bytes 884744 | tf_op jit(solution)/shard_map/ppermute | solution.py:32
  17.1 0.6 collective-permute-start.4
  17.6 0.1 fusion.13
  17.8 1.0 fusion.14
  18.8 1.2 multiply_reduce_fusion
  21.3 0.6 multiply_reduce_fusion.1
  22.1 2.7 %collective-permute-start.6 = (bf16[128,1152]{1,0:T(8,128)(2,1)S(1)}, bf16[128,1152]{1,0:T(8,128)(2,1)S(1)}, u32[]{:S(2)}, u32[]{:S(2)}) collective-permute-start(bf16[128,1152]{1,0:T(8,128)(2,1)S(1)} %collective-permute-done.2.refs_10_), channel_id=1, source_target_pairs={{0,12},{1,13},{2,14},{3,15},{4,0},{5,1},{6,2},{7,3},{8,4},{9,5},{1... | collective-permute-start | bytes 884744 | tf_op jit(solution)/shard_map/ppermute | solution.py:32
  24.9 8.4 %collective-permute-done.4.refs_4_ = bf16[64,1152]{1,0:T(8,128)(2,1)S(1)} collective-permute-done((bf16[64,1152]{1,0:T(8,128)(2,1)S(1)}, bf16[64,1152]{1,0:T(8,128)(2,1)S(1)}, u32[]{:S(2)}, u32[]{:S(2)}) %collective-permute-start.4) | collective-permute-done | bytes 147488 | tf_op jit(solution)/shard_map/ppermute | solution.py:32
  33.2 1.3 collective-permute-start.8
  34.5 0.6 multiply_reduce-precision_fusion
  35.7 1.2 pad_maximum_fusion.16
  37.0 0.3 collective-permute-done.8
  37.2 3.0 %collective-permute-start.9 = (bf16[128,1152]{1,0:T(8,128)(2,1)S(1)}, bf16[128,1152]{1,0:T(8,128)(2,1)S(1)}, u32[]{:S(2)}, u32[]{:S(2)}) collective-permute-start(bf16[128,1152]{1,0:T(8,128)(2,1)S(1)} %fusion.6.refs_0_), channel_id=1, source_target_pairs={{0,16},{1,113},{2,18},{3,115},{4,20},{5,117},{6,22},{7,119},{8,24}... | collective-permute-start | bytes 884744 | tf_op jit(solution)/shard_map/ppermute | solution.py:32
  40.2 0.3 collective-permute-start.11
  40.5 2.6 %collective-permute-start.12 = (bf16[64,1152]{1,0:T(8,128)(2,1)S(1)}, bf16[64,1152]{1,0:T(8,128)(2,1)S(1)}, u32[]{:S(2)}, u32[]{:S(2)}) collective-permute-start(bf16[64,1152]{1,0:T(8,128)(2,1)S(1)} %slice.79), channel_id=1, source_target_pairs={{0,12},{1,13},{2,14},{3,15},{4,0},{5,1},{6,2},{7,3},{8,4},{9,5},{1... | collective-permute-start | bytes 442376 | tf_op jit(solution)/shard_map/ppermute | solution.py:32
  43.1 0.9 pad_maximum_fusion.3.refs_9_
  44.0 3.0 %collective-permute-done.10.refs_2_ = bf16[128,1152]{1,0:T(8,128)(2,1)S(1)} collective-permute-done((bf16[128,1152]{1,0:T(8,128)(2,1)S(1)}, bf16[128,1152]{1,0:T(8,128)(2,1)S(1)}, u32[]{:S(2)}, u32[]{:S(2)}) %collective-permute-start.10) | collective-permute-done | bytes 294944 | tf_op jit(solution)/shard_map/ppermute | solution.py:32
  47.0 2.5 %collective-permute-done.9.refs_1_ = bf16[128,1152]{1,0:T(8,128)(2,1)S(1)} collective-permute-done((bf16[128,1152]{1,0:T(8,128)(2,1)S(1)}, bf16[128,1152]{1,0:T(8,128)(2,1)S(1)}, u32[]{:S(2)}, u32[]{:S(2)}) %collective-permute-start.9) | collective-permute-done | bytes 294944 | tf_op jit(solution)/shard_map/ppermute | solution.py:32
  49.6 3.6 %collective-permute-start.13 = (bf16[448,1152]{1,0:T(8,128)(2,1)S(1)}, bf16[448,1152]{1,0:T(8,128)(2,1)S(1)}, u32[]{:S(2)}, u32[]{:S(2)}) collective-permute-start(bf16[448,1152]{1,0:T(8,128)(2,1)S(1)} %pad_maximum_fusion), channel_id=1, source_target_pairs={{0,1},{1,0},{2,3},{3,2},{4,5},{5,4},{6,7},{7,6},{8,9},{9,8},{10,11... | collective-permute-start | bytes 3096584 | tf_op jit(solution)/shard_map/ppermute | solution.py:32
  53.3 2.1 %collective-permute-done.13.refs_5_ = bf16[448,1152]{1,0:T(8,128)(2,1)S(1)} collective-permute-done((bf16[448,1152]{1,0:T(8,128)(2,1)S(1)}, bf16[448,1152]{1,0:T(8,128)(2,1)S(1)}, u32[]{:S(2)}, u32[]{:S(2)}) %collective-permute-start.13) | collective-permute-done | bytes 1032224 | tf_op jit(solution)/shard_map/ppermute | solution.py:32
  55.5 6.7 %pairs.1 = (bf16[1024,1024]{1,0:T(8,128)(2,1)S(1)}, bf16[1024,1152]{1,0:T(8,128)(2,1)S(1)}, bf16[1024,1152]{1,0:T(8,128)(2,1)S(1)}, f32[1024,1]{1,0:T(8,128)S(1)...) custom-call(f32[2]{0:T(128)S(1)} %pad_maximum_fusion.15.par_ref, bf16[128,1152]{1,0:T(8,128)(2,1)S(1)} %fusion.6.refs_0_, ...), custom_call_target="tpu_custom_call" | custom-call | flops 2415919104 | bytes 12582912 | tf_op jit(solution)/shard_map/pairs/pallas_call | solution.py:128
  62.1 1.4 %copy-done = bf16[1024,1152]{1,0:T(8,128)(2,1)} copy-done((bf16[1024,1152]{1,0:T(8,128)(2,1)}, bf16[1024,1152]{1,0:T(8,128)(2,1)S(1)}, u32[]{:S(2)}) %copy-start) | copy-done | bytes 2359320
  63.6 1.3 %copy-done.2 = bf16[1024,1024]{1,0:T(8,128)(2,1)} copy-done((bf16[1024,1024]{1,0:T(8,128)(2,1)}, bf16[1024,1024]{1,0:T(8,128)(2,1)S(1)}, u32[]{:S(2)}) %copy-start.2) | copy-done | bytes 2097176
  64.9 1.4 %copy-done.4 = bf16[1024,1152]{1,0:T(8,128)(2,1)} copy-done((bf16[1024,1152]{1,0:T(8,128)(2,1)}, bf16[1024,1152]{1,0:T(8,128)(2,1)S(1)}, u32[]{:S(2)}) %copy-start.4) | copy-done | bytes 2359320
  66.3 0.2 slice_reduce_fusion
  66.5 0.1 reduce_sum.88
  66.7 0.5 collective-permute-start.14
  67.2 0.8 collective-permute-done.14
  68.1 4.8 %convolution_convert_fusion.1 = f16[512,1152]{1,0:T(8,128)(2,1)} fusion(bf16[1024,1152]{1,0:T(8,128)(2,1)} %copy-done, bf16[1024,1024]{1,0:T(8,128)(2,1)} %copy-done.2), kind=kOutput, calls=%fused_computation.3 | convolution fusion | flops 1208549376 | bytes 4587520 | tf_op jit(solution)/shard_map/dot_general | solution.py:250
  72.9 0.5 collective-permute-start.17
  73.4 0.1 copy.12.image_inv
  73.5 0.1 copy.13.text_inv
  73.6 0.1 copy.14.weight
  73.7 6.0 %convolution_convert_fusion = f16[1024,1152]{1,0:T(8,128)(2,1)} fusion(bf16[1024,1024]{1,0:T(8,128)(2,1)S(1)} %copy-done.3, bf16[1024,1152]{1,0:T(8,128)(2,1)} %copy-done.4), kind=kOutput, calls=%fused_computation.1 | convolution fusion | flops 2417098752 | bytes 6815744 | tf_op jit(solution)/shard_map/dot_general | solution.py:254
  79.8 0.2 collective-permute-start.16
  80.0 0.1 reduce-precision_convert_fusion
  80.3 2.0 %collective-permute-done.16 = f32[1026]{0:T(1024)S(1)} collective-permute-done((f32[1026]{0:T(1024)S(1)}, f32[1026]{0:T(1024)S(1)}, u32[]{:S(2)}, u32[]{:S(2)}) %collective-permute-start.16) | collective-permute-done | bytes 4136 | tf_op jit(solution)/shard_map/ppermute | solution.py:32
  82.3 2.8 %convolution_add_fusion = f32[512,1152]{1,0:T(8,128)S(1)} fusion(bf16[1024,1152]{1,0:T(8,128)(2,1)S(1)} %copy-done.1, f16[512,1152]{1,0:T(8,128)(2,1)} %collective-permute-done.17, bf16[1024,1024]{1,0:T(8,128)(2,1)S(1)} %copy-done.3), kind=kOutput, calls=%fused_computation.2 | convolution fusion | flops 1209139200 | bytes 6946816 | tf_op jit(solution)/shard_map/dot_general | solution.py:259
  85.1 1.1 collective-permute-start.18
  86.2 0.1 slice_convert_fusion
  86.3 2.8 %collective-permute-done.18 = f32[1026]{0:T(1024)S(1)} collective-permute-done((f32[1026]{0:T(1024)S(1)}, f32[1026]{0:T(1024)S(1)}, u32[]{:S(2)}, u32[]{:S(2)}) %collective-permute-start.18) | collective-permute-done | bytes 4136 | tf_op jit(solution)/shard_map/ppermute | solution.py:32
  89.1 0.5 collective-permute-start.19
  89.7 0.1 fusion.27
  89.8 4.5 %all-to-all-start = ((f16[16,64,1152]{2,1,0:T(8,128)(2,1)}), f16[16,64,1152]{2,1,0:T(8,128)(2,1)}, u32[]{:S(2)}, u32[]{:S(2)}) async-start(f16[16,64,1152]{2,1,0:T(8,128)(2,1)} %bitcast.22), calls=%async_computation | async-start | bytes 4718592 | tf_op jit(solution)/shard_map/all_to_all | solution.py:263
  94.3 1.0 slice.86.half
  95.3 0.6 add_bitcast_fusion
  96.4 0.8 collective-permute-start.23
  97.2 1.6 %collective-permute-start.22 = (f16[136,1152]{1,0:T(8,128)(2,1)S(1)}, f16[136,1152]{1,0:T(8,128)(2,1)S(1)}, u32[]{:S(2)}, u32[]{:S(2)}) collective-permute-start(f16[136,1152]{1,0:T(8,128)(2,1)S(1)} %fusion.11), channel_id=1, source_target_pairs={{0,32},{1,97},{2,34},{3,99},{4,36},{5,101},{6,38},{7,103},{8,40},{... | collective-permute-start | bytes 940040 | tf_op jit(solution)/shard_map/ppermute | solution.py:32
  98.9 2.3 %collective-permute-start.21 = (f16[136,1152]{1,0:T(8,128)(2,1)S(1)}, f16[136,1152]{1,0:T(8,128)(2,1)S(1)}, u32[]{:S(2)}, u32[]{:S(2)}) collective-permute-start(f16[136,1152]{1,0:T(8,128)(2,1)S(1)} %fusion.10), channel_id=1, source_target_pairs={{0,48},{1,81},{2,50},{3,83},{4,52},{5,85},{6,54},{7,87},{8,56},{9,... | collective-permute-start | bytes 940040 | tf_op jit(solution)/shard_map/ppermute | solution.py:32
  101.3 1.8 %collective-permute-start.20 = (f16[72,1152]{1,0:T(8,128)(2,1)S(1)}, f16[72,1152]{1,0:T(8,128)(2,1)S(1)}, u32[]{:S(2)}, u32[]{:S(2)}) collective-permute-start(f16[72,1152]{1,0:T(8,128)(2,1)S(1)} %fusion.15), channel_id=1, source_target_pairs={{0,64},{1,65},{2,66},{3,67},{4,68},{5,69},{6,70},{7,71},{8,72},{9,... | collective-permute-start | bytes 497672 | tf_op jit(solution)/shard_map/ppermute | solution.py:32
  103.2 8.7 %collective-permute-done.20 = f16[72,1152]{1,0:T(8,128)(2,1)S(1)} collective-permute-done((f16[72,1152]{1,0:T(8,128)(2,1)S(1)}, f16[72,1152]{1,0:T(8,128)(2,1)S(1)}, u32[]{:S(2)}, u32[]{:S(2)}) %collective-permute-start.20) | collective-permute-done | bytes 165920 | tf_op jit(solution)/shard_map/ppermute | solution.py:32
  111.9 10.7 %collective-permute-done.21 = f16[136,1152]{1,0:T(8,128)(2,1)S(1)} collective-permute-done((f16[136,1152]{1,0:T(8,128)(2,1)S(1)}, f16[136,1152]{1,0:T(8,128)(2,1)S(1)}, u32[]{:S(2)}, u32[]{:S(2)}) %collective-permute-start.21) | collective-permute-done | bytes 313376 | tf_op jit(solution)/shard_map/ppermute | solution.py:32
  122.6 0.1 convert_add_fusion.arrived
  122.8 6.2 %collective-permute-start.24 = (f32[72,1152]{1,0:T(8,128)S(1)}, f32[72,1152]{1,0:T(8,128)S(1)}, u32[]{:S(2)}, u32[]{:S(2)}) collective-permute-start(f32[72,1152]{1,0:T(8,128)S(1)} %pad_maximum_fusion.1), channel_id=1, source_target_pairs={{0,1},{1,0},{2,3},{3,2},{4,5},{5,4},{6,7},{7,6},{8,9},{9,8},{10,11... | collective-permute-start | bytes 995336 | tf_op jit(solution)/shard_map/ppermute | solution.py:32
  129.1 2.0 %convert_reduce_fusion.gt = f32[64,1152]{1,0:T(8,128)S(1)} fusion(f16[16,64,1152]{2,1,0:T(8,128)(2,1)} %all-to-all-done), kind=kLoop, calls=%fused_computation | loop fusion | flops 2285568 | bytes 2654208 | tf_op jit(solution)/shard_map/reduce_sum | solution.py:284
  131.1 1.1 finish.1
  (96 shorter events, 1.5 us)
Async XLA Ops:
  0.6 17.0 %copy-start.7 = (bf16[256,1152]{1,0:T(8,128)(2,1)S(1)}, bf16[256,1152]{1,0:T(8,128)(2,1)}, u32[]{:S(2)}) copy-start(bf16[256,1152]{1,0:T(8,128)(2,1)} %param.4) | copy-start | bytes 1769476
  2.0 20.0 %collective-permute-start = (bf16[128,1152]{1,0:T(8,128)(2,1)S(1)}, bf16[128,1152]{1,0:T(8,128)(2,1)S(1)}, u32[]{:S(2)}, u32[]{:S(2)}) collective-permute-start(bf16[128,1152]{1,0:T(8,128)(2,1)S(1)} %fusion.8.refs_6_), channel_id=1, source_target_pairs={{0,4},{1,5},{2,6},{3,7},{4,8},{5,9},{6,10},{7,11},{8,12},{9,13},{1... | collective-permute-start | bytes 884744 | tf_op jit(solution)/shard_map/ppermute | solution.py:32
  4.1 17.9 %collective-permute-start.1 = (bf16[128,1152]{1,0:T(8,128)(2,1)S(1)}, bf16[128,1152]{1,0:T(8,128)(2,1)S(1)}, u32[]{:S(2)}, u32[]{:S(2)}) collective-permute-start(bf16[128,1152]{1,0:T(8,128)(2,1)S(1)} %fusion.8.refs_6_), channel_id=1, source_target_pairs={{0,12},{1,13},{2,14},{3,15},{4,0},{5,1},{6,2},{7,3},{8,4},{9,5},{1... | collective-permute-start | bytes 884744 | tf_op jit(solution)/shard_map/ppermute | solution.py:32
  5.5 16.5 %collective-permute-start.2 = (bf16[128,1152]{1,0:T(8,128)(2,1)S(1)}, bf16[128,1152]{1,0:T(8,128)(2,1)S(1)}, u32[]{:S(2)}, u32[]{:S(2)}) collective-permute-start(bf16[128,1152]{1,0:T(8,128)(2,1)S(1)} %fusion.8.refs_6_), channel_id=1, source_target_pairs={{0,130},{1,131},{2,128},{3,129},{4,134},{5,135},{6,132},{7,133},{8... | collective-permute-start | bytes 884744 | tf_op jit(solution)/shard_map/ppermute | solution.py:32
  10.5 26.4 %collective-permute-start.3 = (bf16[128,1152]{1,0:T(8,128)(2,1)S(1)}, bf16[128,1152]{1,0:T(8,128)(2,1)S(1)}, u32[]{:S(2)}, u32[]{:S(2)}) collective-permute-start(bf16[128,1152]{1,0:T(8,128)(2,1)S(1)} %fusion.6.refs_0_), channel_id=1, source_target_pairs={{0,48},{1,81},{2,50},{3,83},{4,52},{5,85},{6,54},{7,87},{8,56},{9,... | collective-permute-start | bytes 884744 | tf_op jit(solution)/shard_map/ppermute | solution.py:32
  17.1 16.2 %collective-permute-start.4 = (bf16[64,1152]{1,0:T(8,128)(2,1)S(1)}, bf16[64,1152]{1,0:T(8,128)(2,1)S(1)}, u32[]{:S(2)}, u32[]{:S(2)}) collective-permute-start(bf16[64,1152]{1,0:T(8,128)(2,1)S(1)} %constant_dynamic-slice_fusion.1), channel_id=1, source_target_pairs={{0,64},{1,65},{2,66},{3,67},{4,68},{5,69},{6,70},{7,71},{8,72},{9,... | collective-permute-start | bytes 442376 | tf_op jit(solution)/shard_map/ppermute | solution.py:32
  22.0 15.3 %collective-permute-start.5 = (bf16[128,1152]{1,0:T(8,128)(2,1)S(1)}, bf16[128,1152]{1,0:T(8,128)(2,1)S(1)}, u32[]{:S(2)}, u32[]{:S(2)}) collective-permute-start(bf16[128,1152]{1,0:T(8,128)(2,1)S(1)} %collective-permute-done.2.refs_10_), channel_id=1, source_target_pairs={{0,4},{1,5},{2,6},{3,7},{4,8},{5,9},{6,10},{7,11},{8,12},{9,13},{1... | collective-permute-start | bytes 884744 | tf_op jit(solution)/shard_map/ppermute | solution.py:32
  22.1 15.2 %collective-permute-start.6 = (bf16[128,1152]{1,0:T(8,128)(2,1)S(1)}, bf16[128,1152]{1,0:T(8,128)(2,1)S(1)}, u32[]{:S(2)}, u32[]{:S(2)}) collective-permute-start(bf16[128,1152]{1,0:T(8,128)(2,1)S(1)} %collective-permute-done.2.refs_10_), channel_id=1, source_target_pairs={{0,12},{1,13},{2,14},{3,15},{4,0},{5,1},{6,2},{7,3},{8,4},{9,5},{1... | collective-permute-start | bytes 884744 | tf_op jit(solution)/shard_map/ppermute | solution.py:32
  24.8 12.2 %collective-permute-start.7 = (bf16[64,1152]{1,0:T(8,128)(2,1)S(1)}, bf16[64,1152]{1,0:T(8,128)(2,1)}, u32[]{:S(2)}, u32[]{:S(2)}) collective-permute-start(bf16[64,1152]{1,0:T(8,128)(2,1)S(1)} %slice.76), channel_id=1, source_target_pairs={{0,4},{1,5},{2,6},{3,7},{4,8},{5,9},{6,10},{7,11},{8,12},{9,13},{1... | collective-permute-start | bytes 442376 | tf_op jit(solution)/shard_map/ppermute | solution.py:32
  33.2 4.0 %collective-permute-start.8 = (bf16[64,1152]{1,0:T(8,128)(2,1)S(1)}, bf16[64,1152]{1,0:T(8,128)(2,1)S(1)}, u32[]{:S(2)}, u32[]{:S(2)}) collective-permute-start(bf16[64,1152]{1,0:T(8,128)(2,1)S(1)} %slice.77), channel_id=1, source_target_pairs={{0,12},{1,13},{2,14},{3,15},{4,0},{5,1},{6,2},{7,3},{8,4},{9,5},{1... | collective-permute-start | bytes 442376 | tf_op jit(solution)/shard_map/ppermute | solution.py:32
  37.0 10.0 %collective-permute-start.10 = (bf16[128,1152]{1,0:T(8,128)(2,1)S(1)}, bf16[128,1152]{1,0:T(8,128)(2,1)S(1)}, u32[]{:S(2)}, u32[]{:S(2)}) collective-permute-start(bf16[128,1152]{1,0:T(8,128)(2,1)S(1)} %fusion.6.refs_0_), channel_id=1, source_target_pairs={{0,32},{1,97},{2,34},{3,99},{4,36},{5,101},{6,38},{7,103},{8,40},{... | collective-permute-start | bytes 884744 | tf_op jit(solution)/shard_map/ppermute | solution.py:32
  37.2 12.2 %collective-permute-start.9 = (bf16[128,1152]{1,0:T(8,128)(2,1)S(1)}, bf16[128,1152]{1,0:T(8,128)(2,1)S(1)}, u32[]{:S(2)}, u32[]{:S(2)}) collective-permute-start(bf16[128,1152]{1,0:T(8,128)(2,1)S(1)} %fusion.6.refs_0_), channel_id=1, source_target_pairs={{0,16},{1,113},{2,18},{3,115},{4,20},{5,117},{6,22},{7,119},{8,24}... | collective-permute-start | bytes 884744 | tf_op jit(solution)/shard_map/ppermute | solution.py:32
  40.2 6.7 %collective-permute-start.11 = (bf16[64,1152]{1,0:T(8,128)(2,1)S(1)}, bf16[64,1152]{1,0:T(8,128)(2,1)S(1)}, u32[]{:S(2)}, u32[]{:S(2)}) collective-permute-start(bf16[64,1152]{1,0:T(8,128)(2,1)S(1)} %slice.78), channel_id=1, source_target_pairs={{0,4},{1,5},{2,6},{3,7},{4,8},{5,9},{6,10},{7,11},{8,12},{9,13},{1... | collective-permute-start | bytes 442376 | tf_op jit(solution)/shard_map/ppermute | solution.py:32
  40.5 6.5 %collective-permute-start.12 = (bf16[64,1152]{1,0:T(8,128)(2,1)S(1)}, bf16[64,1152]{1,0:T(8,128)(2,1)S(1)}, u32[]{:S(2)}, u32[]{:S(2)}) collective-permute-start(bf16[64,1152]{1,0:T(8,128)(2,1)S(1)} %slice.79), channel_id=1, source_target_pairs={{0,12},{1,13},{2,14},{3,15},{4,0},{5,1},{6,2},{7,3},{8,4},{9,5},{1... | collective-permute-start | bytes 442376 | tf_op jit(solution)/shard_map/ppermute | solution.py:32
  49.6 5.9 %collective-permute-start.13 = (bf16[448,1152]{1,0:T(8,128)(2,1)S(1)}, bf16[448,1152]{1,0:T(8,128)(2,1)S(1)}, u32[]{:S(2)}, u32[]{:S(2)}) collective-permute-start(bf16[448,1152]{1,0:T(8,128)(2,1)S(1)} %pad_maximum_fusion), channel_id=1, source_target_pairs={{0,1},{1,0},{2,3},{3,2},{4,5},{5,4},{6,7},{7,6},{8,9},{9,8},{10,11... | collective-permute-start | bytes 3096584 | tf_op jit(solution)/shard_map/ppermute | solution.py:32
  53.3 13.4 %copy-start.9 = (f32[2]{0:T(128)S(1)}, f32[2]{0:T(128)}, u32[]{:S(2)}) copy-start(f32[2]{0:T(128)} %pad_maximum_fusion.16) | copy-start | bytes 28
  62.1 1.4 %copy-start = (bf16[1024,1152]{1,0:T(8,128)(2,1)}, bf16[1024,1152]{1,0:T(8,128)(2,1)S(1)}, u32[]{:S(2)}) copy-start(bf16[1024,1152]{1,0:T(8,128)(2,1)S(1)} %get-tuple-element.78) | copy-start | bytes 7077892
  63.6 1.3 %copy-start.2 = (bf16[1024,1024]{1,0:T(8,128)(2,1)}, bf16[1024,1024]{1,0:T(8,128)(2,1)S(1)}, u32[]{:S(2)}) copy-start(bf16[1024,1024]{1,0:T(8,128)(2,1)S(1)} %get-tuple-element.77) | copy-start | bytes 6291460
  64.9 1.4 %copy-start.4 = (bf16[1024,1152]{1,0:T(8,128)(2,1)}, bf16[1024,1152]{1,0:T(8,128)(2,1)S(1)}, u32[]{:S(2)}) copy-start(bf16[1024,1152]{1,0:T(8,128)(2,1)S(1)} %get-tuple-element.80) | copy-start | bytes 7077892
  66.7 1.3 collective-permute-start.14
  68.0 4.9 %collective-permute-start.15 = (f32[1026]{0:T(1024)S(1)}, f32[1026]{0:T(1024)S(1)}, u32[]{:S(2)}, u32[]{:S(2)}) collective-permute-start(f32[1026]{0:T(1024)S(1)} %pad_maximum_fusion.13), channel_id=1, source_target_pairs={{0,2},{1,3},{2,0},{3,1},{4,6},{5,7},{6,4},{7,5},{8,10},{9,11},{10,... | collective-permute-start | bytes 12320 | tf_op jit(solution)/shard_map/ppermute | solution.py:32
  68.1 5.5 %copy-start.8 = (f32[64]{0:T(128)S(1)}, f32[64]{0:T(128)}, u32[]{:S(2)}) copy-start(f32[64]{0:T(128)} %multiply_reduce-precision_fusion) | copy-start | bytes 772
  68.1 5.6 %copy-start.3 = (bf16[1024,1024]{1,0:T(8,128)(2,1)S(1)}, bf16[1024,1024]{1,0:T(8,128)(2,1)}, u32[]{:S(2)}) copy-start(bf16[1024,1024]{1,0:T(8,128)(2,1)} %copy-done.2) | copy-start | bytes 6291460
  72.9 9.4 %collective-permute-start.17 = (f16[512,1152]{1,0:T(8,128)(2,1)}, f16[512,1152]{1,0:T(8,128)(2,1)}, u32[]{:S(2)}, u32[]{:S(2)}) collective-permute-start(f16[512,1152]{1,0:T(8,128)(2,1)} %convolution_convert_fusion.1), channel_id=1, source_target_pairs={{0,1},{1,0},{2,3},{3,2},{4,5},{5,4},{6,7},{7,6},{8,9},{9,8},{10,11... | collective-permute-start | bytes 3538952 | tf_op jit(solution)/shard_map/ppermute | solution.py:32
  73.7 8.5 %copy-start.1 = (bf16[1024,1152]{1,0:T(8,128)(2,1)S(1)}, bf16[1024,1152]{1,0:T(8,128)(2,1)}, u32[]{:S(2)}) copy-start(bf16[1024,1152]{1,0:T(8,128)(2,1)} %copy-done) | copy-start | bytes 7077892
  79.8 2.5 %collective-permute-start.16 = (f32[1026]{0:T(1024)S(1)}, f32[1026]{0:T(1024)S(1)}, u32[]{:S(2)}, u32[]{:S(2)}) collective-permute-start(f32[1026]{0:T(1024)S(1)} %fusion.24), channel_id=1, source_target_pairs={{0,4},{1,5},{2,6},{3,7},{4,0},{5,1},{6,2},{7,3},{8,12},{9,13},{10,... | collective-permute-start | bytes 12320 | tf_op jit(solution)/shard_map/ppermute | solution.py:32
  85.1 4.7 %copy-start.6 = (f32[512,1152]{1,0:T(8,128)}, f32[512,1152]{1,0:T(8,128)S(1)}, u32[]{:S(2)}) copy-start(f32[512,1152]{1,0:T(8,128)S(1)} %convolution_add_fusion) | copy-start | bytes 7077892
  85.1 4.0 %collective-permute-start.18 = (f32[1026]{0:T(1024)S(1)}, f32[1026]{0:T(1024)S(1)}, u32[]{:S(2)}, u32[]{:S(2)}) collective-permute-start(f32[1026]{0:T(1024)S(1)} %add.173), channel_id=1, source_target_pairs={{0,130},{1,131},{2,128},{3,129},{4,134},{5,135},{6,132},{7,133},{8... | collective-permute-start | bytes 12320 | tf_op jit(solution)/shard_map/ppermute | solution.py:32
  86.3 3.5 %copy-start.5 = (f16[448,1152]{1,0:T(8,128)(2,1)}, f16[448,1152]{1,0:T(8,128)(2,1)S(1)}, u32[]{:S(2)}) copy-start(f16[448,1152]{1,0:T(8,128)(2,1)S(1)} %slice_convert_fusion) | copy-start | bytes 3096580
  89.1 6.2 %collective-permute-start.19 = (f32[1026]{0:T(1024)S(1)}, f32[1026]{0:T(1024)S(1)}, u32[]{:S(2)}, u32[]{:S(2)}) collective-permute-start(f32[1026]{0:T(1024)S(1)} %add.174), channel_id=1, source_target_pairs={{0,8},{1,9},{2,10},{3,11},{4,12},{5,13},{6,14},{7,15},{8,0},{9,1},... | collective-permute-start | bytes 12320 | tf_op jit(solution)/shard_map/ppermute | solution.py:32
  89.8 39.3 %all-to-all-start = ((f16[16,64,1152]{2,1,0:T(8,128)(2,1)}), f16[16,64,1152]{2,1,0:T(8,128)(2,1)}, u32[]{:S(2)}, u32[]{:S(2)}) async-start(f16[16,64,1152]{2,1,0:T(8,128)(2,1)} %bitcast.22), calls=%async_computation | async-start | bytes 4718592 | tf_op jit(solution)/shard_map/all_to_all | solution.py:263
  94.3 6.9 %slice-start = ((f16[448,1152]{1,0:T(8,128)(2,1)}), f16[64,1152]{1,0:T(8,128)(2,1)S(1)}, s32[]{:S(2)}) async-start(f16[448,1152]{1,0:T(8,128)(2,1)} %copy-done.5), calls=%async_computation.1 | async-start | bytes 294912 | tf_op jit(solution)/shard_map/slice | solution.py:267
  96.4 15.5 %collective-permute-start.23 = (f16[136,1152]{1,0:T(8,128)(2,1)S(1)}, f16[136,1152]{1,0:T(8,128)(2,1)S(1)}, u32[]{:S(2)}, u32[]{:S(2)}) collective-permute-start(f16[136,1152]{1,0:T(8,128)(2,1)S(1)} %fusion.12), channel_id=1, source_target_pairs={{0,16},{1,113},{2,18},{3,115},{4,20},{5,117},{6,22},{7,119},{8,24}... | collective-permute-start | bytes 940040 | tf_op jit(solution)/shard_map/ppermute | solution.py:32
  97.2 14.7 %collective-permute-start.22 = (f16[136,1152]{1,0:T(8,128)(2,1)S(1)}, f16[136,1152]{1,0:T(8,128)(2,1)S(1)}, u32[]{:S(2)}, u32[]{:S(2)}) collective-permute-start(f16[136,1152]{1,0:T(8,128)(2,1)S(1)} %fusion.11), channel_id=1, source_target_pairs={{0,32},{1,97},{2,34},{3,99},{4,36},{5,101},{6,38},{7,103},{8,40},{... | collective-permute-start | bytes 940040 | tf_op jit(solution)/shard_map/ppermute | solution.py:32
  98.9 23.7 %collective-permute-start.21 = (f16[136,1152]{1,0:T(8,128)(2,1)S(1)}, f16[136,1152]{1,0:T(8,128)(2,1)S(1)}, u32[]{:S(2)}, u32[]{:S(2)}) collective-permute-start(f16[136,1152]{1,0:T(8,128)(2,1)S(1)} %fusion.10), channel_id=1, source_target_pairs={{0,48},{1,81},{2,50},{3,83},{4,52},{5,85},{6,54},{7,87},{8,56},{9,... | collective-permute-start | bytes 940040 | tf_op jit(solution)/shard_map/ppermute | solution.py:32
  101.3 10.6 %collective-permute-start.20 = (f16[72,1152]{1,0:T(8,128)(2,1)S(1)}, f16[72,1152]{1,0:T(8,128)(2,1)S(1)}, u32[]{:S(2)}, u32[]{:S(2)}) collective-permute-start(f16[72,1152]{1,0:T(8,128)(2,1)S(1)} %fusion.15), channel_id=1, source_target_pairs={{0,64},{1,65},{2,66},{3,67},{4,68},{5,69},{6,70},{7,71},{8,72},{9,... | collective-permute-start | bytes 497672 | tf_op jit(solution)/shard_map/ppermute | solution.py:32
  122.8 8.3 %collective-permute-start.24 = (f32[72,1152]{1,0:T(8,128)S(1)}, f32[72,1152]{1,0:T(8,128)S(1)}, u32[]{:S(2)}, u32[]{:S(2)}) collective-permute-start(f32[72,1152]{1,0:T(8,128)S(1)} %pad_maximum_fusion.1), channel_id=1, source_target_pairs={{0,1},{1,0},{2,3},{3,2},{4,5},{5,4},{6,7},{7,6},{8,9},{9,8},{10,11... | collective-permute-start | bytes 995336 | tf_op jit(solution)/shard_map/ppermute | solution.py:32

commit v4 on v3

--- a/solution.py
+++ b/solution.py
@@ -44,9 +44,12 @@
     return high, lax.reduce_precision(values - high, 5, 10)
 
 
-def extra_rows(losses, sums, width):
-    rows = [jnp.pad(v, (0, width - v.shape[0])) for v in (*losses, *sums)]
-    return jnp.pad(jnp.stack(rows), ((0, 4), (0, 0))).astype(jnp.float16)
+def two_rows(parts, width):
+    return jnp.pad(jnp.stack(parts), ((0, 0), (0, width - parts[0].shape[0]))).astype(jnp.float16)
+
+
+def extra_rows(losses, sums):
+    return jnp.concatenate([losses, sums, jnp.zeros((4, losses.shape[1]), jnp.float16)])
 
 
 def normalize(embedding):
@@ -128,9 +131,9 @@
     return pl.pallas_call(
         pair_kernel,
         out_shape=(
-            jax.ShapeDtypeStruct((1024, 1024), jnp.bfloat16),
-            jax.ShapeDtypeStruct((1024, width), jnp.bfloat16),
-            jax.ShapeDtypeStruct((1024, width), jnp.bfloat16),
+            pltpu.HBM((1024, 1024), jnp.bfloat16),
+            pltpu.HBM((1024, width), jnp.bfloat16),
+            pltpu.HBM((1024, width), jnp.bfloat16),
             jax.ShapeDtypeStruct((1024, 1), f32),
             jax.ShapeDtypeStruct((1, 1024), f32),
             jax.ShapeDtypeStruct((2, 1024), f32),
@@ -194,19 +197,17 @@
 
 
 def gather(a0, t0, core, own):
+    r1 = send(a0, split_z=1)
     r4 = send(lax.dynamic_slice_in_dim(a0, core * Q, Q, 0), dz=4)
-    r3 = send(a0, split_z=3)
     xm, xp, c0 = send(t0, dx=1), send(t0, dx=-1), send(t0, fy=3)
-    a0, t0, xm, xp, c0 = tied(a0, t0, xm, xp, c0)
+    r1, t0, xm, xp, c0 = tied(r1, t0, xm, xp, c0)
+    r3, r2 = send(r1, split_z=2), send(r1, split_z=1)
     cm, cp = send(c0, dx=1), send(c0, dx=-1)
     f1, f2 = send(xm[:Q], dx=1), send(xp[Q:], dx=-1)
-    r2 = send(a0, split_z=2)
-    a0, r3, r4, cm, cp, f1, f2, *own = tied(a0, r3, r4, cm, cp, f1, f2, *own)
+    r2, r3, r4, cm, cp, f1, f2, *own = tied(r2, r3, r4, cm, cp, f1, f2, *own)
     g1, g2 = send(cm[:Q], dx=1), send(cp[Q:], dx=-1)
-    r1 = send(a0, split_z=1)
+    met = send(jnp.concatenate([r1, r2, r3, r4], axis=0), fc=1)
     far = jnp.concatenate([f1, f2], axis=0)
-    r1, r2, g1, g2, far = tied(r1, r2, g1, g2, far)
-    met = send(jnp.concatenate([r1, r2, r3, r4], axis=0), fc=1)
     far_h = jnp.concatenate([g1, g2], axis=0)
     return [a0, r1, r2, r3, r4, met, t0, xm, xp, far, c0, cm, cp, far_h], own
 
@@ -248,7 +249,9 @@
     plane = jnp.concatenate([lt.reshape(-1), both])
     plane = plane + send(plane, fy=1)
     others = jnp.dot(weights[512:], texts, preferred_element_type=f32).astype(f16)
-    plane, others = tied(plane, others)
+    loss_rows = [parts_of(li_half[k * 128 - Q : k * 128 + Q]) for k in (3, 2, 1)]
+    loss_rows = [two_rows(parts, width) for parts in (*loss_rows, parts_of(li_half[448:]))]
+    plane, others, *loss_rows = tied(plane, others, *loss_rows)
     plane = plane + send(plane, fx=1)
     rows_met = send(others, fc=1)
     gt16 = lax.dot_general(
@@ -264,13 +267,14 @@
     text_loss = lax.dynamic_slice_in_dim(plane, ((yh * 4 + x) * 2 + yl) * Q, Q, 0)
     place = (lax.broadcasted_iota(jnp.int32, (NZ, 2), 0) == z).astype(f32)
     here = parts_of((place * plane[None, 1024:]).reshape(-1) * SUM_SCALE)
-    far = send(jnp.concatenate([flight[384:], extra_rows(parts_of(li_half[448:]), here, width)]), dz=4)
+    sum_rows = two_rows(here, width)
+    far = send(jnp.concatenate([flight[384:], extra_rows(loss_rows[3], sum_rows)]), dz=4)
     three, two, one = (
         send(
             jnp.concatenate(
                 [
                     flight[(k - 1) * 128 : k * 128],
-                    extra_rows(parts_of(li_half[k * 128 - Q : k * 128 + Q]), here, width),
+                    extra_rows(loss_rows[3 - k], sum_rows),
                 ]
             ),
             split_z=k,

time: 134 us -> 139 us (1.037)
  other arithmetic: 12 us -> 19.5 us
  waiting for transfers between devices: 41.4 us -> 38.8 us
  starting transfers between devices: 47 us -> 49.2 us
    concatenate x4 -> x2, other arithmetic: 0.22 us -> 3.22 us  [the longest x1 2.21 us: per_device(): jnp.concatenate([flight[(k - 1) * 128:k * 128], extra_rows(loss_rows[3 -...]
    unnamed x20 -> x14, local copies, waits for them, and re-layouts: 4.22 us -> 1.27 us
    ppermute x25, waiting for transfers between devices: 41.4 us -> 38.8 us  [send(): return lax.ppermute(value, AXES, pairs)]
    ppermute x25, starting transfers between devices: 42.6 us -> 44.7 us  [send(): return lax.ppermute(value, AXES, pairs)]
  transfers between devices with their start and end apart: 26 -> 26, of which waited for: 10 -> 8; matrix products, arithmetic and copies ran while one was open for 18% -> 24% of each run, Pallas kernels for 0% -> 0%
where the time goes in v4:
time: 139 us; the launch traced here: 138 us
  starting transfers between devices  49.2 us (35%)
  waiting for transfers between devices  38.8 us (28%)
  other arithmetic  19.5 us (14%)
  matrix products  13.1 us (9%)
  Pallas kernels  7.63 us (5%)
  local copies, waits for them, and re-layouts  7.14 us (5%)
  between operations  2.91 us (2%)
    ppermute x25, starting transfers between devices, send(): return lax.ppermute(value, AXES, pairs)  44.7 us
    ppermute x25, waiting for transfers between devices, send(): return lax.ppermute(value, AXES, pairs)  38.8 us
    dot_general x1, matrix products, per_device(): lax.dot_general(weights, images, (((0,), (0,)), ((), ())), preferred_elem...  6.81 us
    pallas_call x1, Pallas kernels, pairs_on_device(): pl.pallas_call(pair_kernel, out_shape=(pltpu.HBM((1024, 1024), jnp.bfloat...  6.55 us
    all_to_all x1, starting transfers between devices, per_device(): back_xy = lax.all_to_all(gt16, ('yh', 'x', 'yl'), 0, 0, tiled=True)  4.45 us
    dot_general x1, matrix products, per_device(): jnp.dot(weights[512:], texts, preferred_element_type=f32).astype(f16)  3.52 us
    dot_general x1, matrix products, per_device(): jnp.dot(weights[:512], texts, preferred_element_type=f32)  2.8 us
  transfers between devices with their start and end apart: 26, of which 8 were waited for; matrix products, arithmetic and copies ran while one was open for 24% of the time, Pallas kernels for 0%

profile of v4, /device:TPU:1, one launch (start us, length us, event | category | flops | bytes accessed | tf_op | source)
XLA Modules:
  0.0 138.2 jit_solution(16118443681507446301)
XLA Ops:
  0.7 1.1 constant_dynamic-slice_fusion.3
  1.8 0.1 fusion.4
  2.0 2.1 %collective-permute-start.1 = (bf16[128,1152]{1,0:T(8,128)(2,1)S(1)}, bf16[128,1152]{1,0:T(8,128)(2,1)S(1)}, u32[]{:S(2)}, u32[]{:S(2)}) collective-permute-start(bf16[128,1152]{1,0:T(8,128)(2,1)S(1)} %fusion.5.refs_6_), channel_id=1, source_target_pairs={{0,4},{1,5},{2,6},{3,7},{4,8},{5,9},{6,10},{7,11},{8,12},{9,13},{1... | collective-permute-start | bytes 884744 | tf_op jit(solution)/shard_map/ppermute | solution.py:32
  4.2 1.4 collective-permute-start.2
  5.5 2.8 %collective-permute-start.3 = (bf16[128,1152]{1,0:T(8,128)(2,1)S(1)}, bf16[128,1152]{1,0:T(8,128)(2,1)}, u32[]{:S(2)}, u32[]{:S(2)}) collective-permute-start(bf16[128,1152]{1,0:T(8,128)(2,1)S(1)} %fusion.5.refs_6_), channel_id=1, source_target_pairs={{0,130},{1,131},{2,128},{3,129},{4,134},{5,135},{6,132},{7,133},{8... | collective-permute-start | bytes 884744 | tf_op jit(solution)/shard_map/ppermute | solution.py:32
  8.4 1.1 fusion.2
  9.5 1.1 fusion.3.refs_0_
  10.6 5.7 %collective-permute-start = (bf16[128,1152]{1,0:T(8,128)(2,1)S(1)}, bf16[128,1152]{1,0:T(8,128)(2,1)S(1)}, u32[]{:S(2)}, u32[]{:S(2)}) collective-permute-start(bf16[128,1152]{1,0:T(8,128)(2,1)S(1)} %fusion.3.refs_0_), channel_id=1, source_target_pairs={{0,16},{1,113},{2,18},{3,115},{4,20},{5,117},{6,22},{7,119},{8,24}... | collective-permute-start | bytes 884744 | tf_op jit(solution)/shard_map/ppermute | solution.py:32
  16.2 1.5 %collective-permute-start.6 = (bf16[64,1152]{1,0:T(8,128)(2,1)S(1)}, bf16[64,1152]{1,0:T(8,128)(2,1)S(1)}, u32[]{:S(2)}, u32[]{:S(2)}) collective-permute-start(bf16[64,1152]{1,0:T(8,128)(2,1)S(1)} %constant_dynamic-slice_fusion.1), channel_id=1, source_target_pairs={{0,64},{1,65},{2,66},{3,67},{4,68},{5,69},{6,70},{7,71},{8,72},{9,... | collective-permute-start | bytes 442376 | tf_op jit(solution)/shard_map/ppermute | solution.py:32
  18.0 0.5 fusion.38
  18.5 0.5 fusion.37
  20.3 0.2 multiply_reduce_fusion
  20.6 5.6 %collective-permute-done.refs_1_ = bf16[128,1152]{1,0:T(8,128)(2,1)S(1)} collective-permute-done((bf16[128,1152]{1,0:T(8,128)(2,1)S(1)}, bf16[128,1152]{1,0:T(8,128)(2,1)S(1)}, u32[]{:S(2)}, u32[]{:S(2)}) %collective-permute-start) | collective-permute-done | bytes 294944 | tf_op jit(solution)/shard_map/ppermute | solution.py:32
  26.2 1.3 collective-permute-start.10
  27.6 0.7 multiply_reduce_fusion.1
  28.2 3.1 %collective-permute-start.4 = (bf16[128,1152]{1,0:T(8,128)(2,1)S(1)}, bf16[128,1152]{1,0:T(8,128)(2,1)S(1)}, u32[]{:S(2)}, u32[]{:S(2)}) collective-permute-start(bf16[128,1152]{1,0:T(8,128)(2,1)S(1)} %collective-permute-done.refs_1_), channel_id=1, source_target_pairs={{0,16},{1,113},{2,18},{3,115},{4,20},{5,117},{6,22},{7,119},{8,24}... | collective-permute-start | bytes 884744 | tf_op jit(solution)/shard_map/ppermute | solution.py:32
  31.4 0.2 collective-permute-start.7
  31.6 0.7 slice.76
  32.2 2.5 %collective-permute-start.8 = (bf16[128,1152]{1,0:T(8,128)(2,1)}, bf16[128,1152]{1,0:T(8,128)(2,1)S(1)}, u32[]{:S(2)}, u32[]{:S(2)}) collective-permute-start(bf16[128,1152]{1,0:T(8,128)(2,1)} %collective-permute-done.3.refs_10_), channel_id=1, source_target_pairs={{0,12},{1,13},{2,14},{3,15},{4,0},{5,1},{6,2},{7,3},{8,4},{9,5},{1... | collective-permute-start | bytes 884744 | tf_op jit(solution)/shard_map/ppermute | solution.py:32
  34.7 0.7 copy-done.2
  35.4 0.5 multiply_reduce-precision_fusion
  36.5 0.7 pad_maximum_fusion.16
  37.3 5.4 %collective-permute-done.9 = bf16[64,1152]{1,0:T(8,128)(2,1)} collective-permute-done((bf16[64,1152]{1,0:T(8,128)(2,1)}, bf16[64,1152]{1,0:T(8,128)(2,1)}, u32[]{:S(2)}, u32[]{:S(2)}) %collective-permute-start.9) | collective-permute-done | bytes 147488 | tf_op jit(solution)/shard_map/ppermute | solution.py:32
  42.9 2.8 %collective-permute-start.11 = (bf16[448,1152]{1,0:T(8,128)(2,1)S(1)}, bf16[448,1152]{1,0:T(8,128)(2,1)S(1)}, u32[]{:S(2)}, u32[]{:S(2)}) collective-permute-start(bf16[448,1152]{1,0:T(8,128)(2,1)S(1)} %pad_maximum_fusion), channel_id=1, source_target_pairs={{0,1},{1,0},{2,3},{3,2},{4,5},{5,4},{6,7},{7,6},{8,9},{9,8},{10,11... | collective-permute-start | bytes 3096584 | tf_op jit(solution)/shard_map/ppermute | solution.py:32
  45.9 2.9 %collective-permute-start.13 = (bf16[64,1152]{1,0:T(8,128)(2,1)S(1)}, bf16[64,1152]{1,0:T(8,128)(2,1)S(1)}, u32[]{:S(2)}, u32[]{:S(2)}) collective-permute-start(bf16[64,1152]{1,0:T(8,128)(2,1)S(1)} %slice.79), channel_id=1, source_target_pairs={{0,12},{1,13},{2,14},{3,15},{4,0},{5,1},{6,2},{7,3},{8,4},{9,5},{1... | collective-permute-start | bytes 442376 | tf_op jit(solution)/shard_map/ppermute | solution.py:32
  48.8 0.9 pad_maximum_fusion.9.refs_9_
  49.7 2.8 %collective-permute-done.12 = bf16[64,1152]{1,0:T(8,128)(2,1)S(1)} collective-permute-done((bf16[64,1152]{1,0:T(8,128)(2,1)S(1)}, bf16[64,1152]{1,0:T(8,128)(2,1)S(1)}, u32[]{:S(2)}, u32[]{:S(2)}) %collective-permute-start.12) | collective-permute-done | bytes 147488 | tf_op jit(solution)/shard_map/ppermute | solution.py:32
  52.6 6.6 %pairs.1 = (bf16[1024,1024]{1,0:T(8,128)(2,1)}, bf16[1024,1152]{1,0:T(8,128)(2,1)}, bf16[1024,1152]{1,0:T(8,128)(2,1)}, f32[1024,1]{1,0:T(8,128)S(1)}, f32[1,1024]{1,0:T(1,128)S(1)}, /*index=5*/f32[2,1024]{1,0:T(2,128)S(1)}) custom-call(f32[2]{0:T(128)S(1)} %pad_maximum_fusion.15.par_ref, bf16[128,1152]{1,0:T(8,128)(2,1)S(1)} %fusion.3.refs_0_, ...), custom_call_target="tpu_custom_call" | custom-call | flops 2415919104 | bytes 12582912 | tf_op jit(solution)/shard_map/pairs/pallas_call | solution.py:131
  59.1 0.2 slice_reduce_fusion
  59.5 0.9 collective-permute-start.14
  60.4 0.8 collective-permute-done.14
  61.5 3.5 %convolution_convert_fusion.1 = f16[512,1152]{1,0:T(8,128)(2,1)S(1)} fusion(bf16[1024,1152]{1,0:T(8,128)(2,1)} %get-tuple-element.72, bf16[1024,1024]{1,0:T(8,128)(2,1)} %get-tuple-element.71), kind=kOutput, calls=%fused_computation.3 | convolution fusion | flops 1208549376 | bytes 4587520 | tf_op jit(solution)/shard_map/dot_general | solution.py:251
  65.0 0.6 fusion.18
  65.6 0.6 fusion.16
  66.3 0.6 collective-permute-start.17
  66.8 0.5 iota_compare_fusion.2
  67.4 6.8 %convolution_convert_fusion = f16[1024,1152]{1,0:T(8,128)(2,1)} fusion(bf16[1024,1024]{1,0:T(8,128)(2,1)} %get-tuple-element.71, bf16[1024,1152]{1,0:T(8,128)(2,1)} %get-tuple-element.74), kind=kOutput, calls=%fused_computation.1 | convolution fusion | flops 2417098752 | bytes 6815744 | tf_op jit(solution)/shard_map/dot_general | solution.py:257
  74.2 2.8 %convolution_add_fusion = f32[512,1152]{1,0:T(8,128)S(1)} fusion(bf16[1024,1152]{1,0:T(8,128)(2,1)S(1)} %copy-done.5, f16[512,1152]{1,0:T(8,128)(2,1)} %collective-permute-done.17, bf16[1024,1024]{1,0:T(8,128)(2,1)S(1)} %copy-done.6), kind=kOutput, calls=%fused_computation.2 | convolution fusion | flops 1209139200 | bytes 6946816 | tf_op jit(solution)/shard_map/dot_general | solution.py:262
  77.0 0.9 collective-permute-start.18
  78.0 2.8 %collective-permute-done.18 = f32[1026]{0:T(1024)S(1)} collective-permute-done((f32[1026]{0:T(1024)S(1)}, f32[1026]{0:T(1024)S(1)}, u32[]{:S(2)}, u32[]{:S(2)}) %collective-permute-start.18) | collective-permute-done | bytes 4136 | tf_op jit(solution)/shard_map/ppermute | solution.py:32
  80.8 4.1 %collective-permute-start.19 = (f32[1026]{0:T(1024)S(1)}, f32[1026]{0:T(1024)}, u32[]{:S(2)}, u32[]{:S(2)}) collective-permute-start(f32[1026]{0:T(1024)S(1)} %add.157), channel_id=1, source_target_pairs={{0,8},{1,9},{2,10},{3,11},{4,12},{5,13},{6,14},{7,15},{8,0},{9,1},... | collective-permute-start | bytes 12320 | tf_op jit(solution)/shard_map/ppermute | solution.py:32
  84.9 0.9 fusion.40
  85.8 0.7 slice.94
  86.5 4.4 %all-to-all-start = ((f16[16,64,1152]{2,1,0:T(8,128)(2,1)}), f16[16,64,1152]{2,1,0:T(8,128)(2,1)}, u32[]{:S(2)}, u32[]{:S(2)}) async-start(f16[16,64,1152]{2,1,0:T(8,128)(2,1)} %bitcast.15), calls=%async_computation | async-start | bytes 4718592 | tf_op jit(solution)/shard_map/all_to_all | solution.py:266
  90.9 0.7 add.159
  91.7 0.6 copy-done.4
  92.2 0.7 select_multiply_fusion
  93.1 2.2 %pad_maximum_fusion.1 = (f16[136,1152]{1,0:T(8,128)(2,1)}, f16[136,1152]{1,0:T(8,128)(2,1)}, f16[136,1152]{1,0:T(8,128)(2,1)}) fusion(f16[4,1152]{1,0:T(4,128)(2,1)S(1)} %broadcast.94, f16[2,1152]{1,0:T(2,128)(2,1)S(1)} %pad.31, f16[2,1152]{1,0:T(2,128)(2,1)} %get-tuple-element.85, f16[128,1152]{1,0:T(8,128)(2,1)S(1)} %get-tuple-element.106, ...), kind=kLoop, calls=%fused_computation.17 | loop fusion | flops 1410048 | bytes 1852416 | tf_op jit(solution)/shard_map/concatenate | solution.py:274
  95.3 4.4 %collective-permute-start.21 = (f16[136,1152]{1,0:T(8,128)(2,1)}, f16[136,1152]{1,0:T(8,128)(2,1)}, u32[]{:S(2)}, u32[]{:S(2)}) collective-permute-start(f16[136,1152]{1,0:T(8,128)(2,1)} %get-tuple-element.116), channel_id=1, source_target_pairs={{0,48},{1,81},{2,50},{3,83},{4,52},{5,85},{6,54},{7,87},{8,56},{9,... | collective-permute-start | bytes 940040 | tf_op jit(solution)/shard_map/ppermute | solution.py:32
  99.7 1.5 %collective-permute-start.23 = (f16[136,1152]{1,0:T(8,128)(2,1)}, f16[136,1152]{1,0:T(8,128)(2,1)}, u32[]{:S(2)}, u32[]{:S(2)}) collective-permute-start(f16[136,1152]{1,0:T(8,128)(2,1)} %get-tuple-element.114), channel_id=1, source_target_pairs={{0,16},{1,113},{2,18},{3,115},{4,20},{5,117},{6,22},{7,119},{8,24}... | collective-permute-start | bytes 940040 | tf_op jit(solution)/shard_map/ppermute | solution.py:32
  101.3 1.0 pad_maximum_fusion.11
  102.3 1.2 collective-permute-start.20
  103.4 0.7 copy.12.image_inv
  104.2 0.7 copy.13.text_inv
  104.9 0.7 copy.14.weight
  105.6 11.3 %collective-permute-done.20 = f16[72,1152]{1,0:T(8,128)(2,1)} collective-permute-done((f16[72,1152]{1,0:T(8,128)(2,1)S(1)}, f16[72,1152]{1,0:T(8,128)(2,1)}, u32[]{:S(2)}, u32[]{:S(2)}) %collective-permute-start.20) | collective-permute-done | bytes 165920 | tf_op jit(solution)/shard_map/ppermute | solution.py:32
  116.9 3.0 %collective-permute-done.22 = f16[136,1152]{1,0:T(8,128)(2,1)} collective-permute-done((f16[136,1152]{1,0:T(8,128)(2,1)}, f16[136,1152]{1,0:T(8,128)(2,1)}, u32[]{:S(2)}, u32[]{:S(2)}) %collective-permute-start.22) | collective-permute-done | bytes 313376 | tf_op jit(solution)/shard_map/ppermute | solution.py:32
  119.9 6.9 %collective-permute-done.23 = f16[136,1152]{1,0:T(8,128)(2,1)} collective-permute-done((f16[136,1152]{1,0:T(8,128)(2,1)}, f16[136,1152]{1,0:T(8,128)(2,1)}, u32[]{:S(2)}, u32[]{:S(2)}) %collective-permute-start.23) | collective-permute-done | bytes 313376 | tf_op jit(solution)/shard_map/ppermute | solution.py:32
  126.8 1.3 convert_add_fusion.arrived
  128.2 4.7 %collective-permute-start.24 = (f32[72,1152]{1,0:T(8,128)S(1)}, f32[72,1152]{1,0:T(8,128)S(1)}, u32[]{:S(2)}, u32[]{:S(2)}) collective-permute-start(f32[72,1152]{1,0:T(8,128)S(1)} %pad_maximum_fusion.7), channel_id=1, source_target_pairs={{0,1},{1,0},{2,3},{3,2},{4,5},{5,4},{6,7},{7,6},{8,9},{9,8},{10,11... | collective-permute-start | bytes 995336 | tf_op jit(solution)/shard_map/ppermute | solution.py:32
  132.9 1.3 dynamic-slice_add_fusion
  134.2 0.9 convert_element_type.68.far
  135.2 2.0 %convert_reduce_fusion.gt = f32[64,1152]{1,0:T(8,128)S(1)} fusion(f16[16,64,1152]{2,1,0:T(8,128)(2,1)} %all-to-all-done), kind=kLoop, calls=%fused_computation | loop fusion | flops 2285568 | bytes 2654208 | tf_op jit(solution)/shard_map/reduce_sum | solution.py:288
  137.2 1.1 finish.1
  (71 shorter events, 1.6 us)
Async XLA Ops:
  0.6 17.1 %copy-start.1 = (bf16[256,1152]{1,0:T(8,128)(2,1)S(1)}, bf16[256,1152]{1,0:T(8,128)(2,1)}, u32[]{:S(2)}) copy-start(bf16[256,1152]{1,0:T(8,128)(2,1)} %param.5) | copy-start | bytes 1769476
  0.6 17.2 %copy-start = (bf16[256,1152]{1,0:T(8,128)(2,1)S(1)}, bf16[256,1152]{1,0:T(8,128)(2,1)}, u32[]{:S(2)}) copy-start(bf16[256,1152]{1,0:T(8,128)(2,1)} %param.4) | copy-start | bytes 1769476
  2.0 18.5 %collective-permute-start.1 = (bf16[128,1152]{1,0:T(8,128)(2,1)S(1)}, bf16[128,1152]{1,0:T(8,128)(2,1)S(1)}, u32[]{:S(2)}, u32[]{:S(2)}) collective-permute-start(bf16[128,1152]{1,0:T(8,128)(2,1)S(1)} %fusion.5.refs_6_), channel_id=1, source_target_pairs={{0,4},{1,5},{2,6},{3,7},{4,8},{5,9},{6,10},{7,11},{8,12},{9,13},{1... | collective-permute-start | bytes 884744 | tf_op jit(solution)/shard_map/ppermute | solution.py:32
  4.2 16.4 %collective-permute-start.2 = (bf16[128,1152]{1,0:T(8,128)(2,1)S(1)}, bf16[128,1152]{1,0:T(8,128)(2,1)S(1)}, u32[]{:S(2)}, u32[]{:S(2)}) collective-permute-start(bf16[128,1152]{1,0:T(8,128)(2,1)S(1)} %fusion.5.refs_6_), channel_id=1, source_target_pairs={{0,12},{1,13},{2,14},{3,15},{4,0},{5,1},{6,2},{7,3},{8,4},{9,5},{1... | collective-permute-start | bytes 884744 | tf_op jit(solution)/shard_map/ppermute | solution.py:32
  5.5 15.1 %collective-permute-start.3 = (bf16[128,1152]{1,0:T(8,128)(2,1)S(1)}, bf16[128,1152]{1,0:T(8,128)(2,1)}, u32[]{:S(2)}, u32[]{:S(2)}) collective-permute-start(bf16[128,1152]{1,0:T(8,128)(2,1)S(1)} %fusion.5.refs_6_), channel_id=1, source_target_pairs={{0,130},{1,131},{2,128},{3,129},{4,134},{5,135},{6,132},{7,133},{8... | collective-permute-start | bytes 884744 | tf_op jit(solution)/shard_map/ppermute | solution.py:32
  10.6 15.6 %collective-permute-start = (bf16[128,1152]{1,0:T(8,128)(2,1)S(1)}, bf16[128,1152]{1,0:T(8,128)(2,1)S(1)}, u32[]{:S(2)}, u32[]{:S(2)}) collective-permute-start(bf16[128,1152]{1,0:T(8,128)(2,1)S(1)} %fusion.3.refs_0_), channel_id=1, source_target_pairs={{0,16},{1,113},{2,18},{3,115},{4,20},{5,117},{6,22},{7,119},{8,24}... | collective-permute-start | bytes 884744 | tf_op jit(solution)/shard_map/ppermute | solution.py:32
  16.2 16.0 %collective-permute-start.6 = (bf16[64,1152]{1,0:T(8,128)(2,1)S(1)}, bf16[64,1152]{1,0:T(8,128)(2,1)S(1)}, u32[]{:S(2)}, u32[]{:S(2)}) collective-permute-start(bf16[64,1152]{1,0:T(8,128)(2,1)S(1)} %constant_dynamic-slice_fusion.1), channel_id=1, source_target_pairs={{0,64},{1,65},{2,66},{3,67},{4,68},{5,69},{6,70},{7,71},{8,72},{9,... | collective-permute-start | bytes 442376 | tf_op jit(solution)/shard_map/ppermute | solution.py:32
  26.2 8.5 %collective-permute-start.10 = (bf16[64,1152]{1,0:T(8,128)(2,1)S(1)}, bf16[64,1152]{1,0:T(8,128)(2,1)S(1)}, u32[]{:S(2)}, u32[]{:S(2)}) collective-permute-start(bf16[64,1152]{1,0:T(8,128)(2,1)S(1)} %slice.77), channel_id=1, source_target_pairs={{0,12},{1,13},{2,14},{3,15},{4,0},{5,1},{6,2},{7,3},{8,4},{9,5},{1... | collective-permute-start | bytes 442376 | tf_op jit(solution)/shard_map/ppermute | solution.py:32
  28.2 14.5 %collective-permute-start.4 = (bf16[128,1152]{1,0:T(8,128)(2,1)S(1)}, bf16[128,1152]{1,0:T(8,128)(2,1)S(1)}, u32[]{:S(2)}, u32[]{:S(2)}) collective-permute-start(bf16[128,1152]{1,0:T(8,128)(2,1)S(1)} %collective-permute-done.refs_1_), channel_id=1, source_target_pairs={{0,16},{1,113},{2,18},{3,115},{4,20},{5,117},{6,22},{7,119},{8,24}... | collective-permute-start | bytes 884744 | tf_op jit(solution)/shard_map/ppermute | solution.py:32
  31.4 11.4 %collective-permute-start.5 = (bf16[128,1152]{1,0:T(8,128)(2,1)S(1)}, bf16[128,1152]{1,0:T(8,128)(2,1)S(1)}, u32[]{:S(2)}, u32[]{:S(2)}) collective-permute-start(bf16[128,1152]{1,0:T(8,128)(2,1)S(1)} %collective-permute-done.refs_1_), channel_id=1, source_target_pairs={{0,32},{1,97},{2,34},{3,99},{4,36},{5,101},{6,38},{7,103},{8,40},{... | collective-permute-start | bytes 884744 | tf_op jit(solution)/shard_map/ppermute | solution.py:32
  31.4 11.4 %collective-permute-start.7 = (bf16[128,1152]{1,0:T(8,128)(2,1)}, bf16[128,1152]{1,0:T(8,128)(2,1)S(1)}, u32[]{:S(2)}, u32[]{:S(2)}) collective-permute-start(bf16[128,1152]{1,0:T(8,128)(2,1)} %collective-permute-done.3.refs_10_), channel_id=1, source_target_pairs={{0,4},{1,5},{2,6},{3,7},{4,8},{5,9},{6,10},{7,11},{8,12},{9,13},{1... | collective-permute-start | bytes 884744 | tf_op jit(solution)/shard_map/ppermute | solution.py:32
  32.2 10.5 %collective-permute-start.8 = (bf16[128,1152]{1,0:T(8,128)(2,1)}, bf16[128,1152]{1,0:T(8,128)(2,1)S(1)}, u32[]{:S(2)}, u32[]{:S(2)}) collective-permute-start(bf16[128,1152]{1,0:T(8,128)(2,1)} %collective-permute-done.3.refs_10_), channel_id=1, source_target_pairs={{0,12},{1,13},{2,14},{3,15},{4,0},{5,1},{6,2},{7,3},{8,4},{9,5},{1... | collective-permute-start | bytes 884744 | tf_op jit(solution)/shard_map/ppermute | solution.py:32
  34.7 0.7 copy-start.2
  35.4 7.4 %collective-permute-start.9 = (bf16[64,1152]{1,0:T(8,128)(2,1)}, bf16[64,1152]{1,0:T(8,128)(2,1)}, u32[]{:S(2)}, u32[]{:S(2)}) collective-permute-start(bf16[64,1152]{1,0:T(8,128)(2,1)} %slice.76), channel_id=1, source_target_pairs={{0,4},{1,5},{2,6},{3,7},{4,8},{5,9},{6,10},{7,11},{8,12},{9,13},{1... | collective-permute-start | bytes 442376 | tf_op jit(solution)/shard_map/ppermute | solution.py:32
  35.4 13.4 %copy-start.3 = (bf16[64,1152]{1,0:T(8,128)(2,1)S(1)}, bf16[64,1152]{1,0:T(8,128)(2,1)}, u32[]{:S(2)}) copy-start(bf16[64,1152]{1,0:T(8,128)(2,1)} %copy-done.2) | copy-start | bytes 442372
  42.9 9.7 %collective-permute-start.11 = (bf16[448,1152]{1,0:T(8,128)(2,1)S(1)}, bf16[448,1152]{1,0:T(8,128)(2,1)S(1)}, u32[]{:S(2)}, u32[]{:S(2)}) collective-permute-start(bf16[448,1152]{1,0:T(8,128)(2,1)S(1)} %pad_maximum_fusion), channel_id=1, source_target_pairs={{0,1},{1,0},{2,3},{3,2},{4,5},{5,4},{6,7},{7,6},{8,9},{9,8},{10,11... | collective-permute-start | bytes 3096584 | tf_op jit(solution)/shard_map/ppermute | solution.py:32
  45.8 6.8 %collective-permute-start.12 = (bf16[64,1152]{1,0:T(8,128)(2,1)S(1)}, bf16[64,1152]{1,0:T(8,128)(2,1)S(1)}, u32[]{:S(2)}, u32[]{:S(2)}) collective-permute-start(bf16[64,1152]{1,0:T(8,128)(2,1)S(1)} %slice.78), channel_id=1, source_target_pairs={{0,4},{1,5},{2,6},{3,7},{4,8},{5,9},{6,10},{7,11},{8,12},{9,13},{1... | collective-permute-start | bytes 442376 | tf_op jit(solution)/shard_map/ppermute | solution.py:32
  45.9 6.6 %collective-permute-start.13 = (bf16[64,1152]{1,0:T(8,128)(2,1)S(1)}, bf16[64,1152]{1,0:T(8,128)(2,1)S(1)}, u32[]{:S(2)}, u32[]{:S(2)}) collective-permute-start(bf16[64,1152]{1,0:T(8,128)(2,1)S(1)} %slice.79), channel_id=1, source_target_pairs={{0,12},{1,13},{2,14},{3,15},{4,0},{5,1},{6,2},{7,3},{8,4},{9,5},{1... | collective-permute-start | bytes 442376 | tf_op jit(solution)/shard_map/ppermute | solution.py:32
  59.5 1.7 %collective-permute-start.14 = (f32[514]{0:T(1024)S(1)}, f32[514]{0:T(1024)S(1)}, u32[]{:S(2)}, u32[]{:S(2)}) collective-permute-start(f32[514]{0:T(1024)S(1)} %pad_maximum_fusion.13), channel_id=1, source_target_pairs={{0,1},{1,0},{2,3},{3,2},{4,5},{5,4},{6,7},{7,6},{8,9},{9,8},{10,11... | collective-permute-start | bytes 6176 | tf_op jit(solution)/shard_map/ppermute | solution.py:32
  61.4 4.9 %collective-permute-start.15 = (f32[1026]{0:T(1024)S(1)}, f32[1026]{0:T(1024)S(1)}, u32[]{:S(2)}, u32[]{:S(2)}) collective-permute-start(f32[1026]{0:T(1024)S(1)} %pad_maximum_fusion.12), channel_id=1, source_target_pairs={{0,2},{1,3},{2,0},{3,1},{4,6},{5,7},{6,4},{7,5},{8,10},{9,11},{10,... | collective-permute-start | bytes 12320 | tf_op jit(solution)/shard_map/ppermute | solution.py:32
  66.3 7.9 %collective-permute-start.17 = (f16[512,1152]{1,0:T(8,128)(2,1)S(1)}, f16[512,1152]{1,0:T(8,128)(2,1)}, u32[]{:S(2)}, u32[]{:S(2)}) collective-permute-start(f16[512,1152]{1,0:T(8,128)(2,1)S(1)} %convolution_convert_fusion.1), channel_id=1, source_target_pairs={{0,1},{1,0},{2,3},{3,2},{4,5},{5,4},{6,7},{7,6},{8,9},{9,8},{10,11... | collective-permute-start | bytes 3538952 | tf_op jit(solution)/shard_map/ppermute | solution.py:32
  67.3 6.8 %collective-permute-start.16 = (f32[1026]{0:T(1024)S(1)}, f32[1026]{0:T(1024)S(1)}, u32[]{:S(2)}, u32[]{:S(2)}) collective-permute-start(f32[1026]{0:T(1024)S(1)} %fusion.36), channel_id=1, source_target_pairs={{0,4},{1,5},{2,6},{3,7},{4,0},{5,1},{6,2},{7,3},{8,12},{9,13},{10,... | collective-permute-start | bytes 12320 | tf_op jit(solution)/shard_map/ppermute | solution.py:32
  67.3 6.8 %copy-start.5 = (bf16[1024,1152]{1,0:T(8,128)(2,1)S(1)}, bf16[1024,1152]{1,0:T(8,128)(2,1)}, u32[]{:S(2)}) copy-start(bf16[1024,1152]{1,0:T(8,128)(2,1)} %get-tuple-element.72) | copy-start | bytes 7077892
  67.3 6.8 %copy-start.6 = (bf16[1024,1024]{1,0:T(8,128)(2,1)S(1)}, bf16[1024,1024]{1,0:T(8,128)(2,1)}, u32[]{:S(2)}) copy-start(bf16[1024,1024]{1,0:T(8,128)(2,1)} %get-tuple-element.71) | copy-start | bytes 6291460
  77.0 3.8 %collective-permute-start.18 = (f32[1026]{0:T(1024)S(1)}, f32[1026]{0:T(1024)S(1)}, u32[]{:S(2)}, u32[]{:S(2)}) collective-permute-start(f32[1026]{0:T(1024)S(1)} %add.156), channel_id=1, source_target_pairs={{0,130},{1,131},{2,128},{3,129},{4,134},{5,135},{6,132},{7,133},{8... | collective-permute-start | bytes 12320 | tf_op jit(solution)/shard_map/ppermute | solution.py:32
  80.8 10.1 %collective-permute-start.19 = (f32[1026]{0:T(1024)S(1)}, f32[1026]{0:T(1024)}, u32[]{:S(2)}, u32[]{:S(2)}) collective-permute-start(f32[1026]{0:T(1024)S(1)} %add.157), channel_id=1, source_target_pairs={{0,8},{1,9},{2,10},{3,11},{4,12},{5,13},{6,14},{7,15},{8,0},{9,1},... | collective-permute-start | bytes 12320 | tf_op jit(solution)/shard_map/ppermute | solution.py:32
  86.5 48.7 %all-to-all-start = ((f16[16,64,1152]{2,1,0:T(8,128)(2,1)}), f16[16,64,1152]{2,1,0:T(8,128)(2,1)}, u32[]{:S(2)}, u32[]{:S(2)}) async-start(f16[16,64,1152]{2,1,0:T(8,128)(2,1)} %bitcast.15), calls=%async_computation | async-start | bytes 4718592 | tf_op jit(solution)/shard_map/all_to_all | solution.py:266
  91.6 0.6 copy-start.4
  95.3 21.6 %collective-permute-start.21 = (f16[136,1152]{1,0:T(8,128)(2,1)}, f16[136,1152]{1,0:T(8,128)(2,1)}, u32[]{:S(2)}, u32[]{:S(2)}) collective-permute-start(f16[136,1152]{1,0:T(8,128)(2,1)} %get-tuple-element.116), channel_id=1, source_target_pairs={{0,48},{1,81},{2,50},{3,83},{4,52},{5,85},{6,54},{7,87},{8,56},{9,... | collective-permute-start | bytes 940040 | tf_op jit(solution)/shard_map/ppermute | solution.py:32
  99.7 20.2 %collective-permute-start.22 = (f16[136,1152]{1,0:T(8,128)(2,1)}, f16[136,1152]{1,0:T(8,128)(2,1)}, u32[]{:S(2)}, u32[]{:S(2)}) collective-permute-start(f16[136,1152]{1,0:T(8,128)(2,1)} %get-tuple-element.115), channel_id=1, source_target_pairs={{0,32},{1,97},{2,34},{3,99},{4,36},{5,101},{6,38},{7,103},{8,40},{... | collective-permute-start | bytes 940040 | tf_op jit(solution)/shard_map/ppermute | solution.py:32
  99.7 27.1 %collective-permute-start.23 = (f16[136,1152]{1,0:T(8,128)(2,1)}, f16[136,1152]{1,0:T(8,128)(2,1)}, u32[]{:S(2)}, u32[]{:S(2)}) collective-permute-start(f16[136,1152]{1,0:T(8,128)(2,1)} %get-tuple-element.114), channel_id=1, source_target_pairs={{0,16},{1,113},{2,18},{3,115},{4,20},{5,117},{6,22},{7,119},{8,24}... | collective-permute-start | bytes 940040 | tf_op jit(solution)/shard_map/ppermute | solution.py:32
  102.3 14.6 %collective-permute-start.20 = (f16[72,1152]{1,0:T(8,128)(2,1)S(1)}, f16[72,1152]{1,0:T(8,128)(2,1)}, u32[]{:S(2)}, u32[]{:S(2)}) collective-permute-start(f16[72,1152]{1,0:T(8,128)(2,1)S(1)} %pad_maximum_fusion.11), channel_id=1, source_target_pairs={{0,64},{1,65},{2,66},{3,67},{4,68},{5,69},{6,70},{7,71},{8,72},{9,... | collective-permute-start | bytes 497672 | tf_op jit(solution)/shard_map/ppermute | solution.py:32
  128.2 9.0 %collective-permute-start.24 = (f32[72,1152]{1,0:T(8,128)S(1)}, f32[72,1152]{1,0:T(8,128)S(1)}, u32[]{:S(2)}, u32[]{:S(2)}) collective-permute-start(f32[72,1152]{1,0:T(8,128)S(1)} %pad_maximum_fusion.7), channel_id=1, source_target_pairs={{0,1},{1,0},{2,3},{3,2},{4,5},{5,4},{6,7},{7,6},{8,9},{9,8},{10,11... | collective-permute-start | bytes 995336 | tf_op jit(solution)/shard_map/ppermute | solution.py:32

commit v5 on v4

--- a/solution.py
+++ b/solution.py
@@ -36,20 +36,14 @@
     return lax.reduce_precision(value, 8, 7)
 
 
-SUM_SCALE = 2.0**-14
-
-
 def parts_of(values):
     high = lax.reduce_precision(values, 5, 10)
     return high, lax.reduce_precision(values - high, 5, 10)
 
 
-def two_rows(parts, width):
-    return jnp.pad(jnp.stack(parts), ((0, 0), (0, width - parts[0].shape[0]))).astype(jnp.float16)
-
-
-def extra_rows(losses, sums):
-    return jnp.concatenate([losses, sums, jnp.zeros((4, losses.shape[1]), jnp.float16)])
+def extra_rows(parts, width):
+    rows = jnp.stack(parts)
+    return jnp.pad(rows, ((0, 6), (0, width - rows.shape[1]))).astype(jnp.float16)
 
 
 def normalize(embedding):
@@ -155,7 +149,7 @@
 
 
 def finish_kernel(
-    half, far, arrived, met, gt, image_unit, text_unit, image_inv, text_inv, weight, loss, here, gi_out, gt_out, loss_out, both_out
+    half, far, arrived, met, gt, image_unit, text_unit, image_inv, text_inv, weight, loss, gi_out, gt_out, loss_out
 ):
     core = lax.axis_index("core")
     own = arrived[pl.ds(pl.multiple_of(core * Q, Q), Q), :]
@@ -168,12 +162,6 @@
     near = arrived[128:130, 0:128] + met[Q : Q + 2, 0:128]
     near = jnp.where(core == 0, near[:, :Q], near[:, Q:]) + far[Q : Q + 2, 0:Q]
     loss_out[...] = loss[...] + near[0:1] + near[1:2]
-    sums = arrived[130:132, 0:128] + met[Q + 2 : Q + 4, 0:128] + far[Q + 2 : Q + 4, 0:128] + here[...]
-    sums = sums[0:1] + sums[1:2]
-    total = sums[:, 0:2]
-    for k in range(1, NZ):
-        total = total + sums[:, 2 * k : 2 * k + 2]
-    both_out[...] = total * (1.0 / SUM_SCALE)
 
 
 def finish(*args):
@@ -185,7 +173,6 @@
             shape,
             shape,
             jax.ShapeDtypeStruct((1, Q), jnp.float32),
-            jax.ShapeDtypeStruct((1, 2), jnp.float32),
         ),
         compiler_params=pltpu.CompilerParams(vmem_limit_bytes=12 * 1024 * 1024),
         name="finish",
@@ -246,52 +233,41 @@
     met = send(jnp.concatenate([li[512:], both]), fc=1)
     met, weights = tied(met, weights)
     li_half, both = li[:512] + met[:512], both + met[512:]
-    plane = jnp.concatenate([lt.reshape(-1), both])
-    plane = plane + send(plane, fy=1)
+    both = both + send(both, fz=1)
     others = jnp.dot(weights[512:], texts, preferred_element_type=f32).astype(f16)
-    loss_rows = [parts_of(li_half[k * 128 - Q : k * 128 + Q]) for k in (3, 2, 1)]
-    loss_rows = [two_rows(parts, width) for parts in (*loss_rows, parts_of(li_half[448:]))]
-    plane, others, *loss_rows = tied(plane, others, *loss_rows)
-    plane = plane + send(plane, fx=1)
+    loss_rows = [parts_of(li_half[k * 128 - Q : k * 128 + Q]) for k in (1, 2, 3)]
+    loss_rows = [extra_rows(parts, width) for parts in (*loss_rows, parts_of(li_half[448:]))]
+    both, others, *loss_rows = tied(both, others, *loss_rows)
+    both = both + send(both, fz=2)
     rows_met = send(others, fc=1)
     gt16 = lax.dot_general(
         weights, images, (((0,), (0,)), ((), ())), preferred_element_type=f32
     ).astype(f16)
-    plane, gt16, rows_met = tied(plane, gt16, rows_met)
-    plane = plane + send(plane, fy=3)
+    both, gt16, rows_met = tied(both, gt16, rows_met)
+    back_xy = lax.all_to_all(gt16, ("yh", "x", "yl"), 0, 0, tiled=True)
+    both = both + send(both, fz=4)
     half = jnp.dot(weights[:512], texts, preferred_element_type=f32) + rows_met.astype(f32)
     flight = half[Q:].astype(f16)
-    plane, gt16, half, flight = tied(plane, gt16, half, flight)
-    plane = plane + send(plane, fx=2)
-    back_xy = lax.all_to_all(gt16, ("yh", "x", "yl"), 0, 0, tiled=True)
-    text_loss = lax.dynamic_slice_in_dim(plane, ((yh * 4 + x) * 2 + yl) * Q, Q, 0)
-    place = (lax.broadcasted_iota(jnp.int32, (NZ, 2), 0) == z).astype(f32)
-    here = parts_of((place * plane[None, 1024:]).reshape(-1) * SUM_SCALE)
-    sum_rows = two_rows(here, width)
-    far = send(jnp.concatenate([flight[384:], extra_rows(loss_rows[3], sum_rows)]), dz=4)
+    both, half, flight = tied(both, half, flight)
+    far = send(jnp.concatenate([flight[384:], loss_rows[3]]), dz=4)
     three, two, one = (
-        send(
-            jnp.concatenate(
-                [
-                    flight[(k - 1) * 128 : k * 128],
-                    extra_rows(loss_rows[3 - k], sum_rows),
-                ]
-            ),
-            split_z=k,
-        )
-        for k in (3, 2, 1)
+        send(jnp.concatenate([flight[(k - 1) * 128 : k * 128], loss_rows[k - 1]]), split_z=k) for k in (3, 2, 1)
     )
     far, three, two, one = tied(far, three, two, one)
     arrived = one.astype(f32) + two.astype(f32) + three.astype(f32)
     theirs = jnp.concatenate([lax.dynamic_slice_in_dim(arrived, (1 - core) * Q, Q, 0), arrived[128:]])
     met = send(theirs, fc=1)
     gt_own = jnp.sum(back_xy.reshape(16, Q, -1).astype(f32), axis=0)
-    here_row = jnp.pad(jnp.stack(here), ((0, 0), (0, 128 - 2 * NZ)))
-    grad_image, grad_text, image_loss, both = finish(
+    grad_image, grad_text, image_loss = finish(
         half[:Q], far.astype(f32), arrived, met, gt_own, image_unit, text_unit, image_inv, text_inv,
-        match_weight[:, None], (li_half[:Q] + match_loss)[None], here_row,
-    )
-    image_loss, both, text_loss = image_loss.reshape(Q), both.reshape(2), text_loss + match_loss
+        match_weight[:, None], (li_half[:Q] + match_loss)[None],
+    )
+    lt, both, _ = tied(lt, both, back_xy)
+    plane = jnp.concatenate([lt.reshape(-1), both])
+    for move in (dict(fy=1), dict(fx=1), dict(fy=3), dict(fx=2)):
+        plane = plane + send(plane, **move)
+    text_loss = lax.dynamic_slice_in_dim(plane, ((yh * 4 + x) * 2 + yl) * Q, Q, 0) + match_loss
+    image_loss, both = image_loss.reshape(Q), plane[1024:]
     return (grad_image, grad_text, image_loss, text_loss, both)
 
 

time: 139 us -> 133 us (0.957)
  starting transfers between devices: 49.2 us -> 63.4 us
  other arithmetic: 19.5 us -> 10.1 us
  waiting for transfers between devices: 38.8 us -> 32 us
  matrix products: 13.1 us -> 9.44 us
    ppermute x25 -> x28, starting transfers between devices: 44.7 us -> 58.8 us  [send(): return lax.ppermute(value, AXES, pairs)]
    ppermute x25 -> x28, waiting for transfers between devices: 38.8 us -> 32 us  [send(): return lax.ppermute(value, AXES, pairs)]
    concatenate x2 -> x4, other arithmetic: 3.22 us -> 0.27 us  [the longest x3 0.23 us: per_device(): jnp.concatenate([flight[(k - 1) * 128:k * 128], loss_rows[k - 1]])]
    dot_general x1, matrix products: 6.81 us -> 4.24 us  [per_device(): lax.dot_general(weights, images, (((0,), (0,)), ((), ())), preferred_elem...]
  transfers between devices with their start and end apart: 26 -> 29, of which waited for: 8 -> 9; matrix products, arithmetic and copies ran while one was open for 24% -> 15% of each run, Pallas kernels for 0% -> 0%
where the time goes in v5:
time: 133 us; the launch traced here: 132 us
  starting transfers between devices  63.4 us (48%)
  waiting for transfers between devices  32 us (24%)
  other arithmetic  10.1 us (8%)
  matrix products  9.44 us (7%)
  Pallas kernels  7.58 us (6%)
  local copies, waits for them, and re-layouts  6.17 us (5%)
  between operations  3.03 us (2%)
    ppermute x28, starting transfers between devices, send(): return lax.ppermute(value, AXES, pairs)  58.8 us
    ppermute x28, waiting for transfers between devices, send(): return lax.ppermute(value, AXES, pairs)  32 us
    pallas_call x1, Pallas kernels, pairs_on_device(): pl.pallas_call(pair_kernel, out_shape=(pltpu.HBM((1024, 1024), jnp.bfloat...  6.51 us
    all_to_all x1, starting transfers between devices, per_device(): back_xy = lax.all_to_all(gt16, ('yh', 'x', 'yl'), 0, 0, tiled=True)  4.67 us
    dot_general x1, matrix products, per_device(): lax.dot_general(weights, images, (((0,), (0,)), ((), ())), preferred_elem...  4.24 us
    dot_general x1, matrix products, per_device(): jnp.dot(weights[512:], texts, preferred_element_type=f32).astype(f16)  3.65 us
  transfers between devices with their start and end apart: 29, of which 9 were waited for; matrix products, arithmetic and copies ran while one was open for 15% of the time, Pallas kernels for 0%

profile of v5, /device:TPU:1, one launch (start us, length us, event | category | flops | bytes accessed | tf_op | source)
XLA Modules:
  0.0 131.8 jit_solution(12089624572202133164)
XLA Ops:
  0.7 1.1 constant_dynamic-slice_fusion.3
  1.8 0.1 fusion.4
  1.9 0.1 fusion.5.refs_6_
  2.0 2.1 %collective-permute-start.1 = (bf16[128,1152]{1,0:T(8,128)(2,1)S(1)}, bf16[128,1152]{1,0:T(8,128)(2,1)S(1)}, u32[]{:S(2)}, u32[]{:S(2)}) collective-permute-start(bf16[128,1152]{1,0:T(8,128)(2,1)S(1)} %fusion.5.refs_6_), channel_id=1, source_target_pairs={{0,4},{1,5},{2,6},{3,7},{4,8},{5,9},{6,10},{7,11},{8,12},{9,13},{1... | collective-permute-start | bytes 884744 | tf_op jit(solution)/shard_map/ppermute | solution.py:32
  4.2 1.4 %collective-permute-start.2 = (bf16[128,1152]{1,0:T(8,128)(2,1)S(1)}, bf16[128,1152]{1,0:T(8,128)(2,1)S(1)}, u32[]{:S(2)}, u32[]{:S(2)}) collective-permute-start(bf16[128,1152]{1,0:T(8,128)(2,1)S(1)} %fusion.5.refs_6_), channel_id=1, source_target_pairs={{0,12},{1,13},{2,14},{3,15},{4,0},{5,1},{6,2},{7,3},{8,4},{9,5},{1... | collective-permute-start | bytes 884744 | tf_op jit(solution)/shard_map/ppermute | solution.py:32
  5.5 2.8 %collective-permute-start.3 = (bf16[128,1152]{1,0:T(8,128)(2,1)S(1)}, bf16[128,1152]{1,0:T(8,128)(2,1)}, u32[]{:S(2)}, u32[]{:S(2)}) collective-permute-start(bf16[128,1152]{1,0:T(8,128)(2,1)S(1)} %fusion.5.refs_6_), channel_id=1, source_target_pairs={{0,130},{1,131},{2,128},{3,129},{4,134},{5,135},{6,132},{7,133},{8... | collective-permute-start | bytes 884744 | tf_op jit(solution)/shard_map/ppermute | solution.py:32
  8.4 1.1 fusion.2
  9.5 1.1 fusion.3.refs_0_
  10.6 5.7 %collective-permute-start = (bf16[128,1152]{1,0:T(8,128)(2,1)S(1)}, bf16[128,1152]{1,0:T(8,128)(2,1)S(1)}, u32[]{:S(2)}, u32[]{:S(2)}) collective-permute-start(bf16[128,1152]{1,0:T(8,128)(2,1)S(1)} %fusion.3.refs_0_), channel_id=1, source_target_pairs={{0,16},{1,113},{2,18},{3,115},{4,20},{5,117},{6,22},{7,119},{8,24}... | collective-permute-start | bytes 884744 | tf_op jit(solution)/shard_map/ppermute | solution.py:32
  16.2 1.5 %collective-permute-start.6 = (bf16[64,1152]{1,0:T(8,128)(2,1)S(1)}, bf16[64,1152]{1,0:T(8,128)(2,1)S(1)}, u32[]{:S(2)}, u32[]{:S(2)}) collective-permute-start(bf16[64,1152]{1,0:T(8,128)(2,1)S(1)} %constant_dynamic-slice_fusion.1), channel_id=1, source_target_pairs={{0,64},{1,65},{2,66},{3,67},{4,68},{5,69},{6,70},{7,71},{8,72},{9,... | collective-permute-start | bytes 442376 | tf_op jit(solution)/shard_map/ppermute | solution.py:32
  17.7 0.1 fusion.7
  17.8 0.1 fusion.6
  19.3 0.2 multiply_reduce_fusion
  19.6 6.6 %collective-permute-done.refs_1_ = bf16[128,1152]{1,0:T(8,128)(2,1)S(1)} collective-permute-done((bf16[128,1152]{1,0:T(8,128)(2,1)S(1)}, bf16[128,1152]{1,0:T(8,128)(2,1)S(1)}, u32[]{:S(2)}, u32[]{:S(2)}) %collective-permute-start) | collective-permute-done | bytes 294944 | tf_op jit(solution)/shard_map/ppermute | solution.py:32
  26.2 1.3 %collective-permute-start.10 = (bf16[64,1152]{1,0:T(8,128)(2,1)S(1)}, bf16[64,1152]{1,0:T(8,128)(2,1)S(1)}, u32[]{:S(2)}, u32[]{:S(2)}) collective-permute-start(bf16[64,1152]{1,0:T(8,128)(2,1)S(1)} %slice.77), channel_id=1, source_target_pairs={{0,12},{1,13},{2,14},{3,15},{4,0},{5,1},{6,2},{7,3},{8,4},{9,5},{1... | collective-permute-start | bytes 442376 | tf_op jit(solution)/shard_map/ppermute | solution.py:32
  27.6 0.6 multiply_reduce_fusion.1
  28.2 3.4 %collective-permute-start.4 = (bf16[128,1152]{1,0:T(8,128)(2,1)S(1)}, bf16[128,1152]{1,0:T(8,128)(2,1)S(1)}, u32[]{:S(2)}, u32[]{:S(2)}) collective-permute-start(bf16[128,1152]{1,0:T(8,128)(2,1)S(1)} %collective-permute-done.refs_1_), channel_id=1, source_target_pairs={{0,16},{1,113},{2,18},{3,115},{4,20},{5,117},{6,22},{7,119},{8,24}... | collective-permute-start | bytes 884744 | tf_op jit(solution)/shard_map/ppermute | solution.py:32
  31.6 0.7 slice.76
  32.3 2.7 %collective-permute-start.8 = (bf16[128,1152]{1,0:T(8,128)(2,1)}, bf16[128,1152]{1,0:T(8,128)(2,1)S(1)}, u32[]{:S(2)}, u32[]{:S(2)}) collective-permute-start(bf16[128,1152]{1,0:T(8,128)(2,1)} %collective-permute-done.3.refs_10_), channel_id=1, source_target_pairs={{0,12},{1,13},{2,14},{3,15},{4,0},{5,1},{6,2},{7,3},{8,4},{9,5},{1... | collective-permute-start | bytes 884744 | tf_op jit(solution)/shard_map/ppermute | solution.py:32
  35.0 0.7 copy-done.3
  35.6 0.6 multiply_reduce-precision_fusion
  36.9 1.3 pad_maximum_fusion.12
  38.2 4.9 %collective-permute-done.9 = bf16[64,1152]{1,0:T(8,128)(2,1)} collective-permute-done((bf16[64,1152]{1,0:T(8,128)(2,1)}, bf16[64,1152]{1,0:T(8,128)(2,1)}, u32[]{:S(2)}, u32[]{:S(2)}) %collective-permute-start.9) | collective-permute-done | bytes 147488 | tf_op jit(solution)/shard_map/ppermute | solution.py:32
  43.1 2.8 %collective-permute-start.11 = (bf16[448,1152]{1,0:T(8,128)(2,1)S(1)}, bf16[448,1152]{1,0:T(8,128)(2,1)S(1)}, u32[]{:S(2)}, u32[]{:S(2)}) collective-permute-start(bf16[448,1152]{1,0:T(8,128)(2,1)S(1)} %pad_maximum_fusion), channel_id=1, source_target_pairs={{0,1},{1,0},{2,3},{3,2},{4,5},{5,4},{6,7},{7,6},{8,9},{9,8},{10,11... | collective-permute-start | bytes 3096584 | tf_op jit(solution)/shard_map/ppermute | solution.py:32
  46.1 2.9 %collective-permute-start.13 = (bf16[64,1152]{1,0:T(8,128)(2,1)S(1)}, bf16[64,1152]{1,0:T(8,128)(2,1)S(1)}, u32[]{:S(2)}, u32[]{:S(2)}) collective-permute-start(bf16[64,1152]{1,0:T(8,128)(2,1)S(1)} %slice.79), channel_id=1, source_target_pairs={{0,12},{1,13},{2,14},{3,15},{4,0},{5,1},{6,2},{7,3},{8,4},{9,5},{1... | collective-permute-start | bytes 442376 | tf_op jit(solution)/shard_map/ppermute | solution.py:32
  49.1 0.9 pad_maximum_fusion.6.refs_9_
  50.0 2.8 %collective-permute-done.12 = bf16[64,1152]{1,0:T(8,128)(2,1)S(1)} collective-permute-done((bf16[64,1152]{1,0:T(8,128)(2,1)S(1)}, bf16[64,1152]{1,0:T(8,128)(2,1)S(1)}, u32[]{:S(2)}, u32[]{:S(2)}) %collective-permute-start.12) | collective-permute-done | bytes 147488 | tf_op jit(solution)/shard_map/ppermute | solution.py:32
  52.8 6.5 %pairs.1 = (bf16[1024,1024]{1,0:T(8,128)(2,1)}, bf16[1024,1152]{1,0:T(8,128)(2,1)}, bf16[1024,1152]{1,0:T(8,128)(2,1)}, f32[1024,1]{1,0:T(8,128)S(1)}, f32[1,1024]{1,0:T(1,128)S(1)}, /*index=5*/f32[2,1024]{1,0:T(2,128)S(1)}) custom-call(f32[2]{0:T(128)S(1)} %pad_maximum_fusion.11.par_ref, bf16[128,1152]{1,0:T(8,128)(2,1)S(1)} %fusion.3.refs_0_, ...), custom_call_target="tpu_custom_call" | custom-call | flops 2415919104 | bytes 12582912 | tf_op jit(solution)/shard_map/pairs/pallas_call | solution.py:125
  59.3 0.2 slice_reduce_fusion
  59.6 0.1 reduce_sum.88
  59.7 0.9 collective-permute-start.14
  60.6 0.8 collective-permute-done.14
  61.4 0.1 fusion.38
  61.6 2.3 %collective-permute-start.15 = (f32[2]{0:T(128)S(1)}, f32[2]{0:T(128)S(1)}, u32[]{:S(2)}, u32[]{:S(2)}) collective-permute-start(f32[2]{0:T(128)S(1)} %slice_add_fusion.1), channel_id=1, source_target_pairs={{0,16},{1,17},{2,18},{3,19},{4,20},{5,21},{6,22},{7,23},{8,24},{9,... | collective-permute-start | bytes 32 | tf_op jit(solution)/shard_map/ppermute | solution.py:32
  64.0 3.6 %convolution_convert_fusion.1 = f16[512,1152]{1,0:T(8,128)(2,1)S(1)} fusion(bf16[1024,1152]{1,0:T(8,128)(2,1)} %get-tuple-element.71, bf16[1024,1024]{1,0:T(8,128)(2,1)} %get-tuple-element.70), kind=kOutput, calls=%fused_computation.3 | convolution fusion | flops 1208549376 | bytes 4587520 | tf_op jit(solution)/shard_map/dot_general | solution.py:237
  67.7 0.7 collective-permute-start.17
  68.4 4.2 %convolution_convert_fusion = f16[1024,1152]{1,0:T(8,128)(2,1)} fusion(bf16[1024,1024]{1,0:T(8,128)(2,1)S(1)} %copy-done.8, bf16[1024,1152]{1,0:T(8,128)(2,1)S(1)} %copy-done.9), kind=kOutput, calls=%fused_computation.1 | convolution fusion | flops 2417098752 | bytes 6815744 | tf_op jit(solution)/shard_map/dot_general | solution.py:243
  72.7 3.3 %collective-permute-done.16 = f32[2]{0:T(128)S(1)} collective-permute-done((f32[2]{0:T(128)S(1)}, f32[2]{0:T(128)S(1)}, u32[]{:S(2)}, u32[]{:S(2)}) %collective-permute-start.16) | collective-permute-done | bytes 40 | tf_op jit(solution)/shard_map/ppermute | solution.py:32
  76.0 1.6 %convolution_add_fusion = f32[512,1152]{1,0:T(8,128)S(1)} fusion(bf16[1024,1152]{1,0:T(8,128)(2,1)S(1)} %copy-done.7, f16[512,1152]{1,0:T(8,128)(2,1)S(1)} %collective-permute-done.17, bf16[1024,1024]{1,0:T(8,128)(2,1)S(1)} %copy-done.8), kind=kOutput, calls=%fused_computation.2 | convolution fusion | flops 1209139200 | bytes 6946816 | tf_op jit(solution)/shard_map/dot_general | solution.py:249
  77.5 1.4 %copy-done = f32[512,1152]{1,0:T(8,128)} copy-done((f32[512,1152]{1,0:T(8,128)}, f32[512,1152]{1,0:T(8,128)S(1)}, u32[]{:S(2)}) %copy-start) | copy-done | bytes 2359320
  79.0 0.1 slice_convert_fusion
  79.1 3.1 %collective-permute-start.18 = (f32[2]{0:T(128)S(1)}, f32[2]{0:T(128)S(1)}, u32[]{:S(2)}, u32[]{:S(2)}) collective-permute-start(f32[2]{0:T(128)S(1)} %add.161), channel_id=1, source_target_pairs={{0,64},{1,65},{2,66},{3,67},{4,68},{5,69},{6,70},{7,71},{8,72},{9,... | collective-permute-start | bytes 32 | tf_op jit(solution)/shard_map/ppermute | solution.py:32
  82.2 4.7 %all-to-all-start = ((f16[16,64,1152]{2,1,0:T(8,128)(2,1)}), f16[16,64,1152]{2,1,0:T(8,128)(2,1)}, u32[]{:S(2)}, u32[]{:S(2)}) async-start(f16[16,64,1152]{2,1,0:T(8,128)(2,1)} %bitcast.37), calls=%async_computation | async-start | bytes 4718592 | tf_op jit(solution)/shard_map/all_to_all | solution.py:247
  86.9 0.2 fusion.49
  87.1 1.2 collective-permute-start.24
  88.4 0.7 collective-permute-start.22
  89.2 0.6 collective-permute-start.21
  89.9 2.5 %collective-permute-start.20 = (f16[136,1152]{1,0:T(8,128)(2,1)S(1)}, f16[136,1152]{1,0:T(8,128)(2,1)S(1)}, u32[]{:S(2)}, u32[]{:S(2)}) collective-permute-start(f16[136,1152]{1,0:T(8,128)(2,1)S(1)} %pad_maximum_fusion.2), channel_id=1, source_target_pairs={{0,48},{1,81},{2,50},{3,83},{4,52},{5,85},{6,54},{7,87},{8,56},{9,... | collective-permute-start | bytes 940040 | tf_op jit(solution)/shard_map/ppermute | solution.py:32
  92.4 2.5 %collective-permute-start.19 = (f16[72,1152]{1,0:T(8,128)(2,1)S(1)}, f16[72,1152]{1,0:T(8,128)(2,1)S(1)}, u32[]{:S(2)}, u32[]{:S(2)}) collective-permute-start(f16[72,1152]{1,0:T(8,128)(2,1)S(1)} %pad_maximum_fusion.8), channel_id=1, source_target_pairs={{0,64},{1,65},{2,66},{3,67},{4,68},{5,69},{6,70},{7,71},{8,72},{9,... | collective-permute-start | bytes 497672 | tf_op jit(solution)/shard_map/ppermute | solution.py:32
  94.9 5.2 %collective-permute-done.24 = f32[1026]{0:T(1024)S(1)} collective-permute-done((f32[1026]{0:T(1024)S(1)}, f32[1026]{0:T(1024)S(1)}, u32[]{:S(2)}, u32[]{:S(2)}) %collective-permute-start.24) | collective-permute-done | bytes 4136 | tf_op jit(solution)/shard_map/ppermute | solution.py:32
  100.2 8.7 %collective-permute-start.25 = (f32[1026]{0:T(1024)S(1)}, f32[1026]{0:T(1024)S(1)}, u32[]{:S(2)}, u32[]{:S(2)}) collective-permute-start(f32[1026]{0:T(1024)S(1)} %fusion.46), channel_id=1, source_target_pairs={{0,4},{1,5},{2,6},{3,7},{4,0},{5,1},{6,2},{7,3},{8,12},{9,13},{10,... | collective-permute-start | bytes 12320 | tf_op jit(solution)/shard_map/ppermute | solution.py:32
  108.9 5.5 %collective-permute-done.25 = f32[1026]{0:T(1024)S(1)} collective-permute-done((f32[1026]{0:T(1024)S(1)}, f32[1026]{0:T(1024)S(1)}, u32[]{:S(2)}, u32[]{:S(2)}) %collective-permute-start.25) | collective-permute-done | bytes 4136 | tf_op jit(solution)/shard_map/ppermute | solution.py:32
  114.4 1.3 %collective-permute-start.26 = (f32[1026]{0:T(1024)S(1)}, f32[1026]{0:T(1024)S(1)}, u32[]{:S(2)}, u32[]{:S(2)}) collective-permute-start(f32[1026]{0:T(1024)S(1)} %add.169), channel_id=1, source_target_pairs={{0,130},{1,131},{2,128},{3,129},{4,134},{5,135},{6,132},{7,133},{8... | collective-permute-start | bytes 12320 | tf_op jit(solution)/shard_map/ppermute | solution.py:32
  115.7 2.8 %collective-permute-done.26 = f32[1026]{0:T(1024)S(1)} collective-permute-done((f32[1026]{0:T(1024)S(1)}, f32[1026]{0:T(1024)S(1)}, u32[]{:S(2)}, u32[]{:S(2)}) %collective-permute-start.26) | collective-permute-done | bytes 4136 | tf_op jit(solution)/shard_map/ppermute | solution.py:32
  118.5 2.6 %collective-permute-start.27 = (f32[1026]{0:T(1024)S(1)}, f32[1026]{0:T(1024)S(1)}, u32[]{:S(2)}, u32[]{:S(2)}) collective-permute-start(f32[1026]{0:T(1024)S(1)} %add.170), channel_id=1, source_target_pairs={{0,8},{1,9},{2,10},{3,11},{4,12},{5,13},{6,14},{7,15},{8,0},{9,1},... | collective-permute-start | bytes 12320 | tf_op jit(solution)/shard_map/ppermute | solution.py:32
  121.1 0.1 copy.12.image_inv
  121.4 1.0 slice.93.half
  122.4 0.1 collective-permute-done.27
  122.5 0.1 convert_add_fusion.arrived
  122.7 4.8 %collective-permute-start.23 = (f32[72,1152]{1,0:T(8,128)S(1)}, f32[72,1152]{1,0:T(8,128)S(1)}, u32[]{:S(2)}, u32[]{:S(2)}) collective-permute-start(f32[72,1152]{1,0:T(8,128)S(1)} %pad_maximum_fusion.1), channel_id=1, source_target_pairs={{0,1},{1,0},{2,3},{3,2},{4,5},{5,4},{6,7},{7,6},{8,9},{9,8},{10,11... | collective-permute-start | bytes 995336 | tf_op jit(solution)/shard_map/ppermute | solution.py:32
  127.6 0.6 dynamic-slice_add_fusion
  128.1 0.5 slice.103
  128.7 2.0 %convert_reduce_fusion.gt = f32[64,1152]{1,0:T(8,128)S(1)} fusion(f16[16,64,1152]{2,1,0:T(8,128)(2,1)} %all-to-all-done), kind=kLoop, calls=%fused_computation | loop fusion | flops 2285568 | bytes 2654208 | tf_op jit(solution)/shard_map/reduce_sum | solution.py:260
  130.7 1.1 finish.1
  (80 shorter events, 1.2 us)
Async XLA Ops:
  0.6 17.1 %copy-start.2 = (bf16[256,1152]{1,0:T(8,128)(2,1)S(1)}, bf16[256,1152]{1,0:T(8,128)(2,1)}, u32[]{:S(2)}) copy-start(bf16[256,1152]{1,0:T(8,128)(2,1)} %param.5) | copy-start | bytes 1769476
  0.6 17.2 %copy-start.1 = (bf16[256,1152]{1,0:T(8,128)(2,1)S(1)}, bf16[256,1152]{1,0:T(8,128)(2,1)}, u32[]{:S(2)}) copy-start(bf16[256,1152]{1,0:T(8,128)(2,1)} %param.4) | copy-start | bytes 1769476
  2.0 17.5 %collective-permute-start.1 = (bf16[128,1152]{1,0:T(8,128)(2,1)S(1)}, bf16[128,1152]{1,0:T(8,128)(2,1)S(1)}, u32[]{:S(2)}, u32[]{:S(2)}) collective-permute-start(bf16[128,1152]{1,0:T(8,128)(2,1)S(1)} %fusion.5.refs_6_), channel_id=1, source_target_pairs={{0,4},{1,5},{2,6},{3,7},{4,8},{5,9},{6,10},{7,11},{8,12},{9,13},{1... | collective-permute-start | bytes 884744 | tf_op jit(solution)/shard_map/ppermute | solution.py:32
  4.2 15.4 %collective-permute-start.2 = (bf16[128,1152]{1,0:T(8,128)(2,1)S(1)}, bf16[128,1152]{1,0:T(8,128)(2,1)S(1)}, u32[]{:S(2)}, u32[]{:S(2)}) collective-permute-start(bf16[128,1152]{1,0:T(8,128)(2,1)S(1)} %fusion.5.refs_6_), channel_id=1, source_target_pairs={{0,12},{1,13},{2,14},{3,15},{4,0},{5,1},{6,2},{7,3},{8,4},{9,5},{1... | collective-permute-start | bytes 884744 | tf_op jit(solution)/shard_map/ppermute | solution.py:32
  5.5 14.1 %collective-permute-start.3 = (bf16[128,1152]{1,0:T(8,128)(2,1)S(1)}, bf16[128,1152]{1,0:T(8,128)(2,1)}, u32[]{:S(2)}, u32[]{:S(2)}) collective-permute-start(bf16[128,1152]{1,0:T(8,128)(2,1)S(1)} %fusion.5.refs_6_), channel_id=1, source_target_pairs={{0,130},{1,131},{2,128},{3,129},{4,134},{5,135},{6,132},{7,133},{8... | collective-permute-start | bytes 884744 | tf_op jit(solution)/shard_map/ppermute | solution.py:32
  10.6 15.6 %collective-permute-start = (bf16[128,1152]{1,0:T(8,128)(2,1)S(1)}, bf16[128,1152]{1,0:T(8,128)(2,1)S(1)}, u32[]{:S(2)}, u32[]{:S(2)}) collective-permute-start(bf16[128,1152]{1,0:T(8,128)(2,1)S(1)} %fusion.3.refs_0_), channel_id=1, source_target_pairs={{0,16},{1,113},{2,18},{3,115},{4,20},{5,117},{6,22},{7,119},{8,24}... | collective-permute-start | bytes 884744 | tf_op jit(solution)/shard_map/ppermute | solution.py:32
  16.2 16.1 %collective-permute-start.6 = (bf16[64,1152]{1,0:T(8,128)(2,1)S(1)}, bf16[64,1152]{1,0:T(8,128)(2,1)S(1)}, u32[]{:S(2)}, u32[]{:S(2)}) collective-permute-start(bf16[64,1152]{1,0:T(8,128)(2,1)S(1)} %constant_dynamic-slice_fusion.1), channel_id=1, source_target_pairs={{0,64},{1,65},{2,66},{3,67},{4,68},{5,69},{6,70},{7,71},{8,72},{9,... | collective-permute-start | bytes 442376 | tf_op jit(solution)/shard_map/ppermute | solution.py:32
  26.2 8.8 %collective-permute-start.10 = (bf16[64,1152]{1,0:T(8,128)(2,1)S(1)}, bf16[64,1152]{1,0:T(8,128)(2,1)S(1)}, u32[]{:S(2)}, u32[]{:S(2)}) collective-permute-start(bf16[64,1152]{1,0:T(8,128)(2,1)S(1)} %slice.77), channel_id=1, source_target_pairs={{0,12},{1,13},{2,14},{3,15},{4,0},{5,1},{6,2},{7,3},{8,4},{9,5},{1... | collective-permute-start | bytes 442376 | tf_op jit(solution)/shard_map/ppermute | solution.py:32
  28.2 14.8 %collective-permute-start.4 = (bf16[128,1152]{1,0:T(8,128)(2,1)S(1)}, bf16[128,1152]{1,0:T(8,128)(2,1)S(1)}, u32[]{:S(2)}, u32[]{:S(2)}) collective-permute-start(bf16[128,1152]{1,0:T(8,128)(2,1)S(1)} %collective-permute-done.refs_1_), channel_id=1, source_target_pairs={{0,16},{1,113},{2,18},{3,115},{4,20},{5,117},{6,22},{7,119},{8,24}... | collective-permute-start | bytes 884744 | tf_op jit(solution)/shard_map/ppermute | solution.py:32
  31.6 11.4 %collective-permute-start.5 = (bf16[128,1152]{1,0:T(8,128)(2,1)S(1)}, bf16[128,1152]{1,0:T(8,128)(2,1)S(1)}, u32[]{:S(2)}, u32[]{:S(2)}) collective-permute-start(bf16[128,1152]{1,0:T(8,128)(2,1)S(1)} %collective-permute-done.refs_1_), channel_id=1, source_target_pairs={{0,32},{1,97},{2,34},{3,99},{4,36},{5,101},{6,38},{7,103},{8,40},{... | collective-permute-start | bytes 884744 | tf_op jit(solution)/shard_map/ppermute | solution.py:32
  31.6 11.4 %collective-permute-start.7 = (bf16[128,1152]{1,0:T(8,128)(2,1)}, bf16[128,1152]{1,0:T(8,128)(2,1)S(1)}, u32[]{:S(2)}, u32[]{:S(2)}) collective-permute-start(bf16[128,1152]{1,0:T(8,128)(2,1)} %collective-permute-done.3.refs_10_), channel_id=1, source_target_pairs={{0,4},{1,5},{2,6},{3,7},{4,8},{5,9},{6,10},{7,11},{8,12},{9,13},{1... | collective-permute-start | bytes 884744 | tf_op jit(solution)/shard_map/ppermute | solution.py:32
  32.3 10.7 %collective-permute-start.8 = (bf16[128,1152]{1,0:T(8,128)(2,1)}, bf16[128,1152]{1,0:T(8,128)(2,1)S(1)}, u32[]{:S(2)}, u32[]{:S(2)}) collective-permute-start(bf16[128,1152]{1,0:T(8,128)(2,1)} %collective-permute-done.3.refs_10_), channel_id=1, source_target_pairs={{0,12},{1,13},{2,14},{3,15},{4,0},{5,1},{6,2},{7,3},{8,4},{9,5},{1... | collective-permute-start | bytes 884744 | tf_op jit(solution)/shard_map/ppermute | solution.py:32
  35.0 0.7 copy-start.3
  35.6 7.4 %collective-permute-start.9 = (bf16[64,1152]{1,0:T(8,128)(2,1)}, bf16[64,1152]{1,0:T(8,128)(2,1)}, u32[]{:S(2)}, u32[]{:S(2)}) collective-permute-start(bf16[64,1152]{1,0:T(8,128)(2,1)} %slice.76), channel_id=1, source_target_pairs={{0,4},{1,5},{2,6},{3,7},{4,8},{5,9},{6,10},{7,11},{8,12},{9,13},{1... | collective-permute-start | bytes 442376 | tf_op jit(solution)/shard_map/ppermute | solution.py:32
  35.6 13.4 %copy-start.4 = (bf16[64,1152]{1,0:T(8,128)(2,1)S(1)}, bf16[64,1152]{1,0:T(8,128)(2,1)}, u32[]{:S(2)}) copy-start(bf16[64,1152]{1,0:T(8,128)(2,1)} %copy-done.3) | copy-start | bytes 442372
  43.1 9.7 %collective-permute-start.11 = (bf16[448,1152]{1,0:T(8,128)(2,1)S(1)}, bf16[448,1152]{1,0:T(8,128)(2,1)S(1)}, u32[]{:S(2)}, u32[]{:S(2)}) collective-permute-start(bf16[448,1152]{1,0:T(8,128)(2,1)S(1)} %pad_maximum_fusion), channel_id=1, source_target_pairs={{0,1},{1,0},{2,3},{3,2},{4,5},{5,4},{6,7},{7,6},{8,9},{9,8},{10,11... | collective-permute-start | bytes 3096584 | tf_op jit(solution)/shard_map/ppermute | solution.py:32
  46.0 6.8 %collective-permute-start.12 = (bf16[64,1152]{1,0:T(8,128)(2,1)S(1)}, bf16[64,1152]{1,0:T(8,128)(2,1)S(1)}, u32[]{:S(2)}, u32[]{:S(2)}) collective-permute-start(bf16[64,1152]{1,0:T(8,128)(2,1)S(1)} %slice.78), channel_id=1, source_target_pairs={{0,4},{1,5},{2,6},{3,7},{4,8},{5,9},{6,10},{7,11},{8,12},{9,13},{1... | collective-permute-start | bytes 442376 | tf_op jit(solution)/shard_map/ppermute | solution.py:32
  46.1 6.6 %collective-permute-start.13 = (bf16[64,1152]{1,0:T(8,128)(2,1)S(1)}, bf16[64,1152]{1,0:T(8,128)(2,1)S(1)}, u32[]{:S(2)}, u32[]{:S(2)}) collective-permute-start(bf16[64,1152]{1,0:T(8,128)(2,1)S(1)} %slice.79), channel_id=1, source_target_pairs={{0,12},{1,13},{2,14},{3,15},{4,0},{5,1},{6,2},{7,3},{8,4},{9,5},{1... | collective-permute-start | bytes 442376 | tf_op jit(solution)/shard_map/ppermute | solution.py:32
  52.8 6.9 %copy-start.6 = (f32[2]{0:T(128)S(1)}, f32[2]{0:T(128)}, u32[]{:S(2)}) copy-start(f32[2]{0:T(128)} %pad_maximum_fusion.12) | copy-start | bytes 28
  59.7 1.7 %collective-permute-start.14 = (f32[514]{0:T(1024)S(1)}, f32[514]{0:T(1024)S(1)}, u32[]{:S(2)}, u32[]{:S(2)}) collective-permute-start(f32[514]{0:T(1024)S(1)} %pad_maximum_fusion.10), channel_id=1, source_target_pairs={{0,1},{1,0},{2,3},{3,2},{4,5},{5,4},{6,7},{7,6},{8,9},{9,8},{10,11... | collective-permute-start | bytes 6176 | tf_op jit(solution)/shard_map/ppermute | solution.py:32
  61.6 6.0 %collective-permute-start.15 = (f32[2]{0:T(128)S(1)}, f32[2]{0:T(128)S(1)}, u32[]{:S(2)}, u32[]{:S(2)}) collective-permute-start(f32[2]{0:T(128)S(1)} %slice_add_fusion.1), channel_id=1, source_target_pairs={{0,16},{1,17},{2,18},{3,19},{4,20},{5,21},{6,22},{7,23},{8,24},{9,... | collective-permute-start | bytes 32 | tf_op jit(solution)/shard_map/ppermute | solution.py:32
  64.0 4.4 %copy-start.8 = (bf16[1024,1024]{1,0:T(8,128)(2,1)S(1)}, bf16[1024,1024]{1,0:T(8,128)(2,1)}, u32[]{:S(2)}) copy-start(bf16[1024,1024]{1,0:T(8,128)(2,1)} %get-tuple-element.70) | copy-start | bytes 6291460
  64.0 4.4 %copy-start.9 = (bf16[1024,1152]{1,0:T(8,128)(2,1)S(1)}, bf16[1024,1152]{1,0:T(8,128)(2,1)}, u32[]{:S(2)}) copy-start(bf16[1024,1152]{1,0:T(8,128)(2,1)} %get-tuple-element.73) | copy-start | bytes 7077892
  67.7 8.3 %collective-permute-start.17 = (f16[512,1152]{1,0:T(8,128)(2,1)S(1)}, f16[512,1152]{1,0:T(8,128)(2,1)S(1)}, u32[]{:S(2)}, u32[]{:S(2)}) collective-permute-start(f16[512,1152]{1,0:T(8,128)(2,1)S(1)} %convolution_convert_fusion.1), channel_id=1, source_target_pairs={{0,1},{1,0},{2,3},{3,2},{4,5},{5,4},{6,7},{7,6},{8,9},{9,8},{10,11... | collective-permute-start | bytes 3538952 | tf_op jit(solution)/shard_map/ppermute | solution.py:32
  68.4 7.5 %copy-start.7 = (bf16[1024,1152]{1,0:T(8,128)(2,1)S(1)}, bf16[1024,1152]{1,0:T(8,128)(2,1)}, u32[]{:S(2)}) copy-start(bf16[1024,1152]{1,0:T(8,128)(2,1)} %get-tuple-element.71) | copy-start | bytes 7077892
  72.6 3.3 %collective-permute-start.16 = (f32[2]{0:T(128)S(1)}, f32[2]{0:T(128)S(1)}, u32[]{:S(2)}, u32[]{:S(2)}) collective-permute-start(f32[2]{0:T(128)S(1)} %add.159), channel_id=1, source_target_pairs={{0,32},{1,33},{2,34},{3,35},{4,36},{5,37},{6,38},{7,39},{8,40},{9,... | collective-permute-start | bytes 32 | tf_op jit(solution)/shard_map/ppermute | solution.py:32
  77.5 1.5 %copy-start = (f32[512,1152]{1,0:T(8,128)}, f32[512,1152]{1,0:T(8,128)S(1)}, u32[]{:S(2)}) copy-start(f32[512,1152]{1,0:T(8,128)S(1)} %convolution_add_fusion) | copy-start | bytes 7077892
  79.1 7.8 %collective-permute-start.18 = (f32[2]{0:T(128)S(1)}, f32[2]{0:T(128)S(1)}, u32[]{:S(2)}, u32[]{:S(2)}) collective-permute-start(f32[2]{0:T(128)S(1)} %add.161), channel_id=1, source_target_pairs={{0,64},{1,65},{2,66},{3,67},{4,68},{5,69},{6,70},{7,71},{8,72},{9,... | collective-permute-start | bytes 32 | tf_op jit(solution)/shard_map/ppermute | solution.py:32
  82.2 46.5 %all-to-all-start = ((f16[16,64,1152]{2,1,0:T(8,128)(2,1)}), f16[16,64,1152]{2,1,0:T(8,128)(2,1)}, u32[]{:S(2)}, u32[]{:S(2)}) async-start(f16[16,64,1152]{2,1,0:T(8,128)(2,1)} %bitcast.37), calls=%async_computation | async-start | bytes 4718592 | tf_op jit(solution)/shard_map/all_to_all | solution.py:247
  86.9 34.5 %copy-start.5 = (f32[64]{0:T(128)S(1)}, f32[64]{0:T(128)}, u32[]{:S(2)}) copy-start(f32[64]{0:T(128)} %multiply_reduce-precision_fusion) | copy-start | bytes 772
  87.1 13.0 %collective-permute-start.24 = (f32[1026]{0:T(1024)S(1)}, f32[1026]{0:T(1024)S(1)}, u32[]{:S(2)}, u32[]{:S(2)}) collective-permute-start(f32[1026]{0:T(1024)S(1)} %pad_maximum_fusion.9), channel_id=1, source_target_pairs={{0,2},{1,3},{2,0},{3,1},{4,6},{5,7},{6,4},{7,5},{8,10},{9,11},{10,... | collective-permute-start | bytes 12320 | tf_op jit(solution)/shard_map/ppermute | solution.py:32
  88.4 34.1 %collective-permute-start.22 = (f16[136,1152]{1,0:T(8,128)(2,1)S(1)}, f16[136,1152]{1,0:T(8,128)(2,1)S(1)}, u32[]{:S(2)}, u32[]{:S(2)}) collective-permute-start(f16[136,1152]{1,0:T(8,128)(2,1)S(1)} %pad_maximum_fusion.4), channel_id=1, source_target_pairs={{0,16},{1,113},{2,18},{3,115},{4,20},{5,117},{6,22},{7,119},{8,24}... | collective-permute-start | bytes 940040 | tf_op jit(solution)/shard_map/ppermute | solution.py:32
  89.2 33.4 %collective-permute-start.21 = (f16[136,1152]{1,0:T(8,128)(2,1)S(1)}, f16[136,1152]{1,0:T(8,128)(2,1)S(1)}, u32[]{:S(2)}, u32[]{:S(2)}) collective-permute-start(f16[136,1152]{1,0:T(8,128)(2,1)S(1)} %pad_maximum_fusion.3), channel_id=1, source_target_pairs={{0,32},{1,97},{2,34},{3,99},{4,36},{5,101},{6,38},{7,103},{8,40},{... | collective-permute-start | bytes 940040 | tf_op jit(solution)/shard_map/ppermute | solution.py:32
  89.9 32.7 %collective-permute-start.20 = (f16[136,1152]{1,0:T(8,128)(2,1)S(1)}, f16[136,1152]{1,0:T(8,128)(2,1)S(1)}, u32[]{:S(2)}, u32[]{:S(2)}) collective-permute-start(f16[136,1152]{1,0:T(8,128)(2,1)S(1)} %pad_maximum_fusion.2), channel_id=1, source_target_pairs={{0,48},{1,81},{2,50},{3,83},{4,52},{5,85},{6,54},{7,87},{8,56},{9,... | collective-permute-start | bytes 940040 | tf_op jit(solution)/shard_map/ppermute | solution.py:32
  92.4 30.1 %collective-permute-start.19 = (f16[72,1152]{1,0:T(8,128)(2,1)S(1)}, f16[72,1152]{1,0:T(8,128)(2,1)S(1)}, u32[]{:S(2)}, u32[]{:S(2)}) collective-permute-start(f16[72,1152]{1,0:T(8,128)(2,1)S(1)} %pad_maximum_fusion.8), channel_id=1, source_target_pairs={{0,64},{1,65},{2,66},{3,67},{4,68},{5,69},{6,70},{7,71},{8,72},{9,... | collective-permute-start | bytes 497672 | tf_op jit(solution)/shard_map/ppermute | solution.py:32
  100.2 14.2 %collective-permute-start.25 = (f32[1026]{0:T(1024)S(1)}, f32[1026]{0:T(1024)S(1)}, u32[]{:S(2)}, u32[]{:S(2)}) collective-permute-start(f32[1026]{0:T(1024)S(1)} %fusion.46), channel_id=1, source_target_pairs={{0,4},{1,5},{2,6},{3,7},{4,0},{5,1},{6,2},{7,3},{8,12},{9,13},{10,... | collective-permute-start | bytes 12320 | tf_op jit(solution)/shard_map/ppermute | solution.py:32
  114.4 4.1 %collective-permute-start.26 = (f32[1026]{0:T(1024)S(1)}, f32[1026]{0:T(1024)S(1)}, u32[]{:S(2)}, u32[]{:S(2)}) collective-permute-start(f32[1026]{0:T(1024)S(1)} %add.169), channel_id=1, source_target_pairs={{0,130},{1,131},{2,128},{3,129},{4,134},{5,135},{6,132},{7,133},{8... | collective-permute-start | bytes 12320 | tf_op jit(solution)/shard_map/ppermute | solution.py:32
  118.5 4.0 %collective-permute-start.27 = (f32[1026]{0:T(1024)S(1)}, f32[1026]{0:T(1024)S(1)}, u32[]{:S(2)}, u32[]{:S(2)}) collective-permute-start(f32[1026]{0:T(1024)S(1)} %add.170), channel_id=1, source_target_pairs={{0,8},{1,9},{2,10},{3,11},{4,12},{5,13},{6,14},{7,15},{8,0},{9,1},... | collective-permute-start | bytes 12320 | tf_op jit(solution)/shard_map/ppermute | solution.py:32
  122.7 8.0 %collective-permute-start.23 = (f32[72,1152]{1,0:T(8,128)S(1)}, f32[72,1152]{1,0:T(8,128)S(1)}, u32[]{:S(2)}, u32[]{:S(2)}) collective-permute-start(f32[72,1152]{1,0:T(8,128)S(1)} %pad_maximum_fusion.1), channel_id=1, source_target_pairs={{0,1},{1,0},{2,3},{3,2},{4,5},{5,4},{6,7},{7,6},{8,9},{9,8},{10,11... | collective-permute-start | bytes 995336 | tf_op jit(solution)/shard_map/ppermute | solution.py:32

commit v6 on v5

--- a/solution.py
+++ b/solution.py
@@ -248,24 +248,26 @@
     both = both + send(both, fz=4)
     half = jnp.dot(weights[:512], texts, preferred_element_type=f32) + rows_met.astype(f32)
     flight = half[Q:].astype(f16)
-    both, half, flight = tied(both, half, flight)
+    both, half, flight = tied(both, half[:Q], flight)
     far = send(jnp.concatenate([flight[384:], loss_rows[3]]), dz=4)
     three, two, one = (
         send(jnp.concatenate([flight[(k - 1) * 128 : k * 128], loss_rows[k - 1]]), split_z=k) for k in (3, 2, 1)
     )
-    far, three, two, one = tied(far, three, two, one)
+    plane = jnp.concatenate([lt.reshape(-1), both])
+    plane = plane + send(plane, fy=1)
+    plane, far, three = tied(plane, far, three)
+    for move in (dict(fx=1), dict(fy=3)):
+        plane = plane + send(plane, **move)
     arrived = one.astype(f32) + two.astype(f32) + three.astype(f32)
     theirs = jnp.concatenate([lax.dynamic_slice_in_dim(arrived, (1 - core) * Q, Q, 0), arrived[128:]])
+    plane, far, arrived, theirs = tied(plane, far, arrived, theirs)
     met = send(theirs, fc=1)
+    plane = plane + send(plane, fx=2)
     gt_own = jnp.sum(back_xy.reshape(16, Q, -1).astype(f32), axis=0)
     grad_image, grad_text, image_loss = finish(
-        half[:Q], far.astype(f32), arrived, met, gt_own, image_unit, text_unit, image_inv, text_inv,
+        half, far.astype(f32), arrived, met, gt_own, image_unit, text_unit, image_inv, text_inv,
         match_weight[:, None], (li_half[:Q] + match_loss)[None],
     )
-    lt, both, _ = tied(lt, both, back_xy)
-    plane = jnp.concatenate([lt.reshape(-1), both])
-    for move in (dict(fy=1), dict(fx=1), dict(fy=3), dict(fx=2)):
-        plane = plane + send(plane, **move)
     text_loss = lax.dynamic_slice_in_dim(plane, ((yh * 4 + x) * 2 + yl) * Q, Q, 0) + match_loss
     image_loss, both = image_loss.reshape(Q), plane[1024:]
     return (grad_image, grad_text, image_loss, text_loss, both)

time: 133 us -> 139 us (1.045)
  the two profiles are of different devices: /device:TPU:1 before, /device:TPU:70 now
where the time goes in v6:
time: 139 us
  starting transfers between devices  56.2 us (40%)
  waiting for transfers between devices  45.2 us (33%)
  matrix products  13.1 us (9%)
  other arithmetic  10.1 us (7%)
  Pallas kernels  7.62 us (5%)
  local copies, waits for them, and re-layouts  3.75 us (3%)
  between operations  3.02 us (2%)
    ppermute x28, starting transfers between devices, send(): return lax.ppermute(value, AXES, pairs)  51.6 us
    ppermute x28, waiting for transfers between devices, send(): return lax.ppermute(value, AXES, pairs)  45.2 us
    dot_general x1, matrix products, per_device(): lax.dot_general(weights, images, (((0,), (0,)), ((), ())), preferred_elem...  6.82 us
    pallas_call x1, Pallas kernels, pairs_on_device(): pl.pallas_call(pair_kernel, out_shape=(pltpu.HBM((1024, 1024), jnp.bfloat...  6.56 us
    all_to_all x1, starting transfers between devices, per_device(): back_xy = lax.all_to_all(gt16, ('yh', 'x', 'yl'), 0, 0, tiled=True)  4.59 us
    dot_general x1, matrix products, per_device(): jnp.dot(weights[512:], texts, preferred_element_type=f32).astype(f16)  3.51 us
    dot_general x1, matrix products, per_device(): jnp.dot(weights[:512], texts, preferred_element_type=f32)  2.8 us
  transfers between devices with their start and end apart: 29, of which 13 were waited for; matrix products, arithmetic and copies ran while one was open for 15% of the time, Pallas kernels for 0%

profile of v6, /device:TPU:70, one launch (start us, length us, event | category | flops | bytes accessed | tf_op | source)
XLA Modules:
  0.0 139.0 jit_solution(10210567710203815108)
XLA Ops:
  0.7 1.1 constant_dynamic-slice_fusion.3
  1.8 0.1 fusion.4
  1.9 0.1 fusion.5.refs_6_
  2.0 0.6 collective-permute-start.1
  2.6 1.5 %collective-permute-start.2 = (bf16[128,1152]{1,0:T(8,128)(2,1)S(1)}, bf16[128,1152]{1,0:T(8,128)(2,1)S(1)}, u32[]{:S(2)}, u32[]{:S(2)}) collective-permute-start(bf16[128,1152]{1,0:T(8,128)(2,1)S(1)} %fusion.5.refs_6_), channel_id=1, source_target_pairs={{0,12},{1,13},{2,14},{3,15},{4,0},{5,1},{6,2},{7,3},{8,4},{9,5},{1... | collective-permute-start | bytes 884744 | tf_op jit(solution)/shard_map/ppermute | solution.py:32
  4.2 3.0 %collective-permute-start.3 = (bf16[128,1152]{1,0:T(8,128)(2,1)S(1)}, bf16[128,1152]{1,0:T(8,128)(2,1)}, u32[]{:S(2)}, u32[]{:S(2)}) collective-permute-start(bf16[128,1152]{1,0:T(8,128)(2,1)S(1)} %fusion.5.refs_6_), channel_id=1, source_target_pairs={{0,130},{1,131},{2,128},{3,129},{4,134},{5,135},{6,132},{7,133},{8... | collective-permute-start | bytes 884744 | tf_op jit(solution)/shard_map/ppermute | solution.py:32
  7.2 1.1 fusion.2
  8.3 1.1 fusion.3.refs_0_
  9.4 2.0 %collective-permute-start = (bf16[128,1152]{1,0:T(8,128)(2,1)S(1)}, bf16[128,1152]{1,0:T(8,128)(2,1)S(1)}, u32[]{:S(2)}, u32[]{:S(2)}) collective-permute-start(bf16[128,1152]{1,0:T(8,128)(2,1)S(1)} %fusion.3.refs_0_), channel_id=1, source_target_pairs={{0,16},{1,113},{2,18},{3,115},{4,20},{5,117},{6,22},{7,119},{8,24}... | collective-permute-start | bytes 884744 | tf_op jit(solution)/shard_map/ppermute | solution.py:32
  11.4 4.6 %collective-permute-start.6 = (bf16[64,1152]{1,0:T(8,128)(2,1)S(1)}, bf16[64,1152]{1,0:T(8,128)(2,1)S(1)}, u32[]{:S(2)}, u32[]{:S(2)}) collective-permute-start(bf16[64,1152]{1,0:T(8,128)(2,1)S(1)} %constant_dynamic-slice_fusion.1), channel_id=1, source_target_pairs={{0,64},{1,65},{2,66},{3,67},{4,68},{5,69},{6,70},{7,71},{8,72},{9,... | collective-permute-start | bytes 442376 | tf_op jit(solution)/shard_map/ppermute | solution.py:32
  16.0 0.1 fusion.7
  16.1 0.1 fusion.6
  17.6 0.2 multiply_reduce_fusion
  17.9 3.0 %collective-permute-done.refs_1_ = bf16[128,1152]{1,0:T(8,128)(2,1)S(1)} collective-permute-done((bf16[128,1152]{1,0:T(8,128)(2,1)S(1)}, bf16[128,1152]{1,0:T(8,128)(2,1)S(1)}, u32[]{:S(2)}, u32[]{:S(2)}) %collective-permute-start) | collective-permute-done | bytes 294944 | tf_op jit(solution)/shard_map/ppermute | solution.py:32
  20.9 0.9 collective-permute-start.10
  21.8 0.7 multiply_reduce_fusion.1
  22.5 4.1 %collective-permute-start.4 = (bf16[128,1152]{1,0:T(8,128)(2,1)S(1)}, bf16[128,1152]{1,0:T(8,128)(2,1)S(1)}, u32[]{:S(2)}, u32[]{:S(2)}) collective-permute-start(bf16[128,1152]{1,0:T(8,128)(2,1)S(1)} %collective-permute-done.refs_1_), channel_id=1, source_target_pairs={{0,16},{1,113},{2,18},{3,115},{4,20},{5,117},{6,22},{7,119},{8,24}... | collective-permute-start | bytes 884744 | tf_op jit(solution)/shard_map/ppermute | solution.py:32
  26.6 3.1 %collective-permute-start.5 = (bf16[128,1152]{1,0:T(8,128)(2,1)S(1)}, bf16[128,1152]{1,0:T(8,128)(2,1)S(1)}, u32[]{:S(2)}, u32[]{:S(2)}) collective-permute-start(bf16[128,1152]{1,0:T(8,128)(2,1)S(1)} %collective-permute-done.refs_1_), channel_id=1, source_target_pairs={{0,32},{1,97},{2,34},{3,99},{4,36},{5,101},{6,38},{7,103},{8,40},{... | collective-permute-start | bytes 884744 | tf_op jit(solution)/shard_map/ppermute | solution.py:32
  29.8 2.4 %collective-permute-start.7 = (bf16[128,1152]{1,0:T(8,128)(2,1)}, bf16[128,1152]{1,0:T(8,128)(2,1)S(1)}, u32[]{:S(2)}, u32[]{:S(2)}) collective-permute-start(bf16[128,1152]{1,0:T(8,128)(2,1)} %collective-permute-done.3.refs_10_), channel_id=1, source_target_pairs={{0,4},{1,5},{2,6},{3,7},{4,8},{5,9},{6,10},{7,11},{8,12},{9,13},{1... | collective-permute-start | bytes 884744 | tf_op jit(solution)/shard_map/ppermute | solution.py:32
  32.2 0.7 slice.76
  32.9 0.7 copy-done.2
  33.5 3.2 %collective-permute-start.9 = (bf16[64,1152]{1,0:T(8,128)(2,1)}, bf16[64,1152]{1,0:T(8,128)(2,1)}, u32[]{:S(2)}, u32[]{:S(2)}) collective-permute-start(bf16[64,1152]{1,0:T(8,128)(2,1)} %slice.76), channel_id=1, source_target_pairs={{0,4},{1,5},{2,6},{3,7},{4,8},{5,9},{6,10},{7,11},{8,12},{9,13},{1... | collective-permute-start | bytes 442376 | tf_op jit(solution)/shard_map/ppermute | solution.py:32
  36.8 0.5 multiply_reduce-precision_fusion
  37.9 1.3 pad_maximum_fusion.12
  39.2 1.2 collective-permute-done.9
  40.4 0.8 collective-permute-done.8.refs_12_
  41.5 3.0 %collective-permute-start.12 = (bf16[64,1152]{1,0:T(8,128)(2,1)S(1)}, bf16[64,1152]{1,0:T(8,128)(2,1)S(1)}, u32[]{:S(2)}, u32[]{:S(2)}) collective-permute-start(bf16[64,1152]{1,0:T(8,128)(2,1)S(1)} %slice.78), channel_id=1, source_target_pairs={{0,4},{1,5},{2,6},{3,7},{4,8},{5,9},{6,10},{7,11},{8,12},{9,13},{1... | collective-permute-start | bytes 442376 | tf_op jit(solution)/shard_map/ppermute | solution.py:32
  44.5 0.3 collective-permute-start.13
  44.8 0.9 pad_maximum_fusion.6.refs_9_
  45.7 2.5 %collective-permute-done.12 = bf16[64,1152]{1,0:T(8,128)(2,1)S(1)} collective-permute-done((bf16[64,1152]{1,0:T(8,128)(2,1)S(1)}, bf16[64,1152]{1,0:T(8,128)(2,1)S(1)}, u32[]{:S(2)}, u32[]{:S(2)}) %collective-permute-start.12) | collective-permute-done | bytes 147488 | tf_op jit(solution)/shard_map/ppermute | solution.py:32
  48.3 3.7 %collective-permute-done.13 = bf16[64,1152]{1,0:T(8,128)(2,1)S(1)} collective-permute-done((bf16[64,1152]{1,0:T(8,128)(2,1)S(1)}, bf16[64,1152]{1,0:T(8,128)(2,1)S(1)}, u32[]{:S(2)}, u32[]{:S(2)}) %collective-permute-start.13) | collective-permute-done | bytes 147488 | tf_op jit(solution)/shard_map/ppermute | solution.py:32
  52.0 6.6 %pairs.1 = (bf16[1024,1024]{1,0:T(8,128)(2,1)}, bf16[1024,1152]{1,0:T(8,128)(2,1)}, bf16[1024,1152]{1,0:T(8,128)(2,1)}, f32[1024,1]{1,0:T(8,128)S(1)}, f32[1,1024]{1,0:T(1,128)S(1)}, /*index=5*/f32[2,1024]{1,0:T(2,128)S(1)}) custom-call(f32[2]{0:T(128)S(1)} %pad_maximum_fusion.11.par_ref, bf16[128,1152]{1,0:T(8,128)(2,1)S(1)} %fusion.3.refs_0_, ...), custom_call_target="tpu_custom_call" | custom-call | flops 2415919104 | bytes 12582912 | tf_op jit(solution)/shard_map/pairs/pallas_call | solution.py:125
  58.6 0.2 slice_reduce_fusion
  58.8 0.1 reduce_sum.88
  59.0 1.2 collective-permute-done.14
  60.5 3.5 %convolution_convert_fusion.1 = f16[512,1152]{1,0:T(8,128)(2,1)S(1)} fusion(bf16[1024,1152]{1,0:T(8,128)(2,1)} %get-tuple-element.72, bf16[1024,1024]{1,0:T(8,128)(2,1)} %get-tuple-element.71), kind=kOutput, calls=%fused_computation.3 | convolution fusion | flops 1208549376 | bytes 4587520 | tf_op jit(solution)/shard_map/dot_general | solution.py:237
  64.1 0.3 collective-permute-start.17
  64.3 6.8 %convolution_convert_fusion = f16[1024,1152]{1,0:T(8,128)(2,1)} fusion(bf16[1024,1024]{1,0:T(8,128)(2,1)} %get-tuple-element.71, bf16[1024,1152]{1,0:T(8,128)(2,1)} %get-tuple-element.74), kind=kOutput, calls=%fused_computation.1 | convolution fusion | flops 2417098752 | bytes 6815744 | tf_op jit(solution)/shard_map/dot_general | solution.py:243
  71.1 2.7 %collective-permute-start.16 = (f32[2]{0:T(128)S(1)}, f32[2]{0:T(128)S(1)}, u32[]{:S(2)}, u32[]{:S(2)}) collective-permute-start(f32[2]{0:T(128)S(1)} %add.159), channel_id=1, source_target_pairs={{0,32},{1,33},{2,34},{3,35},{4,36},{5,37},{6,38},{7,39},{8,40},{9,... | collective-permute-start | bytes 32 | tf_op jit(solution)/shard_map/ppermute | solution.py:32
  73.8 1.8 %collective-permute-done.16 = f32[2]{0:T(128)S(1)} collective-permute-done((f32[2]{0:T(128)S(1)}, f32[2]{0:T(128)S(1)}, u32[]{:S(2)}, u32[]{:S(2)}) %collective-permute-start.16) | collective-permute-done | bytes 40 | tf_op jit(solution)/shard_map/ppermute | solution.py:32
  75.6 2.8 %convolution_add_fusion = f32[512,1152]{1,0:T(8,128)S(1)} fusion(bf16[1024,1152]{1,0:T(8,128)(2,1)S(1)} %copy-done.6, f16[512,1152]{1,0:T(8,128)(2,1)} %collective-permute-done.17, bf16[1024,1024]{1,0:T(8,128)(2,1)S(1)} %copy-done.7), kind=kOutput, calls=%fused_computation.2 | convolution fusion | flops 1209139200 | bytes 6946816 | tf_op jit(solution)/shard_map/dot_general | solution.py:249
  78.4 0.1 slice_convert_fusion
  78.6 3.2 %collective-permute-start.18 = (f32[2]{0:T(128)S(1)}, f32[2]{0:T(128)S(1)}, u32[]{:S(2)}, u32[]{:S(2)}) collective-permute-start(f32[2]{0:T(128)S(1)} %add.161), channel_id=1, source_target_pairs={{0,64},{1,65},{2,66},{3,67},{4,68},{5,69},{6,70},{7,71},{8,72},{9,... | collective-permute-start | bytes 32 | tf_op jit(solution)/shard_map/ppermute | solution.py:32
  81.7 4.6 %all-to-all-start = ((f16[16,64,1152]{2,1,0:T(8,128)(2,1)}), f16[16,64,1152]{2,1,0:T(8,128)(2,1)}, u32[]{:S(2)}, u32[]{:S(2)}) async-start(f16[16,64,1152]{2,1,0:T(8,128)(2,1)} %bitcast.37), calls=%async_computation | async-start | bytes 4718592 | tf_op jit(solution)/shard_map/all_to_all | solution.py:247
  86.3 0.2 fusion.49
  86.6 1.7 %collective-permute-start.24 = (f16[136,1152]{1,0:T(8,128)(2,1)S(1)}, f16[136,1152]{1,0:T(8,128)(2,1)S(1)}, u32[]{:S(2)}, u32[]{:S(2)}) collective-permute-start(f16[136,1152]{1,0:T(8,128)(2,1)S(1)} %pad_maximum_fusion.3), channel_id=1, source_target_pairs={{0,16},{1,113},{2,18},{3,115},{4,20},{5,117},{6,22},{7,119},{8,24}... | collective-permute-start | bytes 940040 | tf_op jit(solution)/shard_map/ppermute | solution.py:32
  88.4 2.0 %collective-permute-start.25 = (f16[136,1152]{1,0:T(8,128)(2,1)S(1)}, f16[136,1152]{1,0:T(8,128)(2,1)S(1)}, u32[]{:S(2)}, u32[]{:S(2)}) collective-permute-start(f16[136,1152]{1,0:T(8,128)(2,1)S(1)} %pad_maximum_fusion.4), channel_id=1, source_target_pairs={{0,32},{1,97},{2,34},{3,99},{4,36},{5,101},{6,38},{7,103},{8,40},{... | collective-permute-start | bytes 940040 | tf_op jit(solution)/shard_map/ppermute | solution.py:32
  90.5 3.6 %collective-permute-start.21 = (f16[136,1152]{1,0:T(8,128)(2,1)S(1)}, f16[136,1152]{1,0:T(8,128)(2,1)S(1)}, u32[]{:S(2)}, u32[]{:S(2)}) collective-permute-start(f16[136,1152]{1,0:T(8,128)(2,1)S(1)} %pad_maximum_fusion.2), channel_id=1, source_target_pairs={{0,48},{1,81},{2,50},{3,83},{4,52},{5,85},{6,54},{7,87},{8,56},{9,... | collective-permute-start | bytes 940040 | tf_op jit(solution)/shard_map/ppermute | solution.py:32
  94.1 1.5 %collective-permute-start.19 = (f32[1026]{0:T(1024)S(1)}, f32[1026]{0:T(1024)S(1)}, u32[]{:S(2)}, u32[]{:S(2)}) collective-permute-start(f32[1026]{0:T(1024)S(1)} %pad_maximum_fusion.9), channel_id=1, source_target_pairs={{0,2},{1,3},{2,0},{3,1},{4,6},{5,7},{6,4},{7,5},{8,10},{9,11},{10,... | collective-permute-start | bytes 12320 | tf_op jit(solution)/shard_map/ppermute | solution.py:32
  95.6 2.7 %collective-permute-start.20 = (f16[72,1152]{1,0:T(8,128)(2,1)S(1)}, f16[72,1152]{1,0:T(8,128)(2,1)S(1)}, u32[]{:S(2)}, u32[]{:S(2)}) collective-permute-start(f16[72,1152]{1,0:T(8,128)(2,1)S(1)} %pad_maximum_fusion.8), channel_id=1, source_target_pairs={{0,64},{1,65},{2,66},{3,67},{4,68},{5,69},{6,70},{7,71},{8,72},{9,... | collective-permute-start | bytes 497672 | tf_op jit(solution)/shard_map/ppermute | solution.py:32
  98.3 14.1 %collective-permute-done.19 = f32[1026]{0:T(1024)S(1)} collective-permute-done((f32[1026]{0:T(1024)S(1)}, f32[1026]{0:T(1024)S(1)}, u32[]{:S(2)}, u32[]{:S(2)}) %collective-permute-start.19) | collective-permute-done | bytes 4136 | tf_op jit(solution)/shard_map/ppermute | solution.py:32
  112.4 7.8 %collective-permute-done.20 = f16[72,1152]{1,0:T(8,128)(2,1)S(1)} collective-permute-done((f16[72,1152]{1,0:T(8,128)(2,1)S(1)}, f16[72,1152]{1,0:T(8,128)(2,1)S(1)}, u32[]{:S(2)}, u32[]{:S(2)}) %collective-permute-start.20) | collective-permute-done | bytes 165920 | tf_op jit(solution)/shard_map/ppermute | solution.py:32
  120.2 0.8 collective-permute-done.21
  121.1 0.9 collective-permute-start.22
  122.0 0.1 convert_add_fusion.arrived
  122.1 2.7 %collective-permute-done.22 = f32[1026]{0:T(1024)S(1)} collective-permute-done((f32[1026]{0:T(1024)S(1)}, f32[1026]{0:T(1024)S(1)}, u32[]{:S(2)}, u32[]{:S(2)}) %collective-permute-start.22) | collective-permute-done | bytes 4136 | tf_op jit(solution)/shard_map/ppermute | solution.py:32
  124.8 2.7 %collective-permute-start.23 = (f32[1026]{0:T(1024)S(1)}, f32[1026]{0:T(1024)S(1)}, u32[]{:S(2)}, u32[]{:S(2)}) collective-permute-start(f32[1026]{0:T(1024)S(1)} %add.165), channel_id=1, source_target_pairs={{0,130},{1,131},{2,128},{3,129},{4,134},{5,135},{6,132},{7,133},{8... | collective-permute-start | bytes 12320 | tf_op jit(solution)/shard_map/ppermute | solution.py:32
  127.5 2.1 %collective-permute-done.23 = f32[1026]{0:T(1024)S(1)} collective-permute-done((f32[1026]{0:T(1024)S(1)}, f32[1026]{0:T(1024)S(1)}, u32[]{:S(2)}, u32[]{:S(2)}) %collective-permute-start.23) | collective-permute-done | bytes 4136 | tf_op jit(solution)/shard_map/ppermute | solution.py:32
  129.7 1.4 %collective-permute-start.27 = (f32[1026]{0:T(1024)S(1)}, f32[1026]{0:T(1024)S(1)}, u32[]{:S(2)}, u32[]{:S(2)}) collective-permute-start(f32[1026]{0:T(1024)S(1)} %add.166), channel_id=1, source_target_pairs={{0,8},{1,9},{2,10},{3,11},{4,12},{5,13},{6,14},{7,15},{8,0},{9,1},... | collective-permute-start | bytes 12320 | tf_op jit(solution)/shard_map/ppermute | solution.py:32
  131.4 3.4 %collective-permute-done.27 = f32[1026]{0:T(1024)S(1)} collective-permute-done((f32[1026]{0:T(1024)S(1)}, f32[1026]{0:T(1024)S(1)}, u32[]{:S(2)}, u32[]{:S(2)}) %collective-permute-start.27) | collective-permute-done | bytes 4136 | tf_op jit(solution)/shard_map/ppermute | solution.py:32
  134.8 0.6 dynamic-slice_add_fusion
  135.4 0.5 slice.104
  135.9 2.0 %convert_reduce_fusion.gt = f32[64,1152]{1,0:T(8,128)S(1)} fusion(f16[16,64,1152]{2,1,0:T(8,128)(2,1)} %all-to-all-done), kind=kLoop, calls=%fused_computation | loop fusion | flops 2285568 | bytes 2654208 | tf_op jit(solution)/shard_map/reduce_sum | solution.py:266
  138.0 1.1 finish.1
  (76 shorter events, 1.6 us)
Async XLA Ops:
  0.6 15.3 %copy-start.1 = (bf16[256,1152]{1,0:T(8,128)(2,1)S(1)}, bf16[256,1152]{1,0:T(8,128)(2,1)}, u32[]{:S(2)}) copy-start(bf16[256,1152]{1,0:T(8,128)(2,1)} %param.5) | copy-start | bytes 1769476
  0.6 15.4 %copy-start = (bf16[256,1152]{1,0:T(8,128)(2,1)S(1)}, bf16[256,1152]{1,0:T(8,128)(2,1)}, u32[]{:S(2)}) copy-start(bf16[256,1152]{1,0:T(8,128)(2,1)} %param.4) | copy-start | bytes 1769476
  2.0 15.8 %collective-permute-start.1 = (bf16[128,1152]{1,0:T(8,128)(2,1)S(1)}, bf16[128,1152]{1,0:T(8,128)(2,1)S(1)}, u32[]{:S(2)}, u32[]{:S(2)}) collective-permute-start(bf16[128,1152]{1,0:T(8,128)(2,1)S(1)} %fusion.5.refs_6_), channel_id=1, source_target_pairs={{0,4},{1,5},{2,6},{3,7},{4,8},{5,9},{6,10},{7,11},{8,12},{9,13},{1... | collective-permute-start | bytes 884744 | tf_op jit(solution)/shard_map/ppermute | solution.py:32
  2.6 15.2 %collective-permute-start.2 = (bf16[128,1152]{1,0:T(8,128)(2,1)S(1)}, bf16[128,1152]{1,0:T(8,128)(2,1)S(1)}, u32[]{:S(2)}, u32[]{:S(2)}) collective-permute-start(bf16[128,1152]{1,0:T(8,128)(2,1)S(1)} %fusion.5.refs_6_), channel_id=1, source_target_pairs={{0,12},{1,13},{2,14},{3,15},{4,0},{5,1},{6,2},{7,3},{8,4},{9,5},{1... | collective-permute-start | bytes 884744 | tf_op jit(solution)/shard_map/ppermute | solution.py:32
  4.2 13.7 %collective-permute-start.3 = (bf16[128,1152]{1,0:T(8,128)(2,1)S(1)}, bf16[128,1152]{1,0:T(8,128)(2,1)}, u32[]{:S(2)}, u32[]{:S(2)}) collective-permute-start(bf16[128,1152]{1,0:T(8,128)(2,1)S(1)} %fusion.5.refs_6_), channel_id=1, source_target_pairs={{0,130},{1,131},{2,128},{3,129},{4,134},{5,135},{6,132},{7,133},{8... | collective-permute-start | bytes 884744 | tf_op jit(solution)/shard_map/ppermute | solution.py:32
  9.4 11.5 %collective-permute-start = (bf16[128,1152]{1,0:T(8,128)(2,1)S(1)}, bf16[128,1152]{1,0:T(8,128)(2,1)S(1)}, u32[]{:S(2)}, u32[]{:S(2)}) collective-permute-start(bf16[128,1152]{1,0:T(8,128)(2,1)S(1)} %fusion.3.refs_0_), channel_id=1, source_target_pairs={{0,16},{1,113},{2,18},{3,115},{4,20},{5,117},{6,22},{7,119},{8,24}... | collective-permute-start | bytes 884744 | tf_op jit(solution)/shard_map/ppermute | solution.py:32
  11.4 21.5 %collective-permute-start.6 = (bf16[64,1152]{1,0:T(8,128)(2,1)S(1)}, bf16[64,1152]{1,0:T(8,128)(2,1)S(1)}, u32[]{:S(2)}, u32[]{:S(2)}) collective-permute-start(bf16[64,1152]{1,0:T(8,128)(2,1)S(1)} %constant_dynamic-slice_fusion.1), channel_id=1, source_target_pairs={{0,64},{1,65},{2,66},{3,67},{4,68},{5,69},{6,70},{7,71},{8,72},{9,... | collective-permute-start | bytes 442376 | tf_op jit(solution)/shard_map/ppermute | solution.py:32
  20.9 11.9 %collective-permute-start.10 = (bf16[64,1152]{1,0:T(8,128)(2,1)S(1)}, bf16[64,1152]{1,0:T(8,128)(2,1)S(1)}, u32[]{:S(2)}, u32[]{:S(2)}) collective-permute-start(bf16[64,1152]{1,0:T(8,128)(2,1)S(1)} %slice.77), channel_id=1, source_target_pairs={{0,12},{1,13},{2,14},{3,15},{4,0},{5,1},{6,2},{7,3},{8,4},{9,5},{1... | collective-permute-start | bytes 442376 | tf_op jit(solution)/shard_map/ppermute | solution.py:32
  22.5 17.9 %collective-permute-start.4 = (bf16[128,1152]{1,0:T(8,128)(2,1)S(1)}, bf16[128,1152]{1,0:T(8,128)(2,1)S(1)}, u32[]{:S(2)}, u32[]{:S(2)}) collective-permute-start(bf16[128,1152]{1,0:T(8,128)(2,1)S(1)} %collective-permute-done.refs_1_), channel_id=1, source_target_pairs={{0,16},{1,113},{2,18},{3,115},{4,20},{5,117},{6,22},{7,119},{8,24}... | collective-permute-start | bytes 884744 | tf_op jit(solution)/shard_map/ppermute | solution.py:32
  26.6 13.8 %collective-permute-start.5 = (bf16[128,1152]{1,0:T(8,128)(2,1)S(1)}, bf16[128,1152]{1,0:T(8,128)(2,1)S(1)}, u32[]{:S(2)}, u32[]{:S(2)}) collective-permute-start(bf16[128,1152]{1,0:T(8,128)(2,1)S(1)} %collective-permute-done.refs_1_), channel_id=1, source_target_pairs={{0,32},{1,97},{2,34},{3,99},{4,36},{5,101},{6,38},{7,103},{8,40},{... | collective-permute-start | bytes 884744 | tf_op jit(solution)/shard_map/ppermute | solution.py:32
  29.8 10.6 %collective-permute-start.7 = (bf16[128,1152]{1,0:T(8,128)(2,1)}, bf16[128,1152]{1,0:T(8,128)(2,1)S(1)}, u32[]{:S(2)}, u32[]{:S(2)}) collective-permute-start(bf16[128,1152]{1,0:T(8,128)(2,1)} %collective-permute-done.3.refs_10_), channel_id=1, source_target_pairs={{0,4},{1,5},{2,6},{3,7},{4,8},{5,9},{6,10},{7,11},{8,12},{9,13},{1... | collective-permute-start | bytes 884744 | tf_op jit(solution)/shard_map/ppermute | solution.py:32
  32.9 8.4 %collective-permute-start.8 = (bf16[128,1152]{1,0:T(8,128)(2,1)}, bf16[128,1152]{1,0:T(8,128)(2,1)S(1)}, u32[]{:S(2)}, u32[]{:S(2)}) collective-permute-start(bf16[128,1152]{1,0:T(8,128)(2,1)} %collective-permute-done.3.refs_10_), channel_id=1, source_target_pairs={{0,12},{1,13},{2,14},{3,15},{4,0},{5,1},{6,2},{7,3},{8,4},{9,5},{1... | collective-permute-start | bytes 884744 | tf_op jit(solution)/shard_map/ppermute | solution.py:32
  32.9 0.7 copy-start.2
  33.5 6.9 %collective-permute-start.9 = (bf16[64,1152]{1,0:T(8,128)(2,1)}, bf16[64,1152]{1,0:T(8,128)(2,1)}, u32[]{:S(2)}, u32[]{:S(2)}) collective-permute-start(bf16[64,1152]{1,0:T(8,128)(2,1)} %slice.76), channel_id=1, source_target_pairs={{0,4},{1,5},{2,6},{3,7},{4,8},{5,9},{6,10},{7,11},{8,12},{9,13},{1... | collective-permute-start | bytes 442376 | tf_op jit(solution)/shard_map/ppermute | solution.py:32
  36.8 8.0 %copy-start.3 = (bf16[64,1152]{1,0:T(8,128)(2,1)S(1)}, bf16[64,1152]{1,0:T(8,128)(2,1)}, u32[]{:S(2)}) copy-start(bf16[64,1152]{1,0:T(8,128)(2,1)} %copy-done.2) | copy-start | bytes 442372
  41.3 10.7 %collective-permute-start.11 = (bf16[448,1152]{1,0:T(8,128)(2,1)S(1)}, bf16[448,1152]{1,0:T(8,128)(2,1)S(1)}, u32[]{:S(2)}, u32[]{:S(2)}) collective-permute-start(bf16[448,1152]{1,0:T(8,128)(2,1)S(1)} %pad_maximum_fusion), channel_id=1, source_target_pairs={{0,1},{1,0},{2,3},{3,2},{4,5},{5,4},{6,7},{7,6},{8,9},{9,8},{10,11... | collective-permute-start | bytes 3096584 | tf_op jit(solution)/shard_map/ppermute | solution.py:32
  41.5 6.7 %collective-permute-start.12 = (bf16[64,1152]{1,0:T(8,128)(2,1)S(1)}, bf16[64,1152]{1,0:T(8,128)(2,1)S(1)}, u32[]{:S(2)}, u32[]{:S(2)}) collective-permute-start(bf16[64,1152]{1,0:T(8,128)(2,1)S(1)} %slice.78), channel_id=1, source_target_pairs={{0,4},{1,5},{2,6},{3,7},{4,8},{5,9},{6,10},{7,11},{8,12},{9,13},{1... | collective-permute-start | bytes 442376 | tf_op jit(solution)/shard_map/ppermute | solution.py:32
  44.5 7.4 %collective-permute-start.13 = (bf16[64,1152]{1,0:T(8,128)(2,1)S(1)}, bf16[64,1152]{1,0:T(8,128)(2,1)S(1)}, u32[]{:S(2)}, u32[]{:S(2)}) collective-permute-start(bf16[64,1152]{1,0:T(8,128)(2,1)S(1)} %slice.79), channel_id=1, source_target_pairs={{0,12},{1,13},{2,14},{3,15},{4,0},{5,1},{6,2},{7,3},{8,4},{9,5},{1... | collective-permute-start | bytes 442376 | tf_op jit(solution)/shard_map/ppermute | solution.py:32
  52.0 6.9 %copy-start.5 = (f32[2]{0:T(128)S(1)}, f32[2]{0:T(128)}, u32[]{:S(2)}) copy-start(f32[2]{0:T(128)} %pad_maximum_fusion.12) | copy-start | bytes 28
  58.9 1.3 collective-permute-start.14
  60.4 3.7 %collective-permute-start.15 = (f32[2]{0:T(128)S(1)}, f32[2]{0:T(128)S(1)}, u32[]{:S(2)}, u32[]{:S(2)}) collective-permute-start(f32[2]{0:T(128)S(1)} %slice_add_fusion.1), channel_id=1, source_target_pairs={{0,16},{1,17},{2,18},{3,19},{4,20},{5,21},{6,22},{7,23},{8,24},{9,... | collective-permute-start | bytes 32 | tf_op jit(solution)/shard_map/ppermute | solution.py:32
  64.1 11.5 %collective-permute-start.17 = (f16[512,1152]{1,0:T(8,128)(2,1)S(1)}, f16[512,1152]{1,0:T(8,128)(2,1)}, u32[]{:S(2)}, u32[]{:S(2)}) collective-permute-start(f16[512,1152]{1,0:T(8,128)(2,1)S(1)} %convolution_convert_fusion.1), channel_id=1, source_target_pairs={{0,1},{1,0},{2,3},{3,2},{4,5},{5,4},{6,7},{7,6},{8,9},{9,8},{10,11... | collective-permute-start | bytes 3538952 | tf_op jit(solution)/shard_map/ppermute | solution.py:32
  64.3 11.3 %copy-start.6 = (bf16[1024,1152]{1,0:T(8,128)(2,1)S(1)}, bf16[1024,1152]{1,0:T(8,128)(2,1)}, u32[]{:S(2)}) copy-start(bf16[1024,1152]{1,0:T(8,128)(2,1)} %get-tuple-element.72) | copy-start | bytes 7077892
  64.3 11.3 %copy-start.7 = (bf16[1024,1024]{1,0:T(8,128)(2,1)S(1)}, bf16[1024,1024]{1,0:T(8,128)(2,1)}, u32[]{:S(2)}) copy-start(bf16[1024,1024]{1,0:T(8,128)(2,1)} %get-tuple-element.71) | copy-start | bytes 6291460
  71.1 4.4 %collective-permute-start.16 = (f32[2]{0:T(128)S(1)}, f32[2]{0:T(128)S(1)}, u32[]{:S(2)}, u32[]{:S(2)}) collective-permute-start(f32[2]{0:T(128)S(1)} %add.159), channel_id=1, source_target_pairs={{0,32},{1,33},{2,34},{3,35},{4,36},{5,37},{6,38},{7,39},{8,40},{9,... | collective-permute-start | bytes 32 | tf_op jit(solution)/shard_map/ppermute | solution.py:32
  78.6 7.8 %collective-permute-start.18 = (f32[2]{0:T(128)S(1)}, f32[2]{0:T(128)S(1)}, u32[]{:S(2)}, u32[]{:S(2)}) collective-permute-start(f32[2]{0:T(128)S(1)} %add.161), channel_id=1, source_target_pairs={{0,64},{1,65},{2,66},{3,67},{4,68},{5,69},{6,70},{7,71},{8,72},{9,... | collective-permute-start | bytes 32 | tf_op jit(solution)/shard_map/ppermute | solution.py:32
  81.7 54.2 %all-to-all-start = ((f16[16,64,1152]{2,1,0:T(8,128)(2,1)}), f16[16,64,1152]{2,1,0:T(8,128)(2,1)}, u32[]{:S(2)}, u32[]{:S(2)}) async-start(f16[16,64,1152]{2,1,0:T(8,128)(2,1)} %bitcast.37), calls=%async_computation | async-start | bytes 4718592 | tf_op jit(solution)/shard_map/all_to_all | solution.py:247
  86.6 44.7 %copy-start.4 = (f32[64]{0:T(128)S(1)}, f32[64]{0:T(128)}, u32[]{:S(2)}) copy-start(f32[64]{0:T(128)} %multiply_reduce-precision_fusion) | copy-start | bytes 772
  86.6 35.3 %collective-permute-start.24 = (f16[136,1152]{1,0:T(8,128)(2,1)S(1)}, f16[136,1152]{1,0:T(8,128)(2,1)S(1)}, u32[]{:S(2)}, u32[]{:S(2)}) collective-permute-start(f16[136,1152]{1,0:T(8,128)(2,1)S(1)} %pad_maximum_fusion.3), channel_id=1, source_target_pairs={{0,16},{1,113},{2,18},{3,115},{4,20},{5,117},{6,22},{7,119},{8,24}... | collective-permute-start | bytes 940040 | tf_op jit(solution)/shard_map/ppermute | solution.py:32
  88.4 33.5 %collective-permute-start.25 = (f16[136,1152]{1,0:T(8,128)(2,1)S(1)}, f16[136,1152]{1,0:T(8,128)(2,1)S(1)}, u32[]{:S(2)}, u32[]{:S(2)}) collective-permute-start(f16[136,1152]{1,0:T(8,128)(2,1)S(1)} %pad_maximum_fusion.4), channel_id=1, source_target_pairs={{0,32},{1,97},{2,34},{3,99},{4,36},{5,101},{6,38},{7,103},{8,40},{... | collective-permute-start | bytes 940040 | tf_op jit(solution)/shard_map/ppermute | solution.py:32
  90.5 30.6 %collective-permute-start.21 = (f16[136,1152]{1,0:T(8,128)(2,1)S(1)}, f16[136,1152]{1,0:T(8,128)(2,1)S(1)}, u32[]{:S(2)}, u32[]{:S(2)}) collective-permute-start(f16[136,1152]{1,0:T(8,128)(2,1)S(1)} %pad_maximum_fusion.2), channel_id=1, source_target_pairs={{0,48},{1,81},{2,50},{3,83},{4,52},{5,85},{6,54},{7,87},{8,56},{9,... | collective-permute-start | bytes 940040 | tf_op jit(solution)/shard_map/ppermute | solution.py:32
  94.1 18.3 %collective-permute-start.19 = (f32[1026]{0:T(1024)S(1)}, f32[1026]{0:T(1024)S(1)}, u32[]{:S(2)}, u32[]{:S(2)}) collective-permute-start(f32[1026]{0:T(1024)S(1)} %pad_maximum_fusion.9), channel_id=1, source_target_pairs={{0,2},{1,3},{2,0},{3,1},{4,6},{5,7},{6,4},{7,5},{8,10},{9,11},{10,... | collective-permute-start | bytes 12320 | tf_op jit(solution)/shard_map/ppermute | solution.py:32
  95.6 24.7 %collective-permute-start.20 = (f16[72,1152]{1,0:T(8,128)(2,1)S(1)}, f16[72,1152]{1,0:T(8,128)(2,1)S(1)}, u32[]{:S(2)}, u32[]{:S(2)}) collective-permute-start(f16[72,1152]{1,0:T(8,128)(2,1)S(1)} %pad_maximum_fusion.8), channel_id=1, source_target_pairs={{0,64},{1,65},{2,66},{3,67},{4,68},{5,69},{6,70},{7,71},{8,72},{9,... | collective-permute-start | bytes 497672 | tf_op jit(solution)/shard_map/ppermute | solution.py:32
  121.1 3.7 %collective-permute-start.22 = (f32[1026]{0:T(1024)S(1)}, f32[1026]{0:T(1024)S(1)}, u32[]{:S(2)}, u32[]{:S(2)}) collective-permute-start(f32[1026]{0:T(1024)S(1)} %fusion.46), channel_id=1, source_target_pairs={{0,4},{1,5},{2,6},{3,7},{4,0},{5,1},{6,2},{7,3},{8,12},{9,13},{10,... | collective-permute-start | bytes 12320 | tf_op jit(solution)/shard_map/ppermute | solution.py:32
  124.8 4.9 %collective-permute-start.23 = (f32[1026]{0:T(1024)S(1)}, f32[1026]{0:T(1024)S(1)}, u32[]{:S(2)}, u32[]{:S(2)}) collective-permute-start(f32[1026]{0:T(1024)S(1)} %add.165), channel_id=1, source_target_pairs={{0,130},{1,131},{2,128},{3,129},{4,134},{5,135},{6,132},{7,133},{8... | collective-permute-start | bytes 12320 | tf_op jit(solution)/shard_map/ppermute | solution.py:32
  129.7 5.2 %collective-permute-start.27 = (f32[1026]{0:T(1024)S(1)}, f32[1026]{0:T(1024)S(1)}, u32[]{:S(2)}, u32[]{:S(2)}) collective-permute-start(f32[1026]{0:T(1024)S(1)} %add.166), channel_id=1, source_target_pairs={{0,8},{1,9},{2,10},{3,11},{4,12},{5,13},{6,14},{7,15},{8,0},{9,1},... | collective-permute-start | bytes 12320 | tf_op jit(solution)/shard_map/ppermute | solution.py:32
  131.4 6.6 %collective-permute-start.26 = (f32[72,1152]{1,0:T(8,128)S(1)}, f32[72,1152]{1,0:T(8,128)S(1)}, u32[]{:S(2)}, u32[]{:S(2)}) collective-permute-start(f32[72,1152]{1,0:T(8,128)S(1)} %pad_maximum_fusion.1), channel_id=1, source_target_pairs={{0,1},{1,0},{2,3},{3,2},{4,5},{5,4},{6,7},{7,6},{8,9},{9,8},{10,11... | collective-permute-start | bytes 995336 | tf_op jit(solution)/shard_map/ppermute | solution.py:32

commit v7 on v6

--- a/solution.py
+++ b/solution.py
@@ -248,24 +248,22 @@
     both = both + send(both, fz=4)
     half = jnp.dot(weights[:512], texts, preferred_element_type=f32) + rows_met.astype(f32)
     flight = half[Q:].astype(f16)
-    both, half, flight = tied(both, half[:Q], flight)
+    both, half, flight = tied(both, half, flight)
     far = send(jnp.concatenate([flight[384:], loss_rows[3]]), dz=4)
     three, two, one = (
         send(jnp.concatenate([flight[(k - 1) * 128 : k * 128], loss_rows[k - 1]]), split_z=k) for k in (3, 2, 1)
     )
     plane = jnp.concatenate([lt.reshape(-1), both])
-    plane = plane + send(plane, fy=1)
-    plane, far, three = tied(plane, far, three)
-    for move in (dict(fx=1), dict(fy=3)):
+    for move in (dict(fy=1), dict(fx=1), dict(fy=3)):
         plane = plane + send(plane, **move)
+    plane, far, three, two, one = tied(plane, far, three, two, one)
     arrived = one.astype(f32) + two.astype(f32) + three.astype(f32)
     theirs = jnp.concatenate([lax.dynamic_slice_in_dim(arrived, (1 - core) * Q, Q, 0), arrived[128:]])
-    plane, far, arrived, theirs = tied(plane, far, arrived, theirs)
     met = send(theirs, fc=1)
     plane = plane + send(plane, fx=2)
     gt_own = jnp.sum(back_xy.reshape(16, Q, -1).astype(f32), axis=0)
     grad_image, grad_text, image_loss = finish(
-        half, far.astype(f32), arrived, met, gt_own, image_unit, text_unit, image_inv, text_inv,
+        half[:Q], far.astype(f32), arrived, met, gt_own, image_unit, text_unit, image_inv, text_inv,
         match_weight[:, None], (li_half[:Q] + match_loss)[None],
     )
     text_loss = lax.dynamic_slice_in_dim(plane, ((yh * 4 + x) * 2 + yl) * Q, Q, 0) + match_loss

time: 139 us -> 132 us (0.950)
  the two profiles are of different devices: /device:TPU:70 before, /device:TPU:1 now
where the time goes in v7:
time: 132 us; the launch traced here: 130 us
  starting transfers between devices  63.1 us (48%)
  waiting for transfers between devices  30.8 us (23%)
  other arithmetic  10.1 us (8%)
  matrix products  9.42 us (7%)
  Pallas kernels  7.57 us (6%)
  local copies, waits for them, and re-layouts  6.17 us (5%)
  between operations  3.03 us (2%)
    ppermute x28, starting transfers between devices, send(): return lax.ppermute(value, AXES, pairs)  58.5 us
    ppermute x28, waiting for transfers between devices, send(): return lax.ppermute(value, AXES, pairs)  30.8 us
    pallas_call x1, Pallas kernels, pairs_on_device(): pl.pallas_call(pair_kernel, out_shape=(pltpu.HBM((1024, 1024), jnp.bfloat...  6.51 us
    all_to_all x1, starting transfers between devices, per_device(): back_xy = lax.all_to_all(gt16, ('yh', 'x', 'yl'), 0, 0, tiled=True)  4.66 us
    dot_general x1, matrix products, per_device(): lax.dot_general(weights, images, (((0,), (0,)), ((), ())), preferred_elem...  4.24 us
    dot_general x1, matrix products, per_device(): jnp.dot(weights[512:], texts, preferred_element_type=f32).astype(f16)  3.65 us
  transfers between devices with their start and end apart: 29, of which 8 were waited for; matrix products, arithmetic and copies ran while one was open for 15% of the time, Pallas kernels for 0%

profile of v7, /device:TPU:1, one launch (start us, length us, event | category | flops | bytes accessed | tf_op | source)
XLA Modules:
  0.0 130.2 jit_solution(13286665605179509818)
XLA Ops:
  0.7 1.1 constant_dynamic-slice_fusion.3
  1.8 0.1 fusion.4
  1.9 0.1 fusion.5.refs_6_
  2.0 2.1 %collective-permute-start.1 = (bf16[128,1152]{1,0:T(8,128)(2,1)S(1)}, bf16[128,1152]{1,0:T(8,128)(2,1)S(1)}, u32[]{:S(2)}, u32[]{:S(2)}) collective-permute-start(bf16[128,1152]{1,0:T(8,128)(2,1)S(1)} %fusion.5.refs_6_), channel_id=1, source_target_pairs={{0,4},{1,5},{2,6},{3,7},{4,8},{5,9},{6,10},{7,11},{8,12},{9,13},{1... | collective-permute-start | bytes 884744 | tf_op jit(solution)/shard_map/ppermute | solution.py:32
  4.2 1.4 %collective-permute-start.2 = (bf16[128,1152]{1,0:T(8,128)(2,1)S(1)}, bf16[128,1152]{1,0:T(8,128)(2,1)S(1)}, u32[]{:S(2)}, u32[]{:S(2)}) collective-permute-start(bf16[128,1152]{1,0:T(8,128)(2,1)S(1)} %fusion.5.refs_6_), channel_id=1, source_target_pairs={{0,12},{1,13},{2,14},{3,15},{4,0},{5,1},{6,2},{7,3},{8,4},{9,5},{1... | collective-permute-start | bytes 884744 | tf_op jit(solution)/shard_map/ppermute | solution.py:32
  5.5 2.8 %collective-permute-start.3 = (bf16[128,1152]{1,0:T(8,128)(2,1)S(1)}, bf16[128,1152]{1,0:T(8,128)(2,1)}, u32[]{:S(2)}, u32[]{:S(2)}) collective-permute-start(bf16[128,1152]{1,0:T(8,128)(2,1)S(1)} %fusion.5.refs_6_), channel_id=1, source_target_pairs={{0,130},{1,131},{2,128},{3,129},{4,134},{5,135},{6,132},{7,133},{8... | collective-permute-start | bytes 884744 | tf_op jit(solution)/shard_map/ppermute | solution.py:32
  8.4 1.1 fusion.2
  9.5 1.1 fusion.3.refs_0_
  10.6 5.7 %collective-permute-start = (bf16[128,1152]{1,0:T(8,128)(2,1)S(1)}, bf16[128,1152]{1,0:T(8,128)(2,1)S(1)}, u32[]{:S(2)}, u32[]{:S(2)}) collective-permute-start(bf16[128,1152]{1,0:T(8,128)(2,1)S(1)} %fusion.3.refs_0_), channel_id=1, source_target_pairs={{0,16},{1,113},{2,18},{3,115},{4,20},{5,117},{6,22},{7,119},{8,24}... | collective-permute-start | bytes 884744 | tf_op jit(solution)/shard_map/ppermute | solution.py:32
  16.2 1.5 %collective-permute-start.6 = (bf16[64,1152]{1,0:T(8,128)(2,1)S(1)}, bf16[64,1152]{1,0:T(8,128)(2,1)S(1)}, u32[]{:S(2)}, u32[]{:S(2)}) collective-permute-start(bf16[64,1152]{1,0:T(8,128)(2,1)S(1)} %constant_dynamic-slice_fusion.1), channel_id=1, source_target_pairs={{0,64},{1,65},{2,66},{3,67},{4,68},{5,69},{6,70},{7,71},{8,72},{9,... | collective-permute-start | bytes 442376 | tf_op jit(solution)/shard_map/ppermute | solution.py:32
  17.7 0.1 fusion.7
  17.8 0.1 fusion.6
  19.3 0.2 multiply_reduce_fusion
  19.6 6.6 %collective-permute-done.refs_1_ = bf16[128,1152]{1,0:T(8,128)(2,1)S(1)} collective-permute-done((bf16[128,1152]{1,0:T(8,128)(2,1)S(1)}, bf16[128,1152]{1,0:T(8,128)(2,1)S(1)}, u32[]{:S(2)}, u32[]{:S(2)}) %collective-permute-start) | collective-permute-done | bytes 294944 | tf_op jit(solution)/shard_map/ppermute | solution.py:32
  26.2 1.3 %collective-permute-start.10 = (bf16[64,1152]{1,0:T(8,128)(2,1)S(1)}, bf16[64,1152]{1,0:T(8,128)(2,1)S(1)}, u32[]{:S(2)}, u32[]{:S(2)}) collective-permute-start(bf16[64,1152]{1,0:T(8,128)(2,1)S(1)} %slice.77), channel_id=1, source_target_pairs={{0,12},{1,13},{2,14},{3,15},{4,0},{5,1},{6,2},{7,3},{8,4},{9,5},{1... | collective-permute-start | bytes 442376 | tf_op jit(solution)/shard_map/ppermute | solution.py:32
  27.6 0.6 multiply_reduce_fusion.1
  28.2 3.4 %collective-permute-start.4 = (bf16[128,1152]{1,0:T(8,128)(2,1)S(1)}, bf16[128,1152]{1,0:T(8,128)(2,1)S(1)}, u32[]{:S(2)}, u32[]{:S(2)}) collective-permute-start(bf16[128,1152]{1,0:T(8,128)(2,1)S(1)} %collective-permute-done.refs_1_), channel_id=1, source_target_pairs={{0,16},{1,113},{2,18},{3,115},{4,20},{5,117},{6,22},{7,119},{8,24}... | collective-permute-start | bytes 884744 | tf_op jit(solution)/shard_map/ppermute | solution.py:32
  31.6 0.7 slice.76
  32.3 2.7 %collective-permute-start.8 = (bf16[128,1152]{1,0:T(8,128)(2,1)}, bf16[128,1152]{1,0:T(8,128)(2,1)S(1)}, u32[]{:S(2)}, u32[]{:S(2)}) collective-permute-start(bf16[128,1152]{1,0:T(8,128)(2,1)} %collective-permute-done.3.refs_10_), channel_id=1, source_target_pairs={{0,12},{1,13},{2,14},{3,15},{4,0},{5,1},{6,2},{7,3},{8,4},{9,5},{1... | collective-permute-start | bytes 884744 | tf_op jit(solution)/shard_map/ppermute | solution.py:32
  35.0 0.7 copy-done.3
  35.6 0.6 multiply_reduce-precision_fusion
  36.9 1.3 pad_maximum_fusion.12
  38.2 4.9 %collective-permute-done.9 = bf16[64,1152]{1,0:T(8,128)(2,1)} collective-permute-done((bf16[64,1152]{1,0:T(8,128)(2,1)}, bf16[64,1152]{1,0:T(8,128)(2,1)}, u32[]{:S(2)}, u32[]{:S(2)}) %collective-permute-start.9) | collective-permute-done | bytes 147488 | tf_op jit(solution)/shard_map/ppermute | solution.py:32
  43.1 2.8 %collective-permute-start.11 = (bf16[448,1152]{1,0:T(8,128)(2,1)S(1)}, bf16[448,1152]{1,0:T(8,128)(2,1)S(1)}, u32[]{:S(2)}, u32[]{:S(2)}) collective-permute-start(bf16[448,1152]{1,0:T(8,128)(2,1)S(1)} %pad_maximum_fusion), channel_id=1, source_target_pairs={{0,1},{1,0},{2,3},{3,2},{4,5},{5,4},{6,7},{7,6},{8,9},{9,8},{10,11... | collective-permute-start | bytes 3096584 | tf_op jit(solution)/shard_map/ppermute | solution.py:32
  46.1 2.9 %collective-permute-start.13 = (bf16[64,1152]{1,0:T(8,128)(2,1)S(1)}, bf16[64,1152]{1,0:T(8,128)(2,1)S(1)}, u32[]{:S(2)}, u32[]{:S(2)}) collective-permute-start(bf16[64,1152]{1,0:T(8,128)(2,1)S(1)} %slice.79), channel_id=1, source_target_pairs={{0,12},{1,13},{2,14},{3,15},{4,0},{5,1},{6,2},{7,3},{8,4},{9,5},{1... | collective-permute-start | bytes 442376 | tf_op jit(solution)/shard_map/ppermute | solution.py:32
  49.1 0.9 pad_maximum_fusion.6.refs_9_
  50.0 2.8 %collective-permute-done.12 = bf16[64,1152]{1,0:T(8,128)(2,1)S(1)} collective-permute-done((bf16[64,1152]{1,0:T(8,128)(2,1)S(1)}, bf16[64,1152]{1,0:T(8,128)(2,1)S(1)}, u32[]{:S(2)}, u32[]{:S(2)}) %collective-permute-start.12) | collective-permute-done | bytes 147488 | tf_op jit(solution)/shard_map/ppermute | solution.py:32
  52.8 6.5 %pairs.1 = (bf16[1024,1024]{1,0:T(8,128)(2,1)}, bf16[1024,1152]{1,0:T(8,128)(2,1)}, bf16[1024,1152]{1,0:T(8,128)(2,1)}, f32[1024,1]{1,0:T(8,128)S(1)}, f32[1,1024]{1,0:T(1,128)S(1)}, /*index=5*/f32[2,1024]{1,0:T(2,128)S(1)}) custom-call(f32[2]{0:T(128)S(1)} %pad_maximum_fusion.11.par_ref, bf16[128,1152]{1,0:T(8,128)(2,1)S(1)} %fusion.3.refs_0_, ...), custom_call_target="tpu_custom_call" | custom-call | flops 2415919104 | bytes 12582912 | tf_op jit(solution)/shard_map/pairs/pallas_call | solution.py:125
  59.3 0.2 slice_reduce_fusion
  59.6 0.1 reduce_sum.88
  59.7 0.9 collective-permute-start.14
  60.6 0.8 collective-permute-done.14
  61.5 0.1 fusion.38
  61.6 2.3 %collective-permute-start.15 = (f32[2]{0:T(128)S(1)}, f32[2]{0:T(128)S(1)}, u32[]{:S(2)}, u32[]{:S(2)}) collective-permute-start(f32[2]{0:T(128)S(1)} %slice_add_fusion.1), channel_id=1, source_target_pairs={{0,16},{1,17},{2,18},{3,19},{4,20},{5,21},{6,22},{7,23},{8,24},{9,... | collective-permute-start | bytes 32 | tf_op jit(solution)/shard_map/ppermute | solution.py:32
  64.0 3.6 %convolution_convert_fusion.1 = f16[512,1152]{1,0:T(8,128)(2,1)S(1)} fusion(bf16[1024,1152]{1,0:T(8,128)(2,1)} %get-tuple-element.70, bf16[1024,1024]{1,0:T(8,128)(2,1)} %get-tuple-element.69), kind=kOutput, calls=%fused_computation.3 | convolution fusion | flops 1208549376 | bytes 4587520 | tf_op jit(solution)/shard_map/dot_general | solution.py:237
  67.7 0.7 collective-permute-start.17
  68.4 4.2 %convolution_convert_fusion = f16[1024,1152]{1,0:T(8,128)(2,1)} fusion(bf16[1024,1024]{1,0:T(8,128)(2,1)S(1)} %copy-done.8, bf16[1024,1152]{1,0:T(8,128)(2,1)S(1)} %copy-done.9), kind=kOutput, calls=%fused_computation.1 | convolution fusion | flops 2417098752 | bytes 6815744 | tf_op jit(solution)/shard_map/dot_general | solution.py:243
  72.7 3.3 %collective-permute-done.16 = f32[2]{0:T(128)S(1)} collective-permute-done((f32[2]{0:T(128)S(1)}, f32[2]{0:T(128)S(1)}, u32[]{:S(2)}, u32[]{:S(2)}) %collective-permute-start.16) | collective-permute-done | bytes 40 | tf_op jit(solution)/shard_map/ppermute | solution.py:32
  76.0 1.5 %convolution_add_fusion = f32[512,1152]{1,0:T(8,128)S(1)} fusion(bf16[1024,1152]{1,0:T(8,128)(2,1)S(1)} %copy-done.7, f16[512,1152]{1,0:T(8,128)(2,1)S(1)} %collective-permute-done.17, bf16[1024,1024]{1,0:T(8,128)(2,1)S(1)} %copy-done.8), kind=kOutput, calls=%fused_computation.2 | convolution fusion | flops 1209139200 | bytes 6946816 | tf_op jit(solution)/shard_map/dot_general | solution.py:249
  77.5 1.4 %copy-done = f32[512,1152]{1,0:T(8,128)} copy-done((f32[512,1152]{1,0:T(8,128)}, f32[512,1152]{1,0:T(8,128)S(1)}, u32[]{:S(2)}) %copy-start) | copy-done | bytes 2359320
  78.9 0.1 slice_convert_fusion
  79.1 3.1 %collective-permute-start.18 = (f32[2]{0:T(128)S(1)}, f32[2]{0:T(128)S(1)}, u32[]{:S(2)}, u32[]{:S(2)}) collective-permute-start(f32[2]{0:T(128)S(1)} %add.161), channel_id=1, source_target_pairs={{0,64},{1,65},{2,66},{3,67},{4,68},{5,69},{6,70},{7,71},{8,72},{9,... | collective-permute-start | bytes 32 | tf_op jit(solution)/shard_map/ppermute | solution.py:32
  82.2 4.7 %all-to-all-start = ((f16[16,64,1152]{2,1,0:T(8,128)(2,1)}), f16[16,64,1152]{2,1,0:T(8,128)(2,1)}, u32[]{:S(2)}, u32[]{:S(2)}) async-start(f16[16,64,1152]{2,1,0:T(8,128)(2,1)} %bitcast.37), calls=%async_computation | async-start | bytes 4718592 | tf_op jit(solution)/shard_map/all_to_all | solution.py:247
  86.9 0.2 fusion.49
  87.2 0.7 collective-permute-start.25
  88.0 0.6 collective-permute-start.24
  88.7 2.5 %collective-permute-start.23 = (f16[136,1152]{1,0:T(8,128)(2,1)S(1)}, f16[136,1152]{1,0:T(8,128)(2,1)S(1)}, u32[]{:S(2)}, u32[]{:S(2)}) collective-permute-start(f16[136,1152]{1,0:T(8,128)(2,1)S(1)} %pad_maximum_fusion.2), channel_id=1, source_target_pairs={{0,48},{1,81},{2,50},{3,83},{4,52},{5,85},{6,54},{7,87},{8,56},{9,... | collective-permute-start | bytes 940040 | tf_op jit(solution)/shard_map/ppermute | solution.py:32
  91.2 1.1 collective-permute-start.19
  92.3 2.5 %collective-permute-start.22 = (f16[72,1152]{1,0:T(8,128)(2,1)S(1)}, f16[72,1152]{1,0:T(8,128)(2,1)S(1)}, u32[]{:S(2)}, u32[]{:S(2)}) collective-permute-start(f16[72,1152]{1,0:T(8,128)(2,1)S(1)} %pad_maximum_fusion.8), channel_id=1, source_target_pairs={{0,64},{1,65},{2,66},{3,67},{4,68},{5,69},{6,70},{7,71},{8,72},{9,... | collective-permute-start | bytes 497672 | tf_op jit(solution)/shard_map/ppermute | solution.py:32
  94.8 5.3 %collective-permute-done.19 = f32[1026]{0:T(1024)S(1)} collective-permute-done((f32[1026]{0:T(1024)S(1)}, f32[1026]{0:T(1024)S(1)}, u32[]{:S(2)}, u32[]{:S(2)}) %collective-permute-start.19) | collective-permute-done | bytes 4136 | tf_op jit(solution)/shard_map/ppermute | solution.py:32
  100.1 8.7 %collective-permute-start.20 = (f32[1026]{0:T(1024)S(1)}, f32[1026]{0:T(1024)S(1)}, u32[]{:S(2)}, u32[]{:S(2)}) collective-permute-start(f32[1026]{0:T(1024)S(1)} %fusion.46), channel_id=1, source_target_pairs={{0,4},{1,5},{2,6},{3,7},{4,0},{5,1},{6,2},{7,3},{8,12},{9,13},{10,... | collective-permute-start | bytes 12320 | tf_op jit(solution)/shard_map/ppermute | solution.py:32
  108.9 5.5 %collective-permute-done.20 = f32[1026]{0:T(1024)S(1)} collective-permute-done((f32[1026]{0:T(1024)S(1)}, f32[1026]{0:T(1024)S(1)}, u32[]{:S(2)}, u32[]{:S(2)}) %collective-permute-start.20) | collective-permute-done | bytes 4136 | tf_op jit(solution)/shard_map/ppermute | solution.py:32
  114.4 1.3 %collective-permute-start.21 = (f32[1026]{0:T(1024)S(1)}, f32[1026]{0:T(1024)S(1)}, u32[]{:S(2)}, u32[]{:S(2)}) collective-permute-start(f32[1026]{0:T(1024)S(1)} %add.165), channel_id=1, source_target_pairs={{0,130},{1,131},{2,128},{3,129},{4,134},{5,135},{6,132},{7,133},{8... | collective-permute-start | bytes 12320 | tf_op jit(solution)/shard_map/ppermute | solution.py:32
  115.7 0.1 copy.12.image_inv
  115.8 0.1 copy.13.text_inv
  116.0 1.0 slice.93.half
  117.0 1.5 %collective-permute-done.21 = f32[1026]{0:T(1024)S(1)} collective-permute-done((f32[1026]{0:T(1024)S(1)}, f32[1026]{0:T(1024)S(1)}, u32[]{:S(2)}, u32[]{:S(2)}) %collective-permute-start.21) | collective-permute-done | bytes 4136 | tf_op jit(solution)/shard_map/ppermute | solution.py:32
  118.5 2.4 %collective-permute-start.27 = (f32[1026]{0:T(1024)S(1)}, f32[1026]{0:T(1024)S(1)}, u32[]{:S(2)}, u32[]{:S(2)}) collective-permute-start(f32[1026]{0:T(1024)S(1)} %add.166), channel_id=1, source_target_pairs={{0,8},{1,9},{2,10},{3,11},{4,12},{5,13},{6,14},{7,15},{8,0},{9,1},... | collective-permute-start | bytes 12320 | tf_op jit(solution)/shard_map/ppermute | solution.py:32
  120.9 0.1 convert_add_fusion.arrived
  121.1 4.8 %collective-permute-start.26 = (f32[72,1152]{1,0:T(8,128)S(1)}, f32[72,1152]{1,0:T(8,128)S(1)}, u32[]{:S(2)}, u32[]{:S(2)}) collective-permute-start(f32[72,1152]{1,0:T(8,128)S(1)} %pad_maximum_fusion.1), channel_id=1, source_target_pairs={{0,1},{1,0},{2,3},{3,2},{4,5},{5,4},{6,7},{7,6},{8,9},{9,8},{10,11... | collective-permute-start | bytes 995336 | tf_op jit(solution)/shard_map/ppermute | solution.py:32
  126.0 0.6 dynamic-slice_add_fusion
  126.6 0.5 slice.103
  127.1 2.0 %convert_reduce_fusion.gt = f32[64,1152]{1,0:T(8,128)S(1)} fusion(f16[16,64,1152]{2,1,0:T(8,128)(2,1)} %all-to-all-done), kind=kLoop, calls=%fused_computation | loop fusion | flops 2285568 | bytes 2654208 | tf_op jit(solution)/shard_map/reduce_sum | solution.py:264
  129.2 1.1 finish.1
  (80 shorter events, 1.1 us)
Async XLA Ops:
  0.6 17.1 %copy-start.2 = (bf16[256,1152]{1,0:T(8,128)(2,1)S(1)}, bf16[256,1152]{1,0:T(8,128)(2,1)}, u32[]{:S(2)}) copy-start(bf16[256,1152]{1,0:T(8,128)(2,1)} %param.5) | copy-start | bytes 1769476
  0.6 17.2 %copy-start.1 = (bf16[256,1152]{1,0:T(8,128)(2,1)S(1)}, bf16[256,1152]{1,0:T(8,128)(2,1)}, u32[]{:S(2)}) copy-start(bf16[256,1152]{1,0:T(8,128)(2,1)} %param.4) | copy-start | bytes 1769476
  2.0 17.5 %collective-permute-start.1 = (bf16[128,1152]{1,0:T(8,128)(2,1)S(1)}, bf16[128,1152]{1,0:T(8,128)(2,1)S(1)}, u32[]{:S(2)}, u32[]{:S(2)}) collective-permute-start(bf16[128,1152]{1,0:T(8,128)(2,1)S(1)} %fusion.5.refs_6_), channel_id=1, source_target_pairs={{0,4},{1,5},{2,6},{3,7},{4,8},{5,9},{6,10},{7,11},{8,12},{9,13},{1... | collective-permute-start | bytes 884744 | tf_op jit(solution)/shard_map/ppermute | solution.py:32
  4.2 15.4 %collective-permute-start.2 = (bf16[128,1152]{1,0:T(8,128)(2,1)S(1)}, bf16[128,1152]{1,0:T(8,128)(2,1)S(1)}, u32[]{:S(2)}, u32[]{:S(2)}) collective-permute-start(bf16[128,1152]{1,0:T(8,128)(2,1)S(1)} %fusion.5.refs_6_), channel_id=1, source_target_pairs={{0,12},{1,13},{2,14},{3,15},{4,0},{5,1},{6,2},{7,3},{8,4},{9,5},{1... | collective-permute-start | bytes 884744 | tf_op jit(solution)/shard_map/ppermute | solution.py:32
  5.5 14.1 %collective-permute-start.3 = (bf16[128,1152]{1,0:T(8,128)(2,1)S(1)}, bf16[128,1152]{1,0:T(8,128)(2,1)}, u32[]{:S(2)}, u32[]{:S(2)}) collective-permute-start(bf16[128,1152]{1,0:T(8,128)(2,1)S(1)} %fusion.5.refs_6_), channel_id=1, source_target_pairs={{0,130},{1,131},{2,128},{3,129},{4,134},{5,135},{6,132},{7,133},{8... | collective-permute-start | bytes 884744 | tf_op jit(solution)/shard_map/ppermute | solution.py:32
  10.6 15.6 %collective-permute-start = (bf16[128,1152]{1,0:T(8,128)(2,1)S(1)}, bf16[128,1152]{1,0:T(8,128)(2,1)S(1)}, u32[]{:S(2)}, u32[]{:S(2)}) collective-permute-start(bf16[128,1152]{1,0:T(8,128)(2,1)S(1)} %fusion.3.refs_0_), channel_id=1, source_target_pairs={{0,16},{1,113},{2,18},{3,115},{4,20},{5,117},{6,22},{7,119},{8,24}... | collective-permute-start | bytes 884744 | tf_op jit(solution)/shard_map/ppermute | solution.py:32
  16.2 16.1 %collective-permute-start.6 = (bf16[64,1152]{1,0:T(8,128)(2,1)S(1)}, bf16[64,1152]{1,0:T(8,128)(2,1)S(1)}, u32[]{:S(2)}, u32[]{:S(2)}) collective-permute-start(bf16[64,1152]{1,0:T(8,128)(2,1)S(1)} %constant_dynamic-slice_fusion.1), channel_id=1, source_target_pairs={{0,64},{1,65},{2,66},{3,67},{4,68},{5,69},{6,70},{7,71},{8,72},{9,... | collective-permute-start | bytes 442376 | tf_op jit(solution)/shard_map/ppermute | solution.py:32
  26.2 8.8 %collective-permute-start.10 = (bf16[64,1152]{1,0:T(8,128)(2,1)S(1)}, bf16[64,1152]{1,0:T(8,128)(2,1)S(1)}, u32[]{:S(2)}, u32[]{:S(2)}) collective-permute-start(bf16[64,1152]{1,0:T(8,128)(2,1)S(1)} %slice.77), channel_id=1, source_target_pairs={{0,12},{1,13},{2,14},{3,15},{4,0},{5,1},{6,2},{7,3},{8,4},{9,5},{1... | collective-permute-start | bytes 442376 | tf_op jit(solution)/shard_map/ppermute | solution.py:32
  28.2 14.8 %collective-permute-start.4 = (bf16[128,1152]{1,0:T(8,128)(2,1)S(1)}, bf16[128,1152]{1,0:T(8,128)(2,1)S(1)}, u32[]{:S(2)}, u32[]{:S(2)}) collective-permute-start(bf16[128,1152]{1,0:T(8,128)(2,1)S(1)} %collective-permute-done.refs_1_), channel_id=1, source_target_pairs={{0,16},{1,113},{2,18},{3,115},{4,20},{5,117},{6,22},{7,119},{8,24}... | collective-permute-start | bytes 884744 | tf_op jit(solution)/shard_map/ppermute | solution.py:32
  31.6 11.4 %collective-permute-start.5 = (bf16[128,1152]{1,0:T(8,128)(2,1)S(1)}, bf16[128,1152]{1,0:T(8,128)(2,1)S(1)}, u32[]{:S(2)}, u32[]{:S(2)}) collective-permute-start(bf16[128,1152]{1,0:T(8,128)(2,1)S(1)} %collective-permute-done.refs_1_), channel_id=1, source_target_pairs={{0,32},{1,97},{2,34},{3,99},{4,36},{5,101},{6,38},{7,103},{8,40},{... | collective-permute-start | bytes 884744 | tf_op jit(solution)/shard_map/ppermute | solution.py:32
  31.6 11.4 %collective-permute-start.7 = (bf16[128,1152]{1,0:T(8,128)(2,1)}, bf16[128,1152]{1,0:T(8,128)(2,1)S(1)}, u32[]{:S(2)}, u32[]{:S(2)}) collective-permute-start(bf16[128,1152]{1,0:T(8,128)(2,1)} %collective-permute-done.3.refs_10_), channel_id=1, source_target_pairs={{0,4},{1,5},{2,6},{3,7},{4,8},{5,9},{6,10},{7,11},{8,12},{9,13},{1... | collective-permute-start | bytes 884744 | tf_op jit(solution)/shard_map/ppermute | solution.py:32
  32.3 10.7 %collective-permute-start.8 = (bf16[128,1152]{1,0:T(8,128)(2,1)}, bf16[128,1152]{1,0:T(8,128)(2,1)S(1)}, u32[]{:S(2)}, u32[]{:S(2)}) collective-permute-start(bf16[128,1152]{1,0:T(8,128)(2,1)} %collective-permute-done.3.refs_10_), channel_id=1, source_target_pairs={{0,12},{1,13},{2,14},{3,15},{4,0},{5,1},{6,2},{7,3},{8,4},{9,5},{1... | collective-permute-start | bytes 884744 | tf_op jit(solution)/shard_map/ppermute | solution.py:32
  35.0 0.7 copy-start.3
  35.6 7.4 %collective-permute-start.9 = (bf16[64,1152]{1,0:T(8,128)(2,1)}, bf16[64,1152]{1,0:T(8,128)(2,1)}, u32[]{:S(2)}, u32[]{:S(2)}) collective-permute-start(bf16[64,1152]{1,0:T(8,128)(2,1)} %slice.76), channel_id=1, source_target_pairs={{0,4},{1,5},{2,6},{3,7},{4,8},{5,9},{6,10},{7,11},{8,12},{9,13},{1... | collective-permute-start | bytes 442376 | tf_op jit(solution)/shard_map/ppermute | solution.py:32
  35.6 13.4 %copy-start.4 = (bf16[64,1152]{1,0:T(8,128)(2,1)S(1)}, bf16[64,1152]{1,0:T(8,128)(2,1)}, u32[]{:S(2)}) copy-start(bf16[64,1152]{1,0:T(8,128)(2,1)} %copy-done.3) | copy-start | bytes 442372
  43.1 9.7 %collective-permute-start.11 = (bf16[448,1152]{1,0:T(8,128)(2,1)S(1)}, bf16[448,1152]{1,0:T(8,128)(2,1)S(1)}, u32[]{:S(2)}, u32[]{:S(2)}) collective-permute-start(bf16[448,1152]{1,0:T(8,128)(2,1)S(1)} %pad_maximum_fusion), channel_id=1, source_target_pairs={{0,1},{1,0},{2,3},{3,2},{4,5},{5,4},{6,7},{7,6},{8,9},{9,8},{10,11... | collective-permute-start | bytes 3096584 | tf_op jit(solution)/shard_map/ppermute | solution.py:32
  46.0 6.8 %collective-permute-start.12 = (bf16[64,1152]{1,0:T(8,128)(2,1)S(1)}, bf16[64,1152]{1,0:T(8,128)(2,1)S(1)}, u32[]{:S(2)}, u32[]{:S(2)}) collective-permute-start(bf16[64,1152]{1,0:T(8,128)(2,1)S(1)} %slice.78), channel_id=1, source_target_pairs={{0,4},{1,5},{2,6},{3,7},{4,8},{5,9},{6,10},{7,11},{8,12},{9,13},{1... | collective-permute-start | bytes 442376 | tf_op jit(solution)/shard_map/ppermute | solution.py:32
  46.1 6.6 %collective-permute-start.13 = (bf16[64,1152]{1,0:T(8,128)(2,1)S(1)}, bf16[64,1152]{1,0:T(8,128)(2,1)S(1)}, u32[]{:S(2)}, u32[]{:S(2)}) collective-permute-start(bf16[64,1152]{1,0:T(8,128)(2,1)S(1)} %slice.79), channel_id=1, source_target_pairs={{0,12},{1,13},{2,14},{3,15},{4,0},{5,1},{6,2},{7,3},{8,4},{9,5},{1... | collective-permute-start | bytes 442376 | tf_op jit(solution)/shard_map/ppermute | solution.py:32
  52.8 6.9 %copy-start.6 = (f32[2]{0:T(128)S(1)}, f32[2]{0:T(128)}, u32[]{:S(2)}) copy-start(f32[2]{0:T(128)} %pad_maximum_fusion.12) | copy-start | bytes 28
  59.7 1.7 %collective-permute-start.14 = (f32[514]{0:T(1024)S(1)}, f32[514]{0:T(1024)S(1)}, u32[]{:S(2)}, u32[]{:S(2)}) collective-permute-start(f32[514]{0:T(1024)S(1)} %pad_maximum_fusion.10), channel_id=1, source_target_pairs={{0,1},{1,0},{2,3},{3,2},{4,5},{5,4},{6,7},{7,6},{8,9},{9,8},{10,11... | collective-permute-start | bytes 6176 | tf_op jit(solution)/shard_map/ppermute | solution.py:32
  61.6 6.0 %collective-permute-start.15 = (f32[2]{0:T(128)S(1)}, f32[2]{0:T(128)S(1)}, u32[]{:S(2)}, u32[]{:S(2)}) collective-permute-start(f32[2]{0:T(128)S(1)} %slice_add_fusion.1), channel_id=1, source_target_pairs={{0,16},{1,17},{2,18},{3,19},{4,20},{5,21},{6,22},{7,23},{8,24},{9,... | collective-permute-start | bytes 32 | tf_op jit(solution)/shard_map/ppermute | solution.py:32
  64.0 4.4 %copy-start.8 = (bf16[1024,1024]{1,0:T(8,128)(2,1)S(1)}, bf16[1024,1024]{1,0:T(8,128)(2,1)}, u32[]{:S(2)}) copy-start(bf16[1024,1024]{1,0:T(8,128)(2,1)} %get-tuple-element.69) | copy-start | bytes 6291460
  64.0 4.4 %copy-start.9 = (bf16[1024,1152]{1,0:T(8,128)(2,1)S(1)}, bf16[1024,1152]{1,0:T(8,128)(2,1)}, u32[]{:S(2)}) copy-start(bf16[1024,1152]{1,0:T(8,128)(2,1)} %get-tuple-element.72) | copy-start | bytes 7077892
  67.7 8.3 %collective-permute-start.17 = (f16[512,1152]{1,0:T(8,128)(2,1)S(1)}, f16[512,1152]{1,0:T(8,128)(2,1)S(1)}, u32[]{:S(2)}, u32[]{:S(2)}) collective-permute-start(f16[512,1152]{1,0:T(8,128)(2,1)S(1)} %convolution_convert_fusion.1), channel_id=1, source_target_pairs={{0,1},{1,0},{2,3},{3,2},{4,5},{5,4},{6,7},{7,6},{8,9},{9,8},{10,11... | collective-permute-start | bytes 3538952 | tf_op jit(solution)/shard_map/ppermute | solution.py:32
  68.4 7.5 %copy-start.7 = (bf16[1024,1152]{1,0:T(8,128)(2,1)S(1)}, bf16[1024,1152]{1,0:T(8,128)(2,1)}, u32[]{:S(2)}) copy-start(bf16[1024,1152]{1,0:T(8,128)(2,1)} %get-tuple-element.70) | copy-start | bytes 7077892
  72.6 3.3 %collective-permute-start.16 = (f32[2]{0:T(128)S(1)}, f32[2]{0:T(128)S(1)}, u32[]{:S(2)}, u32[]{:S(2)}) collective-permute-start(f32[2]{0:T(128)S(1)} %add.159), channel_id=1, source_target_pairs={{0,32},{1,33},{2,34},{3,35},{4,36},{5,37},{6,38},{7,39},{8,40},{9,... | collective-permute-start | bytes 32 | tf_op jit(solution)/shard_map/ppermute | solution.py:32
  77.5 1.5 %copy-start = (f32[512,1152]{1,0:T(8,128)}, f32[512,1152]{1,0:T(8,128)S(1)}, u32[]{:S(2)}) copy-start(f32[512,1152]{1,0:T(8,128)S(1)} %convolution_add_fusion) | copy-start | bytes 7077892
  79.1 7.8 %collective-permute-start.18 = (f32[2]{0:T(128)S(1)}, f32[2]{0:T(128)S(1)}, u32[]{:S(2)}, u32[]{:S(2)}) collective-permute-start(f32[2]{0:T(128)S(1)} %add.161), channel_id=1, source_target_pairs={{0,64},{1,65},{2,66},{3,67},{4,68},{5,69},{6,70},{7,71},{8,72},{9,... | collective-permute-start | bytes 32 | tf_op jit(solution)/shard_map/ppermute | solution.py:32
  82.2 44.9 %all-to-all-start = ((f16[16,64,1152]{2,1,0:T(8,128)(2,1)}), f16[16,64,1152]{2,1,0:T(8,128)(2,1)}, u32[]{:S(2)}, u32[]{:S(2)}) async-start(f16[16,64,1152]{2,1,0:T(8,128)(2,1)} %bitcast.37), calls=%async_computation | async-start | bytes 4718592 | tf_op jit(solution)/shard_map/all_to_all | solution.py:247
  86.9 29.0 %copy-start.5 = (f32[64]{0:T(128)S(1)}, f32[64]{0:T(128)}, u32[]{:S(2)}) copy-start(f32[64]{0:T(128)} %multiply_reduce-precision_fusion) | copy-start | bytes 772
  87.2 31.3 %collective-permute-start.25 = (f16[136,1152]{1,0:T(8,128)(2,1)S(1)}, f16[136,1152]{1,0:T(8,128)(2,1)S(1)}, u32[]{:S(2)}, u32[]{:S(2)}) collective-permute-start(f16[136,1152]{1,0:T(8,128)(2,1)S(1)} %pad_maximum_fusion.4), channel_id=1, source_target_pairs={{0,16},{1,113},{2,18},{3,115},{4,20},{5,117},{6,22},{7,119},{8,24}... | collective-permute-start | bytes 940040 | tf_op jit(solution)/shard_map/ppermute | solution.py:32
  88.0 30.5 %collective-permute-start.24 = (f16[136,1152]{1,0:T(8,128)(2,1)S(1)}, f16[136,1152]{1,0:T(8,128)(2,1)S(1)}, u32[]{:S(2)}, u32[]{:S(2)}) collective-permute-start(f16[136,1152]{1,0:T(8,128)(2,1)S(1)} %pad_maximum_fusion.3), channel_id=1, source_target_pairs={{0,32},{1,97},{2,34},{3,99},{4,36},{5,101},{6,38},{7,103},{8,40},{... | collective-permute-start | bytes 940040 | tf_op jit(solution)/shard_map/ppermute | solution.py:32
  88.7 29.9 %collective-permute-start.23 = (f16[136,1152]{1,0:T(8,128)(2,1)S(1)}, f16[136,1152]{1,0:T(8,128)(2,1)S(1)}, u32[]{:S(2)}, u32[]{:S(2)}) collective-permute-start(f16[136,1152]{1,0:T(8,128)(2,1)S(1)} %pad_maximum_fusion.2), channel_id=1, source_target_pairs={{0,48},{1,81},{2,50},{3,83},{4,52},{5,85},{6,54},{7,87},{8,56},{9,... | collective-permute-start | bytes 940040 | tf_op jit(solution)/shard_map/ppermute | solution.py:32
  91.2 9.0 %collective-permute-start.19 = (f32[1026]{0:T(1024)S(1)}, f32[1026]{0:T(1024)S(1)}, u32[]{:S(2)}, u32[]{:S(2)}) collective-permute-start(f32[1026]{0:T(1024)S(1)} %pad_maximum_fusion.9), channel_id=1, source_target_pairs={{0,2},{1,3},{2,0},{3,1},{4,6},{5,7},{6,4},{7,5},{8,10},{9,11},{10,... | collective-permute-start | bytes 12320 | tf_op jit(solution)/shard_map/ppermute | solution.py:32
  92.3 26.2 %collective-permute-start.22 = (f16[72,1152]{1,0:T(8,128)(2,1)S(1)}, f16[72,1152]{1,0:T(8,128)(2,1)S(1)}, u32[]{:S(2)}, u32[]{:S(2)}) collective-permute-start(f16[72,1152]{1,0:T(8,128)(2,1)S(1)} %pad_maximum_fusion.8), channel_id=1, source_target_pairs={{0,64},{1,65},{2,66},{3,67},{4,68},{5,69},{6,70},{7,71},{8,72},{9,... | collective-permute-start | bytes 497672 | tf_op jit(solution)/shard_map/ppermute | solution.py:32
  100.1 14.2 %collective-permute-start.20 = (f32[1026]{0:T(1024)S(1)}, f32[1026]{0:T(1024)S(1)}, u32[]{:S(2)}, u32[]{:S(2)}) collective-permute-start(f32[1026]{0:T(1024)S(1)} %fusion.46), channel_id=1, source_target_pairs={{0,4},{1,5},{2,6},{3,7},{4,0},{5,1},{6,2},{7,3},{8,12},{9,13},{10,... | collective-permute-start | bytes 12320 | tf_op jit(solution)/shard_map/ppermute | solution.py:32
  114.4 4.1 %collective-permute-start.21 = (f32[1026]{0:T(1024)S(1)}, f32[1026]{0:T(1024)S(1)}, u32[]{:S(2)}, u32[]{:S(2)}) collective-permute-start(f32[1026]{0:T(1024)S(1)} %add.165), channel_id=1, source_target_pairs={{0,130},{1,131},{2,128},{3,129},{4,134},{5,135},{6,132},{7,133},{8... | collective-permute-start | bytes 12320 | tf_op jit(solution)/shard_map/ppermute | solution.py:32
  118.5 7.5 %collective-permute-start.27 = (f32[1026]{0:T(1024)S(1)}, f32[1026]{0:T(1024)S(1)}, u32[]{:S(2)}, u32[]{:S(2)}) collective-permute-start(f32[1026]{0:T(1024)S(1)} %add.166), channel_id=1, source_target_pairs={{0,8},{1,9},{2,10},{3,11},{4,12},{5,13},{6,14},{7,15},{8,0},{9,1},... | collective-permute-start | bytes 12320 | tf_op jit(solution)/shard_map/ppermute | solution.py:32
  121.1 8.0 %collective-permute-start.26 = (f32[72,1152]{1,0:T(8,128)S(1)}, f32[72,1152]{1,0:T(8,128)S(1)}, u32[]{:S(2)}, u32[]{:S(2)}) collective-permute-start(f32[72,1152]{1,0:T(8,128)S(1)} %pad_maximum_fusion.1), channel_id=1, source_target_pairs={{0,1},{1,0},{2,3},{3,2},{4,5},{5,4},{6,7},{7,6},{8,9},{9,8},{10,11... | collective-permute-start | bytes 995336 | tf_op jit(solution)/shard_map/ppermute | solution.py:32

commit v8 on v7

--- a/solution.py
+++ b/solution.py
@@ -233,7 +233,7 @@
     met = send(jnp.concatenate([li[512:], both]), fc=1)
     met, weights = tied(met, weights)
     li_half, both = li[:512] + met[:512], both + met[512:]
-    both = both + send(both, fz=1)
+    both = both + send(both, fz=4)
     others = jnp.dot(weights[512:], texts, preferred_element_type=f32).astype(f16)
     loss_rows = [parts_of(li_half[k * 128 - Q : k * 128 + Q]) for k in (1, 2, 3)]
     loss_rows = [extra_rows(parts, width) for parts in (*loss_rows, parts_of(li_half[448:]))]
@@ -245,7 +245,7 @@
     ).astype(f16)
     both, gt16, rows_met = tied(both, gt16, rows_met)
     back_xy = lax.all_to_all(gt16, ("yh", "x", "yl"), 0, 0, tiled=True)
-    both = both + send(both, fz=4)
+    both = both + send(both, fz=1)
     half = jnp.dot(weights[:512], texts, preferred_element_type=f32) + rows_met.astype(f32)
     flight = half[Q:].astype(f16)
     both, half, flight = tied(both, half, flight)

time: 132 us -> 132 us (level)
  starting transfers between devices: 63.1 us -> 64.8 us
  waiting for transfers between devices: 30.8 us -> 29.4 us
    ppermute x28, starting transfers between devices: 58.5 us -> 60.1 us  [send(): return lax.ppermute(value, AXES, pairs)]
    ppermute x28, waiting for transfers between devices: 30.8 us -> 29.4 us  [send(): return lax.ppermute(value, AXES, pairs)]
  transfers between devices with their start and end apart: 29 -> 29, of which waited for: 8 -> 9; matrix products, arithmetic and copies ran while one was open for 15% -> 15% of each run, Pallas kernels for 0% -> 0%
where the time goes in v8:
time: 132 us; the launch traced here: 131 us
  starting transfers between devices  64.8 us (49%)
  waiting for transfers between devices  29.4 us (22%)
  other arithmetic  10.1 us (8%)
  matrix products  9.42 us (7%)
  Pallas kernels  7.57 us (6%)
  local copies, waits for them, and re-layouts  6.17 us (5%)
  between operations  3.01 us (2%)
    ppermute x28, starting transfers between devices, send(): return lax.ppermute(value, AXES, pairs)  60.1 us
    ppermute x28, waiting for transfers between devices, send(): return lax.ppermute(value, AXES, pairs)  29.4 us
    pallas_call x1, Pallas kernels, pairs_on_device(): pl.pallas_call(pair_kernel, out_shape=(pltpu.HBM((1024, 1024), jnp.bfloat...  6.51 us
    all_to_all x1, starting transfers between devices, per_device(): back_xy = lax.all_to_all(gt16, ('yh', 'x', 'yl'), 0, 0, tiled=True)  4.66 us
    dot_general x1, matrix products, per_device(): lax.dot_general(weights, images, (((0,), (0,)), ((), ())), preferred_elem...  4.23 us
    dot_general x1, matrix products, per_device(): jnp.dot(weights[512:], texts, preferred_element_type=f32).astype(f16)  3.65 us
  transfers between devices with their start and end apart: 29, of which 9 were waited for; matrix products, arithmetic and copies ran while one was open for 15% of the time, Pallas kernels for 0%

profile of v8, /device:TPU:1, one launch (start us, length us, event | category | flops | bytes accessed | tf_op | source)
XLA Modules:
  0.0 130.5 jit_solution(6760400754316459226)
XLA Ops:
  0.7 1.1 constant_dynamic-slice_fusion.3
  1.8 0.1 fusion.4
  1.9 0.1 fusion.5.refs_6_
  2.0 2.1 %collective-permute-start.1 = (bf16[128,1152]{1,0:T(8,128)(2,1)S(1)}, bf16[128,1152]{1,0:T(8,128)(2,1)S(1)}, u32[]{:S(2)}, u32[]{:S(2)}) collective-permute-start(bf16[128,1152]{1,0:T(8,128)(2,1)S(1)} %fusion.5.refs_6_), channel_id=1, source_target_pairs={{0,4},{1,5},{2,6},{3,7},{4,8},{5,9},{6,10},{7,11},{8,12},{9,13},{1... | collective-permute-start | bytes 884744 | tf_op jit(solution)/shard_map/ppermute | solution.py:32
  4.2 1.4 %collective-permute-start.2 = (bf16[128,1152]{1,0:T(8,128)(2,1)S(1)}, bf16[128,1152]{1,0:T(8,128)(2,1)S(1)}, u32[]{:S(2)}, u32[]{:S(2)}) collective-permute-start(bf16[128,1152]{1,0:T(8,128)(2,1)S(1)} %fusion.5.refs_6_), channel_id=1, source_target_pairs={{0,12},{1,13},{2,14},{3,15},{4,0},{5,1},{6,2},{7,3},{8,4},{9,5},{1... | collective-permute-start | bytes 884744 | tf_op jit(solution)/shard_map/ppermute | solution.py:32
  5.5 2.8 %collective-permute-start.3 = (bf16[128,1152]{1,0:T(8,128)(2,1)S(1)}, bf16[128,1152]{1,0:T(8,128)(2,1)}, u32[]{:S(2)}, u32[]{:S(2)}) collective-permute-start(bf16[128,1152]{1,0:T(8,128)(2,1)S(1)} %fusion.5.refs_6_), channel_id=1, source_target_pairs={{0,130},{1,131},{2,128},{3,129},{4,134},{5,135},{6,132},{7,133},{8... | collective-permute-start | bytes 884744 | tf_op jit(solution)/shard_map/ppermute | solution.py:32
  8.4 1.1 fusion.2
  9.5 1.1 fusion.3.refs_0_
  10.6 5.7 %collective-permute-start = (bf16[128,1152]{1,0:T(8,128)(2,1)S(1)}, bf16[128,1152]{1,0:T(8,128)(2,1)S(1)}, u32[]{:S(2)}, u32[]{:S(2)}) collective-permute-start(bf16[128,1152]{1,0:T(8,128)(2,1)S(1)} %fusion.3.refs_0_), channel_id=1, source_target_pairs={{0,16},{1,113},{2,18},{3,115},{4,20},{5,117},{6,22},{7,119},{8,24}... | collective-permute-start | bytes 884744 | tf_op jit(solution)/shard_map/ppermute | solution.py:32
  16.2 1.5 %collective-permute-start.6 = (bf16[64,1152]{1,0:T(8,128)(2,1)S(1)}, bf16[64,1152]{1,0:T(8,128)(2,1)S(1)}, u32[]{:S(2)}, u32[]{:S(2)}) collective-permute-start(bf16[64,1152]{1,0:T(8,128)(2,1)S(1)} %constant_dynamic-slice_fusion.1), channel_id=1, source_target_pairs={{0,64},{1,65},{2,66},{3,67},{4,68},{5,69},{6,70},{7,71},{8,72},{9,... | collective-permute-start | bytes 442376 | tf_op jit(solution)/shard_map/ppermute | solution.py:32
  17.7 0.1 fusion.7
  17.8 0.1 fusion.6
  19.3 0.2 multiply_reduce_fusion
  19.6 6.6 %collective-permute-done.refs_1_ = bf16[128,1152]{1,0:T(8,128)(2,1)S(1)} collective-permute-done((bf16[128,1152]{1,0:T(8,128)(2,1)S(1)}, bf16[128,1152]{1,0:T(8,128)(2,1)S(1)}, u32[]{:S(2)}, u32[]{:S(2)}) %collective-permute-start) | collective-permute-done | bytes 294944 | tf_op jit(solution)/shard_map/ppermute | solution.py:32
  26.2 1.3 %collective-permute-start.10 = (bf16[64,1152]{1,0:T(8,128)(2,1)S(1)}, bf16[64,1152]{1,0:T(8,128)(2,1)S(1)}, u32[]{:S(2)}, u32[]{:S(2)}) collective-permute-start(bf16[64,1152]{1,0:T(8,128)(2,1)S(1)} %slice.77), channel_id=1, source_target_pairs={{0,12},{1,13},{2,14},{3,15},{4,0},{5,1},{6,2},{7,3},{8,4},{9,5},{1... | collective-permute-start | bytes 442376 | tf_op jit(solution)/shard_map/ppermute | solution.py:32
  27.6 0.6 multiply_reduce_fusion.1
  28.2 3.4 %collective-permute-start.4 = (bf16[128,1152]{1,0:T(8,128)(2,1)S(1)}, bf16[128,1152]{1,0:T(8,128)(2,1)S(1)}, u32[]{:S(2)}, u32[]{:S(2)}) collective-permute-start(bf16[128,1152]{1,0:T(8,128)(2,1)S(1)} %collective-permute-done.refs_1_), channel_id=1, source_target_pairs={{0,16},{1,113},{2,18},{3,115},{4,20},{5,117},{6,22},{7,119},{8,24}... | collective-permute-start | bytes 884744 | tf_op jit(solution)/shard_map/ppermute | solution.py:32
  31.6 0.7 slice.76
  32.3 2.7 %collective-permute-start.8 = (bf16[128,1152]{1,0:T(8,128)(2,1)}, bf16[128,1152]{1,0:T(8,128)(2,1)S(1)}, u32[]{:S(2)}, u32[]{:S(2)}) collective-permute-start(bf16[128,1152]{1,0:T(8,128)(2,1)} %collective-permute-done.3.refs_10_), channel_id=1, source_target_pairs={{0,12},{1,13},{2,14},{3,15},{4,0},{5,1},{6,2},{7,3},{8,4},{9,5},{1... | collective-permute-start | bytes 884744 | tf_op jit(solution)/shard_map/ppermute | solution.py:32
  35.0 0.7 copy-done.3
  35.6 0.6 multiply_reduce-precision_fusion
  36.9 1.3 pad_maximum_fusion.12
  38.2 4.9 %collective-permute-done.9 = bf16[64,1152]{1,0:T(8,128)(2,1)} collective-permute-done((bf16[64,1152]{1,0:T(8,128)(2,1)}, bf16[64,1152]{1,0:T(8,128)(2,1)}, u32[]{:S(2)}, u32[]{:S(2)}) %collective-permute-start.9) | collective-permute-done | bytes 147488 | tf_op jit(solution)/shard_map/ppermute | solution.py:32
  43.1 2.8 %collective-permute-start.11 = (bf16[448,1152]{1,0:T(8,128)(2,1)S(1)}, bf16[448,1152]{1,0:T(8,128)(2,1)S(1)}, u32[]{:S(2)}, u32[]{:S(2)}) collective-permute-start(bf16[448,1152]{1,0:T(8,128)(2,1)S(1)} %pad_maximum_fusion), channel_id=1, source_target_pairs={{0,1},{1,0},{2,3},{3,2},{4,5},{5,4},{6,7},{7,6},{8,9},{9,8},{10,11... | collective-permute-start | bytes 3096584 | tf_op jit(solution)/shard_map/ppermute | solution.py:32
  46.1 2.9 %collective-permute-start.13 = (bf16[64,1152]{1,0:T(8,128)(2,1)S(1)}, bf16[64,1152]{1,0:T(8,128)(2,1)S(1)}, u32[]{:S(2)}, u32[]{:S(2)}) collective-permute-start(bf16[64,1152]{1,0:T(8,128)(2,1)S(1)} %slice.79), channel_id=1, source_target_pairs={{0,12},{1,13},{2,14},{3,15},{4,0},{5,1},{6,2},{7,3},{8,4},{9,5},{1... | collective-permute-start | bytes 442376 | tf_op jit(solution)/shard_map/ppermute | solution.py:32
  49.1 0.9 pad_maximum_fusion.6.refs_9_
  50.0 2.8 %collective-permute-done.12 = bf16[64,1152]{1,0:T(8,128)(2,1)S(1)} collective-permute-done((bf16[64,1152]{1,0:T(8,128)(2,1)S(1)}, bf16[64,1152]{1,0:T(8,128)(2,1)S(1)}, u32[]{:S(2)}, u32[]{:S(2)}) %collective-permute-start.12) | collective-permute-done | bytes 147488 | tf_op jit(solution)/shard_map/ppermute | solution.py:32
  52.8 6.5 %pairs.1 = (bf16[1024,1024]{1,0:T(8,128)(2,1)}, bf16[1024,1152]{1,0:T(8,128)(2,1)}, bf16[1024,1152]{1,0:T(8,128)(2,1)}, f32[1024,1]{1,0:T(8,128)S(1)}, f32[1,1024]{1,0:T(1,128)S(1)}, /*index=5*/f32[2,1024]{1,0:T(2,128)S(1)}) custom-call(f32[2]{0:T(128)S(1)} %pad_maximum_fusion.11.par_ref, bf16[128,1152]{1,0:T(8,128)(2,1)S(1)} %fusion.3.refs_0_, ...), custom_call_target="tpu_custom_call" | custom-call | flops 2415919104 | bytes 12582912 | tf_op jit(solution)/shard_map/pairs/pallas_call | solution.py:125
  59.3 0.2 slice_reduce_fusion
  59.6 0.1 reduce_sum.88
  59.7 0.9 collective-permute-start.14
  60.6 0.8 collective-permute-done.14
  61.5 0.1 fusion.38
  61.6 1.2 collective-permute-start.15
  62.9 3.7 %convolution_convert_fusion.1 = f16[512,1152]{1,0:T(8,128)(2,1)S(1)} fusion(bf16[1024,1152]{1,0:T(8,128)(2,1)} %get-tuple-element.70, bf16[1024,1024]{1,0:T(8,128)(2,1)} %get-tuple-element.69), kind=kOutput, calls=%fused_computation.3 | convolution fusion | flops 1208549376 | bytes 4587520 | tf_op jit(solution)/shard_map/dot_general | solution.py:237
  66.6 1.5 %collective-permute-done.15 = f32[2]{0:T(128)S(1)} collective-permute-done((f32[2]{0:T(128)S(1)}, f32[2]{0:T(128)S(1)}, u32[]{:S(2)}, u32[]{:S(2)}) %collective-permute-start.15) | collective-permute-done | bytes 40 | tf_op jit(solution)/shard_map/ppermute | solution.py:32
  68.0 1.5 %collective-permute-start.17 = (f16[512,1152]{1,0:T(8,128)(2,1)S(1)}, f16[512,1152]{1,0:T(8,128)(2,1)S(1)}, u32[]{:S(2)}, u32[]{:S(2)}) collective-permute-start(f16[512,1152]{1,0:T(8,128)(2,1)S(1)} %convolution_convert_fusion.1), channel_id=1, source_target_pairs={{0,1},{1,0},{2,3},{3,2},{4,5},{5,4},{6,7},{7,6},{8,9},{9,8},{10,11... | collective-permute-start | bytes 3538952 | tf_op jit(solution)/shard_map/ppermute | solution.py:32
  69.5 4.2 %convolution_convert_fusion = f16[1024,1152]{1,0:T(8,128)(2,1)} fusion(bf16[1024,1024]{1,0:T(8,128)(2,1)S(1)} %copy-done.8, bf16[1024,1152]{1,0:T(8,128)(2,1)S(1)} %copy-done.9), kind=kOutput, calls=%fused_computation.1 | convolution fusion | flops 2417098752 | bytes 6815744 | tf_op jit(solution)/shard_map/dot_general | solution.py:243
  73.8 2.4 %collective-permute-start.16 = (f32[2]{0:T(128)S(1)}, f32[2]{0:T(128)S(1)}, u32[]{:S(2)}, u32[]{:S(2)}) collective-permute-start(f32[2]{0:T(128)S(1)} %add.159), channel_id=1, source_target_pairs={{0,32},{1,33},{2,34},{3,35},{4,36},{5,37},{6,38},{7,39},{8,40},{9,... | collective-permute-start | bytes 32 | tf_op jit(solution)/shard_map/ppermute | solution.py:32
  76.1 0.9 collective-permute-done.16
  77.1 1.5 %convolution_add_fusion = f32[512,1152]{1,0:T(8,128)S(1)} fusion(bf16[1024,1152]{1,0:T(8,128)(2,1)S(1)} %copy-done.7, f16[512,1152]{1,0:T(8,128)(2,1)S(1)} %collective-permute-done.17, bf16[1024,1024]{1,0:T(8,128)(2,1)S(1)} %copy-done.8), kind=kOutput, calls=%fused_computation.2 | convolution fusion | flops 1209139200 | bytes 6946816 | tf_op jit(solution)/shard_map/dot_general | solution.py:249
  78.6 1.4 %copy-done = f32[512,1152]{1,0:T(8,128)} copy-done((f32[512,1152]{1,0:T(8,128)}, f32[512,1152]{1,0:T(8,128)S(1)}, u32[]{:S(2)}) %copy-start) | copy-done | bytes 2359320
  80.1 0.1 slice_convert_fusion
  80.2 2.3 %collective-permute-start.18 = (f32[2]{0:T(128)S(1)}, f32[2]{0:T(128)S(1)}, u32[]{:S(2)}, u32[]{:S(2)}) collective-permute-start(f32[2]{0:T(128)S(1)} %add.161), channel_id=1, source_target_pairs={{0,16},{1,17},{2,18},{3,19},{4,20},{5,21},{6,22},{7,23},{8,24},{9,... | collective-permute-start | bytes 32 | tf_op jit(solution)/shard_map/ppermute | solution.py:32
  82.5 4.7 %all-to-all-start = ((f16[16,64,1152]{2,1,0:T(8,128)(2,1)}), f16[16,64,1152]{2,1,0:T(8,128)(2,1)}, u32[]{:S(2)}, u32[]{:S(2)}) async-start(f16[16,64,1152]{2,1,0:T(8,128)(2,1)} %bitcast.37), calls=%async_computation | async-start | bytes 4718592 | tf_op jit(solution)/shard_map/all_to_all | solution.py:247
  87.2 0.2 fusion.49
  87.5 0.4 collective-permute-start.25
  88.0 1.9 %collective-permute-start.24 = (f16[136,1152]{1,0:T(8,128)(2,1)S(1)}, f16[136,1152]{1,0:T(8,128)(2,1)S(1)}, u32[]{:S(2)}, u32[]{:S(2)}) collective-permute-start(f16[136,1152]{1,0:T(8,128)(2,1)S(1)} %pad_maximum_fusion.3), channel_id=1, source_target_pairs={{0,32},{1,97},{2,34},{3,99},{4,36},{5,101},{6,38},{7,103},{8,40},{... | collective-permute-start | bytes 940040 | tf_op jit(solution)/shard_map/ppermute | solution.py:32
  90.0 1.6 %collective-permute-start.23 = (f16[136,1152]{1,0:T(8,128)(2,1)S(1)}, f16[136,1152]{1,0:T(8,128)(2,1)S(1)}, u32[]{:S(2)}, u32[]{:S(2)}) collective-permute-start(f16[136,1152]{1,0:T(8,128)(2,1)S(1)} %pad_maximum_fusion.2), channel_id=1, source_target_pairs={{0,48},{1,81},{2,50},{3,83},{4,52},{5,85},{6,54},{7,87},{8,56},{9,... | collective-permute-start | bytes 940040 | tf_op jit(solution)/shard_map/ppermute | solution.py:32
  91.6 1.1 collective-permute-start.19
  92.7 3.0 %collective-permute-start.22 = (f16[72,1152]{1,0:T(8,128)(2,1)S(1)}, f16[72,1152]{1,0:T(8,128)(2,1)S(1)}, u32[]{:S(2)}, u32[]{:S(2)}) collective-permute-start(f16[72,1152]{1,0:T(8,128)(2,1)S(1)} %pad_maximum_fusion.8), channel_id=1, source_target_pairs={{0,64},{1,65},{2,66},{3,67},{4,68},{5,69},{6,70},{7,71},{8,72},{9,... | collective-permute-start | bytes 497672 | tf_op jit(solution)/shard_map/ppermute | solution.py:32
  95.7 4.7 %collective-permute-done.19 = f32[1026]{0:T(1024)S(1)} collective-permute-done((f32[1026]{0:T(1024)S(1)}, f32[1026]{0:T(1024)S(1)}, u32[]{:S(2)}, u32[]{:S(2)}) %collective-permute-start.19) | collective-permute-done | bytes 4136 | tf_op jit(solution)/shard_map/ppermute | solution.py:32
  100.5 8.7 %collective-permute-start.20 = (f32[1026]{0:T(1024)S(1)}, f32[1026]{0:T(1024)S(1)}, u32[]{:S(2)}, u32[]{:S(2)}) collective-permute-start(f32[1026]{0:T(1024)S(1)} %fusion.46), channel_id=1, source_target_pairs={{0,4},{1,5},{2,6},{3,7},{4,0},{5,1},{6,2},{7,3},{8,12},{9,13},{10,... | collective-permute-start | bytes 12320 | tf_op jit(solution)/shard_map/ppermute | solution.py:32
  109.2 5.5 %collective-permute-done.20 = f32[1026]{0:T(1024)S(1)} collective-permute-done((f32[1026]{0:T(1024)S(1)}, f32[1026]{0:T(1024)S(1)}, u32[]{:S(2)}, u32[]{:S(2)}) %collective-permute-start.20) | collective-permute-done | bytes 4136 | tf_op jit(solution)/shard_map/ppermute | solution.py:32
  114.7 1.3 collective-permute-start.21
  116.3 1.0 slice.93.half
  117.3 1.6 %collective-permute-done.21 = f32[1026]{0:T(1024)S(1)} collective-permute-done((f32[1026]{0:T(1024)S(1)}, f32[1026]{0:T(1024)S(1)}, u32[]{:S(2)}, u32[]{:S(2)}) %collective-permute-start.21) | collective-permute-done | bytes 4136 | tf_op jit(solution)/shard_map/ppermute | solution.py:32
  118.9 2.3 %collective-permute-start.27 = (f32[1026]{0:T(1024)S(1)}, f32[1026]{0:T(1024)S(1)}, u32[]{:S(2)}, u32[]{:S(2)}) collective-permute-start(f32[1026]{0:T(1024)S(1)} %add.166), channel_id=1, source_target_pairs={{0,8},{1,9},{2,10},{3,11},{4,12},{5,13},{6,14},{7,15},{8,0},{9,1},... | collective-permute-start | bytes 12320 | tf_op jit(solution)/shard_map/ppermute | solution.py:32
  121.2 0.1 convert_add_fusion.arrived
  121.4 4.9 %collective-permute-start.26 = (f32[72,1152]{1,0:T(8,128)S(1)}, f32[72,1152]{1,0:T(8,128)S(1)}, u32[]{:S(2)}, u32[]{:S(2)}) collective-permute-start(f32[72,1152]{1,0:T(8,128)S(1)} %pad_maximum_fusion.1), channel_id=1, source_target_pairs={{0,1},{1,0},{2,3},{3,2},{4,5},{5,4},{6,7},{7,6},{8,9},{9,8},{10,11... | collective-permute-start | bytes 995336 | tf_op jit(solution)/shard_map/ppermute | solution.py:32
  126.3 0.6 dynamic-slice_add_fusion
  126.9 0.5 slice.103
  127.4 2.0 %convert_reduce_fusion.gt = f32[64,1152]{1,0:T(8,128)S(1)} fusion(f16[16,64,1152]{2,1,0:T(8,128)(2,1)} %all-to-all-done), kind=kLoop, calls=%fused_computation | loop fusion | flops 2285568 | bytes 2654208 | tf_op jit(solution)/shard_map/reduce_sum | solution.py:264
  129.5 1.1 finish.1
  (80 shorter events, 1.3 us)
Async XLA Ops:
  0.6 17.1 %copy-start.2 = (bf16[256,1152]{1,0:T(8,128)(2,1)S(1)}, bf16[256,1152]{1,0:T(8,128)(2,1)}, u32[]{:S(2)}) copy-start(bf16[256,1152]{1,0:T(8,128)(2,1)} %param.5) | copy-start | bytes 1769476
  0.6 17.2 %copy-start.1 = (bf16[256,1152]{1,0:T(8,128)(2,1)S(1)}, bf16[256,1152]{1,0:T(8,128)(2,1)}, u32[]{:S(2)}) copy-start(bf16[256,1152]{1,0:T(8,128)(2,1)} %param.4) | copy-start | bytes 1769476
  2.0 17.5 %collective-permute-start.1 = (bf16[128,1152]{1,0:T(8,128)(2,1)S(1)}, bf16[128,1152]{1,0:T(8,128)(2,1)S(1)}, u32[]{:S(2)}, u32[]{:S(2)}) collective-permute-start(bf16[128,1152]{1,0:T(8,128)(2,1)S(1)} %fusion.5.refs_6_), channel_id=1, source_target_pairs={{0,4},{1,5},{2,6},{3,7},{4,8},{5,9},{6,10},{7,11},{8,12},{9,13},{1... | collective-permute-start | bytes 884744 | tf_op jit(solution)/shard_map/ppermute | solution.py:32
  4.2 15.4 %collective-permute-start.2 = (bf16[128,1152]{1,0:T(8,128)(2,1)S(1)}, bf16[128,1152]{1,0:T(8,128)(2,1)S(1)}, u32[]{:S(2)}, u32[]{:S(2)}) collective-permute-start(bf16[128,1152]{1,0:T(8,128)(2,1)S(1)} %fusion.5.refs_6_), channel_id=1, source_target_pairs={{0,12},{1,13},{2,14},{3,15},{4,0},{5,1},{6,2},{7,3},{8,4},{9,5},{1... | collective-permute-start | bytes 884744 | tf_op jit(solution)/shard_map/ppermute | solution.py:32
  5.5 14.1 %collective-permute-start.3 = (bf16[128,1152]{1,0:T(8,128)(2,1)S(1)}, bf16[128,1152]{1,0:T(8,128)(2,1)}, u32[]{:S(2)}, u32[]{:S(2)}) collective-permute-start(bf16[128,1152]{1,0:T(8,128)(2,1)S(1)} %fusion.5.refs_6_), channel_id=1, source_target_pairs={{0,130},{1,131},{2,128},{3,129},{4,134},{5,135},{6,132},{7,133},{8... | collective-permute-start | bytes 884744 | tf_op jit(solution)/shard_map/ppermute | solution.py:32
  10.6 15.6 %collective-permute-start = (bf16[128,1152]{1,0:T(8,128)(2,1)S(1)}, bf16[128,1152]{1,0:T(8,128)(2,1)S(1)}, u32[]{:S(2)}, u32[]{:S(2)}) collective-permute-start(bf16[128,1152]{1,0:T(8,128)(2,1)S(1)} %fusion.3.refs_0_), channel_id=1, source_target_pairs={{0,16},{1,113},{2,18},{3,115},{4,20},{5,117},{6,22},{7,119},{8,24}... | collective-permute-start | bytes 884744 | tf_op jit(solution)/shard_map/ppermute | solution.py:32
  16.2 16.1 %collective-permute-start.6 = (bf16[64,1152]{1,0:T(8,128)(2,1)S(1)}, bf16[64,1152]{1,0:T(8,128)(2,1)S(1)}, u32[]{:S(2)}, u32[]{:S(2)}) collective-permute-start(bf16[64,1152]{1,0:T(8,128)(2,1)S(1)} %constant_dynamic-slice_fusion.1), channel_id=1, source_target_pairs={{0,64},{1,65},{2,66},{3,67},{4,68},{5,69},{6,70},{7,71},{8,72},{9,... | collective-permute-start | bytes 442376 | tf_op jit(solution)/shard_map/ppermute | solution.py:32
  26.2 8.8 %collective-permute-start.10 = (bf16[64,1152]{1,0:T(8,128)(2,1)S(1)}, bf16[64,1152]{1,0:T(8,128)(2,1)S(1)}, u32[]{:S(2)}, u32[]{:S(2)}) collective-permute-start(bf16[64,1152]{1,0:T(8,128)(2,1)S(1)} %slice.77), channel_id=1, source_target_pairs={{0,12},{1,13},{2,14},{3,15},{4,0},{5,1},{6,2},{7,3},{8,4},{9,5},{1... | collective-permute-start | bytes 442376 | tf_op jit(solution)/shard_map/ppermute | solution.py:32
  28.2 14.8 %collective-permute-start.4 = (bf16[128,1152]{1,0:T(8,128)(2,1)S(1)}, bf16[128,1152]{1,0:T(8,128)(2,1)S(1)}, u32[]{:S(2)}, u32[]{:S(2)}) collective-permute-start(bf16[128,1152]{1,0:T(8,128)(2,1)S(1)} %collective-permute-done.refs_1_), channel_id=1, source_target_pairs={{0,16},{1,113},{2,18},{3,115},{4,20},{5,117},{6,22},{7,119},{8,24}... | collective-permute-start | bytes 884744 | tf_op jit(solution)/shard_map/ppermute | solution.py:32
  31.6 11.4 %collective-permute-start.5 = (bf16[128,1152]{1,0:T(8,128)(2,1)S(1)}, bf16[128,1152]{1,0:T(8,128)(2,1)S(1)}, u32[]{:S(2)}, u32[]{:S(2)}) collective-permute-start(bf16[128,1152]{1,0:T(8,128)(2,1)S(1)} %collective-permute-done.refs_1_), channel_id=1, source_target_pairs={{0,32},{1,97},{2,34},{3,99},{4,36},{5,101},{6,38},{7,103},{8,40},{... | collective-permute-start | bytes 884744 | tf_op jit(solution)/shard_map/ppermute | solution.py:32
  31.6 11.4 %collective-permute-start.7 = (bf16[128,1152]{1,0:T(8,128)(2,1)}, bf16[128,1152]{1,0:T(8,128)(2,1)S(1)}, u32[]{:S(2)}, u32[]{:S(2)}) collective-permute-start(bf16[128,1152]{1,0:T(8,128)(2,1)} %collective-permute-done.3.refs_10_), channel_id=1, source_target_pairs={{0,4},{1,5},{2,6},{3,7},{4,8},{5,9},{6,10},{7,11},{8,12},{9,13},{1... | collective-permute-start | bytes 884744 | tf_op jit(solution)/shard_map/ppermute | solution.py:32
  32.3 10.7 %collective-permute-start.8 = (bf16[128,1152]{1,0:T(8,128)(2,1)}, bf16[128,1152]{1,0:T(8,128)(2,1)S(1)}, u32[]{:S(2)}, u32[]{:S(2)}) collective-permute-start(bf16[128,1152]{1,0:T(8,128)(2,1)} %collective-permute-done.3.refs_10_), channel_id=1, source_target_pairs={{0,12},{1,13},{2,14},{3,15},{4,0},{5,1},{6,2},{7,3},{8,4},{9,5},{1... | collective-permute-start | bytes 884744 | tf_op jit(solution)/shard_map/ppermute | solution.py:32
  35.0 0.7 copy-start.3
  35.6 7.4 %collective-permute-start.9 = (bf16[64,1152]{1,0:T(8,128)(2,1)}, bf16[64,1152]{1,0:T(8,128)(2,1)}, u32[]{:S(2)}, u32[]{:S(2)}) collective-permute-start(bf16[64,1152]{1,0:T(8,128)(2,1)} %slice.76), channel_id=1, source_target_pairs={{0,4},{1,5},{2,6},{3,7},{4,8},{5,9},{6,10},{7,11},{8,12},{9,13},{1... | collective-permute-start | bytes 442376 | tf_op jit(solution)/shard_map/ppermute | solution.py:32
  35.6 13.4 %copy-start.4 = (bf16[64,1152]{1,0:T(8,128)(2,1)S(1)}, bf16[64,1152]{1,0:T(8,128)(2,1)}, u32[]{:S(2)}) copy-start(bf16[64,1152]{1,0:T(8,128)(2,1)} %copy-done.3) | copy-start | bytes 442372
  43.1 9.7 %collective-permute-start.11 = (bf16[448,1152]{1,0:T(8,128)(2,1)S(1)}, bf16[448,1152]{1,0:T(8,128)(2,1)S(1)}, u32[]{:S(2)}, u32[]{:S(2)}) collective-permute-start(bf16[448,1152]{1,0:T(8,128)(2,1)S(1)} %pad_maximum_fusion), channel_id=1, source_target_pairs={{0,1},{1,0},{2,3},{3,2},{4,5},{5,4},{6,7},{7,6},{8,9},{9,8},{10,11... | collective-permute-start | bytes 3096584 | tf_op jit(solution)/shard_map/ppermute | solution.py:32
  46.0 6.8 %collective-permute-start.12 = (bf16[64,1152]{1,0:T(8,128)(2,1)S(1)}, bf16[64,1152]{1,0:T(8,128)(2,1)S(1)}, u32[]{:S(2)}, u32[]{:S(2)}) collective-permute-start(bf16[64,1152]{1,0:T(8,128)(2,1)S(1)} %slice.78), channel_id=1, source_target_pairs={{0,4},{1,5},{2,6},{3,7},{4,8},{5,9},{6,10},{7,11},{8,12},{9,13},{1... | collective-permute-start | bytes 442376 | tf_op jit(solution)/shard_map/ppermute | solution.py:32
  46.1 6.6 %collective-permute-start.13 = (bf16[64,1152]{1,0:T(8,128)(2,1)S(1)}, bf16[64,1152]{1,0:T(8,128)(2,1)S(1)}, u32[]{:S(2)}, u32[]{:S(2)}) collective-permute-start(bf16[64,1152]{1,0:T(8,128)(2,1)S(1)} %slice.79), channel_id=1, source_target_pairs={{0,12},{1,13},{2,14},{3,15},{4,0},{5,1},{6,2},{7,3},{8,4},{9,5},{1... | collective-permute-start | bytes 442376 | tf_op jit(solution)/shard_map/ppermute | solution.py:32
  52.8 6.9 %copy-start.6 = (f32[2]{0:T(128)S(1)}, f32[2]{0:T(128)}, u32[]{:S(2)}) copy-start(f32[2]{0:T(128)} %pad_maximum_fusion.12) | copy-start | bytes 28
  59.7 1.7 %collective-permute-start.14 = (f32[514]{0:T(1024)S(1)}, f32[514]{0:T(1024)S(1)}, u32[]{:S(2)}, u32[]{:S(2)}) collective-permute-start(f32[514]{0:T(1024)S(1)} %pad_maximum_fusion.10), channel_id=1, source_target_pairs={{0,1},{1,0},{2,3},{3,2},{4,5},{5,4},{6,7},{7,6},{8,9},{9,8},{10,11... | collective-permute-start | bytes 6176 | tf_op jit(solution)/shard_map/ppermute | solution.py:32
  61.6 6.4 %collective-permute-start.15 = (f32[2]{0:T(128)S(1)}, f32[2]{0:T(128)S(1)}, u32[]{:S(2)}, u32[]{:S(2)}) collective-permute-start(f32[2]{0:T(128)S(1)} %slice_add_fusion.1), channel_id=1, source_target_pairs={{0,64},{1,65},{2,66},{3,67},{4,68},{5,69},{6,70},{7,71},{8,72},{9,... | collective-permute-start | bytes 32 | tf_op jit(solution)/shard_map/ppermute | solution.py:32
  62.9 6.7 %copy-start.8 = (bf16[1024,1024]{1,0:T(8,128)(2,1)S(1)}, bf16[1024,1024]{1,0:T(8,128)(2,1)}, u32[]{:S(2)}) copy-start(bf16[1024,1024]{1,0:T(8,128)(2,1)} %get-tuple-element.69) | copy-start | bytes 6291460
  62.9 6.7 %copy-start.9 = (bf16[1024,1152]{1,0:T(8,128)(2,1)S(1)}, bf16[1024,1152]{1,0:T(8,128)(2,1)}, u32[]{:S(2)}) copy-start(bf16[1024,1152]{1,0:T(8,128)(2,1)} %get-tuple-element.72) | copy-start | bytes 7077892
  68.0 9.0 %collective-permute-start.17 = (f16[512,1152]{1,0:T(8,128)(2,1)S(1)}, f16[512,1152]{1,0:T(8,128)(2,1)S(1)}, u32[]{:S(2)}, u32[]{:S(2)}) collective-permute-start(f16[512,1152]{1,0:T(8,128)(2,1)S(1)} %convolution_convert_fusion.1), channel_id=1, source_target_pairs={{0,1},{1,0},{2,3},{3,2},{4,5},{5,4},{6,7},{7,6},{8,9},{9,8},{10,11... | collective-permute-start | bytes 3538952 | tf_op jit(solution)/shard_map/ppermute | solution.py:32
  69.5 7.5 %copy-start.7 = (bf16[1024,1152]{1,0:T(8,128)(2,1)S(1)}, bf16[1024,1152]{1,0:T(8,128)(2,1)}, u32[]{:S(2)}) copy-start(bf16[1024,1152]{1,0:T(8,128)(2,1)} %get-tuple-element.70) | copy-start | bytes 7077892
  73.8 3.3 %collective-permute-start.16 = (f32[2]{0:T(128)S(1)}, f32[2]{0:T(128)S(1)}, u32[]{:S(2)}, u32[]{:S(2)}) collective-permute-start(f32[2]{0:T(128)S(1)} %add.159), channel_id=1, source_target_pairs={{0,32},{1,33},{2,34},{3,35},{4,36},{5,37},{6,38},{7,39},{8,40},{9,... | collective-permute-start | bytes 32 | tf_op jit(solution)/shard_map/ppermute | solution.py:32
  78.6 1.5 %copy-start = (f32[512,1152]{1,0:T(8,128)}, f32[512,1152]{1,0:T(8,128)S(1)}, u32[]{:S(2)}) copy-start(f32[512,1152]{1,0:T(8,128)S(1)} %convolution_add_fusion) | copy-start | bytes 7077892
  80.2 7.0 %collective-permute-start.18 = (f32[2]{0:T(128)S(1)}, f32[2]{0:T(128)S(1)}, u32[]{:S(2)}, u32[]{:S(2)}) collective-permute-start(f32[2]{0:T(128)S(1)} %add.161), channel_id=1, source_target_pairs={{0,16},{1,17},{2,18},{3,19},{4,20},{5,21},{6,22},{7,23},{8,24},{9,... | collective-permute-start | bytes 32 | tf_op jit(solution)/shard_map/ppermute | solution.py:32
  82.5 44.9 %all-to-all-start = ((f16[16,64,1152]{2,1,0:T(8,128)(2,1)}), f16[16,64,1152]{2,1,0:T(8,128)(2,1)}, u32[]{:S(2)}, u32[]{:S(2)}) async-start(f16[16,64,1152]{2,1,0:T(8,128)(2,1)} %bitcast.37), calls=%async_computation | async-start | bytes 4718592 | tf_op jit(solution)/shard_map/all_to_all | solution.py:247
  87.2 29.0 %copy-start.5 = (f32[64]{0:T(128)S(1)}, f32[64]{0:T(128)}, u32[]{:S(2)}) copy-start(f32[64]{0:T(128)} %multiply_reduce-precision_fusion) | copy-start | bytes 772
  87.5 31.4 %collective-permute-start.25 = (f16[136,1152]{1,0:T(8,128)(2,1)S(1)}, f16[136,1152]{1,0:T(8,128)(2,1)S(1)}, u32[]{:S(2)}, u32[]{:S(2)}) collective-permute-start(f16[136,1152]{1,0:T(8,128)(2,1)S(1)} %pad_maximum_fusion.4), channel_id=1, source_target_pairs={{0,16},{1,113},{2,18},{3,115},{4,20},{5,117},{6,22},{7,119},{8,24}... | collective-permute-start | bytes 940040 | tf_op jit(solution)/shard_map/ppermute | solution.py:32
  88.0 30.9 %collective-permute-start.24 = (f16[136,1152]{1,0:T(8,128)(2,1)S(1)}, f16[136,1152]{1,0:T(8,128)(2,1)S(1)}, u32[]{:S(2)}, u32[]{:S(2)}) collective-permute-start(f16[136,1152]{1,0:T(8,128)(2,1)S(1)} %pad_maximum_fusion.3), channel_id=1, source_target_pairs={{0,32},{1,97},{2,34},{3,99},{4,36},{5,101},{6,38},{7,103},{8,40},{... | collective-permute-start | bytes 940040 | tf_op jit(solution)/shard_map/ppermute | solution.py:32
  90.0 28.9 %collective-permute-start.23 = (f16[136,1152]{1,0:T(8,128)(2,1)S(1)}, f16[136,1152]{1,0:T(8,128)(2,1)S(1)}, u32[]{:S(2)}, u32[]{:S(2)}) collective-permute-start(f16[136,1152]{1,0:T(8,128)(2,1)S(1)} %pad_maximum_fusion.2), channel_id=1, source_target_pairs={{0,48},{1,81},{2,50},{3,83},{4,52},{5,85},{6,54},{7,87},{8,56},{9,... | collective-permute-start | bytes 940040 | tf_op jit(solution)/shard_map/ppermute | solution.py:32
  91.6 8.9 %collective-permute-start.19 = (f32[1026]{0:T(1024)S(1)}, f32[1026]{0:T(1024)S(1)}, u32[]{:S(2)}, u32[]{:S(2)}) collective-permute-start(f32[1026]{0:T(1024)S(1)} %pad_maximum_fusion.9), channel_id=1, source_target_pairs={{0,2},{1,3},{2,0},{3,1},{4,6},{5,7},{6,4},{7,5},{8,10},{9,11},{10,... | collective-permute-start | bytes 12320 | tf_op jit(solution)/shard_map/ppermute | solution.py:32
  92.7 26.1 %collective-permute-start.22 = (f16[72,1152]{1,0:T(8,128)(2,1)S(1)}, f16[72,1152]{1,0:T(8,128)(2,1)S(1)}, u32[]{:S(2)}, u32[]{:S(2)}) collective-permute-start(f16[72,1152]{1,0:T(8,128)(2,1)S(1)} %pad_maximum_fusion.8), channel_id=1, source_target_pairs={{0,64},{1,65},{2,66},{3,67},{4,68},{5,69},{6,70},{7,71},{8,72},{9,... | collective-permute-start | bytes 497672 | tf_op jit(solution)/shard_map/ppermute | solution.py:32
  100.5 14.3 %collective-permute-start.20 = (f32[1026]{0:T(1024)S(1)}, f32[1026]{0:T(1024)S(1)}, u32[]{:S(2)}, u32[]{:S(2)}) collective-permute-start(f32[1026]{0:T(1024)S(1)} %fusion.46), channel_id=1, source_target_pairs={{0,4},{1,5},{2,6},{3,7},{4,0},{5,1},{6,2},{7,3},{8,12},{9,13},{10,... | collective-permute-start | bytes 12320 | tf_op jit(solution)/shard_map/ppermute | solution.py:32
  114.7 4.1 %collective-permute-start.21 = (f32[1026]{0:T(1024)S(1)}, f32[1026]{0:T(1024)S(1)}, u32[]{:S(2)}, u32[]{:S(2)}) collective-permute-start(f32[1026]{0:T(1024)S(1)} %add.165), channel_id=1, source_target_pairs={{0,130},{1,131},{2,128},{3,129},{4,134},{5,135},{6,132},{7,133},{8... | collective-permute-start | bytes 12320 | tf_op jit(solution)/shard_map/ppermute | solution.py:32
  118.9 7.4 %collective-permute-start.27 = (f32[1026]{0:T(1024)S(1)}, f32[1026]{0:T(1024)S(1)}, u32[]{:S(2)}, u32[]{:S(2)}) collective-permute-start(f32[1026]{0:T(1024)S(1)} %add.166), channel_id=1, source_target_pairs={{0,8},{1,9},{2,10},{3,11},{4,12},{5,13},{6,14},{7,15},{8,0},{9,1},... | collective-permute-start | bytes 12320 | tf_op jit(solution)/shard_map/ppermute | solution.py:32
  121.4 8.0 %collective-permute-start.26 = (f32[72,1152]{1,0:T(8,128)S(1)}, f32[72,1152]{1,0:T(8,128)S(1)}, u32[]{:S(2)}, u32[]{:S(2)}) collective-permute-start(f32[72,1152]{1,0:T(8,128)S(1)} %pad_maximum_fusion.1), channel_id=1, source_target_pairs={{0,1},{1,0},{2,3},{3,2},{4,5},{5,4},{6,7},{7,6},{8,9},{9,8},{10,11... | collective-permute-start | bytes 995336 | tf_op jit(solution)/shard_map/ppermute | solution.py:32
